TPU v7x, 32 devices: a whole 2x2x4 slice. The times are simulated.
32 devices in a mesh: pipe: 4 (over y, core), ctx: 4 (over z), tp: 2 (over x).
Axes of the slice: x: 2, y: 2, z: 4, core: 2. Of those that a mesh axis runs over, the one named last changes fastest.
Arguments:
- queries: bfloat16 [4, 512, 4096], P('pipe', 'ctx', 'tp'), may hold values from -15 to 15
- keys: bfloat16 [4, 512, 1024], P('pipe', 'ctx', 'tp'), may hold values from -5 to 5
- values: bfloat16 [4, 512, 1024], P('pipe', 'ctx', 'tp'), may hold values from -5 to 5
- span_ids: int32 [4, 8], P('pipe', 'ctx'), may hold values from 0 to 7, each once within a row
- cotangent: bfloat16 [4, 512, 4096], P('pipe', 'ctx'), may hold values from -6 to 6
Outputs:
- attention: bfloat16 [4, 512, 4096], P('pipe', 'ctx', 'tp')
- grad_out: bfloat16 [4, 4096, 4096], P('pipe', 'ctx', 'tp')
Inputs may be any that keep to these rules, and one draw needn't show every extreme that they name: `span_ids`: each row is a permutation of 0 to 7.
All inputs are finite; a program needn't handle non-finite values.
Results may differ from a plain program's by a relative error of at most 0.015.
Values may be sent and summed in bfloat16 or wider, within the bound.
No kernel may reach another device: no remote copies, remote signals or barrier semaphores. Data moves between devices by JAX's collectives and lax.ppermute only.
A program may use at most 64 MiB of HBM per device.

v0:
```python
import functools
import math

import jax
import jax.numpy as jnp
from jax import lax
from jax.experimental import pallas as pl
from jax.experimental.pallas import tpu as pltpu
from jax.sharding import PartitionSpec as P

HQ = 32
HK = 8
HD = 128
TAG = 16
TILE = 256
VMEM = pl.BlockSpec(memory_space=pltpu.VMEM)
SMEM = pl.BlockSpec(memory_space=pltpu.SMEM)
ANY = pl.BlockSpec(memory_space=pl.ANY)


def ring_order(n):
    return list(range(0, n, 2)) + list(range(1, n, 2))[::-1]


def around(x, shift):
    n = lax.axis_size("ctx")
    order = ring_order(n)
    return lax.ppermute(x, "ctx", [(order[q], order[(q + shift) % n]) for q in range(n)])


def swap(x, axis, mask):
    return lax.ppermute(x, axis, [(i, i ^ mask) for i in range(lax.axis_size(axis))])


def params(mib):
    return pltpu.CompilerParams(vmem_limit_bytes=mib * 2**20)


def after(x, *others):
    return lax.optimization_barrier((x, *others))[0]


def pack_kernel(span_ref, key_ref, value_ref, packed_ref, place_ref):
    tokens, width = key_ref.shape[1:]
    packed_ref[:tokens, :width] = key_ref[0]
    packed_ref[:tokens, width:] = value_ref[0]
    spans = span_ref.shape[1]
    span = tokens // spans
    lane = lax.broadcasted_iota(jnp.int32, (TAG, 2 * width), 1)
    row = lax.broadcasted_iota(jnp.int32, place_ref.shape, 0)
    ids = jnp.zeros(lane.shape, jnp.float32)
    base = jnp.zeros(row.shape, jnp.int32)
    for j in range(spans):
        ids = jnp.where(lane // span == j, span_ref[0, j].astype(jnp.float32), ids)
        base = jnp.where(row // span == j, span_ref[0, j] * span, base)
    packed_ref[tokens:, :] = ids.astype(jnp.bfloat16)
    place_ref[...] = (base + row % span).astype(jnp.float32)


def fetch_kernel(place_ref, query_ref, out_ref):
    out_ref[...] = query_ref[...]


def turn_kernel(n, ready_ref, cot_ref, *out_refs):
    me = lax.axis_index("ctx")
    side = lax.axis_index("tp") & 1
    half = cot_ref.shape[2] // n // 2
    place = jnp.where(me % 2 == 0, me // 2, n - 1 - me // 2)
    for s in range(n):
        to = (place + s) % n
        block = jnp.where(to < (n + 1) // 2, 2 * to, 2 * (n - to) - 1)
        at = pl.multiple_of((block * 2 + side) * half, 128)
        out_refs[s][...] = cot_ref[0, :, pl.ds(at, half)].T


def join_kernel(*refs):
    tokens = refs[0].shape[1]
    for s, ref in enumerate(refs[:-1]):
        refs[-1][:, s * tokens : (s + 1) * tokens] = ref[...]


def attention_kernel(group, scale, n, spans, place_ref, query_ref, *refs):
    kv_refs, (whole_ref, *part_refs) = refs[:n], refs[n:]
    tokens = query_ref.shape[1]
    width = kv_refs[0].shape[1] // 2
    heads = width // HD
    span = tokens // spans
    lane = lax.broadcasted_iota(jnp.int32, (1, tokens), 1)
    inner = (lane % span).astype(jnp.float32)
    key_pos = jnp.concatenate(
        [ref[tokens : tokens + 1, :tokens].astype(jnp.float32) * span + inner for ref in kv_refs],
        axis=1,
    )
    hidden = jnp.where(key_pos <= place_ref[:, :1], 0.0, -1e30)
    hidden = jnp.concatenate([hidden] * group, axis=0)
    for j in range(heads):
        first = j * group * HD
        out_ref = part_refs[j * len(part_refs) // heads]
        key_block = jnp.concatenate([ref[:tokens, j * HD : (j + 1) * HD] for ref in kv_refs], axis=0)
        value_block = jnp.concatenate(
            [ref[:tokens, width + j * HD : width + (j + 1) * HD] for ref in kv_refs], axis=0
        )
        queries = jnp.concatenate(
            [query_ref[0, :, first + g * HD : first + (g + 1) * HD] for g in range(group)], axis=0
        )
        scores = lax.dot_general(
            queries, key_block, (((1,), (1,)), ((), ())), preferred_element_type=jnp.float32
        )
        scores = jnp.where(hidden < 0.0, hidden, scores)
        top = jnp.max(scores, axis=1, keepdims=True)
        weights = jnp.exp2((scores - top) * (scale * math.log2(math.e)))
        total = jnp.sum(weights, axis=1, keepdims=True)
        mixed = jnp.dot(
            weights.astype(jnp.bfloat16), value_block, preferred_element_type=jnp.float32
        )
        mixed = (mixed / total).astype(jnp.bfloat16)
        for g in range(group):
            at, piece = first + g * HD, mixed[g * tokens : (g + 1) * tokens]
            whole_ref[0, :, at : at + HD] = piece
            at %= out_ref.shape[2]
            out_ref[0, :, at : at + HD] = piece


def left_sides(refs, tokens, first, slots):
    near, far, near_other, far_other = refs
    here = slice(first * tokens, (first + slots) * tokens)
    side = lax.axis_index("tp") & 1
    return (
        (side, jnp.concatenate([near[:, here], far[:, here]], axis=1)),
        (1 - side, jnp.concatenate([near_other[:, here], far_other[:, here]], axis=1)),
    )


def early_kernel(slots, *refs):
    att_refs, cot_refs, total_ref = refs[: 2 * slots], refs[2 * slots : -1], refs[-1]
    half = cot_refs[0].shape[0]
    tokens = att_refs[0].shape[1]
    wide = TILE if total_ref.shape[1] % TILE == 0 else total_ref.shape[1]
    for j in range(total_ref.shape[1] // wide):
        columns = slice(j * wide, (j + 1) * wide)
        rows = jnp.concatenate([ref[0, :, columns] for ref in att_refs], axis=0)
        for at, left in left_sides(cot_refs, tokens, 0, slots):
            total_ref[pl.ds(pl.multiple_of(at * half, half), half), columns] = jnp.dot(
                left, rows, preferred_element_type=jnp.float32
            )


def finish_kernel(slots, first, start, carried, width, *refs):
    att_refs, cot_refs = refs[: 2 * slots], refs[2 * slots : 2 * slots + 4]
    out_ref, held, sems = refs[-3:]
    total_ref = refs[2 * slots + 4] if carried else None
    half = cot_refs[0].shape[0]
    tokens = att_refs[0].shape[1]
    wide = held.shape[2]
    copies = []
    for j in range(width // wide):
        columns = slice(j * wide, (j + 1) * wide)
        rows = jnp.concatenate([ref[0, :, columns] for ref in att_refs], axis=0)
        if j >= 2:
            copies[j - 2].wait()
        for at, left in left_sides(cot_refs, tokens, first, slots):
            here = pl.ds(pl.multiple_of(at * half, half), half)
            value = jnp.dot(left, rows, preferred_element_type=jnp.float32)
            if carried:
                value = value + total_ref[here, columns]
            held[j % 2, here, :] = value.astype(jnp.bfloat16)
        copies.append(
            pltpu.make_async_copy(
                held.at[j % 2],
                out_ref.at[0, :, start + j * wide : start + (j + 1) * wide],
                sems.at[j % 2],
            )
        )
        copies[-1].start()
    for copy in copies[-2:]:
        copy.wait()


def local(queries, keys, values, span_ids, cotangent):
    n = lax.axis_size("ctx")
    far = lax.axis_size("pipe") // 2
    tokens, width = keys.shape[1:]
    spans = span_ids.shape[1]
    heads = queries.shape[2]
    parts = 2 if width % (2 * HD) == 0 else 1
    chunk = heads // parts
    features = cotangent.shape[2] // n
    half = features // 2

    packed, place = pl.pallas_call(
        pack_kernel,
        out_shape=[
            jax.ShapeDtypeStruct((tokens + TAG, 2 * width), jnp.bfloat16),
            jax.ShapeDtypeStruct((tokens, 128), jnp.float32),
        ],
        in_specs=[SMEM, VMEM, VMEM],
        out_specs=[VMEM] * 2,
        compiler_params=params(16),
        name="pack",
    )(span_ids, keys, values)
    kv = [packed] + [around(packed, s) for s in range(1, n)]
    query_held = pl.pallas_call(
        fetch_kernel,
        out_shape=jax.ShapeDtypeStruct(queries.shape, jnp.bfloat16),
        in_specs=[ANY, VMEM],
        out_specs=VMEM,
        compiler_params=params(16),
        name="fetch",
    )(place, queries)
    turned = pl.pallas_call(
        functools.partial(turn_kernel, n),
        out_shape=[jax.ShapeDtypeStruct((half, tokens), jnp.bfloat16)] * n,
        in_specs=[ANY, VMEM],
        out_specs=[VMEM] * n,
        compiler_params=params(16),
        name="turn",
    )(place, cotangent)
    query_held = after(query_held, *turned)
    attention, *pieces = pl.pallas_call(
        functools.partial(attention_kernel, HQ // HK, 1.0 / math.sqrt(HD), n, spans),
        out_shape=[jax.ShapeDtypeStruct(queries.shape, jnp.bfloat16)]
        + [jax.ShapeDtypeStruct((1, tokens, chunk), jnp.bfloat16)] * parts,
        in_specs=[VMEM] * (2 + n),
        out_specs=[VMEM] * (1 + parts),
        compiler_params=params(40),
        name="attend",
    )(place, query_held, *kv)

    near, mirrored = [], []
    for c in range(parts):
        held, sent = [pieces[c]], []
        for s in range(n):
            sent.append(swap(held[s], "pipe", far))
            if s < n - 1:
                arrived = around(held[s], 1)
                held.append(after(arrived, sent[s]) if s < n - 2 else arrived)
        near.append(held)
        mirrored.append(sent)

    turned = [turned[0]] + [around(turned[s], s) for s in range(1, n)]
    mine = pl.pallas_call(
        join_kernel,
        out_shape=jax.ShapeDtypeStruct((half, n * tokens), jnp.bfloat16),
        in_specs=[VMEM] * n,
        out_specs=VMEM,
        compiler_params=params(16),
        name="join",
    )(*turned)
    mine_far = swap(mine, "pipe", far)
    cots = [mine, mine_far, swap(mine, "tp", 1), swap(mine_far, "tp", 1)]

    def attended(c, first, last):
        return near[c][first:last] + mirrored[c][first:last]

    tile = TILE if chunk % TILE == 0 else chunk
    total = pl.pallas_call(
        functools.partial(early_kernel, n - 1),
        out_shape=jax.ShapeDtypeStruct((features, chunk), jnp.float32),
        in_specs=[VMEM] * (2 * n + 2),
        out_specs=VMEM,
        compiler_params=params(40),
        cost_estimate=pl.CostEstimate(
            flops=4 * features * chunk * (n - 1) * tokens,
            bytes_accessed=8 * 2**20,
            transcendentals=0,
        ),
        name="early",
    )(*attended(parts - 1, 0, n - 1), *cots)
    grad_out = None
    for c in range(parts):
        last = c == parts - 1
        slots = 1 if last else n
        operands = attended(c, n - slots, n) + cots + ([total] if last else [])
        specs = [VMEM] * len(operands)
        aliases = {}
        if grad_out is not None:
            aliases = {len(operands): 0}
            operands.append(grad_out)
            specs.append(ANY)
        grad_out = pl.pallas_call(
            functools.partial(finish_kernel, slots, n - slots, c * chunk, last, chunk),
            out_shape=jax.ShapeDtypeStruct((1, features, heads), jnp.bfloat16),
            in_specs=specs,
            out_specs=ANY,
            scratch_shapes=[
                pltpu.VMEM((2, features, tile), jnp.bfloat16),
                pltpu.SemaphoreType.DMA((2,)),
            ],
            input_output_aliases=aliases,
            compiler_params=params(40),
            cost_estimate=pl.CostEstimate(
                flops=4 * features * chunk * slots * tokens,
                bytes_accessed=8 * 2**20,
                transcendentals=0,
            ),
            name="finish",
        )(*operands)
    return (attention, grad_out)


def solution(mesh):
    placed = (
        P("pipe", "ctx", "tp"),
        P("pipe", "ctx", "tp"),
        P("pipe", "ctx", "tp"),
        P("pipe", "ctx"),
        P("pipe", "ctx", None),
    )
    return jax.shard_map(
        local,
        mesh=mesh,
        in_specs=placed,
        out_specs=(P("pipe", "ctx", "tp"), P("pipe", "ctx", "tp")),
        check_vma=False,
    )
```

profile of v0, /device:TPU:0, one launch (start us, length us, event | category | flops | bytes accessed | tf_op | source)
XLA Modules:
  0.0 107.7 jit_solution(5399011329581384688)
XLA Ops:
  0.6 0.9 copy-done.2
  1.5 0.9 copy-done.3
  2.4 0.7 copy-done.4
  3.1 0.6 pack.1
  3.7 3.1 %collective-permute-start.2 = (bf16[144,1024]{1,0:T(8,128)(2,1)S(1)}, bf16[144,1024]{1,0:T(8,128)(2,1)S(1)}, u32[]{:S(2)}, u32[]{:S(2)}) collective-permute-start(bf16[144,1024]{1,0:T(8,128)(2,1)S(1)} %get-tuple-element.22.refs_0_), channel_id=1, source_target_pairs={{0,2},{4,0},{6,4},{2,6},{1,3},{5,1},{7,5},{3,7},{8,10},{12,8},{14,... | collective-permute-start | bytes 884744 | tf_op jit(solution)/shard_map/ppermute | solution.py:28
  6.7 2.5 %collective-permute-start.1 = (bf16[144,1024]{1,0:T(8,128)(2,1)S(1)}, bf16[144,1024]{1,0:T(8,128)(2,1)S(1)}, u32[]{:S(2)}, u32[]{:S(2)}) collective-permute-start(bf16[144,1024]{1,0:T(8,128)(2,1)S(1)} %get-tuple-element.22.refs_0_), channel_id=1, source_target_pairs={{0,6},{4,2},{6,0},{2,4},{1,7},{5,3},{7,1},{3,5},{8,14},{12,10},{14... | collective-permute-start | bytes 884744 | tf_op jit(solution)/shard_map/ppermute | solution.py:28
  9.2 1.6 %collective-permute-start = (bf16[144,1024]{1,0:T(8,128)(2,1)S(1)}, bf16[144,1024]{1,0:T(8,128)(2,1)S(1)}, u32[]{:S(2)}, u32[]{:S(2)}) collective-permute-start(bf16[144,1024]{1,0:T(8,128)(2,1)S(1)} %get-tuple-element.22.refs_0_), channel_id=1, source_target_pairs={{0,4},{4,6},{6,2},{2,0},{1,5},{5,7},{7,3},{3,1},{8,12},{12,14},{14... | collective-permute-start | bytes 884744 | tf_op jit(solution)/shard_map/ppermute | solution.py:28
  10.8 1.2 %copy-done = bf16[1,128,4096]{2,1,0:T(8,128)(2,1)S(1)} copy-done((bf16[1,128,4096]{2,1,0:T(8,128)(2,1)S(1)}, bf16[1,128,4096]{2,1,0:T(8,128)(2,1)}, u32[]{:S(2)}) %copy-start) | copy-done | bytes 1048600
  12.0 0.2 turn.1
  12.2 0.4 collective-permute-start.9
  12.6 2.5 %collective-permute-start.10 = (bf16[512,128]{1,0:T(8,128)(2,1)S(1)}, bf16[512,128]{1,0:T(8,128)(2,1)S(1)}, u32[]{:S(2)}, u32[]{:S(2)}) collective-permute-start(bf16[512,128]{1,0:T(8,128)(2,1)S(1)} %get-tuple-element.19), channel_id=1, source_target_pairs={{0,6},{4,2},{6,0},{2,4},{1,7},{5,3},{7,1},{3,5},{8,14},{12,10},{14... | collective-permute-start | bytes 393224 | tf_op jit(solution)/shard_map/ppermute | solution.py:28
  15.1 15.1 %collective-permute-done.9.refs_1_ = bf16[512,128]{1,0:T(8,128)(2,1)S(1)} collective-permute-done((bf16[512,128]{1,0:T(8,128)(2,1)S(1)}, bf16[512,128]{1,0:T(8,128)(2,1)S(1)}, u32[]{:S(2)}, u32[]{:S(2)}) %collective-permute-start.9) | collective-permute-done | bytes 131104 | tf_op jit(solution)/shard_map/ppermute | solution.py:28
  30.2 3.0 %collective-permute-start.11 = (bf16[512,128]{1,0:T(8,128)(2,1)S(1)}, bf16[512,128]{1,0:T(8,128)(2,1)S(1)}, u32[]{:S(2)}, u32[]{:S(2)}) collective-permute-start(bf16[512,128]{1,0:T(8,128)(2,1)S(1)} %get-tuple-element.20), channel_id=1, source_target_pairs={{0,2},{4,0},{6,4},{2,6},{1,3},{5,1},{7,5},{3,7},{8,10},{12,8},{14,... | collective-permute-start | bytes 393224 | tf_op jit(solution)/shard_map/ppermute | solution.py:28
  33.2 1.0 copy-done.1
  34.3 10.7 %collective-permute-done.11.refs_3_ = bf16[512,128]{1,0:T(8,128)(2,1)S(1)} collective-permute-done((bf16[512,128]{1,0:T(8,128)(2,1)S(1)}, bf16[512,128]{1,0:T(8,128)(2,1)S(1)}, u32[]{:S(2)}, u32[]{:S(2)}) %collective-permute-start.11) | collective-permute-done | bytes 131104 | tf_op jit(solution)/shard_map/ppermute | solution.py:28
  45.0 0.1 join.1.refs_6_.refs_8_.refs_2_
  45.1 1.6 %collective-permute-start.12 = (bf16[512,512]{1,0:T(8,128)(2,1)S(1)}, bf16[512,512]{1,0:T(8,128)(2,1)S(1)}, u32[]{:S(2)}, u32[]{:S(2)}) collective-permute-start(bf16[512,512]{1,0:T(8,128)(2,1)S(1)} %join.1.refs_6_.refs_8_.refs_2_), channel_id=1, source_target_pairs={{0,16},{8,24},{16,0},{24,8},{1,17},{9,25},{17,1},{25,9},{2,18},{10... | collective-permute-start | bytes 1572872 | tf_op jit(solution)/shard_map/ppermute | solution.py:32
  46.7 2.5 %attend.1 = (bf16[1,128,2048]{2,1,0:T(8,128)(2,1)}, bf16[1,128,1024]{2,1,0:T(8,128)(2,1)S(1)}, bf16[1,128,1024]{2,1,0:T(8,128)(2,1)S(1)}) custom-call(f32[128,128]{1,0:T(8,128)S(1)} %get-tuple-element.16.place_ref.ready_ref, bf16[1,128,2048]{2,1,0:T(8,128)(2,1)S(1)} %fetch.1.query_ref, bf16[144,1024]{1,0:T(8,128)(2,1)S(1)} %get-tuple-element.22.refs_0_, ...), custom_call_target="tpu_custom_call" | custom-call | tf_op jit(solution)/shard_map/attend/pallas_call | solution.py:219
  49.3 0.5 collective-permute-start.17
  49.7 1.1 %collective-permute-start.16 = (bf16[1,128,1024]{2,1,0:T(8,128)(2,1)S(1)}, bf16[1,128,1024]{2,1,0:T(8,128)(2,1)S(1)}, u32[]{:S(2)}, u32[]{:S(2)}) collective-permute-start(bf16[1,128,1024]{2,1,0:T(8,128)(2,1)S(1)} %get-tuple-element.27.refs_0_), channel_id=1, source_target_pairs={{0,4},{4,6},{6,2},{2,0},{1,5},{5,7},{7,3},{3,1},{8,12},{12,14},{14... | collective-permute-start | bytes 786440 | tf_op jit(solution)/shard_map/ppermute | solution.py:28
  50.8 1.5 %collective-permute-start.4 = (bf16[1,128,1024]{2,1,0:T(8,128)(2,1)S(1)}, bf16[1,128,1024]{2,1,0:T(8,128)(2,1)S(1)}, u32[]{:S(2)}, u32[]{:S(2)}) collective-permute-start(bf16[1,128,1024]{2,1,0:T(8,128)(2,1)S(1)} %get-tuple-element.24.refs_0_), channel_id=1, source_target_pairs={{0,16},{8,24},{16,0},{24,8},{1,17},{9,25},{17,1},{25,9},{2,18},{10... | collective-permute-start | bytes 786440 | tf_op jit(solution)/shard_map/ppermute | solution.py:32
  52.4 3.1 %collective-permute-start.3 = (bf16[1,128,1024]{2,1,0:T(8,128)(2,1)S(1)}, bf16[1,128,1024]{2,1,0:T(8,128)(2,1)S(1)}, u32[]{:S(2)}, u32[]{:S(2)}) collective-permute-start(bf16[1,128,1024]{2,1,0:T(8,128)(2,1)S(1)} %get-tuple-element.24.refs_0_), channel_id=1, source_target_pairs={{0,4},{4,6},{6,2},{2,0},{1,5},{5,7},{7,3},{3,1},{8,12},{12,14},{14... | collective-permute-start | bytes 786440 | tf_op jit(solution)/shard_map/ppermute | solution.py:28
  55.5 10.2 %collective-permute-done.17.refs_4_ = bf16[1,128,1024]{2,1,0:T(8,128)(2,1)S(1)} collective-permute-done((bf16[1,128,1024]{2,1,0:T(8,128)(2,1)S(1)}, bf16[1,128,1024]{2,1,0:T(8,128)(2,1)S(1)}, u32[]{:S(2)}, u32[]{:S(2)}) %collective-permute-start.17) | collective-permute-done | bytes 262176 | tf_op jit(solution)/shard_map/ppermute | solution.py:32
  65.6 1.6 %collective-permute-start.19 = (bf16[1,128,1024]{2,1,0:T(8,128)(2,1)S(1)}, bf16[1,128,1024]{2,1,0:T(8,128)(2,1)S(1)}, u32[]{:S(2)}, u32[]{:S(2)}) collective-permute-start(bf16[1,128,1024]{2,1,0:T(8,128)(2,1)S(1)} %collective-permute-done.16.refs_1_), channel_id=1, source_target_pairs={{0,16},{8,24},{16,0},{24,8},{1,17},{9,25},{17,1},{25,9},{2,18},{10... | collective-permute-start | bytes 786440 | tf_op jit(solution)/shard_map/ppermute | solution.py:32
  67.2 1.0 collective-permute-start.18
  68.3 3.0 %collective-permute-done.4.refs_3_ = bf16[1,128,1024]{2,1,0:T(8,128)(2,1)S(1)} collective-permute-done((bf16[1,128,1024]{2,1,0:T(8,128)(2,1)S(1)}, bf16[1,128,1024]{2,1,0:T(8,128)(2,1)S(1)}, u32[]{:S(2)}, u32[]{:S(2)}) %collective-permute-start.4) | collective-permute-done | bytes 262176 | tf_op jit(solution)/shard_map/ppermute | solution.py:32
  71.3 1.5 %collective-permute-start.13 = (bf16[512,512]{1,0:T(8,128)(2,1)S(1)}, bf16[512,512]{1,0:T(8,128)(2,1)S(1)}, u32[]{:S(2)}, u32[]{:S(2)}) collective-permute-start(bf16[512,512]{1,0:T(8,128)(2,1)S(1)} %join.1.refs_6_.refs_8_.refs_2_), channel_id=1, source_target_pairs={{0,1},{1,0},{2,3},{3,2},{4,5},{5,4},{6,7},{7,6},{8,9},{9,8},{10,11... | collective-permute-start | bytes 1572872 | tf_op jit(solution)/shard_map/ppermute | solution.py:32
  72.8 1.5 %collective-permute-start.6 = (bf16[1,128,1024]{2,1,0:T(8,128)(2,1)S(1)}, bf16[1,128,1024]{2,1,0:T(8,128)(2,1)S(1)}, u32[]{:S(2)}, u32[]{:S(2)}) collective-permute-start(bf16[1,128,1024]{2,1,0:T(8,128)(2,1)S(1)} %collective-permute-done.3.refs_1_), channel_id=1, source_target_pairs={{0,16},{8,24},{16,0},{24,8},{1,17},{9,25},{17,1},{25,9},{2,18},{10... | collective-permute-start | bytes 786440 | tf_op jit(solution)/shard_map/ppermute | solution.py:32
  74.3 1.0 collective-permute-start.5
  75.4 1.5 %collective-permute-done.19.refs_5_ = bf16[1,128,1024]{2,1,0:T(8,128)(2,1)S(1)} collective-permute-done((bf16[1,128,1024]{2,1,0:T(8,128)(2,1)S(1)}, bf16[1,128,1024]{2,1,0:T(8,128)(2,1)S(1)}, u32[]{:S(2)}, u32[]{:S(2)}) %collective-permute-start.19) | collective-permute-done | bytes 262176 | tf_op jit(solution)/shard_map/ppermute | solution.py:32
  76.9 1.5 %collective-permute-start.14 = (bf16[512,512]{1,0:T(8,128)(2,1)S(1)}, bf16[512,512]{1,0:T(8,128)(2,1)S(1)}, u32[]{:S(2)}, u32[]{:S(2)}) collective-permute-start(bf16[512,512]{1,0:T(8,128)(2,1)S(1)} %collective-permute-done.12.refs_7_.refs_9_.refs_3_), channel_id=1, source_target_pairs={{0,1},{1,0},{2,3},{3,2},{4,5},{5,4},{6,7},{7,6},{8,9},{9,8},{10,11... | collective-permute-start | bytes 1572872 | tf_op jit(solution)/shard_map/ppermute | solution.py:32
  78.4 0.6 collective-permute-start.20
  79.1 1.7 %collective-permute-done.6.refs_4_ = bf16[1,128,1024]{2,1,0:T(8,128)(2,1)S(1)} collective-permute-done((bf16[1,128,1024]{2,1,0:T(8,128)(2,1)S(1)}, bf16[1,128,1024]{2,1,0:T(8,128)(2,1)S(1)}, u32[]{:S(2)}, u32[]{:S(2)}) %collective-permute-start.6) | collective-permute-done | bytes 262176 | tf_op jit(solution)/shard_map/ppermute | solution.py:32
  80.7 2.1 %collective-permute-done.5.refs_2_ = bf16[1,128,1024]{2,1,0:T(8,128)(2,1)S(1)} collective-permute-done((bf16[1,128,1024]{2,1,0:T(8,128)(2,1)S(1)}, bf16[1,128,1024]{2,1,0:T(8,128)(2,1)S(1)}, u32[]{:S(2)}, u32[]{:S(2)}) %collective-permute-start.5) | collective-permute-done | bytes 262176 | tf_op jit(solution)/shard_map/ppermute | solution.py:28
  82.9 2.3 %collective-permute-start.7 = (bf16[1,128,1024]{2,1,0:T(8,128)(2,1)S(1)}, bf16[1,128,1024]{2,1,0:T(8,128)(2,1)S(1)}, u32[]{:S(2)}, u32[]{:S(2)}) collective-permute-start(bf16[1,128,1024]{2,1,0:T(8,128)(2,1)S(1)} %collective-permute-done.5.refs_2_), channel_id=1, source_target_pairs={{0,4},{4,6},{6,2},{2,0},{1,5},{5,7},{7,3},{3,1},{8,12},{12,14},{14... | collective-permute-start | bytes 786440 | tf_op jit(solution)/shard_map/ppermute | solution.py:28
  85.2 0.7 collective-permute-start.15
  85.9 0.2 collective-permute-done.13.refs_8_.refs_10_.refs_4_
  86.1 1.6 %collective-permute-start.21 = (bf16[1,128,1024]{2,1,0:T(8,128)(2,1)S(1)}, bf16[1,128,1024]{2,1,0:T(8,128)(2,1)S(1)}, u32[]{:S(2)}, u32[]{:S(2)}) collective-permute-start(bf16[1,128,1024]{2,1,0:T(8,128)(2,1)S(1)} %collective-permute-done.18.refs_2_), channel_id=1, source_target_pairs={{0,16},{8,24},{16,0},{24,8},{1,17},{9,25},{17,1},{25,9},{2,18},{10... | collective-permute-start | bytes 786440 | tf_op jit(solution)/shard_map/ppermute | solution.py:32
  87.7 0.3 collective-permute-done.20.refs_3_
  87.9 1.5 %collective-permute-start.22 = (bf16[1,128,1024]{2,1,0:T(8,128)(2,1)S(1)}, bf16[1,128,1024]{2,1,0:T(8,128)(2,1)S(1)}, u32[]{:S(2)}, u32[]{:S(2)}) collective-permute-start(bf16[1,128,1024]{2,1,0:T(8,128)(2,1)S(1)} %collective-permute-done.20.refs_3_), channel_id=1, source_target_pairs={{0,16},{8,24},{16,0},{24,8},{1,17},{9,25},{17,1},{25,9},{2,18},{10... | collective-permute-start | bytes 786440 | tf_op jit(solution)/shard_map/ppermute | solution.py:32
  89.5 1.3 %collective-permute-done.7.refs_0_ = bf16[1,128,1024]{2,1,0:T(8,128)(2,1)S(1)} collective-permute-done((bf16[1,128,1024]{2,1,0:T(8,128)(2,1)S(1)}, bf16[1,128,1024]{2,1,0:T(8,128)(2,1)S(1)}, u32[]{:S(2)}, u32[]{:S(2)}) %collective-permute-start.7) | collective-permute-done | bytes 262176 | tf_op jit(solution)/shard_map/ppermute | solution.py:28
  90.8 1.5 %collective-permute-start.8 = (bf16[1,128,1024]{2,1,0:T(8,128)(2,1)S(1)}, bf16[1,128,1024]{2,1,0:T(8,128)(2,1)S(1)}, u32[]{:S(2)}, u32[]{:S(2)}) collective-permute-start(bf16[1,128,1024]{2,1,0:T(8,128)(2,1)S(1)} %collective-permute-done.7.refs_0_), channel_id=1, source_target_pairs={{0,16},{8,24},{16,0},{24,8},{1,17},{9,25},{17,1},{25,9},{2,18},{10... | collective-permute-start | bytes 786440 | tf_op jit(solution)/shard_map/ppermute | solution.py:32
  92.3 2.2 %collective-permute-done.15.refs_5_ = bf16[1,128,1024]{2,1,0:T(8,128)(2,1)S(1)} collective-permute-done((bf16[1,128,1024]{2,1,0:T(8,128)(2,1)S(1)}, bf16[1,128,1024]{2,1,0:T(8,128)(2,1)S(1)}, u32[]{:S(2)}, u32[]{:S(2)}) %collective-permute-start.15) | collective-permute-done | bytes 262176 | tf_op jit(solution)/shard_map/ppermute | solution.py:32
  94.5 1.8 %early.1.refs_6_ = f32[1024,1024]{1,0:T(8,128)S(1)} custom-call(bf16[1,128,1024]{2,1,0:T(8,128)(2,1)S(1)} %get-tuple-element.24.refs_0_, bf16[1,128,1024]{2,1,0:T(8,128)(2,1)S(1)} %collective-permute-done.3.refs_1_, bf16[1,128,1024]{2,1,0:T(8,128)(2,1)S(1)} %collective-permute-done.5.refs_2_, bf16[1,128,1024]{2,1,0:T(8,128)(2,1)S(1)} %collective-permute-done.4.refs_3_, ...), custom_call_target="tpu_custom_call" | custom-call | flops 1610612736 | bytes 8388608 | tf_op jit(solution)/shard_map/early/pallas_call | solution.py:256
  96.3 2.3 %collective-permute-done.21.refs_6_ = bf16[1,128,1024]{2,1,0:T(8,128)(2,1)S(1)} collective-permute-done((bf16[1,128,1024]{2,1,0:T(8,128)(2,1)S(1)}, bf16[1,128,1024]{2,1,0:T(8,128)(2,1)S(1)}, u32[]{:S(2)}, u32[]{:S(2)}) %collective-permute-start.21) | collective-permute-done | bytes 262176 | tf_op jit(solution)/shard_map/ppermute | solution.py:32
  98.6 2.8 %collective-permute-done.22.refs_7_ = bf16[1,128,1024]{2,1,0:T(8,128)(2,1)S(1)} collective-permute-done((bf16[1,128,1024]{2,1,0:T(8,128)(2,1)S(1)}, bf16[1,128,1024]{2,1,0:T(8,128)(2,1)S(1)}, u32[]{:S(2)}, u32[]{:S(2)}) %collective-permute-start.22) | collective-permute-done | bytes 262176 | tf_op jit(solution)/shard_map/ppermute | solution.py:32
  101.4 3.8 %finish.2.refs_7_ = bf16[1,1024,2048]{2,1,0:T(8,128)(2,1)} custom-call(bf16[1,128,1024]{2,1,0:T(8,128)(2,1)S(1)} %get-tuple-element.27.refs_0_, bf16[1,128,1024]{2,1,0:T(8,128)(2,1)S(1)} %collective-permute-done.16.refs_1_, bf16[1,128,1024]{2,1,0:T(8,128)(2,1)S(1)} %collective-permute-done.18.refs_2_, ...), custom_call_target="tpu_custom_call" | custom-call | flops 2147483648 | bytes 8388608 | tf_op jit(solution)/shard_map/finish/pallas_call | solution.py:280
  105.2 2.5 %finish.3 = bf16[1,1024,2048]{2,1,0:T(8,128)(2,1)} custom-call(bf16[1,128,1024]{2,1,0:T(8,128)(2,1)S(1)} %collective-permute-done.7.refs_0_, bf16[1,128,1024]{2,1,0:T(8,128)(2,1)S(1)} %collective-permute-done.8.refs_1_, bf16[512,512]{1,0:T(8,128)(2,1)S(1)} %join.1.refs_6_.refs_8_.refs_2_, ...), custom_call_target="tpu_custom_call", output_to_operand_aliasing={{}: (7, {})} | custom-call | flops 536870912 | bytes 8388608 | tf_op jit(solution)/shard_map/finish/pallas_call | solution.py:280
  (16 shorter events, 0.1 us)
Async XLA Ops:
  0.6 0.9 copy-start.2
  1.5 0.9 copy-start.3
  2.4 0.7 copy-start.4
  3.7 43.1 %collective-permute-start.2 = (bf16[144,1024]{1,0:T(8,128)(2,1)S(1)}, bf16[144,1024]{1,0:T(8,128)(2,1)S(1)}, u32[]{:S(2)}, u32[]{:S(2)}) collective-permute-start(bf16[144,1024]{1,0:T(8,128)(2,1)S(1)} %get-tuple-element.22.refs_0_), channel_id=1, source_target_pairs={{0,2},{4,0},{6,4},{2,6},{1,3},{5,1},{7,5},{3,7},{8,10},{12,8},{14,... | collective-permute-start | bytes 884744 | tf_op jit(solution)/shard_map/ppermute | solution.py:28
  6.7 40.0 %collective-permute-start.1 = (bf16[144,1024]{1,0:T(8,128)(2,1)S(1)}, bf16[144,1024]{1,0:T(8,128)(2,1)S(1)}, u32[]{:S(2)}, u32[]{:S(2)}) collective-permute-start(bf16[144,1024]{1,0:T(8,128)(2,1)S(1)} %get-tuple-element.22.refs_0_), channel_id=1, source_target_pairs={{0,6},{4,2},{6,0},{2,4},{1,7},{5,3},{7,1},{3,5},{8,14},{12,10},{14... | collective-permute-start | bytes 884744 | tf_op jit(solution)/shard_map/ppermute | solution.py:28
  9.2 37.5 %collective-permute-start = (bf16[144,1024]{1,0:T(8,128)(2,1)S(1)}, bf16[144,1024]{1,0:T(8,128)(2,1)S(1)}, u32[]{:S(2)}, u32[]{:S(2)}) collective-permute-start(bf16[144,1024]{1,0:T(8,128)(2,1)S(1)} %get-tuple-element.22.refs_0_), channel_id=1, source_target_pairs={{0,4},{4,6},{6,2},{2,0},{1,5},{5,7},{7,3},{3,1},{8,12},{12,14},{14... | collective-permute-start | bytes 884744 | tf_op jit(solution)/shard_map/ppermute | solution.py:28
  10.8 1.2 %copy-start = (bf16[1,128,4096]{2,1,0:T(8,128)(2,1)S(1)}, bf16[1,128,4096]{2,1,0:T(8,128)(2,1)}, u32[]{:S(2)}) copy-start(bf16[1,128,4096]{2,1,0:T(8,128)(2,1)} %cot_ref.1) | copy-start | bytes 3145732
  12.2 18.0 %collective-permute-start.9 = (bf16[512,128]{1,0:T(8,128)(2,1)S(1)}, bf16[512,128]{1,0:T(8,128)(2,1)S(1)}, u32[]{:S(2)}, u32[]{:S(2)}) collective-permute-start(bf16[512,128]{1,0:T(8,128)(2,1)S(1)} %get-tuple-element.18), channel_id=1, source_target_pairs={{0,4},{4,6},{6,2},{2,0},{1,5},{5,7},{7,3},{3,1},{8,12},{12,14},{14... | collective-permute-start | bytes 393224 | tf_op jit(solution)/shard_map/ppermute | solution.py:28
  12.6 21.7 %collective-permute-start.10 = (bf16[512,128]{1,0:T(8,128)(2,1)S(1)}, bf16[512,128]{1,0:T(8,128)(2,1)S(1)}, u32[]{:S(2)}, u32[]{:S(2)}) collective-permute-start(bf16[512,128]{1,0:T(8,128)(2,1)S(1)} %get-tuple-element.19), channel_id=1, source_target_pairs={{0,6},{4,2},{6,0},{2,4},{1,7},{5,3},{7,1},{3,5},{8,14},{12,10},{14... | collective-permute-start | bytes 393224 | tf_op jit(solution)/shard_map/ppermute | solution.py:28
  30.2 14.8 %collective-permute-start.11 = (bf16[512,128]{1,0:T(8,128)(2,1)S(1)}, bf16[512,128]{1,0:T(8,128)(2,1)S(1)}, u32[]{:S(2)}, u32[]{:S(2)}) collective-permute-start(bf16[512,128]{1,0:T(8,128)(2,1)S(1)} %get-tuple-element.20), channel_id=1, source_target_pairs={{0,2},{4,0},{6,4},{2,6},{1,3},{5,1},{7,5},{3,7},{8,10},{12,8},{14,... | collective-permute-start | bytes 393224 | tf_op jit(solution)/shard_map/ppermute | solution.py:28
  33.2 1.0 copy-start.1
  45.1 29.2 %collective-permute-start.12 = (bf16[512,512]{1,0:T(8,128)(2,1)S(1)}, bf16[512,512]{1,0:T(8,128)(2,1)S(1)}, u32[]{:S(2)}, u32[]{:S(2)}) collective-permute-start(bf16[512,512]{1,0:T(8,128)(2,1)S(1)} %join.1.refs_6_.refs_8_.refs_2_), channel_id=1, source_target_pairs={{0,16},{8,24},{16,0},{24,8},{1,17},{9,25},{17,1},{25,9},{2,18},{10... | collective-permute-start | bytes 1572872 | tf_op jit(solution)/shard_map/ppermute | solution.py:32
  49.3 16.4 %collective-permute-start.17 = (bf16[1,128,1024]{2,1,0:T(8,128)(2,1)S(1)}, bf16[1,128,1024]{2,1,0:T(8,128)(2,1)S(1)}, u32[]{:S(2)}, u32[]{:S(2)}) collective-permute-start(bf16[1,128,1024]{2,1,0:T(8,128)(2,1)S(1)} %get-tuple-element.27.refs_0_), channel_id=1, source_target_pairs={{0,16},{8,24},{16,0},{24,8},{1,17},{9,25},{17,1},{25,9},{2,18},{10... | collective-permute-start | bytes 786440 | tf_op jit(solution)/shard_map/ppermute | solution.py:32
  49.7 15.9 %collective-permute-start.16 = (bf16[1,128,1024]{2,1,0:T(8,128)(2,1)S(1)}, bf16[1,128,1024]{2,1,0:T(8,128)(2,1)S(1)}, u32[]{:S(2)}, u32[]{:S(2)}) collective-permute-start(bf16[1,128,1024]{2,1,0:T(8,128)(2,1)S(1)} %get-tuple-element.27.refs_0_), channel_id=1, source_target_pairs={{0,4},{4,6},{6,2},{2,0},{1,5},{5,7},{7,3},{3,1},{8,12},{12,14},{14... | collective-permute-start | bytes 786440 | tf_op jit(solution)/shard_map/ppermute | solution.py:28
  50.8 20.4 %collective-permute-start.4 = (bf16[1,128,1024]{2,1,0:T(8,128)(2,1)S(1)}, bf16[1,128,1024]{2,1,0:T(8,128)(2,1)S(1)}, u32[]{:S(2)}, u32[]{:S(2)}) collective-permute-start(bf16[1,128,1024]{2,1,0:T(8,128)(2,1)S(1)} %get-tuple-element.24.refs_0_), channel_id=1, source_target_pairs={{0,16},{8,24},{16,0},{24,8},{1,17},{9,25},{17,1},{25,9},{2,18},{10... | collective-permute-start | bytes 786440 | tf_op jit(solution)/shard_map/ppermute | solution.py:32
  52.4 20.4 %collective-permute-start.3 = (bf16[1,128,1024]{2,1,0:T(8,128)(2,1)S(1)}, bf16[1,128,1024]{2,1,0:T(8,128)(2,1)S(1)}, u32[]{:S(2)}, u32[]{:S(2)}) collective-permute-start(bf16[1,128,1024]{2,1,0:T(8,128)(2,1)S(1)} %get-tuple-element.24.refs_0_), channel_id=1, source_target_pairs={{0,4},{4,6},{6,2},{2,0},{1,5},{5,7},{7,3},{3,1},{8,12},{12,14},{14... | collective-permute-start | bytes 786440 | tf_op jit(solution)/shard_map/ppermute | solution.py:28
  65.6 11.2 %collective-permute-start.19 = (bf16[1,128,1024]{2,1,0:T(8,128)(2,1)S(1)}, bf16[1,128,1024]{2,1,0:T(8,128)(2,1)S(1)}, u32[]{:S(2)}, u32[]{:S(2)}) collective-permute-start(bf16[1,128,1024]{2,1,0:T(8,128)(2,1)S(1)} %collective-permute-done.16.refs_1_), channel_id=1, source_target_pairs={{0,16},{8,24},{16,0},{24,8},{1,17},{9,25},{17,1},{25,9},{2,18},{10... | collective-permute-start | bytes 786440 | tf_op jit(solution)/shard_map/ppermute | solution.py:32
  67.2 11.2 %collective-permute-start.18 = (bf16[1,128,1024]{2,1,0:T(8,128)(2,1)S(1)}, bf16[1,128,1024]{2,1,0:T(8,128)(2,1)S(1)}, u32[]{:S(2)}, u32[]{:S(2)}) collective-permute-start(bf16[1,128,1024]{2,1,0:T(8,128)(2,1)S(1)} %collective-permute-done.16.refs_1_), channel_id=1, source_target_pairs={{0,4},{4,6},{6,2},{2,0},{1,5},{5,7},{7,3},{3,1},{8,12},{12,14},{14... | collective-permute-start | bytes 786440 | tf_op jit(solution)/shard_map/ppermute | solution.py:28
  71.3 14.9 %collective-permute-start.13 = (bf16[512,512]{1,0:T(8,128)(2,1)S(1)}, bf16[512,512]{1,0:T(8,128)(2,1)S(1)}, u32[]{:S(2)}, u32[]{:S(2)}) collective-permute-start(bf16[512,512]{1,0:T(8,128)(2,1)S(1)} %join.1.refs_6_.refs_8_.refs_2_), channel_id=1, source_target_pairs={{0,1},{1,0},{2,3},{3,2},{4,5},{5,4},{6,7},{7,6},{8,9},{9,8},{10,11... | collective-permute-start | bytes 1572872 | tf_op jit(solution)/shard_map/ppermute | solution.py:32
  72.8 7.9 %collective-permute-start.6 = (bf16[1,128,1024]{2,1,0:T(8,128)(2,1)S(1)}, bf16[1,128,1024]{2,1,0:T(8,128)(2,1)S(1)}, u32[]{:S(2)}, u32[]{:S(2)}) collective-permute-start(bf16[1,128,1024]{2,1,0:T(8,128)(2,1)S(1)} %collective-permute-done.3.refs_1_), channel_id=1, source_target_pairs={{0,16},{8,24},{16,0},{24,8},{1,17},{9,25},{17,1},{25,9},{2,18},{10... | collective-permute-start | bytes 786440 | tf_op jit(solution)/shard_map/ppermute | solution.py:32
  74.3 8.6 %collective-permute-start.5 = (bf16[1,128,1024]{2,1,0:T(8,128)(2,1)S(1)}, bf16[1,128,1024]{2,1,0:T(8,128)(2,1)S(1)}, u32[]{:S(2)}, u32[]{:S(2)}) collective-permute-start(bf16[1,128,1024]{2,1,0:T(8,128)(2,1)S(1)} %collective-permute-done.3.refs_1_), channel_id=1, source_target_pairs={{0,4},{4,6},{6,2},{2,0},{1,5},{5,7},{7,3},{3,1},{8,12},{12,14},{14... | collective-permute-start | bytes 786440 | tf_op jit(solution)/shard_map/ppermute | solution.py:28
  76.9 17.6 %collective-permute-start.14 = (bf16[512,512]{1,0:T(8,128)(2,1)S(1)}, bf16[512,512]{1,0:T(8,128)(2,1)S(1)}, u32[]{:S(2)}, u32[]{:S(2)}) collective-permute-start(bf16[512,512]{1,0:T(8,128)(2,1)S(1)} %collective-permute-done.12.refs_7_.refs_9_.refs_3_), channel_id=1, source_target_pairs={{0,1},{1,0},{2,3},{3,2},{4,5},{5,4},{6,7},{7,6},{8,9},{9,8},{10,11... | collective-permute-start | bytes 1572872 | tf_op jit(solution)/shard_map/ppermute | solution.py:32
  78.4 9.5 %collective-permute-start.20 = (bf16[1,128,1024]{2,1,0:T(8,128)(2,1)S(1)}, bf16[1,128,1024]{2,1,0:T(8,128)(2,1)S(1)}, u32[]{:S(2)}, u32[]{:S(2)}) collective-permute-start(bf16[1,128,1024]{2,1,0:T(8,128)(2,1)S(1)} %collective-permute-done.18.refs_2_), channel_id=1, source_target_pairs={{0,4},{4,6},{6,2},{2,0},{1,5},{5,7},{7,3},{3,1},{8,12},{12,14},{14... | collective-permute-start | bytes 786440 | tf_op jit(solution)/shard_map/ppermute | solution.py:28
  82.9 7.9 %collective-permute-start.7 = (bf16[1,128,1024]{2,1,0:T(8,128)(2,1)S(1)}, bf16[1,128,1024]{2,1,0:T(8,128)(2,1)S(1)}, u32[]{:S(2)}, u32[]{:S(2)}) collective-permute-start(bf16[1,128,1024]{2,1,0:T(8,128)(2,1)S(1)} %collective-permute-done.5.refs_2_), channel_id=1, source_target_pairs={{0,4},{4,6},{6,2},{2,0},{1,5},{5,7},{7,3},{3,1},{8,12},{12,14},{14... | collective-permute-start | bytes 786440 | tf_op jit(solution)/shard_map/ppermute | solution.py:28
  85.2 9.2 %collective-permute-start.15 = (bf16[1,128,1024]{2,1,0:T(8,128)(2,1)S(1)}, bf16[1,128,1024]{2,1,0:T(8,128)(2,1)S(1)}, u32[]{:S(2)}, u32[]{:S(2)}) collective-permute-start(bf16[1,128,1024]{2,1,0:T(8,128)(2,1)S(1)} %collective-permute-done.5.refs_2_), channel_id=1, source_target_pairs={{0,16},{8,24},{16,0},{24,8},{1,17},{9,25},{17,1},{25,9},{2,18},{10... | collective-permute-start | bytes 786440 | tf_op jit(solution)/shard_map/ppermute | solution.py:32
  86.1 12.4 %collective-permute-start.21 = (bf16[1,128,1024]{2,1,0:T(8,128)(2,1)S(1)}, bf16[1,128,1024]{2,1,0:T(8,128)(2,1)S(1)}, u32[]{:S(2)}, u32[]{:S(2)}) collective-permute-start(bf16[1,128,1024]{2,1,0:T(8,128)(2,1)S(1)} %collective-permute-done.18.refs_2_), channel_id=1, source_target_pairs={{0,16},{8,24},{16,0},{24,8},{1,17},{9,25},{17,1},{25,9},{2,18},{10... | collective-permute-start | bytes 786440 | tf_op jit(solution)/shard_map/ppermute | solution.py:32
  87.9 13.4 %collective-permute-start.22 = (bf16[1,128,1024]{2,1,0:T(8,128)(2,1)S(1)}, bf16[1,128,1024]{2,1,0:T(8,128)(2,1)S(1)}, u32[]{:S(2)}, u32[]{:S(2)}) collective-permute-start(bf16[1,128,1024]{2,1,0:T(8,128)(2,1)S(1)} %collective-permute-done.20.refs_3_), channel_id=1, source_target_pairs={{0,16},{8,24},{16,0},{24,8},{1,17},{9,25},{17,1},{25,9},{2,18},{10... | collective-permute-start | bytes 786440 | tf_op jit(solution)/shard_map/ppermute | solution.py:32
  90.8 14.4 %collective-permute-start.8 = (bf16[1,128,1024]{2,1,0:T(8,128)(2,1)S(1)}, bf16[1,128,1024]{2,1,0:T(8,128)(2,1)S(1)}, u32[]{:S(2)}, u32[]{:S(2)}) collective-permute-start(bf16[1,128,1024]{2,1,0:T(8,128)(2,1)S(1)} %collective-permute-done.7.refs_0_), channel_id=1, source_target_pairs={{0,16},{8,24},{16,0},{24,8},{1,17},{9,25},{17,1},{25,9},{2,18},{10... | collective-permute-start | bytes 786440 | tf_op jit(solution)/shard_map/ppermute | solution.py:32
where the time goes:
time: 108 us
  waiting for transfers between devices  53.4 us (49%)
  starting transfers between devices  37.4 us (35%)
  Pallas kernels  11.5 us (11%)
  local copies, waits for them, and re-layouts  4.72 us (4%)
    ppermute x12, waiting for transfers between devices, around(): lax.ppermute(x, 'ctx', [(order[q], order[(q + shift) % n]) for q in range...  29.6 us
    ppermute x11, waiting for transfers between devices, swap(): lax.ppermute(x, axis, [(i, i ^ mask) for i in range(lax.axis_size(axis))])  23.8 us
    ppermute x12, starting transfers between devices, around(): lax.ppermute(x, 'ctx', [(order[q], order[(q + shift) % n]) for q in range...  22.3 us
    ppermute x11, starting transfers between devices, swap(): lax.ppermute(x, axis, [(i, i ^ mask) for i in range(lax.axis_size(axis))])  15.1 us
    pallas_call x2, Pallas kernels, local(): pl.pallas_call(functools.partial(finish_kernel, slots, n - slots, c * chu...  6.3 us
    unnamed x10, local copies, waits for them, and re-layouts  4.72 us
    pallas_call x1, Pallas kernels, local(): pl.pallas_call(functools.partial(attention_kernel, HQ // HK, 1.0 / math.s...  2.54 us
  transfers between devices with their start and end apart: 23, of which 13 were waited for; matrix products, arithmetic and copies ran while one was open for 0% of the time, Pallas kernels for 8%

commit v1 on v0

--- a/solution.py
+++ b/solution.py
@@ -230,14 +230,15 @@
     for c in range(parts):
         held, sent = [pieces[c]], []
         for s in range(n):
-            sent.append(swap(held[s], "pipe", far))
+            by_ring = s == n - 1 and c < parts - 1
+            sent.append(around(sent[-1], 1) if by_ring else swap(held[s], "pipe", far))
             if s < n - 1:
                 arrived = around(held[s], 1)
                 held.append(after(arrived, sent[s]) if s < n - 2 else arrived)
         near.append(held)
         mirrored.append(sent)
 
-    turned = [turned[0]] + [around(turned[s], s) for s in range(1, n)]
+    turned = [turned[0]] + [around(after(turned[s], attention), s) for s in range(1, n)]
     mine = pl.pallas_call(
         join_kernel,
         out_shape=jax.ShapeDtypeStruct((half, n * tokens), jnp.bfloat16),
@@ -245,7 +246,7 @@
         out_specs=VMEM,
         compiler_params=params(16),
         name="join",
-    )(*turned)
+    )(*turned[:-1], after(turned[-1], *[sent[0] for sent in mirrored]))
     mine_far = swap(mine, "pipe", far)
     cots = [mine, mine_far, swap(mine, "tp", 1), swap(mine_far, "tp", 1)]
 

time: 108 us -> 106 us (0.981)
  waiting for transfers between devices: 53.4 us -> 40.2 us
  starting transfers between devices: 37.4 us -> 48.4 us
    ppermute x11 -> x10, waiting for transfers between devices: 23.8 us -> 7.73 us  [swap(): lax.ppermute(x, axis, [(i, i ^ mask) for i in range(lax.axis_size(axis))])]
    ppermute x12 -> x13, starting transfers between devices: 22.3 us -> 29.6 us  [around(): lax.ppermute(x, 'ctx', [(order[q], order[(q + shift) % n]) for q in range...]
    ppermute x11 -> x10, starting transfers between devices: 15.1 us -> 18.8 us  [swap(): lax.ppermute(x, axis, [(i, i ^ mask) for i in range(lax.axis_size(axis))])]
    ppermute x12 -> x13, waiting for transfers between devices: 29.6 us -> 32.5 us  [around(): lax.ppermute(x, 'ctx', [(order[q], order[(q + shift) % n]) for q in range...]
  transfers between devices with their start and end apart: 23 -> 23, of which waited for: 13 -> 10; matrix products, arithmetic and copies ran while one was open for 0% -> 0% of each run, Pallas kernels for 8% -> 6%
where the time goes in v1:
time: 106 us
  starting transfers between devices  48.4 us (46%)
  waiting for transfers between devices  40.2 us (38%)
  Pallas kernels  11.5 us (11%)
  local copies, waits for them, and re-layouts  4.72 us (4%)
    ppermute x13, waiting for transfers between devices, around(): lax.ppermute(x, 'ctx', [(order[q], order[(q + shift) % n]) for q in range...  32.5 us
    ppermute x13, starting transfers between devices, around(): lax.ppermute(x, 'ctx', [(order[q], order[(q + shift) % n]) for q in range...  29.6 us
    ppermute x10, starting transfers between devices, swap(): lax.ppermute(x, axis, [(i, i ^ mask) for i in range(lax.axis_size(axis))])  18.8 us
    ppermute x10, waiting for transfers between devices, swap(): lax.ppermute(x, axis, [(i, i ^ mask) for i in range(lax.axis_size(axis))])  7.73 us
    pallas_call x2, Pallas kernels, local(): pl.pallas_call(functools.partial(finish_kernel, slots, n - slots, c * chu...  6.27 us
    unnamed x10, local copies, waits for them, and re-layouts  4.72 us
    pallas_call x1, Pallas kernels, local(): pl.pallas_call(functools.partial(attention_kernel, HQ // HK, 1.0 / math.s...  2.54 us
  transfers between devices with their start and end apart: 23, of which 10 were waited for; matrix products, arithmetic and copies ran while one was open for 0% of the time, Pallas kernels for 6%

profile of v1, /device:TPU:0, one launch (start us, length us, event | category | flops | bytes accessed | tf_op | source)
XLA Modules:
  0.0 105.6 jit_solution(5201936391311810168)
XLA Ops:
  0.6 0.9 copy-done.2
  1.5 0.9 copy-done.3
  2.4 0.7 copy-done.4
  3.1 0.6 pack.1
  3.7 3.1 %collective-permute-start.2 = (bf16[144,1024]{1,0:T(8,128)(2,1)S(1)}, bf16[144,1024]{1,0:T(8,128)(2,1)S(1)}, u32[]{:S(2)}, u32[]{:S(2)}) collective-permute-start(bf16[144,1024]{1,0:T(8,128)(2,1)S(1)} %get-tuple-element.26.refs_0_), channel_id=1, source_target_pairs={{0,2},{4,0},{6,4},{2,6},{1,3},{5,1},{7,5},{3,7},{8,10},{12,8},{14,... | collective-permute-start | bytes 884744 | tf_op jit(solution)/shard_map/ppermute | solution.py:28
  6.7 2.5 %collective-permute-start.1 = (bf16[144,1024]{1,0:T(8,128)(2,1)S(1)}, bf16[144,1024]{1,0:T(8,128)(2,1)S(1)}, u32[]{:S(2)}, u32[]{:S(2)}) collective-permute-start(bf16[144,1024]{1,0:T(8,128)(2,1)S(1)} %get-tuple-element.26.refs_0_), channel_id=1, source_target_pairs={{0,6},{4,2},{6,0},{2,4},{1,7},{5,3},{7,1},{3,5},{8,14},{12,10},{14... | collective-permute-start | bytes 884744 | tf_op jit(solution)/shard_map/ppermute | solution.py:28
  9.2 1.6 %collective-permute-start = (bf16[144,1024]{1,0:T(8,128)(2,1)S(1)}, bf16[144,1024]{1,0:T(8,128)(2,1)S(1)}, u32[]{:S(2)}, u32[]{:S(2)}) collective-permute-start(bf16[144,1024]{1,0:T(8,128)(2,1)S(1)} %get-tuple-element.26.refs_0_), channel_id=1, source_target_pairs={{0,4},{4,6},{6,2},{2,0},{1,5},{5,7},{7,3},{3,1},{8,12},{12,14},{14... | collective-permute-start | bytes 884744 | tf_op jit(solution)/shard_map/ppermute | solution.py:28
  10.8 1.0 copy-done.1
  11.9 0.0 copy-start
  11.9 1.2 %copy-done = bf16[1,128,4096]{2,1,0:T(8,128)(2,1)S(1)} copy-done((bf16[1,128,4096]{2,1,0:T(8,128)(2,1)S(1)}, bf16[1,128,4096]{2,1,0:T(8,128)(2,1)}, u32[]{:S(2)}) %copy-start) | copy-done | bytes 1048600
  13.1 0.2 turn.1
  13.3 3.2 %collective-permute-done.2.refs_3_ = bf16[144,1024]{1,0:T(8,128)(2,1)S(1)} collective-permute-done((bf16[144,1024]{1,0:T(8,128)(2,1)S(1)}, bf16[144,1024]{1,0:T(8,128)(2,1)S(1)}, u32[]{:S(2)}, u32[]{:S(2)}) %collective-permute-start.2) | collective-permute-done | bytes 294944 | tf_op jit(solution)/shard_map/ppermute | solution.py:28
  16.5 7.0 %collective-permute-done.1.refs_2_ = bf16[144,1024]{1,0:T(8,128)(2,1)S(1)} collective-permute-done((bf16[144,1024]{1,0:T(8,128)(2,1)S(1)}, bf16[144,1024]{1,0:T(8,128)(2,1)S(1)}, u32[]{:S(2)}, u32[]{:S(2)}) %collective-permute-start.1) | collective-permute-done | bytes 294944 | tf_op jit(solution)/shard_map/ppermute | solution.py:28
  23.5 3.9 %collective-permute-done.refs_1_ = bf16[144,1024]{1,0:T(8,128)(2,1)S(1)} collective-permute-done((bf16[144,1024]{1,0:T(8,128)(2,1)S(1)}, bf16[144,1024]{1,0:T(8,128)(2,1)S(1)}, u32[]{:S(2)}, u32[]{:S(2)}) %collective-permute-start) | collective-permute-done | bytes 294944 | tf_op jit(solution)/shard_map/ppermute | solution.py:28
  27.4 2.5 %attend.1 = (bf16[1,128,2048]{2,1,0:T(8,128)(2,1)}, bf16[1,128,1024]{2,1,0:T(8,128)(2,1)S(1)}, bf16[1,128,1024]{2,1,0:T(8,128)(2,1)S(1)}) custom-call(f32[128,128]{1,0:T(8,128)S(1)} %get-tuple-element.20.place_ref.ready_ref, bf16[1,128,2048]{2,1,0:T(8,128)(2,1)S(1)} %fetch.1.query_ref, bf16[144,1024]{1,0:T(8,128)(2,1)S(1)} %get-tuple-element.26.refs_0_, ...), custom_call_target="tpu_custom_call" | custom-call | tf_op jit(solution)/shard_map/attend/pallas_call | solution.py:219
  29.9 1.6 %collective-permute-start.4 = (bf16[1,128,1024]{2,1,0:T(8,128)(2,1)S(1)}, bf16[1,128,1024]{2,1,0:T(8,128)(2,1)S(1)}, u32[]{:S(2)}, u32[]{:S(2)}) collective-permute-start(bf16[1,128,1024]{2,1,0:T(8,128)(2,1)S(1)} %get-tuple-element.28.refs_0_), channel_id=1, source_target_pairs={{0,16},{8,24},{16,0},{24,8},{1,17},{9,25},{17,1},{25,9},{2,18},{10... | collective-permute-start | bytes 786440 | tf_op jit(solution)/shard_map/ppermute | solution.py:32
  31.5 0.5 collective-permute-start.12
  32.0 7.2 %collective-permute-start.11 = (bf16[512,128]{1,0:T(8,128)(2,1)S(1)}, bf16[512,128]{1,0:T(8,128)(2,1)S(1)}, u32[]{:S(2)}, u32[]{:S(2)}) collective-permute-start(bf16[512,128]{1,0:T(8,128)(2,1)S(1)} %get-tuple-element.33), channel_id=1, source_target_pairs={{0,2},{4,0},{6,4},{2,6},{1,3},{5,1},{7,5},{3,7},{8,10},{12,8},{14,... | collective-permute-start | bytes 393224 | tf_op jit(solution)/shard_map/ppermute | solution.py:28
  39.2 1.9 %collective-permute-start.9 = (bf16[512,128]{1,0:T(8,128)(2,1)S(1)}, bf16[512,128]{1,0:T(8,128)(2,1)S(1)}, u32[]{:S(2)}, u32[]{:S(2)}) collective-permute-start(bf16[512,128]{1,0:T(8,128)(2,1)S(1)} %get-tuple-element.31), channel_id=1, source_target_pairs={{0,4},{4,6},{6,2},{2,0},{1,5},{5,7},{7,3},{3,1},{8,12},{12,14},{14... | collective-permute-start | bytes 393224 | tf_op jit(solution)/shard_map/ppermute | solution.py:28
  41.1 1.5 %collective-permute-start.10 = (bf16[512,128]{1,0:T(8,128)(2,1)S(1)}, bf16[512,128]{1,0:T(8,128)(2,1)S(1)}, u32[]{:S(2)}, u32[]{:S(2)}) collective-permute-start(bf16[512,128]{1,0:T(8,128)(2,1)S(1)} %get-tuple-element.32), channel_id=1, source_target_pairs={{0,6},{4,2},{6,0},{2,4},{1,7},{5,3},{7,1},{3,5},{8,14},{12,10},{14... | collective-permute-start | bytes 393224 | tf_op jit(solution)/shard_map/ppermute | solution.py:28
  42.6 13.4 %collective-permute-done.11.refs_3_ = bf16[512,128]{1,0:T(8,128)(2,1)S(1)} collective-permute-done((bf16[512,128]{1,0:T(8,128)(2,1)S(1)}, bf16[512,128]{1,0:T(8,128)(2,1)S(1)}, u32[]{:S(2)}, u32[]{:S(2)}) %collective-permute-start.11) | collective-permute-done | bytes 131104 | tf_op jit(solution)/shard_map/ppermute | solution.py:28
  56.0 0.0 collective-permute-start.3
  56.0 0.0 collective-permute-done.4.refs_3_
  56.0 0.0 collective-permute-done.12.refs_4_
  56.0 0.0 collective-permute-done.10.refs_2_
  56.0 0.1 join.1.refs_6_.refs_8_.refs_2_
  56.1 7.1 %collective-permute-start.13 = (bf16[512,512]{1,0:T(8,128)(2,1)S(1)}, bf16[512,512]{1,0:T(8,128)(2,1)S(1)}, u32[]{:S(2)}, u32[]{:S(2)}) collective-permute-start(bf16[512,512]{1,0:T(8,128)(2,1)S(1)} %join.1.refs_6_.refs_8_.refs_2_), channel_id=1, source_target_pairs={{0,16},{8,24},{16,0},{24,8},{1,17},{9,25},{17,1},{25,9},{2,18},{10... | collective-permute-start | bytes 1572872 | tf_op jit(solution)/shard_map/ppermute | solution.py:32
  63.2 0.9 collective-permute-start.17
  64.1 0.7 collective-permute-done.3.refs_1_
  64.8 4.8 %collective-permute-start.6 = (bf16[1,128,1024]{2,1,0:T(8,128)(2,1)S(1)}, bf16[1,128,1024]{2,1,0:T(8,128)(2,1)S(1)}, u32[]{:S(2)}, u32[]{:S(2)}) collective-permute-start(bf16[1,128,1024]{2,1,0:T(8,128)(2,1)S(1)} %collective-permute-done.3.refs_1_), channel_id=1, source_target_pairs={{0,16},{8,24},{16,0},{24,8},{1,17},{9,25},{17,1},{25,9},{2,18},{10... | collective-permute-start | bytes 786440 | tf_op jit(solution)/shard_map/ppermute | solution.py:32
  69.6 2.6 %collective-permute-start.5 = (bf16[1,128,1024]{2,1,0:T(8,128)(2,1)S(1)}, bf16[1,128,1024]{2,1,0:T(8,128)(2,1)S(1)}, u32[]{:S(2)}, u32[]{:S(2)}) collective-permute-start(bf16[1,128,1024]{2,1,0:T(8,128)(2,1)S(1)} %collective-permute-done.3.refs_1_), channel_id=1, source_target_pairs={{0,4},{4,6},{6,2},{2,0},{1,5},{5,7},{7,3},{3,1},{8,12},{12,14},{14... | collective-permute-start | bytes 786440 | tf_op jit(solution)/shard_map/ppermute | solution.py:28
  72.3 0.2 collective-permute-start.19
  72.5 3.4 %collective-permute-start.18 = (bf16[1,128,1024]{2,1,0:T(8,128)(2,1)S(1)}, bf16[1,128,1024]{2,1,0:T(8,128)(2,1)S(1)}, u32[]{:S(2)}, u32[]{:S(2)}) collective-permute-start(bf16[1,128,1024]{2,1,0:T(8,128)(2,1)S(1)} %collective-permute-done.17.refs_1_), channel_id=1, source_target_pairs={{0,4},{4,6},{6,2},{2,0},{1,5},{5,7},{7,3},{3,1},{8,12},{12,14},{14... | collective-permute-start | bytes 786440 | tf_op jit(solution)/shard_map/ppermute | solution.py:28
  75.9 3.2 %collective-permute-done.6.refs_4_ = bf16[1,128,1024]{2,1,0:T(8,128)(2,1)S(1)} collective-permute-done((bf16[1,128,1024]{2,1,0:T(8,128)(2,1)S(1)}, bf16[1,128,1024]{2,1,0:T(8,128)(2,1)S(1)}, u32[]{:S(2)}, u32[]{:S(2)}) %collective-permute-start.6) | collective-permute-done | bytes 262176 | tf_op jit(solution)/shard_map/ppermute | solution.py:32
  79.1 1.5 %collective-permute-start.14 = (bf16[512,512]{1,0:T(8,128)(2,1)S(1)}, bf16[512,512]{1,0:T(8,128)(2,1)S(1)}, u32[]{:S(2)}, u32[]{:S(2)}) collective-permute-start(bf16[512,512]{1,0:T(8,128)(2,1)S(1)} %join.1.refs_6_.refs_8_.refs_2_), channel_id=1, source_target_pairs={{0,1},{1,0},{2,3},{3,2},{4,5},{5,4},{6,7},{7,6},{8,9},{9,8},{10,11... | collective-permute-start | bytes 1572872 | tf_op jit(solution)/shard_map/ppermute | solution.py:32
  80.6 0.5 collective-permute-start.15
  81.2 1.7 %collective-permute-start.16 = (bf16[1,128,1024]{2,1,0:T(8,128)(2,1)S(1)}, bf16[1,128,1024]{2,1,0:T(8,128)(2,1)S(1)}, u32[]{:S(2)}, u32[]{:S(2)}) collective-permute-start(bf16[1,128,1024]{2,1,0:T(8,128)(2,1)S(1)} %collective-permute-done.5.refs_2_), channel_id=1, source_target_pairs={{0,16},{8,24},{16,0},{24,8},{1,17},{9,25},{17,1},{25,9},{2,18},{10... | collective-permute-start | bytes 786440 | tf_op jit(solution)/shard_map/ppermute | solution.py:32
  82.8 1.6 %collective-permute-done.18.refs_2_ = bf16[1,128,1024]{2,1,0:T(8,128)(2,1)S(1)} collective-permute-done((bf16[1,128,1024]{2,1,0:T(8,128)(2,1)S(1)}, bf16[1,128,1024]{2,1,0:T(8,128)(2,1)S(1)}, u32[]{:S(2)}, u32[]{:S(2)}) %collective-permute-start.18) | collective-permute-done | bytes 262176 | tf_op jit(solution)/shard_map/ppermute | solution.py:28
  84.4 3.1 %collective-permute-start.7 = (bf16[1,128,1024]{2,1,0:T(8,128)(2,1)S(1)}, bf16[1,128,1024]{2,1,0:T(8,128)(2,1)S(1)}, u32[]{:S(2)}, u32[]{:S(2)}) collective-permute-start(bf16[1,128,1024]{2,1,0:T(8,128)(2,1)S(1)} %collective-permute-done.5.refs_2_), channel_id=1, source_target_pairs={{0,4},{4,6},{6,2},{2,0},{1,5},{5,7},{7,3},{3,1},{8,12},{12,14},{14... | collective-permute-start | bytes 786440 | tf_op jit(solution)/shard_map/ppermute | solution.py:28
  87.5 2.6 %collective-permute-done.16.refs_5_ = bf16[1,128,1024]{2,1,0:T(8,128)(2,1)S(1)} collective-permute-done((bf16[1,128,1024]{2,1,0:T(8,128)(2,1)S(1)}, bf16[1,128,1024]{2,1,0:T(8,128)(2,1)S(1)}, u32[]{:S(2)}, u32[]{:S(2)}) %collective-permute-start.16) | collective-permute-done | bytes 262176 | tf_op jit(solution)/shard_map/ppermute | solution.py:32
  90.1 1.0 collective-permute-start.20
  91.1 1.8 %collective-permute-done.21.refs_6_ = bf16[1,128,1024]{2,1,0:T(8,128)(2,1)S(1)} collective-permute-done((bf16[1,128,1024]{2,1,0:T(8,128)(2,1)S(1)}, bf16[1,128,1024]{2,1,0:T(8,128)(2,1)S(1)}, u32[]{:S(2)}, u32[]{:S(2)}) %collective-permute-start.21) | collective-permute-done | bytes 262176 | tf_op jit(solution)/shard_map/ppermute | solution.py:32
  92.9 1.0 collective-permute-start.22
  93.9 0.9 collective-permute-start.8
  94.8 1.8 %early.1.refs_6_ = f32[1024,1024]{1,0:T(8,128)S(1)} custom-call(bf16[1,128,1024]{2,1,0:T(8,128)(2,1)S(1)} %get-tuple-element.28.refs_0_, bf16[1,128,1024]{2,1,0:T(8,128)(2,1)S(1)} %collective-permute-done.3.refs_1_, bf16[1,128,1024]{2,1,0:T(8,128)(2,1)S(1)} %collective-permute-done.5.refs_2_, bf16[1,128,1024]{2,1,0:T(8,128)(2,1)S(1)} %collective-permute-done.4.refs_3_, ...), custom_call_target="tpu_custom_call" | custom-call | flops 1610612736 | bytes 8388608 | tf_op jit(solution)/shard_map/early/pallas_call | solution.py:257
  96.6 2.7 %collective-permute-done.22.refs_7_ = bf16[1,128,1024]{2,1,0:T(8,128)(2,1)S(1)} collective-permute-done((bf16[1,128,1024]{2,1,0:T(8,128)(2,1)S(1)}, bf16[1,128,1024]{2,1,0:T(8,128)(2,1)S(1)}, u32[]{:S(2)}, u32[]{:S(2)}) %collective-permute-start.22) | collective-permute-done | bytes 262176 | tf_op jit(solution)/shard_map/ppermute | solution.py:28
  99.3 3.8 %finish.2.refs_7_ = bf16[1,1024,2048]{2,1,0:T(8,128)(2,1)} custom-call(bf16[1,128,1024]{2,1,0:T(8,128)(2,1)S(1)} %get-tuple-element.34.refs_0_, bf16[1,128,1024]{2,1,0:T(8,128)(2,1)S(1)} %collective-permute-done.17.refs_1_, bf16[1,128,1024]{2,1,0:T(8,128)(2,1)S(1)} %collective-permute-done.18.refs_2_, ...), custom_call_target="tpu_custom_call" | custom-call | flops 2147483648 | bytes 8388608 | tf_op jit(solution)/shard_map/finish/pallas_call | solution.py:281
  103.1 2.5 %finish.3 = bf16[1,1024,2048]{2,1,0:T(8,128)(2,1)} custom-call(bf16[1,128,1024]{2,1,0:T(8,128)(2,1)S(1)} %collective-permute-done.7.refs_0_, bf16[1,128,1024]{2,1,0:T(8,128)(2,1)S(1)} %collective-permute-done.8.refs_1_, bf16[512,512]{1,0:T(8,128)(2,1)S(1)} %join.1.refs_6_.refs_8_.refs_2_, ...), custom_call_target="tpu_custom_call", output_to_operand_aliasing={{}: (7, {})} | custom-call | flops 536870912 | bytes 8388608 | tf_op jit(solution)/shard_map/finish/pallas_call | solution.py:281
  (16 shorter events, 0.1 us)
Async XLA Ops:
  0.6 0.9 copy-start.2
  1.5 0.9 copy-start.3
  2.4 0.7 copy-start.4
  3.7 12.8 %collective-permute-start.2 = (bf16[144,1024]{1,0:T(8,128)(2,1)S(1)}, bf16[144,1024]{1,0:T(8,128)(2,1)S(1)}, u32[]{:S(2)}, u32[]{:S(2)}) collective-permute-start(bf16[144,1024]{1,0:T(8,128)(2,1)S(1)} %get-tuple-element.26.refs_0_), channel_id=1, source_target_pairs={{0,2},{4,0},{6,4},{2,6},{1,3},{5,1},{7,5},{3,7},{8,10},{12,8},{14,... | collective-permute-start | bytes 884744 | tf_op jit(solution)/shard_map/ppermute | solution.py:28
  6.7 16.8 %collective-permute-start.1 = (bf16[144,1024]{1,0:T(8,128)(2,1)S(1)}, bf16[144,1024]{1,0:T(8,128)(2,1)S(1)}, u32[]{:S(2)}, u32[]{:S(2)}) collective-permute-start(bf16[144,1024]{1,0:T(8,128)(2,1)S(1)} %get-tuple-element.26.refs_0_), channel_id=1, source_target_pairs={{0,6},{4,2},{6,0},{2,4},{1,7},{5,3},{7,1},{3,5},{8,14},{12,10},{14... | collective-permute-start | bytes 884744 | tf_op jit(solution)/shard_map/ppermute | solution.py:28
  9.2 18.2 %collective-permute-start = (bf16[144,1024]{1,0:T(8,128)(2,1)S(1)}, bf16[144,1024]{1,0:T(8,128)(2,1)S(1)}, u32[]{:S(2)}, u32[]{:S(2)}) collective-permute-start(bf16[144,1024]{1,0:T(8,128)(2,1)S(1)} %get-tuple-element.26.refs_0_), channel_id=1, source_target_pairs={{0,4},{4,6},{6,2},{2,0},{1,5},{5,7},{7,3},{3,1},{8,12},{12,14},{14... | collective-permute-start | bytes 884744 | tf_op jit(solution)/shard_map/ppermute | solution.py:28
  10.8 1.0 copy-start.1
  11.9 1.2 %copy-start = (bf16[1,128,4096]{2,1,0:T(8,128)(2,1)S(1)}, bf16[1,128,4096]{2,1,0:T(8,128)(2,1)}, u32[]{:S(2)}) copy-start(bf16[1,128,4096]{2,1,0:T(8,128)(2,1)} %cot_ref.1) | copy-start | bytes 3145732
  29.9 26.0 %collective-permute-start.4 = (bf16[1,128,1024]{2,1,0:T(8,128)(2,1)S(1)}, bf16[1,128,1024]{2,1,0:T(8,128)(2,1)S(1)}, u32[]{:S(2)}, u32[]{:S(2)}) collective-permute-start(bf16[1,128,1024]{2,1,0:T(8,128)(2,1)S(1)} %get-tuple-element.28.refs_0_), channel_id=1, source_target_pairs={{0,16},{8,24},{16,0},{24,8},{1,17},{9,25},{17,1},{25,9},{2,18},{10... | collective-permute-start | bytes 786440 | tf_op jit(solution)/shard_map/ppermute | solution.py:32
  31.5 24.5 %collective-permute-start.12 = (bf16[1,128,1024]{2,1,0:T(8,128)(2,1)S(1)}, bf16[1,128,1024]{2,1,0:T(8,128)(2,1)S(1)}, u32[]{:S(2)}, u32[]{:S(2)}) collective-permute-start(bf16[1,128,1024]{2,1,0:T(8,128)(2,1)S(1)} %get-tuple-element.34.refs_0_), channel_id=1, source_target_pairs={{0,16},{8,24},{16,0},{24,8},{1,17},{9,25},{17,1},{25,9},{2,18},{10... | collective-permute-start | bytes 786440 | tf_op jit(solution)/shard_map/ppermute | solution.py:32
  32.0 24.0 %collective-permute-start.11 = (bf16[512,128]{1,0:T(8,128)(2,1)S(1)}, bf16[512,128]{1,0:T(8,128)(2,1)S(1)}, u32[]{:S(2)}, u32[]{:S(2)}) collective-permute-start(bf16[512,128]{1,0:T(8,128)(2,1)S(1)} %get-tuple-element.33), channel_id=1, source_target_pairs={{0,2},{4,0},{6,4},{2,6},{1,3},{5,1},{7,5},{3,7},{8,10},{12,8},{14,... | collective-permute-start | bytes 393224 | tf_op jit(solution)/shard_map/ppermute | solution.py:28
  39.2 16.8 %collective-permute-start.9 = (bf16[512,128]{1,0:T(8,128)(2,1)S(1)}, bf16[512,128]{1,0:T(8,128)(2,1)S(1)}, u32[]{:S(2)}, u32[]{:S(2)}) collective-permute-start(bf16[512,128]{1,0:T(8,128)(2,1)S(1)} %get-tuple-element.31), channel_id=1, source_target_pairs={{0,4},{4,6},{6,2},{2,0},{1,5},{5,7},{7,3},{3,1},{8,12},{12,14},{14... | collective-permute-start | bytes 393224 | tf_op jit(solution)/shard_map/ppermute | solution.py:28
  41.1 14.9 %collective-permute-start.10 = (bf16[512,128]{1,0:T(8,128)(2,1)S(1)}, bf16[512,128]{1,0:T(8,128)(2,1)S(1)}, u32[]{:S(2)}, u32[]{:S(2)}) collective-permute-start(bf16[512,128]{1,0:T(8,128)(2,1)S(1)} %get-tuple-element.32), channel_id=1, source_target_pairs={{0,6},{4,2},{6,0},{2,4},{1,7},{5,3},{7,1},{3,5},{8,14},{12,10},{14... | collective-permute-start | bytes 393224 | tf_op jit(solution)/shard_map/ppermute | solution.py:28
  56.0 8.9 %collective-permute-start.3 = (bf16[1,128,1024]{2,1,0:T(8,128)(2,1)S(1)}, bf16[1,128,1024]{2,1,0:T(8,128)(2,1)S(1)}, u32[]{:S(2)}, u32[]{:S(2)}) collective-permute-start(bf16[1,128,1024]{2,1,0:T(8,128)(2,1)S(1)} %get-tuple-element.28.refs_0_), channel_id=1, source_target_pairs={{0,4},{4,6},{6,2},{2,0},{1,5},{5,7},{7,3},{3,1},{8,12},{12,14},{14... | collective-permute-start | bytes 786440 | tf_op jit(solution)/shard_map/ppermute | solution.py:28
  56.1 24.5 %collective-permute-start.13 = (bf16[512,512]{1,0:T(8,128)(2,1)S(1)}, bf16[512,512]{1,0:T(8,128)(2,1)S(1)}, u32[]{:S(2)}, u32[]{:S(2)}) collective-permute-start(bf16[512,512]{1,0:T(8,128)(2,1)S(1)} %join.1.refs_6_.refs_8_.refs_2_), channel_id=1, source_target_pairs={{0,16},{8,24},{16,0},{24,8},{1,17},{9,25},{17,1},{25,9},{2,18},{10... | collective-permute-start | bytes 1572872 | tf_op jit(solution)/shard_map/ppermute | solution.py:32
  63.2 9.1 %collective-permute-start.17 = (bf16[1,128,1024]{2,1,0:T(8,128)(2,1)S(1)}, bf16[1,128,1024]{2,1,0:T(8,128)(2,1)S(1)}, u32[]{:S(2)}, u32[]{:S(2)}) collective-permute-start(bf16[1,128,1024]{2,1,0:T(8,128)(2,1)S(1)} %get-tuple-element.34.refs_0_), channel_id=1, source_target_pairs={{0,4},{4,6},{6,2},{2,0},{1,5},{5,7},{7,3},{3,1},{8,12},{12,14},{14... | collective-permute-start | bytes 786440 | tf_op jit(solution)/shard_map/ppermute | solution.py:28
  64.8 14.3 %collective-permute-start.6 = (bf16[1,128,1024]{2,1,0:T(8,128)(2,1)S(1)}, bf16[1,128,1024]{2,1,0:T(8,128)(2,1)S(1)}, u32[]{:S(2)}, u32[]{:S(2)}) collective-permute-start(bf16[1,128,1024]{2,1,0:T(8,128)(2,1)S(1)} %collective-permute-done.3.refs_1_), channel_id=1, source_target_pairs={{0,16},{8,24},{16,0},{24,8},{1,17},{9,25},{17,1},{25,9},{2,18},{10... | collective-permute-start | bytes 786440 | tf_op jit(solution)/shard_map/ppermute | solution.py:32
  69.6 11.5 %collective-permute-start.5 = (bf16[1,128,1024]{2,1,0:T(8,128)(2,1)S(1)}, bf16[1,128,1024]{2,1,0:T(8,128)(2,1)S(1)}, u32[]{:S(2)}, u32[]{:S(2)}) collective-permute-start(bf16[1,128,1024]{2,1,0:T(8,128)(2,1)S(1)} %collective-permute-done.3.refs_1_), channel_id=1, source_target_pairs={{0,4},{4,6},{6,2},{2,0},{1,5},{5,7},{7,3},{3,1},{8,12},{12,14},{14... | collective-permute-start | bytes 786440 | tf_op jit(solution)/shard_map/ppermute | solution.py:28
  72.3 10.6 %collective-permute-start.19 = (bf16[1,128,1024]{2,1,0:T(8,128)(2,1)S(1)}, bf16[1,128,1024]{2,1,0:T(8,128)(2,1)S(1)}, u32[]{:S(2)}, u32[]{:S(2)}) collective-permute-start(bf16[1,128,1024]{2,1,0:T(8,128)(2,1)S(1)} %collective-permute-done.17.refs_1_), channel_id=1, source_target_pairs={{0,16},{8,24},{16,0},{24,8},{1,17},{9,25},{17,1},{25,9},{2,18},{10... | collective-permute-start | bytes 786440 | tf_op jit(solution)/shard_map/ppermute | solution.py:32
  72.5 11.9 %collective-permute-start.18 = (bf16[1,128,1024]{2,1,0:T(8,128)(2,1)S(1)}, bf16[1,128,1024]{2,1,0:T(8,128)(2,1)S(1)}, u32[]{:S(2)}, u32[]{:S(2)}) collective-permute-start(bf16[1,128,1024]{2,1,0:T(8,128)(2,1)S(1)} %collective-permute-done.17.refs_1_), channel_id=1, source_target_pairs={{0,4},{4,6},{6,2},{2,0},{1,5},{5,7},{7,3},{3,1},{8,12},{12,14},{14... | collective-permute-start | bytes 786440 | tf_op jit(solution)/shard_map/ppermute | solution.py:28
  79.1 15.7 %collective-permute-start.14 = (bf16[512,512]{1,0:T(8,128)(2,1)S(1)}, bf16[512,512]{1,0:T(8,128)(2,1)S(1)}, u32[]{:S(2)}, u32[]{:S(2)}) collective-permute-start(bf16[512,512]{1,0:T(8,128)(2,1)S(1)} %join.1.refs_6_.refs_8_.refs_2_), channel_id=1, source_target_pairs={{0,1},{1,0},{2,3},{3,2},{4,5},{5,4},{6,7},{7,6},{8,9},{9,8},{10,11... | collective-permute-start | bytes 1572872 | tf_op jit(solution)/shard_map/ppermute | solution.py:32
  80.6 14.2 %collective-permute-start.15 = (bf16[512,512]{1,0:T(8,128)(2,1)S(1)}, bf16[512,512]{1,0:T(8,128)(2,1)S(1)}, u32[]{:S(2)}, u32[]{:S(2)}) collective-permute-start(bf16[512,512]{1,0:T(8,128)(2,1)S(1)} %collective-permute-done.13.refs_7_.refs_9_.refs_3_), channel_id=1, source_target_pairs={{0,1},{1,0},{2,3},{3,2},{4,5},{5,4},{6,7},{7,6},{8,9},{9,8},{10,11... | collective-permute-start | bytes 1572872 | tf_op jit(solution)/shard_map/ppermute | solution.py:32
  81.2 9.0 %collective-permute-start.16 = (bf16[1,128,1024]{2,1,0:T(8,128)(2,1)S(1)}, bf16[1,128,1024]{2,1,0:T(8,128)(2,1)S(1)}, u32[]{:S(2)}, u32[]{:S(2)}) collective-permute-start(bf16[1,128,1024]{2,1,0:T(8,128)(2,1)S(1)} %collective-permute-done.5.refs_2_), channel_id=1, source_target_pairs={{0,16},{8,24},{16,0},{24,8},{1,17},{9,25},{17,1},{25,9},{2,18},{10... | collective-permute-start | bytes 786440 | tf_op jit(solution)/shard_map/ppermute | solution.py:32
  84.4 8.5 %collective-permute-start.21 = (bf16[1,128,1024]{2,1,0:T(8,128)(2,1)S(1)}, bf16[1,128,1024]{2,1,0:T(8,128)(2,1)S(1)}, u32[]{:S(2)}, u32[]{:S(2)}) collective-permute-start(bf16[1,128,1024]{2,1,0:T(8,128)(2,1)S(1)} %collective-permute-done.18.refs_2_), channel_id=1, source_target_pairs={{0,16},{8,24},{16,0},{24,8},{1,17},{9,25},{17,1},{25,9},{2,18},{10... | collective-permute-start | bytes 786440 | tf_op jit(solution)/shard_map/ppermute | solution.py:32
  84.4 9.5 %collective-permute-start.7 = (bf16[1,128,1024]{2,1,0:T(8,128)(2,1)S(1)}, bf16[1,128,1024]{2,1,0:T(8,128)(2,1)S(1)}, u32[]{:S(2)}, u32[]{:S(2)}) collective-permute-start(bf16[1,128,1024]{2,1,0:T(8,128)(2,1)S(1)} %collective-permute-done.5.refs_2_), channel_id=1, source_target_pairs={{0,4},{4,6},{6,2},{2,0},{1,5},{5,7},{7,3},{3,1},{8,12},{12,14},{14... | collective-permute-start | bytes 786440 | tf_op jit(solution)/shard_map/ppermute | solution.py:28
  90.1 6.5 %collective-permute-start.20 = (bf16[1,128,1024]{2,1,0:T(8,128)(2,1)S(1)}, bf16[1,128,1024]{2,1,0:T(8,128)(2,1)S(1)}, u32[]{:S(2)}, u32[]{:S(2)}) collective-permute-start(bf16[1,128,1024]{2,1,0:T(8,128)(2,1)S(1)} %collective-permute-done.18.refs_2_), channel_id=1, source_target_pairs={{0,4},{4,6},{6,2},{2,0},{1,5},{5,7},{7,3},{3,1},{8,12},{12,14},{14... | collective-permute-start | bytes 786440 | tf_op jit(solution)/shard_map/ppermute | solution.py:28
  92.9 6.4 %collective-permute-start.22 = (bf16[1,128,1024]{2,1,0:T(8,128)(2,1)S(1)}, bf16[1,128,1024]{2,1,0:T(8,128)(2,1)S(1)}, u32[]{:S(2)}, u32[]{:S(2)}) collective-permute-start(bf16[1,128,1024]{2,1,0:T(8,128)(2,1)S(1)} %collective-permute-done.21.refs_6_), channel_id=1, source_target_pairs={{0,4},{4,6},{6,2},{2,0},{1,5},{5,7},{7,3},{3,1},{8,12},{12,14},{14... | collective-permute-start | bytes 786440 | tf_op jit(solution)/shard_map/ppermute | solution.py:28
  93.9 9.2 %collective-permute-start.8 = (bf16[1,128,1024]{2,1,0:T(8,128)(2,1)S(1)}, bf16[1,128,1024]{2,1,0:T(8,128)(2,1)S(1)}, u32[]{:S(2)}, u32[]{:S(2)}) collective-permute-start(bf16[1,128,1024]{2,1,0:T(8,128)(2,1)S(1)} %collective-permute-done.7.refs_0_), channel_id=1, source_target_pairs={{0,16},{8,24},{16,0},{24,8},{1,17},{9,25},{17,1},{25,9},{2,18},{10... | collective-permute-start | bytes 786440 | tf_op jit(solution)/shard_map/ppermute | solution.py:32

commit v2 on v1

--- a/solution.py
+++ b/solution.py
@@ -40,25 +40,25 @@
     return lax.optimization_barrier((x, *others))[0]
 
 
-def pack_kernel(span_ref, key_ref, value_ref, packed_ref, place_ref):
+def pack_kernel(span_ref, key_ref, packed_ref, place_ref):
     tokens, width = key_ref.shape[1:]
-    packed_ref[:tokens, :width] = key_ref[0]
-    packed_ref[:tokens, width:] = value_ref[0]
+    packed_ref[0, :tokens, :] = key_ref[0]
     spans = span_ref.shape[1]
     span = tokens // spans
-    lane = lax.broadcasted_iota(jnp.int32, (TAG, 2 * width), 1)
+    lane = lax.broadcasted_iota(jnp.int32, (TAG, width), 1)
     row = lax.broadcasted_iota(jnp.int32, place_ref.shape, 0)
     ids = jnp.zeros(lane.shape, jnp.float32)
     base = jnp.zeros(row.shape, jnp.int32)
     for j in range(spans):
         ids = jnp.where(lane // span == j, span_ref[0, j].astype(jnp.float32), ids)
         base = jnp.where(row // span == j, span_ref[0, j] * span, base)
-    packed_ref[tokens:, :] = ids.astype(jnp.bfloat16)
+    packed_ref[0, tokens:, :] = ids.astype(jnp.bfloat16)
     place_ref[...] = (base + row % span).astype(jnp.float32)
 
 
-def fetch_kernel(place_ref, query_ref, out_ref):
-    out_ref[...] = query_ref[...]
+def fetch_kernel(place_ref, query_ref, value_ref, query_held, value_held):
+    query_held[...] = query_ref[...]
+    value_held[...] = value_ref[...]
 
 
 def turn_kernel(n, ready_ref, cot_ref, *out_refs):
@@ -80,15 +80,17 @@
 
 
 def attention_kernel(group, scale, n, spans, place_ref, query_ref, *refs):
-    kv_refs, (whole_ref, *part_refs) = refs[:n], refs[n:]
-    tokens = query_ref.shape[1]
-    width = kv_refs[0].shape[1] // 2
+    key_refs, value_refs, (whole_ref, *part_refs) = refs[:n], refs[n : 2 * n], refs[2 * n :]
+    tokens, width = value_refs[0].shape[1:]
     heads = width // HD
     span = tokens // spans
     lane = lax.broadcasted_iota(jnp.int32, (1, tokens), 1)
     inner = (lane % span).astype(jnp.float32)
     key_pos = jnp.concatenate(
-        [ref[tokens : tokens + 1, :tokens].astype(jnp.float32) * span + inner for ref in kv_refs],
+        [
+            ref[0, tokens : tokens + 1, :tokens].astype(jnp.float32) * span + inner
+            for ref in key_refs
+        ],
         axis=1,
     )
     hidden = jnp.where(key_pos <= place_ref[:, :1], 0.0, -1e30)
@@ -96,10 +98,9 @@
     for j in range(heads):
         first = j * group * HD
         out_ref = part_refs[j * len(part_refs) // heads]
-        key_block = jnp.concatenate([ref[:tokens, j * HD : (j + 1) * HD] for ref in kv_refs], axis=0)
-        value_block = jnp.concatenate(
-            [ref[:tokens, width + j * HD : width + (j + 1) * HD] for ref in kv_refs], axis=0
-        )
+        columns = slice(j * HD, (j + 1) * HD)
+        key_block = jnp.concatenate([ref[0, :tokens, columns] for ref in key_refs], axis=0)
+        value_block = jnp.concatenate([ref[0, :, columns] for ref in value_refs], axis=0)
         queries = jnp.concatenate(
             [query_ref[0, :, first + g * HD : first + (g + 1) * HD] for g in range(group)], axis=0
         )
@@ -190,23 +191,26 @@
     packed, place = pl.pallas_call(
         pack_kernel,
         out_shape=[
-            jax.ShapeDtypeStruct((tokens + TAG, 2 * width), jnp.bfloat16),
+            jax.ShapeDtypeStruct((1, tokens + TAG, width), jnp.bfloat16),
             jax.ShapeDtypeStruct((tokens, 128), jnp.float32),
         ],
-        in_specs=[SMEM, VMEM, VMEM],
+        in_specs=[SMEM, VMEM],
         out_specs=[VMEM] * 2,
         compiler_params=params(16),
         name="pack",
-    )(span_ids, keys, values)
-    kv = [packed] + [around(packed, s) for s in range(1, n)]
-    query_held = pl.pallas_call(
+    )(span_ids, keys)
+    key_ring, value_ring = [packed], [values]
+    for _ in range(n - 1):
+        value_ring.append(around(value_ring[-1], 1))
+        key_ring.append(around(key_ring[-1], 1))
+    query_held, value_held = pl.pallas_call(
         fetch_kernel,
-        out_shape=jax.ShapeDtypeStruct(queries.shape, jnp.bfloat16),
-        in_specs=[ANY, VMEM],
-        out_specs=VMEM,
+        out_shape=[jax.ShapeDtypeStruct(x.shape, jnp.bfloat16) for x in (queries, values)],
+        in_specs=[ANY, VMEM, VMEM],
+        out_specs=[VMEM] * 2,
         compiler_params=params(16),
         name="fetch",
-    )(place, queries)
+    )(place, queries, values)
     turned = pl.pallas_call(
         functools.partial(turn_kernel, n),
         out_shape=[jax.ShapeDtypeStruct((half, tokens), jnp.bfloat16)] * n,
@@ -220,11 +224,11 @@
         functools.partial(attention_kernel, HQ // HK, 1.0 / math.sqrt(HD), n, spans),
         out_shape=[jax.ShapeDtypeStruct(queries.shape, jnp.bfloat16)]
         + [jax.ShapeDtypeStruct((1, tokens, chunk), jnp.bfloat16)] * parts,
-        in_specs=[VMEM] * (2 + n),
+        in_specs=[VMEM] * (2 + 2 * n),
         out_specs=[VMEM] * (1 + parts),
         compiler_params=params(40),
         name="attend",
-    )(place, query_held, *kv)
+    )(place, query_held, *key_ring, value_held, *value_ring[1:])
 
     near, mirrored = [], []
     for c in range(parts):
@@ -238,7 +242,7 @@
         near.append(held)
         mirrored.append(sent)
 
-    turned = [turned[0]] + [around(after(turned[s], attention), s) for s in range(1, n)]
+    turned = [turned[0]] + [around(after(turned[s], value_ring[n - 2]), s) for s in range(1, n)]
     mine = pl.pallas_call(
         join_kernel,
         out_shape=jax.ShapeDtypeStruct((half, n * tokens), jnp.bfloat16),

time: 106 us -> 94.5 us (0.89)
  waiting for transfers between devices: 40.2 us -> 29.2 us
    ppermute x13 -> x16, waiting for transfers between devices: 32.5 us -> 26.1 us  [around(): lax.ppermute(x, 'ctx', [(order[q], order[(q + shift) % n]) for q in range...]
    ppermute x10, starting transfers between devices: 18.8 us -> 13.2 us  [swap(): lax.ppermute(x, axis, [(i, i ^ mask) for i in range(lax.axis_size(axis))])]
    ppermute x13 -> x16, starting transfers between devices: 29.6 us -> 34.9 us  [around(): lax.ppermute(x, 'ctx', [(order[q], order[(q + shift) % n]) for q in range...]
    ppermute x10, waiting for transfers between devices: 7.73 us -> 3.07 us  [swap(): lax.ppermute(x, axis, [(i, i ^ mask) for i in range(lax.axis_size(axis))])]
  transfers between devices with their start and end apart: 23 -> 26, of which waited for: 10 -> 9; matrix products, arithmetic and copies ran while one was open for 0% -> 0% of each run, Pallas kernels for 6% -> 6%
where the time goes in v2:
time: 94.5 us; the launch traced here: 94.2 us
  starting transfers between devices  48.1 us (51%)
  waiting for transfers between devices  29.2 us (31%)
  Pallas kernels  11.5 us (12%)
  local copies, waits for them, and re-layouts  4.72 us (5%)
    ppermute x16, starting transfers between devices, around(): lax.ppermute(x, 'ctx', [(order[q], order[(q + shift) % n]) for q in range...  34.9 us
    ppermute x16, waiting for transfers between devices, around(): lax.ppermute(x, 'ctx', [(order[q], order[(q + shift) % n]) for q in range...  26.1 us
    ppermute x10, starting transfers between devices, swap(): lax.ppermute(x, axis, [(i, i ^ mask) for i in range(lax.axis_size(axis))])  13.2 us
    pallas_call x2, Pallas kernels, local(): pl.pallas_call(functools.partial(finish_kernel, slots, n - slots, c * chu...  6.29 us
    unnamed x10, local copies, waits for them, and re-layouts  4.72 us
    ppermute x10, waiting for transfers between devices, swap(): lax.ppermute(x, axis, [(i, i ^ mask) for i in range(lax.axis_size(axis))])  3.07 us
    pallas_call x1, Pallas kernels, local(): pl.pallas_call(functools.partial(attention_kernel, HQ // HK, 1.0 / math.s...  2.51 us
  transfers between devices with their start and end apart: 26, of which 9 were waited for; matrix products, arithmetic and copies ran while one was open for 0% of the time, Pallas kernels for 6%

profile of v2, /device:TPU:0, one launch (start us, length us, event | category | flops | bytes accessed | tf_op | source)
XLA Modules:
  0.0 94.2 jit_solution(13966807075198867975)
XLA Ops:
  0.6 0.9 copy-done.2
  1.5 0.7 copy-done.4
  2.2 0.6 pack.1
  2.8 4.1 %collective-permute-start = (bf16[1,144,512]{2,1,0:T(8,128)(2,1)S(1)}, bf16[1,144,512]{2,1,0:T(8,128)(2,1)S(1)}, u32[]{:S(2)}, u32[]{:S(2)}) collective-permute-start(bf16[1,144,512]{2,1,0:T(8,128)(2,1)S(1)} %get-tuple-element.29.refs_0_), channel_id=1, source_target_pairs={{0,4},{4,6},{6,2},{2,0},{1,5},{5,7},{7,3},{3,1},{8,12},{12,14},{14... | collective-permute-start | bytes 442376 | tf_op jit(solution)/shard_map/ppermute | solution.py:28
  6.8 1.6 %collective-permute-start.3 = (bf16[1,128,512]{2,1,0:T(8,128)(2,1)}, bf16[1,128,512]{2,1,0:T(8,128)(2,1)S(1)}, u32[]{:S(2)}, u32[]{:S(2)}) collective-permute-start(bf16[1,128,512]{2,1,0:T(8,128)(2,1)} %value_ref.1), channel_id=1, source_target_pairs={{0,4},{4,6},{6,2},{2,0},{1,5},{5,7},{7,3},{3,1},{8,12},{12,14},{14... | collective-permute-start | bytes 393224 | tf_op jit(solution)/shard_map/ppermute | solution.py:28
  8.4 2.7 %collective-permute-done.refs_1_ = bf16[1,144,512]{2,1,0:T(8,128)(2,1)S(1)} collective-permute-done((bf16[1,144,512]{2,1,0:T(8,128)(2,1)S(1)}, bf16[1,144,512]{2,1,0:T(8,128)(2,1)S(1)}, u32[]{:S(2)}, u32[]{:S(2)}) %collective-permute-start) | collective-permute-done | bytes 147488 | tf_op jit(solution)/shard_map/ppermute | solution.py:28
  11.1 3.4 %collective-permute-start.1 = (bf16[1,144,512]{2,1,0:T(8,128)(2,1)S(1)}, bf16[1,144,512]{2,1,0:T(8,128)(2,1)S(1)}, u32[]{:S(2)}, u32[]{:S(2)}) collective-permute-start(bf16[1,144,512]{2,1,0:T(8,128)(2,1)S(1)} %collective-permute-done.refs_1_), channel_id=1, source_target_pairs={{0,4},{4,6},{6,2},{2,0},{1,5},{5,7},{7,3},{3,1},{8,12},{12,14},{14... | collective-permute-start | bytes 442376 | tf_op jit(solution)/shard_map/ppermute | solution.py:28
  14.5 1.9 %collective-permute-start.4 = (bf16[1,128,512]{2,1,0:T(8,128)(2,1)S(1)}, bf16[1,128,512]{2,1,0:T(8,128)(2,1)S(1)}, u32[]{:S(2)}, u32[]{:S(2)}) collective-permute-start(bf16[1,128,512]{2,1,0:T(8,128)(2,1)S(1)} %collective-permute-done.3.refs_5_), channel_id=1, source_target_pairs={{0,4},{4,6},{6,2},{2,0},{1,5},{5,7},{7,3},{3,1},{8,12},{12,14},{14... | collective-permute-start | bytes 393224 | tf_op jit(solution)/shard_map/ppermute | solution.py:28
  16.4 2.3 %collective-permute-done.1.refs_2_ = bf16[1,144,512]{2,1,0:T(8,128)(2,1)S(1)} collective-permute-done((bf16[1,144,512]{2,1,0:T(8,128)(2,1)S(1)}, bf16[1,144,512]{2,1,0:T(8,128)(2,1)S(1)}, u32[]{:S(2)}, u32[]{:S(2)}) %collective-permute-start.1) | collective-permute-done | bytes 147488 | tf_op jit(solution)/shard_map/ppermute | solution.py:28
  18.7 3.4 %collective-permute-start.2 = (bf16[1,144,512]{2,1,0:T(8,128)(2,1)S(1)}, bf16[1,144,512]{2,1,0:T(8,128)(2,1)S(1)}, u32[]{:S(2)}, u32[]{:S(2)}) collective-permute-start(bf16[1,144,512]{2,1,0:T(8,128)(2,1)S(1)} %collective-permute-done.1.refs_2_), channel_id=1, source_target_pairs={{0,4},{4,6},{6,2},{2,0},{1,5},{5,7},{7,3},{3,1},{8,12},{12,14},{14... | collective-permute-start | bytes 442376 | tf_op jit(solution)/shard_map/ppermute | solution.py:28
  22.1 2.5 %collective-permute-start.5 = (bf16[1,128,512]{2,1,0:T(8,128)(2,1)S(1)}, bf16[1,128,512]{2,1,0:T(8,128)(2,1)S(1)}, u32[]{:S(2)}, u32[]{:S(2)}) collective-permute-start(bf16[1,128,512]{2,1,0:T(8,128)(2,1)S(1)} %collective-permute-done.4.refs_6_), channel_id=1, source_target_pairs={{0,4},{4,6},{6,2},{2,0},{1,5},{5,7},{7,3},{3,1},{8,12},{12,14},{14... | collective-permute-start | bytes 393224 | tf_op jit(solution)/shard_map/ppermute | solution.py:28
  24.6 1.2 %copy-done = bf16[1,128,4096]{2,1,0:T(8,128)(2,1)S(1)} copy-done((bf16[1,128,4096]{2,1,0:T(8,128)(2,1)S(1)}, bf16[1,128,4096]{2,1,0:T(8,128)(2,1)}, u32[]{:S(2)}) %copy-start) | copy-done | bytes 1048600
  25.8 0.2 turn.1
  26.0 0.0 copy-start.1
  26.0 1.0 %copy-done.1 = bf16[1,128,2048]{2,1,0:T(8,128)(2,1)S(1)} copy-done((bf16[1,128,2048]{2,1,0:T(8,128)(2,1)S(1)}, bf16[1,128,2048]{2,1,0:T(8,128)(2,1)}, u32[]{:S(2)}) %copy-start.1) | copy-done | bytes 524312
  27.0 0.9 copy-done.3
  28.0 0.0 collective-permute-done.2.refs_3_
  28.0 2.5 %attend.1 = (bf16[1,128,2048]{2,1,0:T(8,128)(2,1)}, bf16[1,128,1024]{2,1,0:T(8,128)(2,1)S(1)}, bf16[1,128,1024]{2,1,0:T(8,128)(2,1)S(1)}) custom-call(f32[128,128]{1,0:T(8,128)S(1)} %get-tuple-element.22.place_ref.ready_ref, bf16[1,128,2048]{2,1,0:T(8,128)(2,1)S(1)} %get-tuple-element.28.query_ref, bf16[1,144,512]{2,1,0:T(8,128)(2,1)S(1)} %get-tuple-element.29.refs_0_, ...), custom_call_target="tpu_custom_call" | custom-call | tf_op jit(solution)/shard_map/attend/pallas_call | solution.py:223
  30.5 1.5 %collective-permute-start.7 = (bf16[1,128,1024]{2,1,0:T(8,128)(2,1)S(1)}, bf16[1,128,1024]{2,1,0:T(8,128)(2,1)S(1)}, u32[]{:S(2)}, u32[]{:S(2)}) collective-permute-start(bf16[1,128,1024]{2,1,0:T(8,128)(2,1)S(1)} %get-tuple-element.32.refs_0_), channel_id=1, source_target_pairs={{0,16},{8,24},{16,0},{24,8},{1,17},{9,25},{17,1},{25,9},{2,18},{10... | collective-permute-start | bytes 786440 | tf_op jit(solution)/shard_map/ppermute | solution.py:32
  32.0 0.5 collective-permute-start.15
  32.5 1.4 %collective-permute-start.14 = (bf16[512,128]{1,0:T(8,128)(2,1)S(1)}, bf16[512,128]{1,0:T(8,128)(2,1)S(1)}, u32[]{:S(2)}, u32[]{:S(2)}) collective-permute-start(bf16[512,128]{1,0:T(8,128)(2,1)S(1)} %get-tuple-element.37), channel_id=1, source_target_pairs={{0,2},{4,0},{6,4},{2,6},{1,3},{5,1},{7,5},{3,7},{8,10},{12,8},{14,... | collective-permute-start | bytes 393224 | tf_op jit(solution)/shard_map/ppermute | solution.py:28
  34.0 2.5 %collective-permute-start.13 = (bf16[512,128]{1,0:T(8,128)(2,1)S(1)}, bf16[512,128]{1,0:T(8,128)(2,1)S(1)}, u32[]{:S(2)}, u32[]{:S(2)}) collective-permute-start(bf16[512,128]{1,0:T(8,128)(2,1)S(1)} %get-tuple-element.36), channel_id=1, source_target_pairs={{0,6},{4,2},{6,0},{2,4},{1,7},{5,3},{7,1},{3,5},{8,14},{12,10},{14... | collective-permute-start | bytes 393224 | tf_op jit(solution)/shard_map/ppermute | solution.py:28
  36.4 0.0 collective-permute-start.12
  36.4 8.0 %collective-permute-done.14.refs_3_ = bf16[512,128]{1,0:T(8,128)(2,1)S(1)} collective-permute-done((bf16[512,128]{1,0:T(8,128)(2,1)S(1)}, bf16[512,128]{1,0:T(8,128)(2,1)S(1)}, u32[]{:S(2)}, u32[]{:S(2)}) %collective-permute-start.14) | collective-permute-done | bytes 131104 | tf_op jit(solution)/shard_map/ppermute | solution.py:28
  44.5 0.1 join.1.refs_6_.refs_8_.refs_2_
  44.6 1.6 %collective-permute-start.16 = (bf16[512,512]{1,0:T(8,128)(2,1)S(1)}, bf16[512,512]{1,0:T(8,128)(2,1)S(1)}, u32[]{:S(2)}, u32[]{:S(2)}) collective-permute-start(bf16[512,512]{1,0:T(8,128)(2,1)S(1)} %join.1.refs_6_.refs_8_.refs_2_), channel_id=1, source_target_pairs={{0,16},{8,24},{16,0},{24,8},{1,17},{9,25},{17,1},{25,9},{2,18},{10... | collective-permute-start | bytes 1572872 | tf_op jit(solution)/shard_map/ppermute | solution.py:32
  46.2 1.9 %collective-permute-start.6 = (bf16[1,128,1024]{2,1,0:T(8,128)(2,1)S(1)}, bf16[1,128,1024]{2,1,0:T(8,128)(2,1)S(1)}, u32[]{:S(2)}, u32[]{:S(2)}) collective-permute-start(bf16[1,128,1024]{2,1,0:T(8,128)(2,1)S(1)} %get-tuple-element.32.refs_0_), channel_id=1, source_target_pairs={{0,4},{4,6},{6,2},{2,0},{1,5},{5,7},{7,3},{3,1},{8,12},{12,14},{14... | collective-permute-start | bytes 786440 | tf_op jit(solution)/shard_map/ppermute | solution.py:28
  48.1 5.6 %collective-permute-done.20.refs_1_ = bf16[1,128,1024]{2,1,0:T(8,128)(2,1)S(1)} collective-permute-done((bf16[1,128,1024]{2,1,0:T(8,128)(2,1)S(1)}, bf16[1,128,1024]{2,1,0:T(8,128)(2,1)S(1)}, u32[]{:S(2)}, u32[]{:S(2)}) %collective-permute-start.20) | collective-permute-done | bytes 262176 | tf_op jit(solution)/shard_map/ppermute | solution.py:28
  53.7 1.6 %collective-permute-start.22 = (bf16[1,128,1024]{2,1,0:T(8,128)(2,1)S(1)}, bf16[1,128,1024]{2,1,0:T(8,128)(2,1)S(1)}, u32[]{:S(2)}, u32[]{:S(2)}) collective-permute-start(bf16[1,128,1024]{2,1,0:T(8,128)(2,1)S(1)} %collective-permute-done.20.refs_1_), channel_id=1, source_target_pairs={{0,16},{8,24},{16,0},{24,8},{1,17},{9,25},{17,1},{25,9},{2,18},{10... | collective-permute-start | bytes 786440 | tf_op jit(solution)/shard_map/ppermute | solution.py:32
  55.2 0.9 collective-permute-start.21
  56.1 1.5 %collective-permute-start.17 = (bf16[512,512]{1,0:T(8,128)(2,1)S(1)}, bf16[512,512]{1,0:T(8,128)(2,1)S(1)}, u32[]{:S(2)}, u32[]{:S(2)}) collective-permute-start(bf16[512,512]{1,0:T(8,128)(2,1)S(1)} %join.1.refs_6_.refs_8_.refs_2_), channel_id=1, source_target_pairs={{0,1},{1,0},{2,3},{3,2},{4,5},{5,4},{6,7},{7,6},{8,9},{9,8},{10,11... | collective-permute-start | bytes 1572872 | tf_op jit(solution)/shard_map/ppermute | solution.py:32
  57.6 0.4 collective-permute-done.6.refs_1_
  58.0 0.5 collective-permute-start.9
  58.6 3.0 %collective-permute-done.22.refs_5_ = bf16[1,128,1024]{2,1,0:T(8,128)(2,1)S(1)} collective-permute-done((bf16[1,128,1024]{2,1,0:T(8,128)(2,1)S(1)}, bf16[1,128,1024]{2,1,0:T(8,128)(2,1)S(1)}, u32[]{:S(2)}, u32[]{:S(2)}) %collective-permute-start.22) | collective-permute-done | bytes 262176 | tf_op jit(solution)/shard_map/ppermute | solution.py:32
  61.6 5.5 %collective-permute-start.8 = (bf16[1,128,1024]{2,1,0:T(8,128)(2,1)S(1)}, bf16[1,128,1024]{2,1,0:T(8,128)(2,1)S(1)}, u32[]{:S(2)}, u32[]{:S(2)}) collective-permute-start(bf16[1,128,1024]{2,1,0:T(8,128)(2,1)S(1)} %collective-permute-done.6.refs_1_), channel_id=1, source_target_pairs={{0,4},{4,6},{6,2},{2,0},{1,5},{5,7},{7,3},{3,1},{8,12},{12,14},{14... | collective-permute-start | bytes 786440 | tf_op jit(solution)/shard_map/ppermute | solution.py:28
  67.1 1.5 %collective-permute-start.18 = (bf16[512,512]{1,0:T(8,128)(2,1)S(1)}, bf16[512,512]{1,0:T(8,128)(2,1)S(1)}, u32[]{:S(2)}, u32[]{:S(2)}) collective-permute-start(bf16[512,512]{1,0:T(8,128)(2,1)S(1)} %collective-permute-done.16.refs_7_.refs_9_.refs_3_), channel_id=1, source_target_pairs={{0,1},{1,0},{2,3},{3,2},{4,5},{5,4},{6,7},{7,6},{8,9},{9,8},{10,11... | collective-permute-start | bytes 1572872 | tf_op jit(solution)/shard_map/ppermute | solution.py:32
  68.6 1.5 %collective-permute-start.24 = (bf16[1,128,1024]{2,1,0:T(8,128)(2,1)S(1)}, bf16[1,128,1024]{2,1,0:T(8,128)(2,1)S(1)}, u32[]{:S(2)}, u32[]{:S(2)}) collective-permute-start(bf16[1,128,1024]{2,1,0:T(8,128)(2,1)S(1)} %collective-permute-done.21.refs_2_), channel_id=1, source_target_pairs={{0,16},{8,24},{16,0},{24,8},{1,17},{9,25},{17,1},{25,9},{2,18},{10... | collective-permute-start | bytes 786440 | tf_op jit(solution)/shard_map/ppermute | solution.py:32
  70.1 4.2 %collective-permute-done.8.refs_2_ = bf16[1,128,1024]{2,1,0:T(8,128)(2,1)S(1)} collective-permute-done((bf16[1,128,1024]{2,1,0:T(8,128)(2,1)S(1)}, bf16[1,128,1024]{2,1,0:T(8,128)(2,1)S(1)}, u32[]{:S(2)}, u32[]{:S(2)}) %collective-permute-start.8) | collective-permute-done | bytes 262176 | tf_op jit(solution)/shard_map/ppermute | solution.py:28
  74.3 2.9 %collective-permute-start.10 = (bf16[1,128,1024]{2,1,0:T(8,128)(2,1)S(1)}, bf16[1,128,1024]{2,1,0:T(8,128)(2,1)S(1)}, u32[]{:S(2)}, u32[]{:S(2)}) collective-permute-start(bf16[1,128,1024]{2,1,0:T(8,128)(2,1)S(1)} %collective-permute-done.8.refs_2_), channel_id=1, source_target_pairs={{0,4},{4,6},{6,2},{2,0},{1,5},{5,7},{7,3},{3,1},{8,12},{12,14},{14... | collective-permute-start | bytes 786440 | tf_op jit(solution)/shard_map/ppermute | solution.py:28
  77.2 1.5 %collective-permute-start.19 = (bf16[1,128,1024]{2,1,0:T(8,128)(2,1)S(1)}, bf16[1,128,1024]{2,1,0:T(8,128)(2,1)S(1)}, u32[]{:S(2)}, u32[]{:S(2)}) collective-permute-start(bf16[1,128,1024]{2,1,0:T(8,128)(2,1)S(1)} %collective-permute-done.8.refs_2_), channel_id=1, source_target_pairs={{0,16},{8,24},{16,0},{24,8},{1,17},{9,25},{17,1},{25,9},{2,18},{10... | collective-permute-start | bytes 786440 | tf_op jit(solution)/shard_map/ppermute | solution.py:32
  78.7 0.0 collective-permute-start.23
  78.7 2.9 %collective-permute-start.25 = (bf16[1,128,1024]{2,1,0:T(8,128)(2,1)S(1)}, bf16[1,128,1024]{2,1,0:T(8,128)(2,1)S(1)}, u32[]{:S(2)}, u32[]{:S(2)}) collective-permute-start(bf16[1,128,1024]{2,1,0:T(8,128)(2,1)S(1)} %collective-permute-done.24.refs_6_), channel_id=1, source_target_pairs={{0,4},{4,6},{6,2},{2,0},{1,5},{5,7},{7,3},{3,1},{8,12},{12,14},{14... | collective-permute-start | bytes 786440 | tf_op jit(solution)/shard_map/ppermute | solution.py:28
  81.7 0.6 collective-permute-done.10.refs_0_
  82.3 1.5 %collective-permute-start.11 = (bf16[1,128,1024]{2,1,0:T(8,128)(2,1)S(1)}, bf16[1,128,1024]{2,1,0:T(8,128)(2,1)S(1)}, u32[]{:S(2)}, u32[]{:S(2)}) collective-permute-start(bf16[1,128,1024]{2,1,0:T(8,128)(2,1)S(1)} %collective-permute-done.10.refs_0_), channel_id=1, source_target_pairs={{0,16},{8,24},{16,0},{24,8},{1,17},{9,25},{17,1},{25,9},{2,18},{10... | collective-permute-start | bytes 786440 | tf_op jit(solution)/shard_map/ppermute | solution.py:32
  83.8 1.8 %early.1.refs_6_ = f32[1024,1024]{1,0:T(8,128)S(1)} custom-call(bf16[1,128,1024]{2,1,0:T(8,128)(2,1)S(1)} %get-tuple-element.32.refs_0_, bf16[1,128,1024]{2,1,0:T(8,128)(2,1)S(1)} %collective-permute-done.6.refs_1_, bf16[1,128,1024]{2,1,0:T(8,128)(2,1)S(1)} %collective-permute-done.8.refs_2_, bf16[1,128,1024]{2,1,0:T(8,128)(2,1)S(1)} %collective-permute-done.7.refs_3_, ...), custom_call_target="tpu_custom_call" | custom-call | flops 1610612736 | bytes 8388608 | tf_op jit(solution)/shard_map/early/pallas_call | solution.py:261
  85.6 2.3 %collective-permute-done.25.refs_7_ = bf16[1,128,1024]{2,1,0:T(8,128)(2,1)S(1)} collective-permute-done((bf16[1,128,1024]{2,1,0:T(8,128)(2,1)S(1)}, bf16[1,128,1024]{2,1,0:T(8,128)(2,1)S(1)}, u32[]{:S(2)}, u32[]{:S(2)}) %collective-permute-start.25) | collective-permute-done | bytes 262176 | tf_op jit(solution)/shard_map/ppermute | solution.py:28
  87.9 3.8 %finish.2.refs_7_ = bf16[1,1024,2048]{2,1,0:T(8,128)(2,1)} custom-call(bf16[1,128,1024]{2,1,0:T(8,128)(2,1)S(1)} %get-tuple-element.38.refs_0_, bf16[1,128,1024]{2,1,0:T(8,128)(2,1)S(1)} %collective-permute-done.20.refs_1_, bf16[1,128,1024]{2,1,0:T(8,128)(2,1)S(1)} %collective-permute-done.21.refs_2_, ...), custom_call_target="tpu_custom_call" | custom-call | flops 2147483648 | bytes 8388608 | tf_op jit(solution)/shard_map/finish/pallas_call | solution.py:285
  91.7 2.5 %finish.3 = bf16[1,1024,2048]{2,1,0:T(8,128)(2,1)} custom-call(bf16[1,128,1024]{2,1,0:T(8,128)(2,1)S(1)} %collective-permute-done.10.refs_0_, bf16[1,128,1024]{2,1,0:T(8,128)(2,1)S(1)} %collective-permute-done.11.refs_1_, bf16[512,512]{1,0:T(8,128)(2,1)S(1)} %join.1.refs_6_.refs_8_.refs_2_, ...), custom_call_target="tpu_custom_call", output_to_operand_aliasing={{}: (7, {})} | custom-call | flops 536870912 | bytes 8388608 | tf_op jit(solution)/shard_map/finish/pallas_call | solution.py:285
  (22 shorter events, 0.1 us)
Async XLA Ops:
  0.6 0.9 copy-start.2
  1.5 0.7 copy-start.4
  2.8 8.3 %collective-permute-start = (bf16[1,144,512]{2,1,0:T(8,128)(2,1)S(1)}, bf16[1,144,512]{2,1,0:T(8,128)(2,1)S(1)}, u32[]{:S(2)}, u32[]{:S(2)}) collective-permute-start(bf16[1,144,512]{2,1,0:T(8,128)(2,1)S(1)} %get-tuple-element.29.refs_0_), channel_id=1, source_target_pairs={{0,4},{4,6},{6,2},{2,0},{1,5},{5,7},{7,3},{3,1},{8,12},{12,14},{14... | collective-permute-start | bytes 442376 | tf_op jit(solution)/shard_map/ppermute | solution.py:28
  6.8 7.6 %collective-permute-start.3 = (bf16[1,128,512]{2,1,0:T(8,128)(2,1)}, bf16[1,128,512]{2,1,0:T(8,128)(2,1)S(1)}, u32[]{:S(2)}, u32[]{:S(2)}) collective-permute-start(bf16[1,128,512]{2,1,0:T(8,128)(2,1)} %value_ref.1), channel_id=1, source_target_pairs={{0,4},{4,6},{6,2},{2,0},{1,5},{5,7},{7,3},{3,1},{8,12},{12,14},{14... | collective-permute-start | bytes 393224 | tf_op jit(solution)/shard_map/ppermute | solution.py:28
  11.1 7.6 %collective-permute-start.1 = (bf16[1,144,512]{2,1,0:T(8,128)(2,1)S(1)}, bf16[1,144,512]{2,1,0:T(8,128)(2,1)S(1)}, u32[]{:S(2)}, u32[]{:S(2)}) collective-permute-start(bf16[1,144,512]{2,1,0:T(8,128)(2,1)S(1)} %collective-permute-done.refs_1_), channel_id=1, source_target_pairs={{0,4},{4,6},{6,2},{2,0},{1,5},{5,7},{7,3},{3,1},{8,12},{12,14},{14... | collective-permute-start | bytes 442376 | tf_op jit(solution)/shard_map/ppermute | solution.py:28
  14.5 7.6 %collective-permute-start.4 = (bf16[1,128,512]{2,1,0:T(8,128)(2,1)S(1)}, bf16[1,128,512]{2,1,0:T(8,128)(2,1)S(1)}, u32[]{:S(2)}, u32[]{:S(2)}) collective-permute-start(bf16[1,128,512]{2,1,0:T(8,128)(2,1)S(1)} %collective-permute-done.3.refs_5_), channel_id=1, source_target_pairs={{0,4},{4,6},{6,2},{2,0},{1,5},{5,7},{7,3},{3,1},{8,12},{12,14},{14... | collective-permute-start | bytes 393224 | tf_op jit(solution)/shard_map/ppermute | solution.py:28
  18.7 9.3 %collective-permute-start.2 = (bf16[1,144,512]{2,1,0:T(8,128)(2,1)S(1)}, bf16[1,144,512]{2,1,0:T(8,128)(2,1)S(1)}, u32[]{:S(2)}, u32[]{:S(2)}) collective-permute-start(bf16[1,144,512]{2,1,0:T(8,128)(2,1)S(1)} %collective-permute-done.1.refs_2_), channel_id=1, source_target_pairs={{0,4},{4,6},{6,2},{2,0},{1,5},{5,7},{7,3},{3,1},{8,12},{12,14},{14... | collective-permute-start | bytes 442376 | tf_op jit(solution)/shard_map/ppermute | solution.py:28
  22.1 5.9 %collective-permute-start.5 = (bf16[1,128,512]{2,1,0:T(8,128)(2,1)S(1)}, bf16[1,128,512]{2,1,0:T(8,128)(2,1)S(1)}, u32[]{:S(2)}, u32[]{:S(2)}) collective-permute-start(bf16[1,128,512]{2,1,0:T(8,128)(2,1)S(1)} %collective-permute-done.4.refs_6_), channel_id=1, source_target_pairs={{0,4},{4,6},{6,2},{2,0},{1,5},{5,7},{7,3},{3,1},{8,12},{12,14},{14... | collective-permute-start | bytes 393224 | tf_op jit(solution)/shard_map/ppermute | solution.py:28
  24.6 1.2 %copy-start = (bf16[1,128,4096]{2,1,0:T(8,128)(2,1)S(1)}, bf16[1,128,4096]{2,1,0:T(8,128)(2,1)}, u32[]{:S(2)}) copy-start(bf16[1,128,4096]{2,1,0:T(8,128)(2,1)} %cot_ref.1) | copy-start | bytes 3145732
  26.0 1.0 %copy-start.1 = (bf16[1,128,2048]{2,1,0:T(8,128)(2,1)S(1)}, bf16[1,128,2048]{2,1,0:T(8,128)(2,1)}, u32[]{:S(2)}) copy-start(bf16[1,128,2048]{2,1,0:T(8,128)(2,1)} %query_ref.1) | copy-start | bytes 1572868
  27.0 0.9 copy-start.3
  30.5 14.0 %collective-permute-start.7 = (bf16[1,128,1024]{2,1,0:T(8,128)(2,1)S(1)}, bf16[1,128,1024]{2,1,0:T(8,128)(2,1)S(1)}, u32[]{:S(2)}, u32[]{:S(2)}) collective-permute-start(bf16[1,128,1024]{2,1,0:T(8,128)(2,1)S(1)} %get-tuple-element.32.refs_0_), channel_id=1, source_target_pairs={{0,16},{8,24},{16,0},{24,8},{1,17},{9,25},{17,1},{25,9},{2,18},{10... | collective-permute-start | bytes 786440 | tf_op jit(solution)/shard_map/ppermute | solution.py:32
  32.0 12.5 %collective-permute-start.15 = (bf16[1,128,1024]{2,1,0:T(8,128)(2,1)S(1)}, bf16[1,128,1024]{2,1,0:T(8,128)(2,1)S(1)}, u32[]{:S(2)}, u32[]{:S(2)}) collective-permute-start(bf16[1,128,1024]{2,1,0:T(8,128)(2,1)S(1)} %get-tuple-element.38.refs_0_), channel_id=1, source_target_pairs={{0,16},{8,24},{16,0},{24,8},{1,17},{9,25},{17,1},{25,9},{2,18},{10... | collective-permute-start | bytes 786440 | tf_op jit(solution)/shard_map/ppermute | solution.py:32
  32.5 11.9 %collective-permute-start.14 = (bf16[512,128]{1,0:T(8,128)(2,1)S(1)}, bf16[512,128]{1,0:T(8,128)(2,1)S(1)}, u32[]{:S(2)}, u32[]{:S(2)}) collective-permute-start(bf16[512,128]{1,0:T(8,128)(2,1)S(1)} %get-tuple-element.37), channel_id=1, source_target_pairs={{0,2},{4,0},{6,4},{2,6},{1,3},{5,1},{7,5},{3,7},{8,10},{12,8},{14,... | collective-permute-start | bytes 393224 | tf_op jit(solution)/shard_map/ppermute | solution.py:28
  34.0 10.5 %collective-permute-start.13 = (bf16[512,128]{1,0:T(8,128)(2,1)S(1)}, bf16[512,128]{1,0:T(8,128)(2,1)S(1)}, u32[]{:S(2)}, u32[]{:S(2)}) collective-permute-start(bf16[512,128]{1,0:T(8,128)(2,1)S(1)} %get-tuple-element.36), channel_id=1, source_target_pairs={{0,6},{4,2},{6,0},{2,4},{1,7},{5,3},{7,1},{3,5},{8,14},{12,10},{14... | collective-permute-start | bytes 393224 | tf_op jit(solution)/shard_map/ppermute | solution.py:28
  36.4 8.1 %collective-permute-start.12 = (bf16[512,128]{1,0:T(8,128)(2,1)S(1)}, bf16[512,128]{1,0:T(8,128)(2,1)S(1)}, u32[]{:S(2)}, u32[]{:S(2)}) collective-permute-start(bf16[512,128]{1,0:T(8,128)(2,1)S(1)} %get-tuple-element.35), channel_id=1, source_target_pairs={{0,4},{4,6},{6,2},{2,0},{1,5},{5,7},{7,3},{3,1},{8,12},{12,14},{14... | collective-permute-start | bytes 393224 | tf_op jit(solution)/shard_map/ppermute | solution.py:28
  44.5 9.2 %collective-permute-start.20 = (bf16[1,128,1024]{2,1,0:T(8,128)(2,1)S(1)}, bf16[1,128,1024]{2,1,0:T(8,128)(2,1)S(1)}, u32[]{:S(2)}, u32[]{:S(2)}) collective-permute-start(bf16[1,128,1024]{2,1,0:T(8,128)(2,1)S(1)} %get-tuple-element.38.refs_0_), channel_id=1, source_target_pairs={{0,4},{4,6},{6,2},{2,0},{1,5},{5,7},{7,3},{3,1},{8,12},{12,14},{14... | collective-permute-start | bytes 786440 | tf_op jit(solution)/shard_map/ppermute | solution.py:28
  44.6 22.4 %collective-permute-start.16 = (bf16[512,512]{1,0:T(8,128)(2,1)S(1)}, bf16[512,512]{1,0:T(8,128)(2,1)S(1)}, u32[]{:S(2)}, u32[]{:S(2)}) collective-permute-start(bf16[512,512]{1,0:T(8,128)(2,1)S(1)} %join.1.refs_6_.refs_8_.refs_2_), channel_id=1, source_target_pairs={{0,16},{8,24},{16,0},{24,8},{1,17},{9,25},{17,1},{25,9},{2,18},{10... | collective-permute-start | bytes 1572872 | tf_op jit(solution)/shard_map/ppermute | solution.py:32
  46.2 11.8 %collective-permute-start.6 = (bf16[1,128,1024]{2,1,0:T(8,128)(2,1)S(1)}, bf16[1,128,1024]{2,1,0:T(8,128)(2,1)S(1)}, u32[]{:S(2)}, u32[]{:S(2)}) collective-permute-start(bf16[1,128,1024]{2,1,0:T(8,128)(2,1)S(1)} %get-tuple-element.32.refs_0_), channel_id=1, source_target_pairs={{0,4},{4,6},{6,2},{2,0},{1,5},{5,7},{7,3},{3,1},{8,12},{12,14},{14... | collective-permute-start | bytes 786440 | tf_op jit(solution)/shard_map/ppermute | solution.py:28
  53.7 7.9 %collective-permute-start.22 = (bf16[1,128,1024]{2,1,0:T(8,128)(2,1)S(1)}, bf16[1,128,1024]{2,1,0:T(8,128)(2,1)S(1)}, u32[]{:S(2)}, u32[]{:S(2)}) collective-permute-start(bf16[1,128,1024]{2,1,0:T(8,128)(2,1)S(1)} %collective-permute-done.20.refs_1_), channel_id=1, source_target_pairs={{0,16},{8,24},{16,0},{24,8},{1,17},{9,25},{17,1},{25,9},{2,18},{10... | collective-permute-start | bytes 786440 | tf_op jit(solution)/shard_map/ppermute | solution.py:32
  55.2 13.3 %collective-permute-start.21 = (bf16[1,128,1024]{2,1,0:T(8,128)(2,1)S(1)}, bf16[1,128,1024]{2,1,0:T(8,128)(2,1)S(1)}, u32[]{:S(2)}, u32[]{:S(2)}) collective-permute-start(bf16[1,128,1024]{2,1,0:T(8,128)(2,1)S(1)} %collective-permute-done.20.refs_1_), channel_id=1, source_target_pairs={{0,4},{4,6},{6,2},{2,0},{1,5},{5,7},{7,3},{3,1},{8,12},{12,14},{14... | collective-permute-start | bytes 786440 | tf_op jit(solution)/shard_map/ppermute | solution.py:28
  56.1 22.6 %collective-permute-start.17 = (bf16[512,512]{1,0:T(8,128)(2,1)S(1)}, bf16[512,512]{1,0:T(8,128)(2,1)S(1)}, u32[]{:S(2)}, u32[]{:S(2)}) collective-permute-start(bf16[512,512]{1,0:T(8,128)(2,1)S(1)} %join.1.refs_6_.refs_8_.refs_2_), channel_id=1, source_target_pairs={{0,1},{1,0},{2,3},{3,2},{4,5},{5,4},{6,7},{7,6},{8,9},{9,8},{10,11... | collective-permute-start | bytes 1572872 | tf_op jit(solution)/shard_map/ppermute | solution.py:32
  58.0 12.0 %collective-permute-start.9 = (bf16[1,128,1024]{2,1,0:T(8,128)(2,1)S(1)}, bf16[1,128,1024]{2,1,0:T(8,128)(2,1)S(1)}, u32[]{:S(2)}, u32[]{:S(2)}) collective-permute-start(bf16[1,128,1024]{2,1,0:T(8,128)(2,1)S(1)} %collective-permute-done.6.refs_1_), channel_id=1, source_target_pairs={{0,16},{8,24},{16,0},{24,8},{1,17},{9,25},{17,1},{25,9},{2,18},{10... | collective-permute-start | bytes 786440 | tf_op jit(solution)/shard_map/ppermute | solution.py:32
  61.6 12.7 %collective-permute-start.8 = (bf16[1,128,1024]{2,1,0:T(8,128)(2,1)S(1)}, bf16[1,128,1024]{2,1,0:T(8,128)(2,1)S(1)}, u32[]{:S(2)}, u32[]{:S(2)}) collective-permute-start(bf16[1,128,1024]{2,1,0:T(8,128)(2,1)S(1)} %collective-permute-done.6.refs_1_), channel_id=1, source_target_pairs={{0,4},{4,6},{6,2},{2,0},{1,5},{5,7},{7,3},{3,1},{8,12},{12,14},{14... | collective-permute-start | bytes 786440 | tf_op jit(solution)/shard_map/ppermute | solution.py:28
  67.1 16.7 %collective-permute-start.18 = (bf16[512,512]{1,0:T(8,128)(2,1)S(1)}, bf16[512,512]{1,0:T(8,128)(2,1)S(1)}, u32[]{:S(2)}, u32[]{:S(2)}) collective-permute-start(bf16[512,512]{1,0:T(8,128)(2,1)S(1)} %collective-permute-done.16.refs_7_.refs_9_.refs_3_), channel_id=1, source_target_pairs={{0,1},{1,0},{2,3},{3,2},{4,5},{5,4},{6,7},{7,6},{8,9},{9,8},{10,11... | collective-permute-start | bytes 1572872 | tf_op jit(solution)/shard_map/ppermute | solution.py:32
  68.6 10.2 %collective-permute-start.24 = (bf16[1,128,1024]{2,1,0:T(8,128)(2,1)S(1)}, bf16[1,128,1024]{2,1,0:T(8,128)(2,1)S(1)}, u32[]{:S(2)}, u32[]{:S(2)}) collective-permute-start(bf16[1,128,1024]{2,1,0:T(8,128)(2,1)S(1)} %collective-permute-done.21.refs_2_), channel_id=1, source_target_pairs={{0,16},{8,24},{16,0},{24,8},{1,17},{9,25},{17,1},{25,9},{2,18},{10... | collective-permute-start | bytes 786440 | tf_op jit(solution)/shard_map/ppermute | solution.py:32
  74.3 8.0 %collective-permute-start.10 = (bf16[1,128,1024]{2,1,0:T(8,128)(2,1)S(1)}, bf16[1,128,1024]{2,1,0:T(8,128)(2,1)S(1)}, u32[]{:S(2)}, u32[]{:S(2)}) collective-permute-start(bf16[1,128,1024]{2,1,0:T(8,128)(2,1)S(1)} %collective-permute-done.8.refs_2_), channel_id=1, source_target_pairs={{0,4},{4,6},{6,2},{2,0},{1,5},{5,7},{7,3},{3,1},{8,12},{12,14},{14... | collective-permute-start | bytes 786440 | tf_op jit(solution)/shard_map/ppermute | solution.py:28
  77.2 6.6 %collective-permute-start.19 = (bf16[1,128,1024]{2,1,0:T(8,128)(2,1)S(1)}, bf16[1,128,1024]{2,1,0:T(8,128)(2,1)S(1)}, u32[]{:S(2)}, u32[]{:S(2)}) collective-permute-start(bf16[1,128,1024]{2,1,0:T(8,128)(2,1)S(1)} %collective-permute-done.8.refs_2_), channel_id=1, source_target_pairs={{0,16},{8,24},{16,0},{24,8},{1,17},{9,25},{17,1},{25,9},{2,18},{10... | collective-permute-start | bytes 786440 | tf_op jit(solution)/shard_map/ppermute | solution.py:32
  78.7 6.9 %collective-permute-start.23 = (bf16[1,128,1024]{2,1,0:T(8,128)(2,1)S(1)}, bf16[1,128,1024]{2,1,0:T(8,128)(2,1)S(1)}, u32[]{:S(2)}, u32[]{:S(2)}) collective-permute-start(bf16[1,128,1024]{2,1,0:T(8,128)(2,1)S(1)} %collective-permute-done.21.refs_2_), channel_id=1, source_target_pairs={{0,4},{4,6},{6,2},{2,0},{1,5},{5,7},{7,3},{3,1},{8,12},{12,14},{14... | collective-permute-start | bytes 786440 | tf_op jit(solution)/shard_map/ppermute | solution.py:28
  78.7 9.2 %collective-permute-start.25 = (bf16[1,128,1024]{2,1,0:T(8,128)(2,1)S(1)}, bf16[1,128,1024]{2,1,0:T(8,128)(2,1)S(1)}, u32[]{:S(2)}, u32[]{:S(2)}) collective-permute-start(bf16[1,128,1024]{2,1,0:T(8,128)(2,1)S(1)} %collective-permute-done.24.refs_6_), channel_id=1, source_target_pairs={{0,4},{4,6},{6,2},{2,0},{1,5},{5,7},{7,3},{3,1},{8,12},{12,14},{14... | collective-permute-start | bytes 786440 | tf_op jit(solution)/shard_map/ppermute | solution.py:28
  82.3 9.4 %collective-permute-start.11 = (bf16[1,128,1024]{2,1,0:T(8,128)(2,1)S(1)}, bf16[1,128,1024]{2,1,0:T(8,128)(2,1)S(1)}, u32[]{:S(2)}, u32[]{:S(2)}) collective-permute-start(bf16[1,128,1024]{2,1,0:T(8,128)(2,1)S(1)} %collective-permute-done.10.refs_0_), channel_id=1, source_target_pairs={{0,16},{8,24},{16,0},{24,8},{1,17},{9,25},{17,1},{25,9},{2,18},{10... | collective-permute-start | bytes 786440 | tf_op jit(solution)/shard_map/ppermute | solution.py:32

commit v3 on v2

--- a/solution.py
+++ b/solution.py
@@ -26,6 +26,18 @@
     n = lax.axis_size("ctx")
     order = ring_order(n)
     return lax.ppermute(x, "ctx", [(order[q], order[(q + shift) % n]) for q in range(n)])
+
+
+def gather(x, ways, gate):
+    n = lax.axis_size("ctx")
+    middle = n // 2 if ways > 0 else (n - 1) // 2
+    held = [x] + [None] * (n - 1)
+    for s in range(1, max(middle, n - 1 - middle) + 1):
+        if s <= middle:
+            held[s] = around(gate(held[s - 1]) if s > 1 else x, 1)
+        if s <= n - 1 - middle:
+            held[n - s] = around(gate(held[n - s + 1]) if s > 1 else x, -1)
+    return held
 
 
 def swap(x, axis, mask):
@@ -122,34 +134,35 @@
             out_ref[0, :, at : at + HD] = piece
 
 
-def left_sides(refs, tokens, first, slots):
+def left_sides(refs, tokens, slots):
     near, far, near_other, far_other = refs
-    here = slice(first * tokens, (first + slots) * tokens)
     side = lax.axis_index("tp") & 1
-    return (
-        (side, jnp.concatenate([near[:, here], far[:, here]], axis=1)),
-        (1 - side, jnp.concatenate([near_other[:, here], far_other[:, here]], axis=1)),
+    columns = [slice(s * tokens, (s + 1) * tokens) for s in slots]
+    return tuple(
+        (at, jnp.concatenate([ref[:, here] for ref in pair for here in columns], axis=1))
+        for at, pair in ((side, (near, far)), (1 - side, (near_other, far_other)))
     )
 
 
 def early_kernel(slots, *refs):
-    att_refs, cot_refs, total_ref = refs[: 2 * slots], refs[2 * slots : -1], refs[-1]
+    att_refs, cot_refs, total_ref = refs[: 2 * len(slots)], refs[2 * len(slots) : -1], refs[-1]
     half = cot_refs[0].shape[0]
     tokens = att_refs[0].shape[1]
     wide = TILE if total_ref.shape[1] % TILE == 0 else total_ref.shape[1]
     for j in range(total_ref.shape[1] // wide):
         columns = slice(j * wide, (j + 1) * wide)
         rows = jnp.concatenate([ref[0, :, columns] for ref in att_refs], axis=0)
-        for at, left in left_sides(cot_refs, tokens, 0, slots):
+        for at, left in left_sides(cot_refs, tokens, slots):
             total_ref[pl.ds(pl.multiple_of(at * half, half), half), columns] = jnp.dot(
                 left, rows, preferred_element_type=jnp.float32
             )
 
 
-def finish_kernel(slots, first, start, carried, width, *refs):
-    att_refs, cot_refs = refs[: 2 * slots], refs[2 * slots : 2 * slots + 4]
+def finish_kernel(slots, start, carried, width, *refs):
+    count = 2 * len(slots)
+    att_refs, cot_refs = refs[:count], refs[count : count + 4]
     out_ref, held, sems = refs[-3:]
-    total_ref = refs[2 * slots + 4] if carried else None
+    total_ref = refs[count + 4] if carried else None
     half = cot_refs[0].shape[0]
     tokens = att_refs[0].shape[1]
     wide = held.shape[2]
@@ -159,7 +172,7 @@
         rows = jnp.concatenate([ref[0, :, columns] for ref in att_refs], axis=0)
         if j >= 2:
             copies[j - 2].wait()
-        for at, left in left_sides(cot_refs, tokens, first, slots):
+        for at, left in left_sides(cot_refs, tokens, slots):
             here = pl.ds(pl.multiple_of(at * half, half), half)
             value = jnp.dot(left, rows, preferred_element_type=jnp.float32)
             if carried:
@@ -199,10 +212,6 @@
         compiler_params=params(16),
         name="pack",
     )(span_ids, keys)
-    key_ring, value_ring = [packed], [values]
-    for _ in range(n - 1):
-        value_ring.append(around(value_ring[-1], 1))
-        key_ring.append(around(key_ring[-1], 1))
     query_held, value_held = pl.pallas_call(
         fetch_kernel,
         out_shape=[jax.ShapeDtypeStruct(x.shape, jnp.bfloat16) for x in (queries, values)],
@@ -219,7 +228,8 @@
         compiler_params=params(16),
         name="turn",
     )(place, cotangent)
-    query_held = after(query_held, *turned)
+    key_ring = gather(packed, 1, lambda x: after(x, query_held))
+    value_ring = gather(values, -1, lambda x: after(x, turned[0]))
     attention, *pieces = pl.pallas_call(
         functools.partial(attention_kernel, HQ // HK, 1.0 / math.sqrt(HD), n, spans),
         out_shape=[jax.ShapeDtypeStruct(queries.shape, jnp.bfloat16)]
@@ -230,19 +240,20 @@
         name="attend",
     )(place, query_held, *key_ring, value_held, *value_ring[1:])
 
-    near, mirrored = [], []
-    for c in range(parts):
-        held, sent = [pieces[c]], []
-        for s in range(n):
-            by_ring = s == n - 1 and c < parts - 1
-            sent.append(around(sent[-1], 1) if by_ring else swap(held[s], "pipe", far))
-            if s < n - 1:
-                arrived = around(held[s], 1)
-                held.append(after(arrived, sent[s]) if s < n - 2 else arrived)
-        near.append(held)
-        mirrored.append(sent)
-
-    turned = [turned[0]] + [around(after(turned[s], value_ring[n - 2]), s) for s in range(1, n)]
+    mirrored = [[swap(piece, "pipe", far)] + [None] * (n - 1) for piece in pieces]
+    near = []
+    for c, piece in enumerate(pieces):
+        sent = mirrored[c][:1]
+        if c:
+            piece = after(piece, near[0][1], near[0][-1])
+            sent = sent + [mirrored[0][1], mirrored[0][-1]]
+        near.append(gather(piece, 1 - 2 * c, lambda x, sent=sent: after(x, *sent)))
+        for s in range(1, n):
+            by_ring = s == n // 2 and c < parts - 1
+            mirrored[c][s] = (
+                around(mirrored[c][s - 1], 1) if by_ring else swap(near[c][s], "pipe", far)
+            )
+    turned = [turned[0]] + [around(after(turned[s], value_ring[n // 2]), s) for s in range(1, n)]
     mine = pl.pallas_call(
         join_kernel,
         out_shape=jax.ShapeDtypeStruct((half, n * tokens), jnp.bfloat16),
@@ -250,16 +261,18 @@
         out_specs=VMEM,
         compiler_params=params(16),
         name="join",
-    )(*turned[:-1], after(turned[-1], *[sent[0] for sent in mirrored]))
+    )(*turned[:-1], after(turned[-1], near[0][1], near[0][-1], *[sent[0] for sent in mirrored]))
     mine_far = swap(mine, "pipe", far)
     cots = [mine, mine_far, swap(mine, "tp", 1), swap(mine_far, "tp", 1)]
 
-    def attended(c, first, last):
-        return near[c][first:last] + mirrored[c][first:last]
+    def attended(c, slots):
+        return [side[c][s] for side in (near, mirrored) for s in slots]
+
+    first_slots = [s for s in range(n) if s != n // 2]
 
     tile = TILE if chunk % TILE == 0 else chunk
     total = pl.pallas_call(
-        functools.partial(early_kernel, n - 1),
+        functools.partial(early_kernel, first_slots),
         out_shape=jax.ShapeDtypeStruct((features, chunk), jnp.float32),
         in_specs=[VMEM] * (2 * n + 2),
         out_specs=VMEM,
@@ -270,12 +283,12 @@
             transcendentals=0,
         ),
         name="early",
-    )(*attended(parts - 1, 0, n - 1), *cots)
+    )(*attended(parts - 1, first_slots), *cots)
     grad_out = None
     for c in range(parts):
         last = c == parts - 1
-        slots = 1 if last else n
-        operands = attended(c, n - slots, n) + cots + ([total] if last else [])
+        slots = [n // 2] if last else list(range(n))
+        operands = attended(c, slots) + cots + ([total] if last else [])
         specs = [VMEM] * len(operands)
         aliases = {}
         if grad_out is not None:
@@ -283,7 +296,7 @@
             operands.append(grad_out)
             specs.append(ANY)
         grad_out = pl.pallas_call(
-            functools.partial(finish_kernel, slots, n - slots, c * chunk, last, chunk),
+            functools.partial(finish_kernel, slots, c * chunk, last, chunk),
             out_shape=jax.ShapeDtypeStruct((1, features, heads), jnp.bfloat16),
             in_specs=specs,
             out_specs=ANY,
@@ -294,7 +307,7 @@
             input_output_aliases=aliases,
             compiler_params=params(40),
             cost_estimate=pl.CostEstimate(
-                flops=4 * features * chunk * slots * tokens,
+                flops=4 * features * chunk * len(slots) * tokens,
                 bytes_accessed=8 * 2**20,
                 transcendentals=0,
             ),

time: 94.5 us -> 106 us (1.12)
  waiting for transfers between devices: 29.2 us -> 49.6 us
  starting transfers between devices: 48.1 us -> 39 us
    ppermute x10, waiting for transfers between devices: 3.07 us -> 22.2 us  [swap(): lax.ppermute(x, axis, [(i, i ^ mask) for i in range(lax.axis_size(axis))])]
    ppermute x16, starting transfers between devices: 34.9 us -> 29.9 us  [around(): lax.ppermute(x, 'ctx', [(order[q], order[(q + shift) % n]) for q in range...]
    ppermute x10, starting transfers between devices: 13.2 us -> 9.18 us  [swap(): lax.ppermute(x, axis, [(i, i ^ mask) for i in range(lax.axis_size(axis))])]
    ppermute x16, waiting for transfers between devices: 26.1 us -> 27.5 us  [around(): lax.ppermute(x, 'ctx', [(order[q], order[(q + shift) % n]) for q in range...]
  transfers between devices with their start and end apart: 26 -> 26, of which waited for: 9 -> 13; matrix products, arithmetic and copies ran while one was open for 0% -> 0% of each run, Pallas kernels for 6% -> 5%
where the time goes in v3:
time: 106 us
  waiting for transfers between devices  49.6 us (47%)
  starting transfers between devices  39 us (37%)
  Pallas kernels  11.5 us (11%)
  local copies, waits for them, and re-layouts  4.72 us (4%)
    ppermute x16, starting transfers between devices, around(): lax.ppermute(x, 'ctx', [(order[q], order[(q + shift) % n]) for q in range...  29.9 us
    ppermute x16, waiting for transfers between devices, around(): lax.ppermute(x, 'ctx', [(order[q], order[(q + shift) % n]) for q in range...  27.5 us
    ppermute x10, waiting for transfers between devices, swap(): lax.ppermute(x, axis, [(i, i ^ mask) for i in range(lax.axis_size(axis))])  22.2 us
    ppermute x10, starting transfers between devices, swap(): lax.ppermute(x, axis, [(i, i ^ mask) for i in range(lax.axis_size(axis))])  9.18 us
    pallas_call x2, Pallas kernels, local(): pl.pallas_call(functools.partial(finish_kernel, slots, c * chunk, last, c...  6.29 us
    unnamed x10, local copies, waits for them, and re-layouts  4.72 us
    pallas_call x1, Pallas kernels, local(): pl.pallas_call(functools.partial(attention_kernel, HQ // HK, 1.0 / math.s...  2.51 us
  transfers between devices with their start and end apart: 26, of which 13 were waited for; matrix products, arithmetic and copies ran while one was open for 0% of the time, Pallas kernels for 5%

profile of v3, /device:TPU:0, one launch (start us, length us, event | category | flops | bytes accessed | tf_op | source)
XLA Modules:
  0.0 105.6 jit_solution(17974427423840812104)
XLA Ops:
  0.6 0.9 copy-done.2
  1.5 0.7 copy-done.4
  2.2 0.6 pack.1
  2.8 4.1 %collective-permute-start = (bf16[1,144,512]{2,1,0:T(8,128)(2,1)S(1)}, bf16[1,144,512]{2,1,0:T(8,128)(2,1)S(1)}, u32[]{:S(2)}, u32[]{:S(2)}) collective-permute-start(bf16[1,144,512]{2,1,0:T(8,128)(2,1)S(1)} %get-tuple-element.24.refs_0_), channel_id=1, source_target_pairs={{0,4},{4,6},{6,2},{2,0},{1,5},{5,7},{7,3},{3,1},{8,12},{12,14},{14... | collective-permute-start | bytes 442376 | tf_op jit(solution)/shard_map/ppermute | solution.py:28
  6.8 1.9 %collective-permute-start.2 = (bf16[1,144,512]{2,1,0:T(8,128)(2,1)S(1)}, bf16[1,144,512]{2,1,0:T(8,128)(2,1)S(1)}, u32[]{:S(2)}, u32[]{:S(2)}) collective-permute-start(bf16[1,144,512]{2,1,0:T(8,128)(2,1)S(1)} %get-tuple-element.24.refs_0_), channel_id=1, source_target_pairs={{0,2},{4,0},{6,4},{2,6},{1,3},{5,1},{7,5},{3,7},{8,10},{12,8},{14,... | collective-permute-start | bytes 442376 | tf_op jit(solution)/shard_map/ppermute | solution.py:28
  8.8 1.0 copy-done.1
  9.8 0.9 copy-done.3
  10.8 0.4 collective-permute-done.refs_1_
  11.1 3.4 %collective-permute-start.1 = (bf16[1,144,512]{2,1,0:T(8,128)(2,1)S(1)}, bf16[1,144,512]{2,1,0:T(8,128)(2,1)S(1)}, u32[]{:S(2)}, u32[]{:S(2)}) collective-permute-start(bf16[1,144,512]{2,1,0:T(8,128)(2,1)S(1)} %collective-permute-done.refs_1_), channel_id=1, source_target_pairs={{0,4},{4,6},{6,2},{2,0},{1,5},{5,7},{7,3},{3,1},{8,12},{12,14},{14... | collective-permute-start | bytes 442376 | tf_op jit(solution)/shard_map/ppermute | solution.py:28
  14.5 0.0 collective-permute-start.3
  14.5 1.2 %copy-done = bf16[1,128,4096]{2,1,0:T(8,128)(2,1)S(1)} copy-done((bf16[1,128,4096]{2,1,0:T(8,128)(2,1)S(1)}, bf16[1,128,4096]{2,1,0:T(8,128)(2,1)}, u32[]{:S(2)}) %copy-start) | copy-done | bytes 1048600
  15.8 0.2 turn.1
  16.0 2.0 %collective-permute-start.5 = (bf16[1,128,512]{2,1,0:T(8,128)(2,1)S(1)}, bf16[1,128,512]{2,1,0:T(8,128)(2,1)S(1)}, u32[]{:S(2)}, u32[]{:S(2)}) collective-permute-start(bf16[1,128,512]{2,1,0:T(8,128)(2,1)S(1)} %collective-permute-done.4.refs_7_), channel_id=1, source_target_pairs={{0,2},{4,0},{6,4},{2,6},{1,3},{5,1},{7,5},{3,7},{8,10},{12,8},{14,... | collective-permute-start | bytes 393224 | tf_op jit(solution)/shard_map/ppermute | solution.py:28
  18.0 6.3 %collective-permute-done.3.refs_5_ = bf16[1,128,512]{2,1,0:T(8,128)(2,1)S(1)} collective-permute-done((bf16[1,128,512]{2,1,0:T(8,128)(2,1)S(1)}, bf16[1,128,512]{2,1,0:T(8,128)(2,1)S(1)}, u32[]{:S(2)}, u32[]{:S(2)}) %collective-permute-start.3) | collective-permute-done | bytes 131104 | tf_op jit(solution)/shard_map/ppermute | solution.py:28
  24.3 2.2 %collective-permute-done.5.refs_6_ = bf16[1,128,512]{2,1,0:T(8,128)(2,1)S(1)} collective-permute-done((bf16[1,128,512]{2,1,0:T(8,128)(2,1)S(1)}, bf16[1,128,512]{2,1,0:T(8,128)(2,1)S(1)}, u32[]{:S(2)}, u32[]{:S(2)}) %collective-permute-start.5) | collective-permute-done | bytes 131104 | tf_op jit(solution)/shard_map/ppermute | solution.py:28
  26.6 2.5 %attend.1 = (bf16[1,128,2048]{2,1,0:T(8,128)(2,1)}, bf16[1,128,1024]{2,1,0:T(8,128)(2,1)S(1)}, bf16[1,128,1024]{2,1,0:T(8,128)(2,1)S(1)}) custom-call(f32[128,128]{1,0:T(8,128)S(1)} %get-tuple-element.22.place_ref.ready_ref, bf16[1,128,2048]{2,1,0:T(8,128)(2,1)S(1)} %get-tuple-element.23.query_ref, bf16[1,144,512]{2,1,0:T(8,128)(2,1)S(1)} %get-tuple-element.24.refs_0_, ...), custom_call_target="tpu_custom_call" | custom-call | tf_op jit(solution)/shard_map/attend/pallas_call | solution.py:233
  29.1 1.5 %collective-permute-start.9 = (bf16[1,128,1024]{2,1,0:T(8,128)(2,1)S(1)}, bf16[1,128,1024]{2,1,0:T(8,128)(2,1)S(1)}, u32[]{:S(2)}, u32[]{:S(2)}) collective-permute-start(bf16[1,128,1024]{2,1,0:T(8,128)(2,1)S(1)} %get-tuple-element.32.refs_0_), channel_id=1, source_target_pairs={{0,16},{8,24},{16,0},{24,8},{1,17},{9,25},{17,1},{25,9},{2,18},{10... | collective-permute-start | bytes 786440 | tf_op jit(solution)/shard_map/ppermute | solution.py:44
  30.6 0.7 collective-permute-start.16
  31.3 0.5 collective-permute-start.17
  31.8 2.3 %collective-permute-start.7 = (bf16[1,128,1024]{2,1,0:T(8,128)(2,1)S(1)}, bf16[1,128,1024]{2,1,0:T(8,128)(2,1)S(1)}, u32[]{:S(2)}, u32[]{:S(2)}) collective-permute-start(bf16[1,128,1024]{2,1,0:T(8,128)(2,1)S(1)} %get-tuple-element.31.refs_0_), channel_id=1, source_target_pairs={{0,2},{4,0},{6,4},{2,6},{1,3},{5,1},{7,5},{3,7},{8,10},{12,8},{14,... | collective-permute-start | bytes 786440 | tf_op jit(solution)/shard_map/ppermute | solution.py:28
  34.1 0.6 collective-permute-start.6
  34.7 3.3 %collective-permute-done.16.refs_3_ = bf16[512,128]{1,0:T(8,128)(2,1)S(1)} collective-permute-done((bf16[512,128]{1,0:T(8,128)(2,1)S(1)}, bf16[512,128]{1,0:T(8,128)(2,1)S(1)}, u32[]{:S(2)}, u32[]{:S(2)}) %collective-permute-start.16) | collective-permute-done | bytes 131104 | tf_op jit(solution)/shard_map/ppermute | solution.py:28
  38.0 0.3 collective-permute-done.9.refs_3_
  38.3 2.4 %collective-permute-start.15 = (bf16[512,128]{1,0:T(8,128)(2,1)S(1)}, bf16[512,128]{1,0:T(8,128)(2,1)S(1)}, u32[]{:S(2)}, u32[]{:S(2)}) collective-permute-start(bf16[512,128]{1,0:T(8,128)(2,1)S(1)} %get-tuple-element.37), channel_id=1, source_target_pairs={{0,6},{4,2},{6,0},{2,4},{1,7},{5,3},{7,1},{3,5},{8,14},{12,10},{14... | collective-permute-start | bytes 393224 | tf_op jit(solution)/shard_map/ppermute | solution.py:28
  40.7 1.8 %collective-permute-done.17.refs_4_ = bf16[1,128,1024]{2,1,0:T(8,128)(2,1)S(1)} collective-permute-done((bf16[1,128,1024]{2,1,0:T(8,128)(2,1)S(1)}, bf16[1,128,1024]{2,1,0:T(8,128)(2,1)S(1)}, u32[]{:S(2)}, u32[]{:S(2)}) %collective-permute-start.17) | collective-permute-done | bytes 262176 | tf_op jit(solution)/shard_map/ppermute | solution.py:44
  42.5 12.0 %collective-permute-done.7.refs_3_ = bf16[1,128,1024]{2,1,0:T(8,128)(2,1)S(1)} collective-permute-done((bf16[1,128,1024]{2,1,0:T(8,128)(2,1)S(1)}, bf16[1,128,1024]{2,1,0:T(8,128)(2,1)S(1)}, u32[]{:S(2)}, u32[]{:S(2)}) %collective-permute-start.7) | collective-permute-done | bytes 262176 | tf_op jit(solution)/shard_map/ppermute | solution.py:28
  54.5 0.1 join.1.refs_6_.refs_8_.refs_2_
  54.6 0.6 collective-permute-start.18
  55.2 1.5 %collective-permute-start.11 = (bf16[1,128,1024]{2,1,0:T(8,128)(2,1)S(1)}, bf16[1,128,1024]{2,1,0:T(8,128)(2,1)S(1)}, u32[]{:S(2)}, u32[]{:S(2)}) collective-permute-start(bf16[1,128,1024]{2,1,0:T(8,128)(2,1)S(1)} %collective-permute-done.7.refs_3_), channel_id=1, source_target_pairs={{0,16},{8,24},{16,0},{24,8},{1,17},{9,25},{17,1},{25,9},{2,18},{10... | collective-permute-start | bytes 786440 | tf_op jit(solution)/shard_map/ppermute | solution.py:44
  56.7 3.4 %collective-permute-start.21 = (bf16[1,128,1024]{2,1,0:T(8,128)(2,1)S(1)}, bf16[1,128,1024]{2,1,0:T(8,128)(2,1)S(1)}, u32[]{:S(2)}, u32[]{:S(2)}) collective-permute-start(bf16[1,128,1024]{2,1,0:T(8,128)(2,1)S(1)} %get-tuple-element.32.refs_0_), channel_id=1, source_target_pairs={{0,4},{4,6},{6,2},{2,0},{1,5},{5,7},{7,3},{3,1},{8,12},{12,14},{14... | collective-permute-start | bytes 786440 | tf_op jit(solution)/shard_map/ppermute | solution.py:28
  60.1 0.5 collective-permute-start.10
  60.6 14.6 %collective-permute-done.11.refs_7_ = bf16[1,128,1024]{2,1,0:T(8,128)(2,1)S(1)} collective-permute-done((bf16[1,128,1024]{2,1,0:T(8,128)(2,1)S(1)}, bf16[1,128,1024]{2,1,0:T(8,128)(2,1)S(1)}, u32[]{:S(2)}, u32[]{:S(2)}) %collective-permute-start.11) | collective-permute-done | bytes 262176 | tf_op jit(solution)/shard_map/ppermute | solution.py:44
  75.2 1.5 %collective-permute-start.19 = (bf16[512,512]{1,0:T(8,128)(2,1)S(1)}, bf16[512,512]{1,0:T(8,128)(2,1)S(1)}, u32[]{:S(2)}, u32[]{:S(2)}) collective-permute-start(bf16[512,512]{1,0:T(8,128)(2,1)S(1)} %join.1.refs_6_.refs_8_.refs_2_), channel_id=1, source_target_pairs={{0,1},{1,0},{2,3},{3,2},{4,5},{5,4},{6,7},{7,6},{8,9},{9,8},{10,11... | collective-permute-start | bytes 1572872 | tf_op jit(solution)/shard_map/ppermute | solution.py:44
  76.7 0.5 collective-permute-start.20
  77.2 0.5 collective-permute-start.22
  77.7 1.5 %collective-permute-start.23 = (bf16[1,128,1024]{2,1,0:T(8,128)(2,1)S(1)}, bf16[1,128,1024]{2,1,0:T(8,128)(2,1)S(1)}, u32[]{:S(2)}, u32[]{:S(2)}) collective-permute-start(bf16[1,128,1024]{2,1,0:T(8,128)(2,1)S(1)} %collective-permute-done.8.refs_2_), channel_id=1, source_target_pairs={{0,16},{8,24},{16,0},{24,8},{1,17},{9,25},{17,1},{25,9},{2,18},{10... | collective-permute-start | bytes 786440 | tf_op jit(solution)/shard_map/ppermute | solution.py:44
  79.2 1.6 %collective-permute-done.10.refs_5_ = bf16[1,128,1024]{2,1,0:T(8,128)(2,1)S(1)} collective-permute-done((bf16[1,128,1024]{2,1,0:T(8,128)(2,1)S(1)}, bf16[1,128,1024]{2,1,0:T(8,128)(2,1)S(1)}, u32[]{:S(2)}, u32[]{:S(2)}) %collective-permute-start.10) | collective-permute-done | bytes 262176 | tf_op jit(solution)/shard_map/ppermute | solution.py:44
  80.8 1.9 %collective-permute-start.12 = (bf16[1,128,1024]{2,1,0:T(8,128)(2,1)S(1)}, bf16[1,128,1024]{2,1,0:T(8,128)(2,1)S(1)}, u32[]{:S(2)}, u32[]{:S(2)}) collective-permute-start(bf16[1,128,1024]{2,1,0:T(8,128)(2,1)S(1)} %collective-permute-done.8.refs_2_), channel_id=1, source_target_pairs={{0,2},{4,0},{6,4},{2,6},{1,3},{5,1},{7,5},{3,7},{8,10},{12,8},{14,... | collective-permute-start | bytes 786440 | tf_op jit(solution)/shard_map/ppermute | solution.py:28
  82.7 3.4 %collective-permute-done.22.refs_4_ = bf16[1,128,1024]{2,1,0:T(8,128)(2,1)S(1)} collective-permute-done((bf16[1,128,1024]{2,1,0:T(8,128)(2,1)S(1)}, bf16[1,128,1024]{2,1,0:T(8,128)(2,1)S(1)}, u32[]{:S(2)}, u32[]{:S(2)}) %collective-permute-start.22) | collective-permute-done | bytes 262176 | tf_op jit(solution)/shard_map/ppermute | solution.py:44
  86.2 3.6 %collective-permute-start.24 = (bf16[1,128,1024]{2,1,0:T(8,128)(2,1)S(1)}, bf16[1,128,1024]{2,1,0:T(8,128)(2,1)S(1)}, u32[]{:S(2)}, u32[]{:S(2)}) collective-permute-start(bf16[1,128,1024]{2,1,0:T(8,128)(2,1)S(1)} %collective-permute-done.6.refs_1_), channel_id=1, source_target_pairs={{0,4},{4,6},{6,2},{2,0},{1,5},{5,7},{7,3},{3,1},{8,12},{12,14},{14... | collective-permute-start | bytes 786440 | tf_op jit(solution)/shard_map/ppermute | solution.py:28
  89.8 3.4 %collective-permute-start.25 = (bf16[1,128,1024]{2,1,0:T(8,128)(2,1)S(1)}, bf16[1,128,1024]{2,1,0:T(8,128)(2,1)S(1)}, u32[]{:S(2)}, u32[]{:S(2)}) collective-permute-start(bf16[1,128,1024]{2,1,0:T(8,128)(2,1)S(1)} %collective-permute-done.10.refs_5_), channel_id=1, source_target_pairs={{0,4},{4,6},{6,2},{2,0},{1,5},{5,7},{7,3},{3,1},{8,12},{12,14},{14... | collective-permute-start | bytes 786440 | tf_op jit(solution)/shard_map/ppermute | solution.py:28
  93.2 0.5 collective-permute-start.13
  93.7 0.5 collective-permute-done.20.refs_9_.refs_11_.refs_5_
  94.3 1.8 %early.1.refs_6_ = f32[1024,1024]{1,0:T(8,128)S(1)} custom-call(bf16[1,128,1024]{2,1,0:T(8,128)(2,1)S(1)} %get-tuple-element.32.refs_0_, bf16[1,128,1024]{2,1,0:T(8,128)(2,1)S(1)} %collective-permute-done.21.refs_1_, bf16[1,128,1024]{2,1,0:T(8,128)(2,1)S(1)} %collective-permute-done.8.refs_2_, bf16[1,128,1024]{2,1,0:T(8,128)(2,1)S(1)} %collective-permute-done.9.refs_3_, ...), custom_call_target="tpu_custom_call" | custom-call | flops 1610612736 | bytes 8388608 | tf_op jit(solution)/shard_map/early/pallas_call | solution.py:274
  96.1 0.4 collective-permute-done.24.refs_2_
  96.4 2.9 %collective-permute-done.25.refs_6_ = bf16[1,128,1024]{2,1,0:T(8,128)(2,1)S(1)} collective-permute-done((bf16[1,128,1024]{2,1,0:T(8,128)(2,1)S(1)}, bf16[1,128,1024]{2,1,0:T(8,128)(2,1)S(1)}, u32[]{:S(2)}, u32[]{:S(2)}) %collective-permute-start.25) | collective-permute-done | bytes 262176 | tf_op jit(solution)/shard_map/ppermute | solution.py:28
  99.3 3.8 %finish.2.refs_7_ = bf16[1,1024,2048]{2,1,0:T(8,128)(2,1)} custom-call(bf16[1,128,1024]{2,1,0:T(8,128)(2,1)S(1)} %get-tuple-element.31.refs_0_, bf16[1,128,1024]{2,1,0:T(8,128)(2,1)S(1)} %collective-permute-done.6.refs_1_, bf16[1,128,1024]{2,1,0:T(8,128)(2,1)S(1)} %collective-permute-done.24.refs_2_, ...), custom_call_target="tpu_custom_call" | custom-call | flops 2147483648 | bytes 8388608 | tf_op jit(solution)/shard_map/finish/pallas_call | solution.py:298
  103.1 2.5 %finish.3 = bf16[1,1024,2048]{2,1,0:T(8,128)(2,1)} custom-call(bf16[1,128,1024]{2,1,0:T(8,128)(2,1)S(1)} %collective-permute-done.12.refs_0_, bf16[1,128,1024]{2,1,0:T(8,128)(2,1)S(1)} %collective-permute-done.13.refs_1_, bf16[512,512]{1,0:T(8,128)(2,1)S(1)} %join.1.refs_6_.refs_8_.refs_2_, ...), custom_call_target="tpu_custom_call", output_to_operand_aliasing={{}: (7, {})} | custom-call | flops 536870912 | bytes 8388608 | tf_op jit(solution)/shard_map/finish/pallas_call | solution.py:298
  (22 shorter events, 0.1 us)
Async XLA Ops:
  0.6 0.9 copy-start.2
  1.5 0.7 copy-start.4
  2.8 8.4 %collective-permute-start = (bf16[1,144,512]{2,1,0:T(8,128)(2,1)S(1)}, bf16[1,144,512]{2,1,0:T(8,128)(2,1)S(1)}, u32[]{:S(2)}, u32[]{:S(2)}) collective-permute-start(bf16[1,144,512]{2,1,0:T(8,128)(2,1)S(1)} %get-tuple-element.24.refs_0_), channel_id=1, source_target_pairs={{0,4},{4,6},{6,2},{2,0},{1,5},{5,7},{7,3},{3,1},{8,12},{12,14},{14... | collective-permute-start | bytes 442376 | tf_op jit(solution)/shard_map/ppermute | solution.py:28
  6.8 9.1 %collective-permute-start.4 = (bf16[1,128,512]{2,1,0:T(8,128)(2,1)}, bf16[1,128,512]{2,1,0:T(8,128)(2,1)S(1)}, u32[]{:S(2)}, u32[]{:S(2)}) collective-permute-start(bf16[1,128,512]{2,1,0:T(8,128)(2,1)} %value_ref.1), channel_id=1, source_target_pairs={{0,2},{4,0},{6,4},{2,6},{1,3},{5,1},{7,5},{3,7},{8,10},{12,8},{14,... | collective-permute-start | bytes 393224 | tf_op jit(solution)/shard_map/ppermute | solution.py:28
  6.8 17.5 %collective-permute-start.2 = (bf16[1,144,512]{2,1,0:T(8,128)(2,1)S(1)}, bf16[1,144,512]{2,1,0:T(8,128)(2,1)S(1)}, u32[]{:S(2)}, u32[]{:S(2)}) collective-permute-start(bf16[1,144,512]{2,1,0:T(8,128)(2,1)S(1)} %get-tuple-element.24.refs_0_), channel_id=1, source_target_pairs={{0,2},{4,0},{6,4},{2,6},{1,3},{5,1},{7,5},{3,7},{8,10},{12,8},{14,... | collective-permute-start | bytes 442376 | tf_op jit(solution)/shard_map/ppermute | solution.py:28
  8.8 1.0 copy-start.1
  9.8 0.9 copy-start.3
  11.1 15.4 %collective-permute-start.1 = (bf16[1,144,512]{2,1,0:T(8,128)(2,1)S(1)}, bf16[1,144,512]{2,1,0:T(8,128)(2,1)S(1)}, u32[]{:S(2)}, u32[]{:S(2)}) collective-permute-start(bf16[1,144,512]{2,1,0:T(8,128)(2,1)S(1)} %collective-permute-done.refs_1_), channel_id=1, source_target_pairs={{0,4},{4,6},{6,2},{2,0},{1,5},{5,7},{7,3},{3,1},{8,12},{12,14},{14... | collective-permute-start | bytes 442376 | tf_op jit(solution)/shard_map/ppermute | solution.py:28
  14.5 9.8 %collective-permute-start.3 = (bf16[1,128,512]{2,1,0:T(8,128)(2,1)S(1)}, bf16[1,128,512]{2,1,0:T(8,128)(2,1)S(1)}, u32[]{:S(2)}, u32[]{:S(2)}) collective-permute-start(bf16[1,128,512]{2,1,0:T(8,128)(2,1)S(1)} %copy-done.3), channel_id=1, source_target_pairs={{0,4},{4,6},{6,2},{2,0},{1,5},{5,7},{7,3},{3,1},{8,12},{12,14},{14... | collective-permute-start | bytes 393224 | tf_op jit(solution)/shard_map/ppermute | solution.py:28
  14.5 1.2 %copy-start = (bf16[1,128,4096]{2,1,0:T(8,128)(2,1)S(1)}, bf16[1,128,4096]{2,1,0:T(8,128)(2,1)}, u32[]{:S(2)}) copy-start(bf16[1,128,4096]{2,1,0:T(8,128)(2,1)} %cot_ref.1) | copy-start | bytes 3145732
  16.0 10.6 %collective-permute-start.5 = (bf16[1,128,512]{2,1,0:T(8,128)(2,1)S(1)}, bf16[1,128,512]{2,1,0:T(8,128)(2,1)S(1)}, u32[]{:S(2)}, u32[]{:S(2)}) collective-permute-start(bf16[1,128,512]{2,1,0:T(8,128)(2,1)S(1)} %collective-permute-done.4.refs_7_), channel_id=1, source_target_pairs={{0,2},{4,0},{6,4},{2,6},{1,3},{5,1},{7,5},{3,7},{8,10},{12,8},{14,... | collective-permute-start | bytes 393224 | tf_op jit(solution)/shard_map/ppermute | solution.py:28
  29.1 9.2 %collective-permute-start.9 = (bf16[1,128,1024]{2,1,0:T(8,128)(2,1)S(1)}, bf16[1,128,1024]{2,1,0:T(8,128)(2,1)S(1)}, u32[]{:S(2)}, u32[]{:S(2)}) collective-permute-start(bf16[1,128,1024]{2,1,0:T(8,128)(2,1)S(1)} %get-tuple-element.32.refs_0_), channel_id=1, source_target_pairs={{0,16},{8,24},{16,0},{24,8},{1,17},{9,25},{17,1},{25,9},{2,18},{10... | collective-permute-start | bytes 786440 | tf_op jit(solution)/shard_map/ppermute | solution.py:44
  30.6 7.4 %collective-permute-start.16 = (bf16[512,128]{1,0:T(8,128)(2,1)S(1)}, bf16[512,128]{1,0:T(8,128)(2,1)S(1)}, u32[]{:S(2)}, u32[]{:S(2)}) collective-permute-start(bf16[512,128]{1,0:T(8,128)(2,1)S(1)} %get-tuple-element.39), channel_id=1, source_target_pairs={{0,2},{4,0},{6,4},{2,6},{1,3},{5,1},{7,5},{3,7},{8,10},{12,8},{14,... | collective-permute-start | bytes 393224 | tf_op jit(solution)/shard_map/ppermute | solution.py:28
  31.3 11.2 %collective-permute-start.17 = (bf16[1,128,1024]{2,1,0:T(8,128)(2,1)S(1)}, bf16[1,128,1024]{2,1,0:T(8,128)(2,1)S(1)}, u32[]{:S(2)}, u32[]{:S(2)}) collective-permute-start(bf16[1,128,1024]{2,1,0:T(8,128)(2,1)S(1)} %get-tuple-element.31.refs_0_), channel_id=1, source_target_pairs={{0,16},{8,24},{16,0},{24,8},{1,17},{9,25},{17,1},{25,9},{2,18},{10... | collective-permute-start | bytes 786440 | tf_op jit(solution)/shard_map/ppermute | solution.py:44
  31.8 22.7 %collective-permute-start.7 = (bf16[1,128,1024]{2,1,0:T(8,128)(2,1)S(1)}, bf16[1,128,1024]{2,1,0:T(8,128)(2,1)S(1)}, u32[]{:S(2)}, u32[]{:S(2)}) collective-permute-start(bf16[1,128,1024]{2,1,0:T(8,128)(2,1)S(1)} %get-tuple-element.31.refs_0_), channel_id=1, source_target_pairs={{0,2},{4,0},{6,4},{2,6},{1,3},{5,1},{7,5},{3,7},{8,10},{12,8},{14,... | collective-permute-start | bytes 786440 | tf_op jit(solution)/shard_map/ppermute | solution.py:28
  34.1 20.4 %collective-permute-start.6 = (bf16[1,128,1024]{2,1,0:T(8,128)(2,1)S(1)}, bf16[1,128,1024]{2,1,0:T(8,128)(2,1)S(1)}, u32[]{:S(2)}, u32[]{:S(2)}) collective-permute-start(bf16[1,128,1024]{2,1,0:T(8,128)(2,1)S(1)} %get-tuple-element.31.refs_0_), channel_id=1, source_target_pairs={{0,4},{4,6},{6,2},{2,0},{1,5},{5,7},{7,3},{3,1},{8,12},{12,14},{14... | collective-permute-start | bytes 786440 | tf_op jit(solution)/shard_map/ppermute | solution.py:28
  38.0 16.5 %collective-permute-start.14 = (bf16[512,128]{1,0:T(8,128)(2,1)S(1)}, bf16[512,128]{1,0:T(8,128)(2,1)S(1)}, u32[]{:S(2)}, u32[]{:S(2)}) collective-permute-start(bf16[512,128]{1,0:T(8,128)(2,1)S(1)} %get-tuple-element.35), channel_id=1, source_target_pairs={{0,4},{4,6},{6,2},{2,0},{1,5},{5,7},{7,3},{3,1},{8,12},{12,14},{14... | collective-permute-start | bytes 393224 | tf_op jit(solution)/shard_map/ppermute | solution.py:28
  38.3 16.2 %collective-permute-start.15 = (bf16[512,128]{1,0:T(8,128)(2,1)S(1)}, bf16[512,128]{1,0:T(8,128)(2,1)S(1)}, u32[]{:S(2)}, u32[]{:S(2)}) collective-permute-start(bf16[512,128]{1,0:T(8,128)(2,1)S(1)} %get-tuple-element.37), channel_id=1, source_target_pairs={{0,6},{4,2},{6,0},{2,4},{1,7},{5,3},{7,1},{3,5},{8,14},{12,10},{14... | collective-permute-start | bytes 393224 | tf_op jit(solution)/shard_map/ppermute | solution.py:28
  54.6 22.0 %collective-permute-start.18 = (bf16[512,512]{1,0:T(8,128)(2,1)S(1)}, bf16[512,512]{1,0:T(8,128)(2,1)S(1)}, u32[]{:S(2)}, u32[]{:S(2)}) collective-permute-start(bf16[512,512]{1,0:T(8,128)(2,1)S(1)} %join.1.refs_6_.refs_8_.refs_2_), channel_id=1, source_target_pairs={{0,16},{8,24},{16,0},{24,8},{1,17},{9,25},{17,1},{25,9},{2,18},{10... | collective-permute-start | bytes 1572872 | tf_op jit(solution)/shard_map/ppermute | solution.py:44
  55.2 20.0 %collective-permute-start.11 = (bf16[1,128,1024]{2,1,0:T(8,128)(2,1)S(1)}, bf16[1,128,1024]{2,1,0:T(8,128)(2,1)S(1)}, u32[]{:S(2)}, u32[]{:S(2)}) collective-permute-start(bf16[1,128,1024]{2,1,0:T(8,128)(2,1)S(1)} %collective-permute-done.7.refs_3_), channel_id=1, source_target_pairs={{0,16},{8,24},{16,0},{24,8},{1,17},{9,25},{17,1},{25,9},{2,18},{10... | collective-permute-start | bytes 786440 | tf_op jit(solution)/shard_map/ppermute | solution.py:44
  56.7 20.5 %collective-permute-start.21 = (bf16[1,128,1024]{2,1,0:T(8,128)(2,1)S(1)}, bf16[1,128,1024]{2,1,0:T(8,128)(2,1)S(1)}, u32[]{:S(2)}, u32[]{:S(2)}) collective-permute-start(bf16[1,128,1024]{2,1,0:T(8,128)(2,1)S(1)} %get-tuple-element.32.refs_0_), channel_id=1, source_target_pairs={{0,4},{4,6},{6,2},{2,0},{1,5},{5,7},{7,3},{3,1},{8,12},{12,14},{14... | collective-permute-start | bytes 786440 | tf_op jit(solution)/shard_map/ppermute | solution.py:28
  60.1 17.6 %collective-permute-start.8 = (bf16[1,128,1024]{2,1,0:T(8,128)(2,1)S(1)}, bf16[1,128,1024]{2,1,0:T(8,128)(2,1)S(1)}, u32[]{:S(2)}, u32[]{:S(2)}) collective-permute-start(bf16[1,128,1024]{2,1,0:T(8,128)(2,1)S(1)} %get-tuple-element.32.refs_0_), channel_id=1, source_target_pairs={{0,2},{4,0},{6,4},{2,6},{1,3},{5,1},{7,5},{3,7},{8,10},{12,8},{14,... | collective-permute-start | bytes 786440 | tf_op jit(solution)/shard_map/ppermute | solution.py:28
  60.1 20.7 %collective-permute-start.10 = (bf16[1,128,1024]{2,1,0:T(8,128)(2,1)S(1)}, bf16[1,128,1024]{2,1,0:T(8,128)(2,1)S(1)}, u32[]{:S(2)}, u32[]{:S(2)}) collective-permute-start(bf16[1,128,1024]{2,1,0:T(8,128)(2,1)S(1)} %collective-permute-done.6.refs_1_), channel_id=1, source_target_pairs={{0,16},{8,24},{16,0},{24,8},{1,17},{9,25},{17,1},{25,9},{2,18},{10... | collective-permute-start | bytes 786440 | tf_op jit(solution)/shard_map/ppermute | solution.py:44
  75.2 18.6 %collective-permute-start.19 = (bf16[512,512]{1,0:T(8,128)(2,1)S(1)}, bf16[512,512]{1,0:T(8,128)(2,1)S(1)}, u32[]{:S(2)}, u32[]{:S(2)}) collective-permute-start(bf16[512,512]{1,0:T(8,128)(2,1)S(1)} %join.1.refs_6_.refs_8_.refs_2_), channel_id=1, source_target_pairs={{0,1},{1,0},{2,3},{3,2},{4,5},{5,4},{6,7},{7,6},{8,9},{9,8},{10,11... | collective-permute-start | bytes 1572872 | tf_op jit(solution)/shard_map/ppermute | solution.py:44
  76.7 17.6 %collective-permute-start.20 = (bf16[512,512]{1,0:T(8,128)(2,1)S(1)}, bf16[512,512]{1,0:T(8,128)(2,1)S(1)}, u32[]{:S(2)}, u32[]{:S(2)}) collective-permute-start(bf16[512,512]{1,0:T(8,128)(2,1)S(1)} %collective-permute-done.18.refs_7_.refs_9_.refs_3_), channel_id=1, source_target_pairs={{0,1},{1,0},{2,3},{3,2},{4,5},{5,4},{6,7},{7,6},{8,9},{9,8},{10,11... | collective-permute-start | bytes 1572872 | tf_op jit(solution)/shard_map/ppermute | solution.py:44
  77.2 9.0 %collective-permute-start.22 = (bf16[1,128,1024]{2,1,0:T(8,128)(2,1)S(1)}, bf16[1,128,1024]{2,1,0:T(8,128)(2,1)S(1)}, u32[]{:S(2)}, u32[]{:S(2)}) collective-permute-start(bf16[1,128,1024]{2,1,0:T(8,128)(2,1)S(1)} %collective-permute-done.21.refs_1_), channel_id=1, source_target_pairs={{0,16},{8,24},{16,0},{24,8},{1,17},{9,25},{17,1},{25,9},{2,18},{10... | collective-permute-start | bytes 786440 | tf_op jit(solution)/shard_map/ppermute | solution.py:44
  77.7 12.1 %collective-permute-start.23 = (bf16[1,128,1024]{2,1,0:T(8,128)(2,1)S(1)}, bf16[1,128,1024]{2,1,0:T(8,128)(2,1)S(1)}, u32[]{:S(2)}, u32[]{:S(2)}) collective-permute-start(bf16[1,128,1024]{2,1,0:T(8,128)(2,1)S(1)} %collective-permute-done.8.refs_2_), channel_id=1, source_target_pairs={{0,16},{8,24},{16,0},{24,8},{1,17},{9,25},{17,1},{25,9},{2,18},{10... | collective-permute-start | bytes 786440 | tf_op jit(solution)/shard_map/ppermute | solution.py:44
  80.8 12.4 %collective-permute-start.12 = (bf16[1,128,1024]{2,1,0:T(8,128)(2,1)S(1)}, bf16[1,128,1024]{2,1,0:T(8,128)(2,1)S(1)}, u32[]{:S(2)}, u32[]{:S(2)}) collective-permute-start(bf16[1,128,1024]{2,1,0:T(8,128)(2,1)S(1)} %collective-permute-done.8.refs_2_), channel_id=1, source_target_pairs={{0,2},{4,0},{6,4},{2,6},{1,3},{5,1},{7,5},{3,7},{8,10},{12,8},{14,... | collective-permute-start | bytes 786440 | tf_op jit(solution)/shard_map/ppermute | solution.py:28
  86.2 10.2 %collective-permute-start.24 = (bf16[1,128,1024]{2,1,0:T(8,128)(2,1)S(1)}, bf16[1,128,1024]{2,1,0:T(8,128)(2,1)S(1)}, u32[]{:S(2)}, u32[]{:S(2)}) collective-permute-start(bf16[1,128,1024]{2,1,0:T(8,128)(2,1)S(1)} %collective-permute-done.6.refs_1_), channel_id=1, source_target_pairs={{0,4},{4,6},{6,2},{2,0},{1,5},{5,7},{7,3},{3,1},{8,12},{12,14},{14... | collective-permute-start | bytes 786440 | tf_op jit(solution)/shard_map/ppermute | solution.py:28
  89.8 9.5 %collective-permute-start.25 = (bf16[1,128,1024]{2,1,0:T(8,128)(2,1)S(1)}, bf16[1,128,1024]{2,1,0:T(8,128)(2,1)S(1)}, u32[]{:S(2)}, u32[]{:S(2)}) collective-permute-start(bf16[1,128,1024]{2,1,0:T(8,128)(2,1)S(1)} %collective-permute-done.10.refs_5_), channel_id=1, source_target_pairs={{0,4},{4,6},{6,2},{2,0},{1,5},{5,7},{7,3},{3,1},{8,12},{12,14},{14... | collective-permute-start | bytes 786440 | tf_op jit(solution)/shard_map/ppermute | solution.py:28
  93.2 9.9 %collective-permute-start.13 = (bf16[1,128,1024]{2,1,0:T(8,128)(2,1)S(1)}, bf16[1,128,1024]{2,1,0:T(8,128)(2,1)S(1)}, u32[]{:S(2)}, u32[]{:S(2)}) collective-permute-start(bf16[1,128,1024]{2,1,0:T(8,128)(2,1)S(1)} %collective-permute-done.12.refs_0_), channel_id=1, source_target_pairs={{0,16},{8,24},{16,0},{24,8},{1,17},{9,25},{17,1},{25,9},{2,18},{10... | collective-permute-start | bytes 786440 | tf_op jit(solution)/shard_map/ppermute | solution.py:44

commit v4 on v3

--- a/solution.py
+++ b/solution.py
@@ -158,11 +158,11 @@
             )
 
 
-def finish_kernel(slots, start, carried, width, *refs):
+def finish_kernel(slots, start, width, *refs):
     count = 2 * len(slots)
     att_refs, cot_refs = refs[:count], refs[count : count + 4]
     out_ref, held, sems = refs[-3:]
-    total_ref = refs[count + 4] if carried else None
+    total_ref = refs[count + 4]
     half = cot_refs[0].shape[0]
     tokens = att_refs[0].shape[1]
     wide = held.shape[2]
@@ -175,9 +175,7 @@
         for at, left in left_sides(cot_refs, tokens, slots):
             here = pl.ds(pl.multiple_of(at * half, half), half)
             value = jnp.dot(left, rows, preferred_element_type=jnp.float32)
-            if carried:
-                value = value + total_ref[here, columns]
-            held[j % 2, here, :] = value.astype(jnp.bfloat16)
+            held[j % 2, here, :] = (value + total_ref[here, columns]).astype(jnp.bfloat16)
         copies.append(
             pltpu.make_async_copy(
                 held.at[j % 2],
@@ -240,19 +238,17 @@
         name="attend",
     )(place, query_held, *key_ring, value_held, *value_ring[1:])
 
-    mirrored = [[swap(piece, "pipe", far)] + [None] * (n - 1) for piece in pieces]
-    near = []
-    for c, piece in enumerate(pieces):
-        sent = mirrored[c][:1]
-        if c:
-            piece = after(piece, near[0][1], near[0][-1])
-            sent = sent + [mirrored[0][1], mirrored[0][-1]]
-        near.append(gather(piece, 1 - 2 * c, lambda x, sent=sent: after(x, *sent)))
-        for s in range(1, n):
-            by_ring = s == n // 2 and c < parts - 1
-            mirrored[c][s] = (
-                around(mirrored[c][s - 1], 1) if by_ring else swap(near[c][s], "pipe", far)
-            )
+    near, mirrored = [], []
+    for c in range(parts):
+        held, sent = [pieces[c]], []
+        for s in range(n):
+            by_ring = s == n - 1 and c < parts - 1
+            sent.append(around(sent[-1], 1) if by_ring else swap(held[s], "pipe", far))
+            if s < n - 1:
+                arrived = around(held[s], 1)
+                held.append(after(arrived, sent[s]) if s < n - 2 else arrived)
+        near.append(held)
+        mirrored.append(sent)
     turned = [turned[0]] + [around(after(turned[s], value_ring[n // 2]), s) for s in range(1, n)]
     mine = pl.pallas_call(
         join_kernel,
@@ -261,17 +257,18 @@
         out_specs=VMEM,
         compiler_params=params(16),
         name="join",
-    )(*turned[:-1], after(turned[-1], near[0][1], near[0][-1], *[sent[0] for sent in mirrored]))
+    )(*turned[:-1], after(turned[-1], *[sent[0] for sent in mirrored]))
     mine_far = swap(mine, "pipe", far)
     cots = [mine, mine_far, swap(mine, "tp", 1), swap(mine_far, "tp", 1)]
 
     def attended(c, slots):
         return [side[c][s] for side in (near, mirrored) for s in slots]
 
-    first_slots = [s for s in range(n) if s != n // 2]
+    first_slots = list(range(n - 1))
 
     tile = TILE if chunk % TILE == 0 else chunk
-    total = pl.pallas_call(
+    totals = [
+        pl.pallas_call(
         functools.partial(early_kernel, first_slots),
         out_shape=jax.ShapeDtypeStruct((features, chunk), jnp.float32),
         in_specs=[VMEM] * (2 * n + 2),
@@ -283,12 +280,13 @@
             transcendentals=0,
         ),
         name="early",
-    )(*attended(parts - 1, first_slots), *cots)
+    )(*attended(c, first_slots), *cots)
+        for c in range(parts)
+    ]
     grad_out = None
     for c in range(parts):
-        last = c == parts - 1
-        slots = [n // 2] if last else list(range(n))
-        operands = attended(c, slots) + cots + ([total] if last else [])
+        slots = [n - 1]
+        operands = attended(c, slots) + cots + [totals[c]]
         specs = [VMEM] * len(operands)
         aliases = {}
         if grad_out is not None:
@@ -296,7 +294,7 @@
             operands.append(grad_out)
             specs.append(ANY)
         grad_out = pl.pallas_call(
-            functools.partial(finish_kernel, slots, c * chunk, last, chunk),
+            functools.partial(finish_kernel, slots, c * chunk, chunk),
             out_shape=jax.ShapeDtypeStruct((1, features, heads), jnp.bfloat16),
             in_specs=specs,
             out_specs=ANY,

time: 106 us -> 96.2 us (0.908)
  waiting for transfers between devices: 49.6 us -> 35.4 us
  starting transfers between devices: 39 us -> 42.8 us
    ppermute x10, waiting for transfers between devices: 22.2 us -> 2.7 us  [swap(): lax.ppermute(x, axis, [(i, i ^ mask) for i in range(lax.axis_size(axis))])]
    ppermute x16, waiting for transfers between devices: 27.5 us -> 32.7 us  [around(): lax.ppermute(x, 'ctx', [(order[q], order[(q + shift) % n]) for q in range...]
    ppermute x16, starting transfers between devices: 29.9 us -> 32.8 us  [around(): lax.ppermute(x, 'ctx', [(order[q], order[(q + shift) % n]) for q in range...]
    pallas_call x1 -> x2, Pallas kernels: 1.79 us -> 3.59 us  [local(): pl.pallas_call(functools.partial(early_kernel, first_slots), out_shape=ja...]
    pallas_call x2, Pallas kernels: 6.29 us -> 5.01 us  [local(): pl.pallas_call(functools.partial(finish_kernel, slots, c * chunk, chunk),...]
  transfers between devices with their start and end apart: 26 -> 26, of which waited for: 13 -> 10; matrix products, arithmetic and copies ran while one was open for 0% -> 0% of each run, Pallas kernels for 5% -> 7%
where the time goes in v4:
time: 96.2 us; the launch traced here: 95.7 us
  starting transfers between devices  42.8 us (44%)
  waiting for transfers between devices  35.4 us (37%)
  Pallas kernels  12 us (12%)
  local copies, waits for them, and re-layouts  4.72 us (5%)
    ppermute x16, starting transfers between devices, around(): lax.ppermute(x, 'ctx', [(order[q], order[(q + shift) % n]) for q in range...  32.8 us
    ppermute x16, waiting for transfers between devices, around(): lax.ppermute(x, 'ctx', [(order[q], order[(q + shift) % n]) for q in range...  32.7 us
    ppermute x10, starting transfers between devices, swap(): lax.ppermute(x, axis, [(i, i ^ mask) for i in range(lax.axis_size(axis))])  10.1 us
    pallas_call x2, Pallas kernels, local(): pl.pallas_call(functools.partial(finish_kernel, slots, c * chunk, chunk),...  5.01 us
    unnamed x10, local copies, waits for them, and re-layouts  4.72 us
    pallas_call x2, Pallas kernels, local(): pl.pallas_call(functools.partial(early_kernel, first_slots), out_shape=ja...  3.59 us
    ppermute x10, waiting for transfers between devices, swap(): lax.ppermute(x, axis, [(i, i ^ mask) for i in range(lax.axis_size(axis))])  2.7 us
    pallas_call x1, Pallas kernels, local(): pl.pallas_call(functools.partial(attention_kernel, HQ // HK, 1.0 / math.s...  2.51 us
  transfers between devices with their start and end apart: 26, of which 10 were waited for; matrix products, arithmetic and copies ran while one was open for 0% of the time, Pallas kernels for 7%

profile of v4, /device:TPU:0, one launch (start us, length us, event | category | flops | bytes accessed | tf_op | source)
XLA Modules:
  0.0 95.7 jit_solution(16642932885724202558)
XLA Ops:
  0.6 0.9 copy-done.2
  1.5 0.7 copy-done.4
  2.2 0.6 pack.1
  2.8 4.1 %collective-permute-start = (bf16[1,144,512]{2,1,0:T(8,128)(2,1)S(1)}, bf16[1,144,512]{2,1,0:T(8,128)(2,1)S(1)}, u32[]{:S(2)}, u32[]{:S(2)}) collective-permute-start(bf16[1,144,512]{2,1,0:T(8,128)(2,1)S(1)} %get-tuple-element.25.refs_0_), channel_id=1, source_target_pairs={{0,4},{4,6},{6,2},{2,0},{1,5},{5,7},{7,3},{3,1},{8,12},{12,14},{14... | collective-permute-start | bytes 442376 | tf_op jit(solution)/shard_map/ppermute | solution.py:28
  6.8 0.0 collective-permute-start.4
  6.8 1.9 %collective-permute-start.2 = (bf16[1,144,512]{2,1,0:T(8,128)(2,1)S(1)}, bf16[1,144,512]{2,1,0:T(8,128)(2,1)S(1)}, u32[]{:S(2)}, u32[]{:S(2)}) collective-permute-start(bf16[1,144,512]{2,1,0:T(8,128)(2,1)S(1)} %get-tuple-element.25.refs_0_), channel_id=1, source_target_pairs={{0,2},{4,0},{6,4},{2,6},{1,3},{5,1},{7,5},{3,7},{8,10},{12,8},{14,... | collective-permute-start | bytes 442376 | tf_op jit(solution)/shard_map/ppermute | solution.py:28
  8.8 1.0 %copy-done.1 = bf16[1,128,2048]{2,1,0:T(8,128)(2,1)S(1)} copy-done((bf16[1,128,2048]{2,1,0:T(8,128)(2,1)S(1)}, bf16[1,128,2048]{2,1,0:T(8,128)(2,1)}, u32[]{:S(2)}) %copy-start.1) | copy-done | bytes 524312
  9.8 0.9 copy-done.3
  10.8 0.4 collective-permute-done.refs_1_
  11.1 3.4 %collective-permute-start.1 = (bf16[1,144,512]{2,1,0:T(8,128)(2,1)S(1)}, bf16[1,144,512]{2,1,0:T(8,128)(2,1)S(1)}, u32[]{:S(2)}, u32[]{:S(2)}) collective-permute-start(bf16[1,144,512]{2,1,0:T(8,128)(2,1)S(1)} %collective-permute-done.refs_1_), channel_id=1, source_target_pairs={{0,4},{4,6},{6,2},{2,0},{1,5},{5,7},{7,3},{3,1},{8,12},{12,14},{14... | collective-permute-start | bytes 442376 | tf_op jit(solution)/shard_map/ppermute | solution.py:28
  14.5 0.0 collective-permute-start.3
  14.5 1.2 %copy-done = bf16[1,128,4096]{2,1,0:T(8,128)(2,1)S(1)} copy-done((bf16[1,128,4096]{2,1,0:T(8,128)(2,1)S(1)}, bf16[1,128,4096]{2,1,0:T(8,128)(2,1)}, u32[]{:S(2)}) %copy-start) | copy-done | bytes 1048600
  15.8 0.2 turn.1
  16.0 2.0 %collective-permute-start.5 = (bf16[1,128,512]{2,1,0:T(8,128)(2,1)S(1)}, bf16[1,128,512]{2,1,0:T(8,128)(2,1)S(1)}, u32[]{:S(2)}, u32[]{:S(2)}) collective-permute-start(bf16[1,128,512]{2,1,0:T(8,128)(2,1)S(1)} %collective-permute-done.4.refs_7_), channel_id=1, source_target_pairs={{0,2},{4,0},{6,4},{2,6},{1,3},{5,1},{7,5},{3,7},{8,10},{12,8},{14,... | collective-permute-start | bytes 393224 | tf_op jit(solution)/shard_map/ppermute | solution.py:28
  18.0 6.3 %collective-permute-done.3.refs_5_ = bf16[1,128,512]{2,1,0:T(8,128)(2,1)S(1)} collective-permute-done((bf16[1,128,512]{2,1,0:T(8,128)(2,1)S(1)}, bf16[1,128,512]{2,1,0:T(8,128)(2,1)S(1)}, u32[]{:S(2)}, u32[]{:S(2)}) %collective-permute-start.3) | collective-permute-done | bytes 131104 | tf_op jit(solution)/shard_map/ppermute | solution.py:28
  24.3 2.2 %collective-permute-done.5.refs_6_ = bf16[1,128,512]{2,1,0:T(8,128)(2,1)S(1)} collective-permute-done((bf16[1,128,512]{2,1,0:T(8,128)(2,1)S(1)}, bf16[1,128,512]{2,1,0:T(8,128)(2,1)S(1)}, u32[]{:S(2)}, u32[]{:S(2)}) %collective-permute-start.5) | collective-permute-done | bytes 131104 | tf_op jit(solution)/shard_map/ppermute | solution.py:28
  26.6 2.5 %attend.1 = (bf16[1,128,2048]{2,1,0:T(8,128)(2,1)}, bf16[1,128,1024]{2,1,0:T(8,128)(2,1)S(1)}, bf16[1,128,1024]{2,1,0:T(8,128)(2,1)S(1)}) custom-call(f32[128,128]{1,0:T(8,128)S(1)} %get-tuple-element.23.place_ref.ready_ref, bf16[1,128,2048]{2,1,0:T(8,128)(2,1)S(1)} %get-tuple-element.24.query_ref, bf16[1,144,512]{2,1,0:T(8,128)(2,1)S(1)} %get-tuple-element.25.refs_0_, ...), custom_call_target="tpu_custom_call" | custom-call | tf_op jit(solution)/shard_map/attend/pallas_call | solution.py:231
  29.1 1.5 %collective-permute-start.7 = (bf16[1,128,1024]{2,1,0:T(8,128)(2,1)S(1)}, bf16[1,128,1024]{2,1,0:T(8,128)(2,1)S(1)}, u32[]{:S(2)}, u32[]{:S(2)}) collective-permute-start(bf16[1,128,1024]{2,1,0:T(8,128)(2,1)S(1)} %get-tuple-element.31.refs_0_), channel_id=1, source_target_pairs={{0,16},{8,24},{16,0},{24,8},{1,17},{9,25},{17,1},{25,9},{2,18},{10... | collective-permute-start | bytes 786440 | tf_op jit(solution)/shard_map/ppermute | solution.py:44
  30.6 0.5 collective-permute-start.15
  31.1 0.7 collective-permute-start.14
  31.8 2.2 %collective-permute-start.12 = (bf16[512,128]{1,0:T(8,128)(2,1)S(1)}, bf16[512,128]{1,0:T(8,128)(2,1)S(1)}, u32[]{:S(2)}, u32[]{:S(2)}) collective-permute-start(bf16[512,128]{1,0:T(8,128)(2,1)S(1)} %get-tuple-element.35), channel_id=1, source_target_pairs={{0,4},{4,6},{6,2},{2,0},{1,5},{5,7},{7,3},{3,1},{8,12},{12,14},{14... | collective-permute-start | bytes 393224 | tf_op jit(solution)/shard_map/ppermute | solution.py:28
  34.0 2.5 %collective-permute-start.13 = (bf16[512,128]{1,0:T(8,128)(2,1)S(1)}, bf16[512,128]{1,0:T(8,128)(2,1)S(1)}, u32[]{:S(2)}, u32[]{:S(2)}) collective-permute-start(bf16[512,128]{1,0:T(8,128)(2,1)S(1)} %get-tuple-element.37), channel_id=1, source_target_pairs={{0,6},{4,2},{6,0},{2,4},{1,7},{5,3},{7,1},{3,5},{8,14},{12,10},{14... | collective-permute-start | bytes 393224 | tf_op jit(solution)/shard_map/ppermute | solution.py:28
  36.5 10.1 %collective-permute-done.14.refs_3_ = bf16[512,128]{1,0:T(8,128)(2,1)S(1)} collective-permute-done((bf16[512,128]{1,0:T(8,128)(2,1)S(1)}, bf16[512,128]{1,0:T(8,128)(2,1)S(1)}, u32[]{:S(2)}, u32[]{:S(2)}) %collective-permute-start.14) | collective-permute-done | bytes 131104 | tf_op jit(solution)/shard_map/ppermute | solution.py:28
  46.6 0.1 join.1.refs_6_.refs_2_
  46.7 1.6 %collective-permute-start.16 = (bf16[512,512]{1,0:T(8,128)(2,1)S(1)}, bf16[512,512]{1,0:T(8,128)(2,1)S(1)}, u32[]{:S(2)}, u32[]{:S(2)}) collective-permute-start(bf16[512,512]{1,0:T(8,128)(2,1)S(1)} %join.1.refs_6_.refs_2_), channel_id=1, source_target_pairs={{0,16},{8,24},{16,0},{24,8},{1,17},{9,25},{17,1},{25,9},{2,18},{10... | collective-permute-start | bytes 1572872 | tf_op jit(solution)/shard_map/ppermute | solution.py:44
  48.3 3.0 %collective-permute-start.6 = (bf16[1,128,1024]{2,1,0:T(8,128)(2,1)S(1)}, bf16[1,128,1024]{2,1,0:T(8,128)(2,1)S(1)}, u32[]{:S(2)}, u32[]{:S(2)}) collective-permute-start(bf16[1,128,1024]{2,1,0:T(8,128)(2,1)S(1)} %get-tuple-element.31.refs_0_), channel_id=1, source_target_pairs={{0,4},{4,6},{6,2},{2,0},{1,5},{5,7},{7,3},{3,1},{8,12},{12,14},{14... | collective-permute-start | bytes 786440 | tf_op jit(solution)/shard_map/ppermute | solution.py:28
  51.3 4.4 %collective-permute-done.20.refs_1_ = bf16[1,128,1024]{2,1,0:T(8,128)(2,1)S(1)} collective-permute-done((bf16[1,128,1024]{2,1,0:T(8,128)(2,1)S(1)}, bf16[1,128,1024]{2,1,0:T(8,128)(2,1)S(1)}, u32[]{:S(2)}, u32[]{:S(2)}) %collective-permute-start.20) | collective-permute-done | bytes 262176 | tf_op jit(solution)/shard_map/ppermute | solution.py:28
  55.8 0.3 collective-permute-start.22
  56.1 1.6 %collective-permute-start.21 = (bf16[1,128,1024]{2,1,0:T(8,128)(2,1)S(1)}, bf16[1,128,1024]{2,1,0:T(8,128)(2,1)S(1)}, u32[]{:S(2)}, u32[]{:S(2)}) collective-permute-start(bf16[1,128,1024]{2,1,0:T(8,128)(2,1)S(1)} %collective-permute-done.20.refs_1_), channel_id=1, source_target_pairs={{0,4},{4,6},{6,2},{2,0},{1,5},{5,7},{7,3},{3,1},{8,12},{12,14},{14... | collective-permute-start | bytes 786440 | tf_op jit(solution)/shard_map/ppermute | solution.py:28
  57.7 3.7 %collective-permute-done.6.refs_1_ = bf16[1,128,1024]{2,1,0:T(8,128)(2,1)S(1)} collective-permute-done((bf16[1,128,1024]{2,1,0:T(8,128)(2,1)S(1)}, bf16[1,128,1024]{2,1,0:T(8,128)(2,1)S(1)}, u32[]{:S(2)}, u32[]{:S(2)}) %collective-permute-start.6) | collective-permute-done | bytes 262176 | tf_op jit(solution)/shard_map/ppermute | solution.py:28
  61.4 0.1 collective-permute-start.9
  61.5 1.8 %collective-permute-start.8 = (bf16[1,128,1024]{2,1,0:T(8,128)(2,1)S(1)}, bf16[1,128,1024]{2,1,0:T(8,128)(2,1)S(1)}, u32[]{:S(2)}, u32[]{:S(2)}) collective-permute-start(bf16[1,128,1024]{2,1,0:T(8,128)(2,1)S(1)} %collective-permute-done.6.refs_1_), channel_id=1, source_target_pairs={{0,4},{4,6},{6,2},{2,0},{1,5},{5,7},{7,3},{3,1},{8,12},{12,14},{14... | collective-permute-start | bytes 786440 | tf_op jit(solution)/shard_map/ppermute | solution.py:28
  63.3 1.8 %collective-permute-done.22.refs_4_ = bf16[1,128,1024]{2,1,0:T(8,128)(2,1)S(1)} collective-permute-done((bf16[1,128,1024]{2,1,0:T(8,128)(2,1)S(1)}, bf16[1,128,1024]{2,1,0:T(8,128)(2,1)S(1)}, u32[]{:S(2)}, u32[]{:S(2)}) %collective-permute-start.22) | collective-permute-done | bytes 262176 | tf_op jit(solution)/shard_map/ppermute | solution.py:44
  65.1 1.5 %collective-permute-start.17 = (bf16[512,512]{1,0:T(8,128)(2,1)S(1)}, bf16[512,512]{1,0:T(8,128)(2,1)S(1)}, u32[]{:S(2)}, u32[]{:S(2)}) collective-permute-start(bf16[512,512]{1,0:T(8,128)(2,1)S(1)} %join.1.refs_6_.refs_2_), channel_id=1, source_target_pairs={{0,1},{1,0},{2,3},{3,2},{4,5},{5,4},{6,7},{7,6},{8,9},{9,8},{10,11... | collective-permute-start | bytes 1572872 | tf_op jit(solution)/shard_map/ppermute | solution.py:44
  66.6 0.5 collective-permute-start.18
  67.2 2.0 %collective-permute-start.24 = (bf16[1,128,1024]{2,1,0:T(8,128)(2,1)S(1)}, bf16[1,128,1024]{2,1,0:T(8,128)(2,1)S(1)}, u32[]{:S(2)}, u32[]{:S(2)}) collective-permute-start(bf16[1,128,1024]{2,1,0:T(8,128)(2,1)S(1)} %collective-permute-done.21.refs_2_), channel_id=1, source_target_pairs={{0,16},{8,24},{16,0},{24,8},{1,17},{9,25},{17,1},{25,9},{2,18},{10... | collective-permute-start | bytes 786440 | tf_op jit(solution)/shard_map/ppermute | solution.py:44
  69.1 0.9 collective-permute-done.9.refs_4_
  70.0 5.9 %collective-permute-start.10 = (bf16[1,128,1024]{2,1,0:T(8,128)(2,1)S(1)}, bf16[1,128,1024]{2,1,0:T(8,128)(2,1)S(1)}, u32[]{:S(2)}, u32[]{:S(2)}) collective-permute-start(bf16[1,128,1024]{2,1,0:T(8,128)(2,1)S(1)} %collective-permute-done.8.refs_2_), channel_id=1, source_target_pairs={{0,4},{4,6},{6,2},{2,0},{1,5},{5,7},{7,3},{3,1},{8,12},{12,14},{14... | collective-permute-start | bytes 786440 | tf_op jit(solution)/shard_map/ppermute | solution.py:28
  75.9 0.0 collective-permute-start.23
  76.0 3.5 %collective-permute-start.25 = (bf16[1,128,1024]{2,1,0:T(8,128)(2,1)S(1)}, bf16[1,128,1024]{2,1,0:T(8,128)(2,1)S(1)}, u32[]{:S(2)}, u32[]{:S(2)}) collective-permute-start(bf16[1,128,1024]{2,1,0:T(8,128)(2,1)S(1)} %collective-permute-done.24.refs_5_), channel_id=1, source_target_pairs={{0,4},{4,6},{6,2},{2,0},{1,5},{5,7},{7,3},{3,1},{8,12},{12,14},{14... | collective-permute-start | bytes 786440 | tf_op jit(solution)/shard_map/ppermute | solution.py:28
  79.5 3.2 %collective-permute-done.10.refs_0_ = bf16[1,128,1024]{2,1,0:T(8,128)(2,1)S(1)} collective-permute-done((bf16[1,128,1024]{2,1,0:T(8,128)(2,1)S(1)}, bf16[1,128,1024]{2,1,0:T(8,128)(2,1)S(1)}, u32[]{:S(2)}, u32[]{:S(2)}) %collective-permute-start.10) | collective-permute-done | bytes 262176 | tf_op jit(solution)/shard_map/ppermute | solution.py:28
  82.7 1.5 %collective-permute-start.19 = (bf16[1,128,1024]{2,1,0:T(8,128)(2,1)S(1)}, bf16[1,128,1024]{2,1,0:T(8,128)(2,1)S(1)}, u32[]{:S(2)}, u32[]{:S(2)}) collective-permute-start(bf16[1,128,1024]{2,1,0:T(8,128)(2,1)S(1)} %collective-permute-done.8.refs_2_), channel_id=1, source_target_pairs={{0,16},{8,24},{16,0},{24,8},{1,17},{9,25},{17,1},{25,9},{2,18},{10... | collective-permute-start | bytes 786440 | tf_op jit(solution)/shard_map/ppermute | solution.py:44
  84.2 0.5 collective-permute-start.11
  84.7 1.8 %early.3.refs_6_ = f32[1024,1024]{1,0:T(8,128)S(1)} custom-call(bf16[1,128,1024]{2,1,0:T(8,128)(2,1)S(1)} %get-tuple-element.40.refs_0_, bf16[1,128,1024]{2,1,0:T(8,128)(2,1)S(1)} %collective-permute-done.20.refs_1_, bf16[1,128,1024]{2,1,0:T(8,128)(2,1)S(1)} %collective-permute-done.21.refs_2_, bf16[1,128,1024]{2,1,0:T(8,128)(2,1)S(1)} %collective-permute-done.15.refs_3_, ...), custom_call_target="tpu_custom_call" | custom-call | flops 1610612736 | bytes 8388608 | tf_op jit(solution)/shard_map/early/pallas_call | solution.py:271
  86.5 2.3 %collective-permute-done.25.refs_1_ = bf16[1,128,1024]{2,1,0:T(8,128)(2,1)S(1)} collective-permute-done((bf16[1,128,1024]{2,1,0:T(8,128)(2,1)S(1)}, bf16[1,128,1024]{2,1,0:T(8,128)(2,1)S(1)}, u32[]{:S(2)}, u32[]{:S(2)}) %collective-permute-start.25) | collective-permute-done | bytes 262176 | tf_op jit(solution)/shard_map/ppermute | solution.py:28
  88.9 2.5 %finish.2.refs_7_ = bf16[1,1024,2048]{2,1,0:T(8,128)(2,1)} custom-call(bf16[1,128,1024]{2,1,0:T(8,128)(2,1)S(1)} %collective-permute-done.23.refs_0_, bf16[1,128,1024]{2,1,0:T(8,128)(2,1)S(1)} %collective-permute-done.25.refs_1_, bf16[512,512]{1,0:T(8,128)(2,1)S(1)} %join.1.refs_6_.refs_2_, bf16[512,512]{1,0:T(8,128)(2,1)S(1)} %collective-permute-done.16.refs_7_.refs_3_, ...), custom_call_target="tpu_custom_call" | custom-call | flops 536870912 | bytes 8388608 | tf_op jit(solution)/shard_map/finish/pallas_call | solution.py:296
  91.4 1.8 %early.2.refs_6_ = f32[1024,1024]{1,0:T(8,128)S(1)} custom-call(bf16[1,128,1024]{2,1,0:T(8,128)(2,1)S(1)} %get-tuple-element.31.refs_0_, bf16[1,128,1024]{2,1,0:T(8,128)(2,1)S(1)} %collective-permute-done.6.refs_1_, bf16[1,128,1024]{2,1,0:T(8,128)(2,1)S(1)} %collective-permute-done.8.refs_2_, bf16[1,128,1024]{2,1,0:T(8,128)(2,1)S(1)} %collective-permute-done.7.refs_3_, ...), custom_call_target="tpu_custom_call" | custom-call | flops 1610612736 | bytes 8388608 | tf_op jit(solution)/shard_map/early/pallas_call | solution.py:271
  93.2 2.5 %finish.3 = bf16[1,1024,2048]{2,1,0:T(8,128)(2,1)} custom-call(bf16[1,128,1024]{2,1,0:T(8,128)(2,1)S(1)} %collective-permute-done.10.refs_0_, bf16[1,128,1024]{2,1,0:T(8,128)(2,1)S(1)} %collective-permute-done.11.refs_1_, bf16[512,512]{1,0:T(8,128)(2,1)S(1)} %join.1.refs_6_.refs_2_, ...), custom_call_target="tpu_custom_call", output_to_operand_aliasing={{}: (7, {})} | custom-call | flops 536870912 | bytes 8388608 | tf_op jit(solution)/shard_map/finish/pallas_call | solution.py:296
  (23 shorter events, 0.1 us)
Async XLA Ops:
  0.6 0.9 copy-start.2
  1.5 0.7 copy-start.4
  2.8 8.4 %collective-permute-start = (bf16[1,144,512]{2,1,0:T(8,128)(2,1)S(1)}, bf16[1,144,512]{2,1,0:T(8,128)(2,1)S(1)}, u32[]{:S(2)}, u32[]{:S(2)}) collective-permute-start(bf16[1,144,512]{2,1,0:T(8,128)(2,1)S(1)} %get-tuple-element.25.refs_0_), channel_id=1, source_target_pairs={{0,4},{4,6},{6,2},{2,0},{1,5},{5,7},{7,3},{3,1},{8,12},{12,14},{14... | collective-permute-start | bytes 442376 | tf_op jit(solution)/shard_map/ppermute | solution.py:28
  6.8 9.1 %collective-permute-start.4 = (bf16[1,128,512]{2,1,0:T(8,128)(2,1)}, bf16[1,128,512]{2,1,0:T(8,128)(2,1)S(1)}, u32[]{:S(2)}, u32[]{:S(2)}) collective-permute-start(bf16[1,128,512]{2,1,0:T(8,128)(2,1)} %value_ref.1), channel_id=1, source_target_pairs={{0,2},{4,0},{6,4},{2,6},{1,3},{5,1},{7,5},{3,7},{8,10},{12,8},{14,... | collective-permute-start | bytes 393224 | tf_op jit(solution)/shard_map/ppermute | solution.py:28
  6.8 17.5 %collective-permute-start.2 = (bf16[1,144,512]{2,1,0:T(8,128)(2,1)S(1)}, bf16[1,144,512]{2,1,0:T(8,128)(2,1)S(1)}, u32[]{:S(2)}, u32[]{:S(2)}) collective-permute-start(bf16[1,144,512]{2,1,0:T(8,128)(2,1)S(1)} %get-tuple-element.25.refs_0_), channel_id=1, source_target_pairs={{0,2},{4,0},{6,4},{2,6},{1,3},{5,1},{7,5},{3,7},{8,10},{12,8},{14,... | collective-permute-start | bytes 442376 | tf_op jit(solution)/shard_map/ppermute | solution.py:28
  8.8 1.0 %copy-start.1 = (bf16[1,128,2048]{2,1,0:T(8,128)(2,1)S(1)}, bf16[1,128,2048]{2,1,0:T(8,128)(2,1)}, u32[]{:S(2)}) copy-start(bf16[1,128,2048]{2,1,0:T(8,128)(2,1)} %query_ref.1) | copy-start | bytes 1572868
  9.8 0.9 copy-start.3
  11.1 15.4 %collective-permute-start.1 = (bf16[1,144,512]{2,1,0:T(8,128)(2,1)S(1)}, bf16[1,144,512]{2,1,0:T(8,128)(2,1)S(1)}, u32[]{:S(2)}, u32[]{:S(2)}) collective-permute-start(bf16[1,144,512]{2,1,0:T(8,128)(2,1)S(1)} %collective-permute-done.refs_1_), channel_id=1, source_target_pairs={{0,4},{4,6},{6,2},{2,0},{1,5},{5,7},{7,3},{3,1},{8,12},{12,14},{14... | collective-permute-start | bytes 442376 | tf_op jit(solution)/shard_map/ppermute | solution.py:28
  14.5 9.8 %collective-permute-start.3 = (bf16[1,128,512]{2,1,0:T(8,128)(2,1)S(1)}, bf16[1,128,512]{2,1,0:T(8,128)(2,1)S(1)}, u32[]{:S(2)}, u32[]{:S(2)}) collective-permute-start(bf16[1,128,512]{2,1,0:T(8,128)(2,1)S(1)} %copy-done.3), channel_id=1, source_target_pairs={{0,4},{4,6},{6,2},{2,0},{1,5},{5,7},{7,3},{3,1},{8,12},{12,14},{14... | collective-permute-start | bytes 393224 | tf_op jit(solution)/shard_map/ppermute | solution.py:28
  14.5 1.2 %copy-start = (bf16[1,128,4096]{2,1,0:T(8,128)(2,1)S(1)}, bf16[1,128,4096]{2,1,0:T(8,128)(2,1)}, u32[]{:S(2)}) copy-start(bf16[1,128,4096]{2,1,0:T(8,128)(2,1)} %cot_ref.1) | copy-start | bytes 3145732
  16.0 10.6 %collective-permute-start.5 = (bf16[1,128,512]{2,1,0:T(8,128)(2,1)S(1)}, bf16[1,128,512]{2,1,0:T(8,128)(2,1)S(1)}, u32[]{:S(2)}, u32[]{:S(2)}) collective-permute-start(bf16[1,128,512]{2,1,0:T(8,128)(2,1)S(1)} %collective-permute-done.4.refs_7_), channel_id=1, source_target_pairs={{0,2},{4,0},{6,4},{2,6},{1,3},{5,1},{7,5},{3,7},{8,10},{12,8},{14,... | collective-permute-start | bytes 393224 | tf_op jit(solution)/shard_map/ppermute | solution.py:28
  29.1 17.5 %collective-permute-start.7 = (bf16[1,128,1024]{2,1,0:T(8,128)(2,1)S(1)}, bf16[1,128,1024]{2,1,0:T(8,128)(2,1)S(1)}, u32[]{:S(2)}, u32[]{:S(2)}) collective-permute-start(bf16[1,128,1024]{2,1,0:T(8,128)(2,1)S(1)} %get-tuple-element.31.refs_0_), channel_id=1, source_target_pairs={{0,16},{8,24},{16,0},{24,8},{1,17},{9,25},{17,1},{25,9},{2,18},{10... | collective-permute-start | bytes 786440 | tf_op jit(solution)/shard_map/ppermute | solution.py:44
  30.6 16.0 %collective-permute-start.15 = (bf16[1,128,1024]{2,1,0:T(8,128)(2,1)S(1)}, bf16[1,128,1024]{2,1,0:T(8,128)(2,1)S(1)}, u32[]{:S(2)}, u32[]{:S(2)}) collective-permute-start(bf16[1,128,1024]{2,1,0:T(8,128)(2,1)S(1)} %get-tuple-element.40.refs_0_), channel_id=1, source_target_pairs={{0,16},{8,24},{16,0},{24,8},{1,17},{9,25},{17,1},{25,9},{2,18},{10... | collective-permute-start | bytes 786440 | tf_op jit(solution)/shard_map/ppermute | solution.py:44
  31.1 15.5 %collective-permute-start.14 = (bf16[512,128]{1,0:T(8,128)(2,1)S(1)}, bf16[512,128]{1,0:T(8,128)(2,1)S(1)}, u32[]{:S(2)}, u32[]{:S(2)}) collective-permute-start(bf16[512,128]{1,0:T(8,128)(2,1)S(1)} %get-tuple-element.39), channel_id=1, source_target_pairs={{0,2},{4,0},{6,4},{2,6},{1,3},{5,1},{7,5},{3,7},{8,10},{12,8},{14,... | collective-permute-start | bytes 393224 | tf_op jit(solution)/shard_map/ppermute | solution.py:28
  31.8 14.8 %collective-permute-start.12 = (bf16[512,128]{1,0:T(8,128)(2,1)S(1)}, bf16[512,128]{1,0:T(8,128)(2,1)S(1)}, u32[]{:S(2)}, u32[]{:S(2)}) collective-permute-start(bf16[512,128]{1,0:T(8,128)(2,1)S(1)} %get-tuple-element.35), channel_id=1, source_target_pairs={{0,4},{4,6},{6,2},{2,0},{1,5},{5,7},{7,3},{3,1},{8,12},{12,14},{14... | collective-permute-start | bytes 393224 | tf_op jit(solution)/shard_map/ppermute | solution.py:28
  34.0 12.6 %collective-permute-start.13 = (bf16[512,128]{1,0:T(8,128)(2,1)S(1)}, bf16[512,128]{1,0:T(8,128)(2,1)S(1)}, u32[]{:S(2)}, u32[]{:S(2)}) collective-permute-start(bf16[512,128]{1,0:T(8,128)(2,1)S(1)} %get-tuple-element.37), channel_id=1, source_target_pairs={{0,6},{4,2},{6,0},{2,4},{1,7},{5,3},{7,1},{3,5},{8,14},{12,10},{14... | collective-permute-start | bytes 393224 | tf_op jit(solution)/shard_map/ppermute | solution.py:28
  46.6 9.2 %collective-permute-start.20 = (bf16[1,128,1024]{2,1,0:T(8,128)(2,1)S(1)}, bf16[1,128,1024]{2,1,0:T(8,128)(2,1)S(1)}, u32[]{:S(2)}, u32[]{:S(2)}) collective-permute-start(bf16[1,128,1024]{2,1,0:T(8,128)(2,1)S(1)} %get-tuple-element.40.refs_0_), channel_id=1, source_target_pairs={{0,4},{4,6},{6,2},{2,0},{1,5},{5,7},{7,3},{3,1},{8,12},{12,14},{14... | collective-permute-start | bytes 786440 | tf_op jit(solution)/shard_map/ppermute | solution.py:28
  46.7 19.9 %collective-permute-start.16 = (bf16[512,512]{1,0:T(8,128)(2,1)S(1)}, bf16[512,512]{1,0:T(8,128)(2,1)S(1)}, u32[]{:S(2)}, u32[]{:S(2)}) collective-permute-start(bf16[512,512]{1,0:T(8,128)(2,1)S(1)} %join.1.refs_6_.refs_2_), channel_id=1, source_target_pairs={{0,16},{8,24},{16,0},{24,8},{1,17},{9,25},{17,1},{25,9},{2,18},{10... | collective-permute-start | bytes 1572872 | tf_op jit(solution)/shard_map/ppermute | solution.py:44
  48.3 13.1 %collective-permute-start.6 = (bf16[1,128,1024]{2,1,0:T(8,128)(2,1)S(1)}, bf16[1,128,1024]{2,1,0:T(8,128)(2,1)S(1)}, u32[]{:S(2)}, u32[]{:S(2)}) collective-permute-start(bf16[1,128,1024]{2,1,0:T(8,128)(2,1)S(1)} %get-tuple-element.31.refs_0_), channel_id=1, source_target_pairs={{0,4},{4,6},{6,2},{2,0},{1,5},{5,7},{7,3},{3,1},{8,12},{12,14},{14... | collective-permute-start | bytes 786440 | tf_op jit(solution)/shard_map/ppermute | solution.py:28
  55.8 9.4 %collective-permute-start.22 = (bf16[1,128,1024]{2,1,0:T(8,128)(2,1)S(1)}, bf16[1,128,1024]{2,1,0:T(8,128)(2,1)S(1)}, u32[]{:S(2)}, u32[]{:S(2)}) collective-permute-start(bf16[1,128,1024]{2,1,0:T(8,128)(2,1)S(1)} %collective-permute-done.20.refs_1_), channel_id=1, source_target_pairs={{0,16},{8,24},{16,0},{24,8},{1,17},{9,25},{17,1},{25,9},{2,18},{10... | collective-permute-start | bytes 786440 | tf_op jit(solution)/shard_map/ppermute | solution.py:44
  56.1 11.1 %collective-permute-start.21 = (bf16[1,128,1024]{2,1,0:T(8,128)(2,1)S(1)}, bf16[1,128,1024]{2,1,0:T(8,128)(2,1)S(1)}, u32[]{:S(2)}, u32[]{:S(2)}) collective-permute-start(bf16[1,128,1024]{2,1,0:T(8,128)(2,1)S(1)} %collective-permute-done.20.refs_1_), channel_id=1, source_target_pairs={{0,4},{4,6},{6,2},{2,0},{1,5},{5,7},{7,3},{3,1},{8,12},{12,14},{14... | collective-permute-start | bytes 786440 | tf_op jit(solution)/shard_map/ppermute | solution.py:28
  61.4 8.6 %collective-permute-start.9 = (bf16[1,128,1024]{2,1,0:T(8,128)(2,1)S(1)}, bf16[1,128,1024]{2,1,0:T(8,128)(2,1)S(1)}, u32[]{:S(2)}, u32[]{:S(2)}) collective-permute-start(bf16[1,128,1024]{2,1,0:T(8,128)(2,1)S(1)} %collective-permute-done.6.refs_1_), channel_id=1, source_target_pairs={{0,16},{8,24},{16,0},{24,8},{1,17},{9,25},{17,1},{25,9},{2,18},{10... | collective-permute-start | bytes 786440 | tf_op jit(solution)/shard_map/ppermute | solution.py:44
  61.5 8.5 %collective-permute-start.8 = (bf16[1,128,1024]{2,1,0:T(8,128)(2,1)S(1)}, bf16[1,128,1024]{2,1,0:T(8,128)(2,1)S(1)}, u32[]{:S(2)}, u32[]{:S(2)}) collective-permute-start(bf16[1,128,1024]{2,1,0:T(8,128)(2,1)S(1)} %collective-permute-done.6.refs_1_), channel_id=1, source_target_pairs={{0,4},{4,6},{6,2},{2,0},{1,5},{5,7},{7,3},{3,1},{8,12},{12,14},{14... | collective-permute-start | bytes 786440 | tf_op jit(solution)/shard_map/ppermute | solution.py:28
  65.1 19.1 %collective-permute-start.17 = (bf16[512,512]{1,0:T(8,128)(2,1)S(1)}, bf16[512,512]{1,0:T(8,128)(2,1)S(1)}, u32[]{:S(2)}, u32[]{:S(2)}) collective-permute-start(bf16[512,512]{1,0:T(8,128)(2,1)S(1)} %join.1.refs_6_.refs_2_), channel_id=1, source_target_pairs={{0,1},{1,0},{2,3},{3,2},{4,5},{5,4},{6,7},{7,6},{8,9},{9,8},{10,11... | collective-permute-start | bytes 1572872 | tf_op jit(solution)/shard_map/ppermute | solution.py:44
  66.6 18.1 %collective-permute-start.18 = (bf16[512,512]{1,0:T(8,128)(2,1)S(1)}, bf16[512,512]{1,0:T(8,128)(2,1)S(1)}, u32[]{:S(2)}, u32[]{:S(2)}) collective-permute-start(bf16[512,512]{1,0:T(8,128)(2,1)S(1)} %collective-permute-done.16.refs_7_.refs_3_), channel_id=1, source_target_pairs={{0,1},{1,0},{2,3},{3,2},{4,5},{5,4},{6,7},{7,6},{8,9},{9,8},{10,11... | collective-permute-start | bytes 1572872 | tf_op jit(solution)/shard_map/ppermute | solution.py:44
  67.2 8.8 %collective-permute-start.24 = (bf16[1,128,1024]{2,1,0:T(8,128)(2,1)S(1)}, bf16[1,128,1024]{2,1,0:T(8,128)(2,1)S(1)}, u32[]{:S(2)}, u32[]{:S(2)}) collective-permute-start(bf16[1,128,1024]{2,1,0:T(8,128)(2,1)S(1)} %collective-permute-done.21.refs_2_), channel_id=1, source_target_pairs={{0,16},{8,24},{16,0},{24,8},{1,17},{9,25},{17,1},{25,9},{2,18},{10... | collective-permute-start | bytes 786440 | tf_op jit(solution)/shard_map/ppermute | solution.py:44
  70.0 12.7 %collective-permute-start.10 = (bf16[1,128,1024]{2,1,0:T(8,128)(2,1)S(1)}, bf16[1,128,1024]{2,1,0:T(8,128)(2,1)S(1)}, u32[]{:S(2)}, u32[]{:S(2)}) collective-permute-start(bf16[1,128,1024]{2,1,0:T(8,128)(2,1)S(1)} %collective-permute-done.8.refs_2_), channel_id=1, source_target_pairs={{0,4},{4,6},{6,2},{2,0},{1,5},{5,7},{7,3},{3,1},{8,12},{12,14},{14... | collective-permute-start | bytes 786440 | tf_op jit(solution)/shard_map/ppermute | solution.py:28
  75.9 10.6 %collective-permute-start.23 = (bf16[1,128,1024]{2,1,0:T(8,128)(2,1)S(1)}, bf16[1,128,1024]{2,1,0:T(8,128)(2,1)S(1)}, u32[]{:S(2)}, u32[]{:S(2)}) collective-permute-start(bf16[1,128,1024]{2,1,0:T(8,128)(2,1)S(1)} %collective-permute-done.21.refs_2_), channel_id=1, source_target_pairs={{0,4},{4,6},{6,2},{2,0},{1,5},{5,7},{7,3},{3,1},{8,12},{12,14},{14... | collective-permute-start | bytes 786440 | tf_op jit(solution)/shard_map/ppermute | solution.py:28
  76.0 12.9 %collective-permute-start.25 = (bf16[1,128,1024]{2,1,0:T(8,128)(2,1)S(1)}, bf16[1,128,1024]{2,1,0:T(8,128)(2,1)S(1)}, u32[]{:S(2)}, u32[]{:S(2)}) collective-permute-start(bf16[1,128,1024]{2,1,0:T(8,128)(2,1)S(1)} %collective-permute-done.24.refs_5_), channel_id=1, source_target_pairs={{0,4},{4,6},{6,2},{2,0},{1,5},{5,7},{7,3},{3,1},{8,12},{12,14},{14... | collective-permute-start | bytes 786440 | tf_op jit(solution)/shard_map/ppermute | solution.py:28
  82.7 8.7 %collective-permute-start.19 = (bf16[1,128,1024]{2,1,0:T(8,128)(2,1)S(1)}, bf16[1,128,1024]{2,1,0:T(8,128)(2,1)S(1)}, u32[]{:S(2)}, u32[]{:S(2)}) collective-permute-start(bf16[1,128,1024]{2,1,0:T(8,128)(2,1)S(1)} %collective-permute-done.8.refs_2_), channel_id=1, source_target_pairs={{0,16},{8,24},{16,0},{24,8},{1,17},{9,25},{17,1},{25,9},{2,18},{10... | collective-permute-start | bytes 786440 | tf_op jit(solution)/shard_map/ppermute | solution.py:44
  84.2 9.0 %collective-permute-start.11 = (bf16[1,128,1024]{2,1,0:T(8,128)(2,1)S(1)}, bf16[1,128,1024]{2,1,0:T(8,128)(2,1)S(1)}, u32[]{:S(2)}, u32[]{:S(2)}) collective-permute-start(bf16[1,128,1024]{2,1,0:T(8,128)(2,1)S(1)} %collective-permute-done.10.refs_0_), channel_id=1, source_target_pairs={{0,16},{8,24},{16,0},{24,8},{1,17},{9,25},{17,1},{25,9},{2,18},{10... | collective-permute-start | bytes 786440 | tf_op jit(solution)/shard_map/ppermute | solution.py:44

commit v5 on v4

--- a/solution.py
+++ b/solution.py
@@ -228,6 +228,17 @@
     )(place, cotangent)
     key_ring = gather(packed, 1, lambda x: after(x, query_held))
     value_ring = gather(values, -1, lambda x: after(x, turned[0]))
+    turned = [turned[0]] + [around(turned[s], s) for s in range(1, n)]
+    mine = pl.pallas_call(
+        join_kernel,
+        out_shape=jax.ShapeDtypeStruct((half, n * tokens), jnp.bfloat16),
+        in_specs=[VMEM] * n,
+        out_specs=VMEM,
+        compiler_params=params(16),
+        name="join",
+    )(*turned)
+    mine_far = swap(mine, "pipe", far)
+    query_held = after(query_held, mine)
     attention, *pieces = pl.pallas_call(
         functools.partial(attention_kernel, HQ // HK, 1.0 / math.sqrt(HD), n, spans),
         out_shape=[jax.ShapeDtypeStruct(queries.shape, jnp.bfloat16)]
@@ -249,16 +260,6 @@
                 held.append(after(arrived, sent[s]) if s < n - 2 else arrived)
         near.append(held)
         mirrored.append(sent)
-    turned = [turned[0]] + [around(after(turned[s], value_ring[n // 2]), s) for s in range(1, n)]
-    mine = pl.pallas_call(
-        join_kernel,
-        out_shape=jax.ShapeDtypeStruct((half, n * tokens), jnp.bfloat16),
-        in_specs=[VMEM] * n,
-        out_specs=VMEM,
-        compiler_params=params(16),
-        name="join",
-    )(*turned[:-1], after(turned[-1], *[sent[0] for sent in mirrored]))
-    mine_far = swap(mine, "pipe", far)
     cots = [mine, mine_far, swap(mine, "tp", 1), swap(mine_far, "tp", 1)]
 
     def attended(c, slots):

time: 96.2 us -> 94.6 us (0.983)
  starting transfers between devices: 42.8 us -> 37.4 us
  waiting for transfers between devices: 35.4 us -> 39.5 us
    ppermute x10, waiting for transfers between devices: 2.7 us -> 22.1 us  [swap(): lax.ppermute(x, axis, [(i, i ^ mask) for i in range(lax.axis_size(axis))])]
    ppermute x16, waiting for transfers between devices: 32.7 us -> 17.4 us  [around(): lax.ppermute(x, 'ctx', [(order[q], order[(q + shift) % n]) for q in range...]
    ppermute x16, starting transfers between devices: 32.8 us -> 24.4 us  [around(): lax.ppermute(x, 'ctx', [(order[q], order[(q + shift) % n]) for q in range...]
    ppermute x10, starting transfers between devices: 10.1 us -> 13 us  [swap(): lax.ppermute(x, axis, [(i, i ^ mask) for i in range(lax.axis_size(axis))])]
  transfers between devices with their start and end apart: 26 -> 26, of which waited for: 10 -> 11; matrix products, arithmetic and copies ran while one was open for 0% -> 0% of each run, Pallas kernels for 7% -> 9%
where the time goes in v5:
time: 94.6 us; the launch traced here: 94.4 us
  waiting for transfers between devices  39.5 us (42%)
  starting transfers between devices  37.4 us (40%)
  Pallas kernels  12 us (13%)
  local copies, waits for them, and re-layouts  4.72 us (5%)
    ppermute x16, starting transfers between devices, around(): lax.ppermute(x, 'ctx', [(order[q], order[(q + shift) % n]) for q in range...  24.4 us
    ppermute x10, waiting for transfers between devices, swap(): lax.ppermute(x, axis, [(i, i ^ mask) for i in range(lax.axis_size(axis))])  22.1 us
    ppermute x16, waiting for transfers between devices, around(): lax.ppermute(x, 'ctx', [(order[q], order[(q + shift) % n]) for q in range...  17.4 us
    ppermute x10, starting transfers between devices, swap(): lax.ppermute(x, axis, [(i, i ^ mask) for i in range(lax.axis_size(axis))])  13 us
    pallas_call x2, Pallas kernels, local(): pl.pallas_call(functools.partial(finish_kernel, slots, c * chunk, chunk),...  5.01 us
    unnamed x10, local copies, waits for them, and re-layouts  4.72 us
    pallas_call x2, Pallas kernels, local(): pl.pallas_call(functools.partial(early_kernel, first_slots), out_shape=ja...  3.59 us
    pallas_call x1, Pallas kernels, local(): pl.pallas_call(functools.partial(attention_kernel, HQ // HK, 1.0 / math.s...  2.51 us
  transfers between devices with their start and end apart: 26, of which 11 were waited for; matrix products, arithmetic and copies ran while one was open for 0% of the time, Pallas kernels for 9%

profile of v5, /device:TPU:0, one launch (start us, length us, event | category | flops | bytes accessed | tf_op | source)
XLA Modules:
  0.0 94.4 jit_solution(4131672496456309957)
XLA Ops:
  0.6 0.9 copy-done.2
  1.5 0.7 copy-done.4
  2.2 0.6 pack.1
  2.8 4.1 %collective-permute-start.3 = (bf16[1,144,512]{2,1,0:T(8,128)(2,1)S(1)}, bf16[1,144,512]{2,1,0:T(8,128)(2,1)S(1)}, u32[]{:S(2)}, u32[]{:S(2)}) collective-permute-start(bf16[1,144,512]{2,1,0:T(8,128)(2,1)S(1)} %get-tuple-element.27.refs_0_), channel_id=1, source_target_pairs={{0,4},{4,6},{6,2},{2,0},{1,5},{5,7},{7,3},{3,1},{8,12},{12,14},{14... | collective-permute-start | bytes 442376 | tf_op jit(solution)/shard_map/ppermute | solution.py:28
  6.9 1.2 %copy-done = bf16[1,128,4096]{2,1,0:T(8,128)(2,1)S(1)} copy-done((bf16[1,128,4096]{2,1,0:T(8,128)(2,1)S(1)}, bf16[1,128,4096]{2,1,0:T(8,128)(2,1)}, u32[]{:S(2)}) %copy-start) | copy-done | bytes 1048600
  8.1 0.2 turn.1
  8.3 3.0 %collective-permute-start = (bf16[512,128]{1,0:T(8,128)(2,1)S(1)}, bf16[512,128]{1,0:T(8,128)(2,1)S(1)}, u32[]{:S(2)}, u32[]{:S(2)}) collective-permute-start(bf16[512,128]{1,0:T(8,128)(2,1)S(1)} %get-tuple-element.23), channel_id=1, source_target_pairs={{0,4},{4,6},{6,2},{2,0},{1,5},{5,7},{7,3},{3,1},{8,12},{12,14},{14... | collective-permute-start | bytes 393224 | tf_op jit(solution)/shard_map/ppermute | solution.py:28
  11.2 1.3 %collective-permute-start.1 = (bf16[512,128]{1,0:T(8,128)(2,1)S(1)}, bf16[512,128]{1,0:T(8,128)(2,1)S(1)}, u32[]{:S(2)}, u32[]{:S(2)}) collective-permute-start(bf16[512,128]{1,0:T(8,128)(2,1)S(1)} %get-tuple-element.24), channel_id=1, source_target_pairs={{0,6},{4,2},{6,0},{2,4},{1,7},{5,3},{7,1},{3,5},{8,14},{12,10},{14... | collective-permute-start | bytes 393224 | tf_op jit(solution)/shard_map/ppermute | solution.py:28
  12.6 0.0 collective-permute-start.5
  12.6 1.0 %copy-done.1 = bf16[1,128,2048]{2,1,0:T(8,128)(2,1)S(1)} copy-done((bf16[1,128,2048]{2,1,0:T(8,128)(2,1)S(1)}, bf16[1,128,2048]{2,1,0:T(8,128)(2,1)}, u32[]{:S(2)}) %copy-start.1) | copy-done | bytes 524312
  13.6 0.9 copy-done.3
  14.6 0.0 collective-permute-done.3.refs_1_
  14.6 3.0 %collective-permute-start.4 = (bf16[1,144,512]{2,1,0:T(8,128)(2,1)S(1)}, bf16[1,144,512]{2,1,0:T(8,128)(2,1)S(1)}, u32[]{:S(2)}, u32[]{:S(2)}) collective-permute-start(bf16[1,144,512]{2,1,0:T(8,128)(2,1)S(1)} %collective-permute-done.3.refs_1_), channel_id=1, source_target_pairs={{0,4},{4,6},{6,2},{2,0},{1,5},{5,7},{7,3},{3,1},{8,12},{12,14},{14... | collective-permute-start | bytes 442376 | tf_op jit(solution)/shard_map/ppermute | solution.py:28
  17.6 2.4 %collective-permute-done.7.refs_7_ = bf16[1,128,512]{2,1,0:T(8,128)(2,1)S(1)} collective-permute-done((bf16[1,128,512]{2,1,0:T(8,128)(2,1)}, bf16[1,128,512]{2,1,0:T(8,128)(2,1)S(1)}, u32[]{:S(2)}, u32[]{:S(2)}) %collective-permute-start.7) | collective-permute-done | bytes 131104 | tf_op jit(solution)/shard_map/ppermute | solution.py:28
  20.0 0.0 collective-permute-start.2
  20.0 0.0 collective-permute-done.refs_1_
  20.0 2.9 %collective-permute-start.6 = (bf16[1,128,512]{2,1,0:T(8,128)(2,1)S(1)}, bf16[1,128,512]{2,1,0:T(8,128)(2,1)S(1)}, u32[]{:S(2)}, u32[]{:S(2)}) collective-permute-start(bf16[1,128,512]{2,1,0:T(8,128)(2,1)S(1)} %copy-done.3), channel_id=1, source_target_pairs={{0,4},{4,6},{6,2},{2,0},{1,5},{5,7},{7,3},{3,1},{8,12},{12,14},{14... | collective-permute-start | bytes 393224 | tf_op jit(solution)/shard_map/ppermute | solution.py:28
  22.9 3.2 %collective-permute-start.8 = (bf16[1,128,512]{2,1,0:T(8,128)(2,1)S(1)}, bf16[1,128,512]{2,1,0:T(8,128)(2,1)S(1)}, u32[]{:S(2)}, u32[]{:S(2)}) collective-permute-start(bf16[1,128,512]{2,1,0:T(8,128)(2,1)S(1)} %collective-permute-done.7.refs_7_), channel_id=1, source_target_pairs={{0,2},{4,0},{6,4},{2,6},{1,3},{5,1},{7,5},{3,7},{8,10},{12,8},{14,... | collective-permute-start | bytes 393224 | tf_op jit(solution)/shard_map/ppermute | solution.py:28
  26.2 9.3 %collective-permute-done.2.refs_3_ = bf16[512,128]{1,0:T(8,128)(2,1)S(1)} collective-permute-done((bf16[512,128]{1,0:T(8,128)(2,1)S(1)}, bf16[512,128]{1,0:T(8,128)(2,1)S(1)}, u32[]{:S(2)}, u32[]{:S(2)}) %collective-permute-start.2) | collective-permute-done | bytes 131104 | tf_op jit(solution)/shard_map/ppermute | solution.py:28
  35.4 0.1 join.1.refs_6_.refs_2_
  35.5 1.6 %collective-permute-start.15 = (bf16[512,512]{1,0:T(8,128)(2,1)S(1)}, bf16[512,512]{1,0:T(8,128)(2,1)S(1)}, u32[]{:S(2)}, u32[]{:S(2)}) collective-permute-start(bf16[512,512]{1,0:T(8,128)(2,1)S(1)} %join.1.refs_6_.refs_2_), channel_id=1, source_target_pairs={{0,16},{8,24},{16,0},{24,8},{1,17},{9,25},{17,1},{25,9},{2,18},{10... | collective-permute-start | bytes 1572872 | tf_op jit(solution)/shard_map/ppermute | solution.py:44
  37.1 0.0 collective-permute-done.5.refs_3_
  37.1 0.6 collective-permute-done.8.refs_6_
  37.7 2.5 %attend.1 = (bf16[1,128,2048]{2,1,0:T(8,128)(2,1)}, bf16[1,128,1024]{2,1,0:T(8,128)(2,1)S(1)}, bf16[1,128,1024]{2,1,0:T(8,128)(2,1)S(1)}) custom-call(f32[128,128]{1,0:T(8,128)S(1)} %get-tuple-element.20.place_ref.ready_ref, bf16[1,128,2048]{2,1,0:T(8,128)(2,1)S(1)} %get-tuple-element.26.query_ref, bf16[1,144,512]{2,1,0:T(8,128)(2,1)S(1)} %get-tuple-element.27.refs_0_, ...), custom_call_target="tpu_custom_call" | custom-call | tf_op jit(solution)/shard_map/attend/pallas_call | solution.py:242
  40.3 1.5 %collective-permute-start.20 = (bf16[1,128,1024]{2,1,0:T(8,128)(2,1)S(1)}, bf16[1,128,1024]{2,1,0:T(8,128)(2,1)S(1)}, u32[]{:S(2)}, u32[]{:S(2)}) collective-permute-start(bf16[1,128,1024]{2,1,0:T(8,128)(2,1)S(1)} %get-tuple-element.35.refs_0_), channel_id=1, source_target_pairs={{0,16},{8,24},{16,0},{24,8},{1,17},{9,25},{17,1},{25,9},{2,18},{10... | collective-permute-start | bytes 786440 | tf_op jit(solution)/shard_map/ppermute | solution.py:44
  41.8 0.5 collective-permute-start.10
  42.3 3.0 %collective-permute-start.9 = (bf16[1,128,1024]{2,1,0:T(8,128)(2,1)S(1)}, bf16[1,128,1024]{2,1,0:T(8,128)(2,1)S(1)}, u32[]{:S(2)}, u32[]{:S(2)}) collective-permute-start(bf16[1,128,1024]{2,1,0:T(8,128)(2,1)S(1)} %get-tuple-element.32.refs_0_), channel_id=1, source_target_pairs={{0,4},{4,6},{6,2},{2,0},{1,5},{5,7},{7,3},{3,1},{8,12},{12,14},{14... | collective-permute-start | bytes 786440 | tf_op jit(solution)/shard_map/ppermute | solution.py:28
  45.3 10.8 %collective-permute-done.20.refs_3_ = bf16[1,128,1024]{2,1,0:T(8,128)(2,1)S(1)} collective-permute-done((bf16[1,128,1024]{2,1,0:T(8,128)(2,1)S(1)}, bf16[1,128,1024]{2,1,0:T(8,128)(2,1)S(1)}, u32[]{:S(2)}, u32[]{:S(2)}) %collective-permute-start.20) | collective-permute-done | bytes 262176 | tf_op jit(solution)/shard_map/ppermute | solution.py:44
  56.1 1.5 %collective-permute-start.16 = (bf16[512,512]{1,0:T(8,128)(2,1)S(1)}, bf16[512,512]{1,0:T(8,128)(2,1)S(1)}, u32[]{:S(2)}, u32[]{:S(2)}) collective-permute-start(bf16[512,512]{1,0:T(8,128)(2,1)S(1)} %join.1.refs_6_.refs_2_), channel_id=1, source_target_pairs={{0,1},{1,0},{2,3},{3,2},{4,5},{5,4},{6,7},{7,6},{8,9},{9,8},{10,11... | collective-permute-start | bytes 1572872 | tf_op jit(solution)/shard_map/ppermute | solution.py:44
  57.6 2.2 %collective-permute-done.10.refs_3_ = bf16[1,128,1024]{2,1,0:T(8,128)(2,1)S(1)} collective-permute-done((bf16[1,128,1024]{2,1,0:T(8,128)(2,1)S(1)}, bf16[1,128,1024]{2,1,0:T(8,128)(2,1)S(1)}, u32[]{:S(2)}, u32[]{:S(2)}) %collective-permute-start.10) | collective-permute-done | bytes 262176 | tf_op jit(solution)/shard_map/ppermute | solution.py:44
  59.8 1.5 %collective-permute-start.22 = (bf16[1,128,1024]{2,1,0:T(8,128)(2,1)S(1)}, bf16[1,128,1024]{2,1,0:T(8,128)(2,1)S(1)}, u32[]{:S(2)}, u32[]{:S(2)}) collective-permute-start(bf16[1,128,1024]{2,1,0:T(8,128)(2,1)S(1)} %collective-permute-done.19.refs_1_), channel_id=1, source_target_pairs={{0,16},{8,24},{16,0},{24,8},{1,17},{9,25},{17,1},{25,9},{2,18},{10... | collective-permute-start | bytes 786440 | tf_op jit(solution)/shard_map/ppermute | solution.py:44
  61.3 0.4 collective-permute-start.11
  61.7 0.5 collective-permute-start.12
  62.2 0.9 collective-permute-done.21.refs_2_
  63.1 1.5 %collective-permute-start.17 = (bf16[512,512]{1,0:T(8,128)(2,1)S(1)}, bf16[512,512]{1,0:T(8,128)(2,1)S(1)}, u32[]{:S(2)}, u32[]{:S(2)}) collective-permute-start(bf16[512,512]{1,0:T(8,128)(2,1)S(1)} %collective-permute-done.15.refs_7_.refs_3_), channel_id=1, source_target_pairs={{0,1},{1,0},{2,3},{3,2},{4,5},{5,4},{6,7},{7,6},{8,9},{9,8},{10,11... | collective-permute-start | bytes 1572872 | tf_op jit(solution)/shard_map/ppermute | solution.py:44
  64.5 4.5 %collective-permute-done.22.refs_4_ = bf16[1,128,1024]{2,1,0:T(8,128)(2,1)S(1)} collective-permute-done((bf16[1,128,1024]{2,1,0:T(8,128)(2,1)S(1)}, bf16[1,128,1024]{2,1,0:T(8,128)(2,1)S(1)}, u32[]{:S(2)}, u32[]{:S(2)}) %collective-permute-start.22) | collective-permute-done | bytes 262176 | tf_op jit(solution)/shard_map/ppermute | solution.py:44
  69.0 1.5 %collective-permute-start.24 = (bf16[1,128,1024]{2,1,0:T(8,128)(2,1)S(1)}, bf16[1,128,1024]{2,1,0:T(8,128)(2,1)S(1)}, u32[]{:S(2)}, u32[]{:S(2)}) collective-permute-start(bf16[1,128,1024]{2,1,0:T(8,128)(2,1)S(1)} %collective-permute-done.21.refs_2_), channel_id=1, source_target_pairs={{0,16},{8,24},{16,0},{24,8},{1,17},{9,25},{17,1},{25,9},{2,18},{10... | collective-permute-start | bytes 786440 | tf_op jit(solution)/shard_map/ppermute | solution.py:44
  70.5 4.1 %collective-permute-done.12.refs_4_ = bf16[1,128,1024]{2,1,0:T(8,128)(2,1)S(1)} collective-permute-done((bf16[1,128,1024]{2,1,0:T(8,128)(2,1)S(1)}, bf16[1,128,1024]{2,1,0:T(8,128)(2,1)S(1)}, u32[]{:S(2)}, u32[]{:S(2)}) %collective-permute-start.12) | collective-permute-done | bytes 262176 | tf_op jit(solution)/shard_map/ppermute | solution.py:44
  74.6 1.5 %collective-permute-start.18 = (bf16[1,128,1024]{2,1,0:T(8,128)(2,1)S(1)}, bf16[1,128,1024]{2,1,0:T(8,128)(2,1)S(1)}, u32[]{:S(2)}, u32[]{:S(2)}) collective-permute-start(bf16[1,128,1024]{2,1,0:T(8,128)(2,1)S(1)} %collective-permute-done.11.refs_2_), channel_id=1, source_target_pairs={{0,16},{8,24},{16,0},{24,8},{1,17},{9,25},{17,1},{25,9},{2,18},{10... | collective-permute-start | bytes 786440 | tf_op jit(solution)/shard_map/ppermute | solution.py:44
  76.1 3.4 %collective-permute-start.23 = (bf16[1,128,1024]{2,1,0:T(8,128)(2,1)S(1)}, bf16[1,128,1024]{2,1,0:T(8,128)(2,1)S(1)}, u32[]{:S(2)}, u32[]{:S(2)}) collective-permute-start(bf16[1,128,1024]{2,1,0:T(8,128)(2,1)S(1)} %collective-permute-done.21.refs_2_), channel_id=1, source_target_pairs={{0,4},{4,6},{6,2},{2,0},{1,5},{5,7},{7,3},{3,1},{8,12},{12,14},{14... | collective-permute-start | bytes 786440 | tf_op jit(solution)/shard_map/ppermute | solution.py:28
  79.6 0.6 collective-permute-done.24.refs_5_
  80.2 2.9 %collective-permute-done.13.refs_0_ = bf16[1,128,1024]{2,1,0:T(8,128)(2,1)S(1)} collective-permute-done((bf16[1,128,1024]{2,1,0:T(8,128)(2,1)S(1)}, bf16[1,128,1024]{2,1,0:T(8,128)(2,1)S(1)}, u32[]{:S(2)}, u32[]{:S(2)}) %collective-permute-start.13) | collective-permute-done | bytes 262176 | tf_op jit(solution)/shard_map/ppermute | solution.py:28
  83.1 1.3 %collective-permute-start.14 = (bf16[1,128,1024]{2,1,0:T(8,128)(2,1)S(1)}, bf16[1,128,1024]{2,1,0:T(8,128)(2,1)S(1)}, u32[]{:S(2)}, u32[]{:S(2)}) collective-permute-start(bf16[1,128,1024]{2,1,0:T(8,128)(2,1)S(1)} %collective-permute-done.13.refs_0_), channel_id=1, source_target_pairs={{0,16},{8,24},{16,0},{24,8},{1,17},{9,25},{17,1},{25,9},{2,18},{10... | collective-permute-start | bytes 786440 | tf_op jit(solution)/shard_map/ppermute | solution.py:44
  84.5 1.8 %early.3.refs_6_ = f32[1024,1024]{1,0:T(8,128)S(1)} custom-call(bf16[1,128,1024]{2,1,0:T(8,128)(2,1)S(1)} %get-tuple-element.35.refs_0_, bf16[1,128,1024]{2,1,0:T(8,128)(2,1)S(1)} %collective-permute-done.19.refs_1_, bf16[1,128,1024]{2,1,0:T(8,128)(2,1)S(1)} %collective-permute-done.21.refs_2_, bf16[1,128,1024]{2,1,0:T(8,128)(2,1)S(1)} %collective-permute-done.20.refs_3_, ...), custom_call_target="tpu_custom_call" | custom-call | flops 1610612736 | bytes 8388608 | tf_op jit(solution)/shard_map/early/pallas_call | solution.py:272
  86.3 1.8 %early.2.refs_6_ = f32[1024,1024]{1,0:T(8,128)S(1)} custom-call(bf16[1,128,1024]{2,1,0:T(8,128)(2,1)S(1)} %get-tuple-element.32.refs_0_, bf16[1,128,1024]{2,1,0:T(8,128)(2,1)S(1)} %collective-permute-done.9.refs_1_, bf16[1,128,1024]{2,1,0:T(8,128)(2,1)S(1)} %collective-permute-done.11.refs_2_, bf16[1,128,1024]{2,1,0:T(8,128)(2,1)S(1)} %collective-permute-done.10.refs_3_, ...), custom_call_target="tpu_custom_call" | custom-call | flops 1610612736 | bytes 8388608 | tf_op jit(solution)/shard_map/early/pallas_call | solution.py:272
  88.1 1.3 %collective-permute-done.25.refs_1_ = bf16[1,128,1024]{2,1,0:T(8,128)(2,1)S(1)} collective-permute-done((bf16[1,128,1024]{2,1,0:T(8,128)(2,1)S(1)}, bf16[1,128,1024]{2,1,0:T(8,128)(2,1)S(1)}, u32[]{:S(2)}, u32[]{:S(2)}) %collective-permute-start.25) | collective-permute-done | bytes 262176 | tf_op jit(solution)/shard_map/ppermute | solution.py:28
  89.4 2.5 %finish.2.refs_7_ = bf16[1,1024,2048]{2,1,0:T(8,128)(2,1)} custom-call(bf16[1,128,1024]{2,1,0:T(8,128)(2,1)S(1)} %collective-permute-done.23.refs_0_, bf16[1,128,1024]{2,1,0:T(8,128)(2,1)S(1)} %collective-permute-done.25.refs_1_, bf16[512,512]{1,0:T(8,128)(2,1)S(1)} %join.1.refs_6_.refs_2_, bf16[512,512]{1,0:T(8,128)(2,1)S(1)} %collective-permute-done.15.refs_7_.refs_3_, ...), custom_call_target="tpu_custom_call" | custom-call | flops 536870912 | bytes 8388608 | tf_op jit(solution)/shard_map/finish/pallas_call | solution.py:297
  91.9 2.5 %finish.3 = bf16[1,1024,2048]{2,1,0:T(8,128)(2,1)} custom-call(bf16[1,128,1024]{2,1,0:T(8,128)(2,1)S(1)} %collective-permute-done.13.refs_0_, bf16[1,128,1024]{2,1,0:T(8,128)(2,1)S(1)} %collective-permute-done.14.refs_1_, bf16[512,512]{1,0:T(8,128)(2,1)S(1)} %join.1.refs_6_.refs_2_, ...), custom_call_target="tpu_custom_call", output_to_operand_aliasing={{}: (7, {})} | custom-call | flops 536870912 | bytes 8388608 | tf_op jit(solution)/shard_map/finish/pallas_call | solution.py:297
  (23 shorter events, 0.1 us)
Async XLA Ops:
  0.6 0.9 copy-start.2
  1.5 0.7 copy-start.4
  2.8 11.8 %collective-permute-start.3 = (bf16[1,144,512]{2,1,0:T(8,128)(2,1)S(1)}, bf16[1,144,512]{2,1,0:T(8,128)(2,1)S(1)}, u32[]{:S(2)}, u32[]{:S(2)}) collective-permute-start(bf16[1,144,512]{2,1,0:T(8,128)(2,1)S(1)} %get-tuple-element.27.refs_0_), channel_id=1, source_target_pairs={{0,4},{4,6},{6,2},{2,0},{1,5},{5,7},{7,3},{3,1},{8,12},{12,14},{14... | collective-permute-start | bytes 442376 | tf_op jit(solution)/shard_map/ppermute | solution.py:28
  6.8 13.2 %collective-permute-start.7 = (bf16[1,128,512]{2,1,0:T(8,128)(2,1)}, bf16[1,128,512]{2,1,0:T(8,128)(2,1)S(1)}, u32[]{:S(2)}, u32[]{:S(2)}) collective-permute-start(bf16[1,128,512]{2,1,0:T(8,128)(2,1)} %value_ref.1), channel_id=1, source_target_pairs={{0,2},{4,0},{6,4},{2,6},{1,3},{5,1},{7,5},{3,7},{8,10},{12,8},{14,... | collective-permute-start | bytes 393224 | tf_op jit(solution)/shard_map/ppermute | solution.py:28
  6.8 1.2 %copy-start = (bf16[1,128,4096]{2,1,0:T(8,128)(2,1)S(1)}, bf16[1,128,4096]{2,1,0:T(8,128)(2,1)}, u32[]{:S(2)}) copy-start(bf16[1,128,4096]{2,1,0:T(8,128)(2,1)} %cot_ref.1) | copy-start | bytes 3145732
  8.3 11.7 %collective-permute-start = (bf16[512,128]{1,0:T(8,128)(2,1)S(1)}, bf16[512,128]{1,0:T(8,128)(2,1)S(1)}, u32[]{:S(2)}, u32[]{:S(2)}) collective-permute-start(bf16[512,128]{1,0:T(8,128)(2,1)S(1)} %get-tuple-element.23), channel_id=1, source_target_pairs={{0,4},{4,6},{6,2},{2,0},{1,5},{5,7},{7,3},{3,1},{8,12},{12,14},{14... | collective-permute-start | bytes 393224 | tf_op jit(solution)/shard_map/ppermute | solution.py:28
  11.2 11.7 %collective-permute-start.1 = (bf16[512,128]{1,0:T(8,128)(2,1)S(1)}, bf16[512,128]{1,0:T(8,128)(2,1)S(1)}, u32[]{:S(2)}, u32[]{:S(2)}) collective-permute-start(bf16[512,128]{1,0:T(8,128)(2,1)S(1)} %get-tuple-element.24), channel_id=1, source_target_pairs={{0,6},{4,2},{6,0},{2,4},{1,7},{5,3},{7,1},{3,5},{8,14},{12,10},{14... | collective-permute-start | bytes 393224 | tf_op jit(solution)/shard_map/ppermute | solution.py:28
  12.6 24.5 %collective-permute-start.5 = (bf16[1,144,512]{2,1,0:T(8,128)(2,1)S(1)}, bf16[1,144,512]{2,1,0:T(8,128)(2,1)S(1)}, u32[]{:S(2)}, u32[]{:S(2)}) collective-permute-start(bf16[1,144,512]{2,1,0:T(8,128)(2,1)S(1)} %get-tuple-element.27.refs_0_), channel_id=1, source_target_pairs={{0,2},{4,0},{6,4},{2,6},{1,3},{5,1},{7,5},{3,7},{8,10},{12,8},{14,... | collective-permute-start | bytes 442376 | tf_op jit(solution)/shard_map/ppermute | solution.py:28
  12.6 1.0 %copy-start.1 = (bf16[1,128,2048]{2,1,0:T(8,128)(2,1)S(1)}, bf16[1,128,2048]{2,1,0:T(8,128)(2,1)}, u32[]{:S(2)}) copy-start(bf16[1,128,2048]{2,1,0:T(8,128)(2,1)} %query_ref.1) | copy-start | bytes 1572868
  13.6 0.9 copy-start.3
  14.6 23.1 %collective-permute-start.4 = (bf16[1,144,512]{2,1,0:T(8,128)(2,1)S(1)}, bf16[1,144,512]{2,1,0:T(8,128)(2,1)S(1)}, u32[]{:S(2)}, u32[]{:S(2)}) collective-permute-start(bf16[1,144,512]{2,1,0:T(8,128)(2,1)S(1)} %collective-permute-done.3.refs_1_), channel_id=1, source_target_pairs={{0,4},{4,6},{6,2},{2,0},{1,5},{5,7},{7,3},{3,1},{8,12},{12,14},{14... | collective-permute-start | bytes 442376 | tf_op jit(solution)/shard_map/ppermute | solution.py:28
  20.0 15.4 %collective-permute-start.2 = (bf16[512,128]{1,0:T(8,128)(2,1)S(1)}, bf16[512,128]{1,0:T(8,128)(2,1)S(1)}, u32[]{:S(2)}, u32[]{:S(2)}) collective-permute-start(bf16[512,128]{1,0:T(8,128)(2,1)S(1)} %get-tuple-element.25), channel_id=1, source_target_pairs={{0,2},{4,0},{6,4},{2,6},{1,3},{5,1},{7,5},{3,7},{8,10},{12,8},{14,... | collective-permute-start | bytes 393224 | tf_op jit(solution)/shard_map/ppermute | solution.py:28
  20.0 17.1 %collective-permute-start.6 = (bf16[1,128,512]{2,1,0:T(8,128)(2,1)S(1)}, bf16[1,128,512]{2,1,0:T(8,128)(2,1)S(1)}, u32[]{:S(2)}, u32[]{:S(2)}) collective-permute-start(bf16[1,128,512]{2,1,0:T(8,128)(2,1)S(1)} %copy-done.3), channel_id=1, source_target_pairs={{0,4},{4,6},{6,2},{2,0},{1,5},{5,7},{7,3},{3,1},{8,12},{12,14},{14... | collective-permute-start | bytes 393224 | tf_op jit(solution)/shard_map/ppermute | solution.py:28
  22.9 14.8 %collective-permute-start.8 = (bf16[1,128,512]{2,1,0:T(8,128)(2,1)S(1)}, bf16[1,128,512]{2,1,0:T(8,128)(2,1)S(1)}, u32[]{:S(2)}, u32[]{:S(2)}) collective-permute-start(bf16[1,128,512]{2,1,0:T(8,128)(2,1)S(1)} %collective-permute-done.7.refs_7_), channel_id=1, source_target_pairs={{0,2},{4,0},{6,4},{2,6},{1,3},{5,1},{7,5},{3,7},{8,10},{12,8},{14,... | collective-permute-start | bytes 393224 | tf_op jit(solution)/shard_map/ppermute | solution.py:28
  35.5 26.1 %collective-permute-start.15 = (bf16[512,512]{1,0:T(8,128)(2,1)S(1)}, bf16[512,512]{1,0:T(8,128)(2,1)S(1)}, u32[]{:S(2)}, u32[]{:S(2)}) collective-permute-start(bf16[512,512]{1,0:T(8,128)(2,1)S(1)} %join.1.refs_6_.refs_2_), channel_id=1, source_target_pairs={{0,16},{8,24},{16,0},{24,8},{1,17},{9,25},{17,1},{25,9},{2,18},{10... | collective-permute-start | bytes 1572872 | tf_op jit(solution)/shard_map/ppermute | solution.py:44
  40.3 15.8 %collective-permute-start.20 = (bf16[1,128,1024]{2,1,0:T(8,128)(2,1)S(1)}, bf16[1,128,1024]{2,1,0:T(8,128)(2,1)S(1)}, u32[]{:S(2)}, u32[]{:S(2)}) collective-permute-start(bf16[1,128,1024]{2,1,0:T(8,128)(2,1)S(1)} %get-tuple-element.35.refs_0_), channel_id=1, source_target_pairs={{0,16},{8,24},{16,0},{24,8},{1,17},{9,25},{17,1},{25,9},{2,18},{10... | collective-permute-start | bytes 786440 | tf_op jit(solution)/shard_map/ppermute | solution.py:44
  41.8 14.3 %collective-permute-start.19 = (bf16[1,128,1024]{2,1,0:T(8,128)(2,1)S(1)}, bf16[1,128,1024]{2,1,0:T(8,128)(2,1)S(1)}, u32[]{:S(2)}, u32[]{:S(2)}) collective-permute-start(bf16[1,128,1024]{2,1,0:T(8,128)(2,1)S(1)} %get-tuple-element.35.refs_0_), channel_id=1, source_target_pairs={{0,4},{4,6},{6,2},{2,0},{1,5},{5,7},{7,3},{3,1},{8,12},{12,14},{14... | collective-permute-start | bytes 786440 | tf_op jit(solution)/shard_map/ppermute | solution.py:28
  41.8 18.0 %collective-permute-start.10 = (bf16[1,128,1024]{2,1,0:T(8,128)(2,1)S(1)}, bf16[1,128,1024]{2,1,0:T(8,128)(2,1)S(1)}, u32[]{:S(2)}, u32[]{:S(2)}) collective-permute-start(bf16[1,128,1024]{2,1,0:T(8,128)(2,1)S(1)} %get-tuple-element.32.refs_0_), channel_id=1, source_target_pairs={{0,16},{8,24},{16,0},{24,8},{1,17},{9,25},{17,1},{25,9},{2,18},{10... | collective-permute-start | bytes 786440 | tf_op jit(solution)/shard_map/ppermute | solution.py:44
  42.3 19.0 %collective-permute-start.9 = (bf16[1,128,1024]{2,1,0:T(8,128)(2,1)S(1)}, bf16[1,128,1024]{2,1,0:T(8,128)(2,1)S(1)}, u32[]{:S(2)}, u32[]{:S(2)}) collective-permute-start(bf16[1,128,1024]{2,1,0:T(8,128)(2,1)S(1)} %get-tuple-element.32.refs_0_), channel_id=1, source_target_pairs={{0,4},{4,6},{6,2},{2,0},{1,5},{5,7},{7,3},{3,1},{8,12},{12,14},{14... | collective-permute-start | bytes 786440 | tf_op jit(solution)/shard_map/ppermute | solution.py:28
  56.1 7.0 %collective-permute-start.21 = (bf16[1,128,1024]{2,1,0:T(8,128)(2,1)S(1)}, bf16[1,128,1024]{2,1,0:T(8,128)(2,1)S(1)}, u32[]{:S(2)}, u32[]{:S(2)}) collective-permute-start(bf16[1,128,1024]{2,1,0:T(8,128)(2,1)S(1)} %collective-permute-done.19.refs_1_), channel_id=1, source_target_pairs={{0,4},{4,6},{6,2},{2,0},{1,5},{5,7},{7,3},{3,1},{8,12},{12,14},{14... | collective-permute-start | bytes 786440 | tf_op jit(solution)/shard_map/ppermute | solution.py:28
  56.1 20.1 %collective-permute-start.16 = (bf16[512,512]{1,0:T(8,128)(2,1)S(1)}, bf16[512,512]{1,0:T(8,128)(2,1)S(1)}, u32[]{:S(2)}, u32[]{:S(2)}) collective-permute-start(bf16[512,512]{1,0:T(8,128)(2,1)S(1)} %join.1.refs_6_.refs_2_), channel_id=1, source_target_pairs={{0,1},{1,0},{2,3},{3,2},{4,5},{5,4},{6,7},{7,6},{8,9},{9,8},{10,11... | collective-permute-start | bytes 1572872 | tf_op jit(solution)/shard_map/ppermute | solution.py:44
  59.8 9.2 %collective-permute-start.22 = (bf16[1,128,1024]{2,1,0:T(8,128)(2,1)S(1)}, bf16[1,128,1024]{2,1,0:T(8,128)(2,1)S(1)}, u32[]{:S(2)}, u32[]{:S(2)}) collective-permute-start(bf16[1,128,1024]{2,1,0:T(8,128)(2,1)S(1)} %collective-permute-done.19.refs_1_), channel_id=1, source_target_pairs={{0,16},{8,24},{16,0},{24,8},{1,17},{9,25},{17,1},{25,9},{2,18},{10... | collective-permute-start | bytes 786440 | tf_op jit(solution)/shard_map/ppermute | solution.py:44
  61.3 9.2 %collective-permute-start.11 = (bf16[1,128,1024]{2,1,0:T(8,128)(2,1)S(1)}, bf16[1,128,1024]{2,1,0:T(8,128)(2,1)S(1)}, u32[]{:S(2)}, u32[]{:S(2)}) collective-permute-start(bf16[1,128,1024]{2,1,0:T(8,128)(2,1)S(1)} %collective-permute-done.9.refs_1_), channel_id=1, source_target_pairs={{0,4},{4,6},{6,2},{2,0},{1,5},{5,7},{7,3},{3,1},{8,12},{12,14},{14... | collective-permute-start | bytes 786440 | tf_op jit(solution)/shard_map/ppermute | solution.py:28
  61.7 13.0 %collective-permute-start.12 = (bf16[1,128,1024]{2,1,0:T(8,128)(2,1)S(1)}, bf16[1,128,1024]{2,1,0:T(8,128)(2,1)S(1)}, u32[]{:S(2)}, u32[]{:S(2)}) collective-permute-start(bf16[1,128,1024]{2,1,0:T(8,128)(2,1)S(1)} %collective-permute-done.9.refs_1_), channel_id=1, source_target_pairs={{0,16},{8,24},{16,0},{24,8},{1,17},{9,25},{17,1},{25,9},{2,18},{10... | collective-permute-start | bytes 786440 | tf_op jit(solution)/shard_map/ppermute | solution.py:44
  63.1 21.4 %collective-permute-start.17 = (bf16[512,512]{1,0:T(8,128)(2,1)S(1)}, bf16[512,512]{1,0:T(8,128)(2,1)S(1)}, u32[]{:S(2)}, u32[]{:S(2)}) collective-permute-start(bf16[512,512]{1,0:T(8,128)(2,1)S(1)} %collective-permute-done.15.refs_7_.refs_3_), channel_id=1, source_target_pairs={{0,1},{1,0},{2,3},{3,2},{4,5},{5,4},{6,7},{7,6},{8,9},{9,8},{10,11... | collective-permute-start | bytes 1572872 | tf_op jit(solution)/shard_map/ppermute | solution.py:44
  69.0 11.2 %collective-permute-start.24 = (bf16[1,128,1024]{2,1,0:T(8,128)(2,1)S(1)}, bf16[1,128,1024]{2,1,0:T(8,128)(2,1)S(1)}, u32[]{:S(2)}, u32[]{:S(2)}) collective-permute-start(bf16[1,128,1024]{2,1,0:T(8,128)(2,1)S(1)} %collective-permute-done.21.refs_2_), channel_id=1, source_target_pairs={{0,16},{8,24},{16,0},{24,8},{1,17},{9,25},{17,1},{25,9},{2,18},{10... | collective-permute-start | bytes 786440 | tf_op jit(solution)/shard_map/ppermute | solution.py:44
  74.6 8.5 %collective-permute-start.13 = (bf16[1,128,1024]{2,1,0:T(8,128)(2,1)S(1)}, bf16[1,128,1024]{2,1,0:T(8,128)(2,1)S(1)}, u32[]{:S(2)}, u32[]{:S(2)}) collective-permute-start(bf16[1,128,1024]{2,1,0:T(8,128)(2,1)S(1)} %collective-permute-done.11.refs_2_), channel_id=1, source_target_pairs={{0,4},{4,6},{6,2},{2,0},{1,5},{5,7},{7,3},{3,1},{8,12},{12,14},{14... | collective-permute-start | bytes 786440 | tf_op jit(solution)/shard_map/ppermute | solution.py:28
  74.6 11.7 %collective-permute-start.18 = (bf16[1,128,1024]{2,1,0:T(8,128)(2,1)S(1)}, bf16[1,128,1024]{2,1,0:T(8,128)(2,1)S(1)}, u32[]{:S(2)}, u32[]{:S(2)}) collective-permute-start(bf16[1,128,1024]{2,1,0:T(8,128)(2,1)S(1)} %collective-permute-done.11.refs_2_), channel_id=1, source_target_pairs={{0,16},{8,24},{16,0},{24,8},{1,17},{9,25},{17,1},{25,9},{2,18},{10... | collective-permute-start | bytes 786440 | tf_op jit(solution)/shard_map/ppermute | solution.py:44
  76.1 11.9 %collective-permute-start.23 = (bf16[1,128,1024]{2,1,0:T(8,128)(2,1)S(1)}, bf16[1,128,1024]{2,1,0:T(8,128)(2,1)S(1)}, u32[]{:S(2)}, u32[]{:S(2)}) collective-permute-start(bf16[1,128,1024]{2,1,0:T(8,128)(2,1)S(1)} %collective-permute-done.21.refs_2_), channel_id=1, source_target_pairs={{0,4},{4,6},{6,2},{2,0},{1,5},{5,7},{7,3},{3,1},{8,12},{12,14},{14... | collective-permute-start | bytes 786440 | tf_op jit(solution)/shard_map/ppermute | solution.py:28
  80.2 9.1 %collective-permute-start.25 = (bf16[1,128,1024]{2,1,0:T(8,128)(2,1)S(1)}, bf16[1,128,1024]{2,1,0:T(8,128)(2,1)S(1)}, u32[]{:S(2)}, u32[]{:S(2)}) collective-permute-start(bf16[1,128,1024]{2,1,0:T(8,128)(2,1)S(1)} %collective-permute-done.24.refs_5_), channel_id=1, source_target_pairs={{0,4},{4,6},{6,2},{2,0},{1,5},{5,7},{7,3},{3,1},{8,12},{12,14},{14... | collective-permute-start | bytes 786440 | tf_op jit(solution)/shard_map/ppermute | solution.py:28
  83.1 8.7 %collective-permute-start.14 = (bf16[1,128,1024]{2,1,0:T(8,128)(2,1)S(1)}, bf16[1,128,1024]{2,1,0:T(8,128)(2,1)S(1)}, u32[]{:S(2)}, u32[]{:S(2)}) collective-permute-start(bf16[1,128,1024]{2,1,0:T(8,128)(2,1)S(1)} %collective-permute-done.13.refs_0_), channel_id=1, source_target_pairs={{0,16},{8,24},{16,0},{24,8},{1,17},{9,25},{17,1},{25,9},{2,18},{10... | collective-permute-start | bytes 786440 | tf_op jit(solution)/shard_map/ppermute | solution.py:44

commit v6 on v5

--- a/solution.py
+++ b/solution.py
@@ -52,7 +52,7 @@
     return lax.optimization_barrier((x, *others))[0]
 
 
-def pack_kernel(span_ref, key_ref, packed_ref, place_ref):
+def pack_kernel(turned_ref, span_ref, key_ref, packed_ref, place_ref):
     tokens, width = key_ref.shape[1:]
     packed_ref[0, :tokens, :] = key_ref[0]
     spans = span_ref.shape[1]
@@ -73,7 +73,7 @@
     value_held[...] = value_ref[...]
 
 
-def turn_kernel(n, ready_ref, cot_ref, *out_refs):
+def turn_kernel(n, cot_ref, *out_refs):
     me = lax.axis_index("ctx")
     side = lax.axis_index("tp") & 1
     half = cot_ref.shape[2] // n // 2
@@ -158,32 +158,33 @@
             )
 
 
-def finish_kernel(slots, start, width, *refs):
+def finish_kernel(slots, start, *refs):
     count = 2 * len(slots)
-    att_refs, cot_refs = refs[:count], refs[count : count + 4]
+    att_refs, cot_refs, total_ref = refs[:count], refs[count : count + 4], refs[count + 4]
     out_ref, held, sems = refs[-3:]
-    total_ref = refs[count + 4]
+    tokens, width = att_refs[0].shape[1:]
+    tall = held.shape[1]
     half = cot_refs[0].shape[0]
-    tokens = att_refs[0].shape[1]
-    wide = held.shape[2]
+    rows = jnp.concatenate([ref[0] for ref in att_refs], axis=0)
     copies = []
-    for j in range(width // wide):
-        columns = slice(j * wide, (j + 1) * wide)
-        rows = jnp.concatenate([ref[0, :, columns] for ref in att_refs], axis=0)
-        if j >= 2:
-            copies[j - 2].wait()
-        for at, left in left_sides(cot_refs, tokens, slots):
-            here = pl.ds(pl.multiple_of(at * half, half), half)
-            value = jnp.dot(left, rows, preferred_element_type=jnp.float32)
-            held[j % 2, here, :] = (value + total_ref[here, columns]).astype(jnp.bfloat16)
-        copies.append(
-            pltpu.make_async_copy(
-                held.at[j % 2],
-                out_ref.at[0, :, start + j * wide : start + (j + 1) * wide],
-                sems.at[j % 2],
+    for at, left in left_sides(cot_refs, tokens, slots):
+        for i in range(half // tall):
+            here = pl.ds(pl.multiple_of(at * half + i * tall, tall), tall)
+            slot = len(copies) % 2
+            if len(copies) >= 2:
+                copies[-2].wait()
+            held[slot] = (
+                total_ref[here, :]
+                + jnp.dot(
+                    left[i * tall : (i + 1) * tall], rows, preferred_element_type=jnp.float32
+                )
+            ).astype(jnp.bfloat16)
+            copies.append(
+                pltpu.make_async_copy(
+                    held.at[slot], out_ref.at[0, here, start : start + width], sems.at[slot]
+                )
             )
-        )
-        copies[-1].start()
+            copies[-1].start()
     for copy in copies[-2:]:
         copy.wait()
 
@@ -199,17 +200,25 @@
     features = cotangent.shape[2] // n
     half = features // 2
 
+    turned = pl.pallas_call(
+        functools.partial(turn_kernel, n),
+        out_shape=[jax.ShapeDtypeStruct((half, tokens), jnp.bfloat16)] * n,
+        in_specs=[VMEM],
+        out_specs=[VMEM] * n,
+        compiler_params=params(16),
+        name="turn",
+    )(cotangent)
     packed, place = pl.pallas_call(
         pack_kernel,
         out_shape=[
             jax.ShapeDtypeStruct((1, tokens + TAG, width), jnp.bfloat16),
             jax.ShapeDtypeStruct((tokens, 128), jnp.float32),
         ],
-        in_specs=[SMEM, VMEM],
+        in_specs=[ANY, SMEM, VMEM],
         out_specs=[VMEM] * 2,
         compiler_params=params(16),
         name="pack",
-    )(span_ids, keys)
+    )(turned[0], span_ids, keys)
     query_held, value_held = pl.pallas_call(
         fetch_kernel,
         out_shape=[jax.ShapeDtypeStruct(x.shape, jnp.bfloat16) for x in (queries, values)],
@@ -218,16 +227,6 @@
         compiler_params=params(16),
         name="fetch",
     )(place, queries, values)
-    turned = pl.pallas_call(
-        functools.partial(turn_kernel, n),
-        out_shape=[jax.ShapeDtypeStruct((half, tokens), jnp.bfloat16)] * n,
-        in_specs=[ANY, VMEM],
-        out_specs=[VMEM] * n,
-        compiler_params=params(16),
-        name="turn",
-    )(place, cotangent)
-    key_ring = gather(packed, 1, lambda x: after(x, query_held))
-    value_ring = gather(values, -1, lambda x: after(x, turned[0]))
     turned = [turned[0]] + [around(turned[s], s) for s in range(1, n)]
     mine = pl.pallas_call(
         join_kernel,
@@ -238,7 +237,8 @@
         name="join",
     )(*turned)
     mine_far = swap(mine, "pipe", far)
-    query_held = after(query_held, mine)
+    key_ring = gather(packed, 1, lambda x: after(x, query_held, mine))
+    value_ring = gather(values, -1, lambda x: after(x, value_held, mine))
     attention, *pieces = pl.pallas_call(
         functools.partial(attention_kernel, HQ // HK, 1.0 / math.sqrt(HD), n, spans),
         out_shape=[jax.ShapeDtypeStruct(queries.shape, jnp.bfloat16)]
@@ -267,7 +267,7 @@
 
     first_slots = list(range(n - 1))
 
-    tile = TILE if chunk % TILE == 0 else chunk
+    tall = TILE if half % TILE == 0 else half
     totals = [
         pl.pallas_call(
         functools.partial(early_kernel, first_slots),
@@ -295,12 +295,12 @@
             operands.append(grad_out)
             specs.append(ANY)
         grad_out = pl.pallas_call(
-            functools.partial(finish_kernel, slots, c * chunk, chunk),
+            functools.partial(finish_kernel, slots, c * chunk),
             out_shape=jax.ShapeDtypeStruct((1, features, heads), jnp.bfloat16),
             in_specs=specs,
             out_specs=ANY,
             scratch_shapes=[
-                pltpu.VMEM((2, features, tile), jnp.bfloat16),
+                pltpu.VMEM((2, tall, chunk), jnp.bfloat16),
                 pltpu.SemaphoreType.DMA((2,)),
             ],
             input_output_aliases=aliases,

time: 94.6 us -> 91.6 us (0.968)
  waiting for transfers between devices: 39.5 us -> 31.1 us
  starting transfers between devices: 37.4 us -> 42.7 us
    ppermute x10, waiting for transfers between devices: 22.1 us -> 6.11 us  [swap(): lax.ppermute(x, axis, [(i, i ^ mask) for i in range(lax.axis_size(axis))])]
    ppermute x16, waiting for transfers between devices: 17.4 us -> 25 us  [around(): lax.ppermute(x, 'ctx', [(order[q], order[(q + shift) % n]) for q in range...]
    ppermute x16, starting transfers between devices: 24.4 us -> 29.6 us  [around(): lax.ppermute(x, 'ctx', [(order[q], order[(q + shift) % n]) for q in range...]
  transfers between devices with their start and end apart: 26 -> 26, of which waited for: 11 -> 13; matrix products, arithmetic and copies ran while one was open for 0% -> 0% of each run, Pallas kernels for 9% -> 10%
where the time goes in v6:
time: 91.6 us; the launch traced here: 91.4 us
  starting transfers between devices  42.7 us (47%)
  waiting for transfers between devices  31.1 us (34%)
  Pallas kernels  12.1 us (13%)
  local copies, waits for them, and re-layouts  4.72 us (5%)
    ppermute x16, starting transfers between devices, around(): lax.ppermute(x, 'ctx', [(order[q], order[(q + shift) % n]) for q in range...  29.6 us
    ppermute x16, waiting for transfers between devices, around(): lax.ppermute(x, 'ctx', [(order[q], order[(q + shift) % n]) for q in range...  25 us
    ppermute x10, starting transfers between devices, swap(): lax.ppermute(x, axis, [(i, i ^ mask) for i in range(lax.axis_size(axis))])  13.1 us
    ppermute x10, waiting for transfers between devices, swap(): lax.ppermute(x, axis, [(i, i ^ mask) for i in range(lax.axis_size(axis))])  6.11 us
    pallas_call x2, Pallas kernels, local(): pl.pallas_call(functools.partial(finish_kernel, slots, c * chunk), out_sh...  5.1 us
    unnamed x10, local copies, waits for them, and re-layouts  4.72 us
    pallas_call x2, Pallas kernels, local(): pl.pallas_call(functools.partial(early_kernel, first_slots), out_shape=ja...  3.59 us
    pallas_call x1, Pallas kernels, local(): pl.pallas_call(functools.partial(attention_kernel, HQ // HK, 1.0 / math.s...  2.51 us
  transfers between devices with their start and end apart: 26, of which 13 were waited for; matrix products, arithmetic and copies ran while one was open for 0% of the time, Pallas kernels for 10%

profile of v6, /device:TPU:0, one launch (start us, length us, event | category | flops | bytes accessed | tf_op | source)
XLA Modules:
  0.0 91.4 jit_solution(3636168980065886033)
XLA Ops:
  0.6 1.2 %copy-done = bf16[1,128,4096]{2,1,0:T(8,128)(2,1)S(1)} copy-done((bf16[1,128,4096]{2,1,0:T(8,128)(2,1)S(1)}, bf16[1,128,4096]{2,1,0:T(8,128)(2,1)}, u32[]{:S(2)}) %copy-start) | copy-done | bytes 1048600
  1.9 0.2 turn.1
  2.1 0.9 copy-done.2
  3.0 0.7 copy-done.4
  3.6 0.6 pack.1
  4.2 4.1 %collective-permute-start = (bf16[1,144,512]{2,1,0:T(8,128)(2,1)S(1)}, bf16[1,144,512]{2,1,0:T(8,128)(2,1)S(1)}, u32[]{:S(2)}, u32[]{:S(2)}) collective-permute-start(bf16[1,144,512]{2,1,0:T(8,128)(2,1)S(1)} %get-tuple-element.22.refs_0_), channel_id=1, source_target_pairs={{0,4},{4,6},{6,2},{2,0},{1,5},{5,7},{7,3},{3,1},{8,12},{12,14},{14... | collective-permute-start | bytes 442376 | tf_op jit(solution)/shard_map/ppermute | solution.py:28
  8.3 1.6 %collective-permute-start.1 = (bf16[512,128]{1,0:T(8,128)(2,1)S(1)}, bf16[512,128]{1,0:T(8,128)(2,1)S(1)}, u32[]{:S(2)}, u32[]{:S(2)}) collective-permute-start(bf16[512,128]{1,0:T(8,128)(2,1)S(1)} %get-tuple-element.23), channel_id=1, source_target_pairs={{0,4},{4,6},{6,2},{2,0},{1,5},{5,7},{7,3},{3,1},{8,12},{12,14},{14... | collective-permute-start | bytes 393224 | tf_op jit(solution)/shard_map/ppermute | solution.py:28
  9.8 0.9 collective-permute-start.3
  10.7 3.5 %collective-permute-start.7 = (bf16[1,128,512]{2,1,0:T(8,128)(2,1)}, bf16[1,128,512]{2,1,0:T(8,128)(2,1)S(1)}, u32[]{:S(2)}, u32[]{:S(2)}) collective-permute-start(bf16[1,128,512]{2,1,0:T(8,128)(2,1)} %value_ref.1), channel_id=1, source_target_pairs={{0,2},{4,0},{6,4},{2,6},{1,3},{5,1},{7,5},{3,7},{8,10},{12,8},{14,... | collective-permute-start | bytes 393224 | tf_op jit(solution)/shard_map/ppermute | solution.py:28
  14.2 1.0 %copy-done.1 = bf16[1,128,2048]{2,1,0:T(8,128)(2,1)S(1)} copy-done((bf16[1,128,2048]{2,1,0:T(8,128)(2,1)S(1)}, bf16[1,128,2048]{2,1,0:T(8,128)(2,1)}, u32[]{:S(2)}) %copy-start.1) | copy-done | bytes 524312
  15.3 0.9 copy-done.3
  16.2 1.6 %collective-permute-start.5 = (bf16[1,144,512]{2,1,0:T(8,128)(2,1)S(1)}, bf16[1,144,512]{2,1,0:T(8,128)(2,1)S(1)}, u32[]{:S(2)}, u32[]{:S(2)}) collective-permute-start(bf16[1,144,512]{2,1,0:T(8,128)(2,1)S(1)} %get-tuple-element.22.refs_0_), channel_id=1, source_target_pairs={{0,2},{4,0},{6,4},{2,6},{1,3},{5,1},{7,5},{3,7},{8,10},{12,8},{14,... | collective-permute-start | bytes 442376 | tf_op jit(solution)/shard_map/ppermute | solution.py:28
  17.8 2.2 %collective-permute-done.2.refs_2_ = bf16[512,128]{1,0:T(8,128)(2,1)S(1)} collective-permute-done((bf16[512,128]{1,0:T(8,128)(2,1)S(1)}, bf16[512,128]{1,0:T(8,128)(2,1)S(1)}, u32[]{:S(2)}, u32[]{:S(2)}) %collective-permute-start.2) | collective-permute-done | bytes 131104 | tf_op jit(solution)/shard_map/ppermute | solution.py:28
  20.0 4.5 %collective-permute-done.3.refs_3_ = bf16[512,128]{1,0:T(8,128)(2,1)S(1)} collective-permute-done((bf16[512,128]{1,0:T(8,128)(2,1)S(1)}, bf16[512,128]{1,0:T(8,128)(2,1)S(1)}, u32[]{:S(2)}, u32[]{:S(2)}) %collective-permute-start.3) | collective-permute-done | bytes 131104 | tf_op jit(solution)/shard_map/ppermute | solution.py:28
  24.5 0.1 join.1.refs_6_.refs_2_
  24.7 3.0 %collective-permute-start.6 = (bf16[1,128,512]{2,1,0:T(8,128)(2,1)S(1)}, bf16[1,128,512]{2,1,0:T(8,128)(2,1)S(1)}, u32[]{:S(2)}, u32[]{:S(2)}) collective-permute-start(bf16[1,128,512]{2,1,0:T(8,128)(2,1)S(1)} %copy-done.3), channel_id=1, source_target_pairs={{0,4},{4,6},{6,2},{2,0},{1,5},{5,7},{7,3},{3,1},{8,12},{12,14},{14... | collective-permute-start | bytes 393224 | tf_op jit(solution)/shard_map/ppermute | solution.py:28
  27.7 1.5 %collective-permute-start.15 = (bf16[512,512]{1,0:T(8,128)(2,1)S(1)}, bf16[512,512]{1,0:T(8,128)(2,1)S(1)}, u32[]{:S(2)}, u32[]{:S(2)}) collective-permute-start(bf16[512,512]{1,0:T(8,128)(2,1)S(1)} %join.1.refs_6_.refs_2_), channel_id=1, source_target_pairs={{0,16},{8,24},{16,0},{24,8},{1,17},{9,25},{17,1},{25,9},{2,18},{10... | collective-permute-start | bytes 1572872 | tf_op jit(solution)/shard_map/ppermute | solution.py:44
  29.2 5.4 %collective-permute-done.6.refs_5_ = bf16[1,128,512]{2,1,0:T(8,128)(2,1)S(1)} collective-permute-done((bf16[1,128,512]{2,1,0:T(8,128)(2,1)S(1)}, bf16[1,128,512]{2,1,0:T(8,128)(2,1)S(1)}, u32[]{:S(2)}, u32[]{:S(2)}) %collective-permute-start.6) | collective-permute-done | bytes 131104 | tf_op jit(solution)/shard_map/ppermute | solution.py:28
  34.7 1.8 %collective-permute-done.5.refs_3_ = bf16[1,144,512]{2,1,0:T(8,128)(2,1)S(1)} collective-permute-done((bf16[1,144,512]{2,1,0:T(8,128)(2,1)S(1)}, bf16[1,144,512]{2,1,0:T(8,128)(2,1)S(1)}, u32[]{:S(2)}, u32[]{:S(2)}) %collective-permute-start.5) | collective-permute-done | bytes 147488 | tf_op jit(solution)/shard_map/ppermute | solution.py:28
  36.4 2.7 %collective-permute-done.8.refs_6_ = bf16[1,128,512]{2,1,0:T(8,128)(2,1)S(1)} collective-permute-done((bf16[1,128,512]{2,1,0:T(8,128)(2,1)S(1)}, bf16[1,128,512]{2,1,0:T(8,128)(2,1)S(1)}, u32[]{:S(2)}, u32[]{:S(2)}) %collective-permute-start.8) | collective-permute-done | bytes 131104 | tf_op jit(solution)/shard_map/ppermute | solution.py:28
  39.2 2.5 %attend.1 = (bf16[1,128,2048]{2,1,0:T(8,128)(2,1)}, bf16[1,128,1024]{2,1,0:T(8,128)(2,1)S(1)}, bf16[1,128,1024]{2,1,0:T(8,128)(2,1)S(1)}) custom-call(f32[128,128]{1,0:T(8,128)S(1)} %get-tuple-element.20.place_ref, bf16[1,128,2048]{2,1,0:T(8,128)(2,1)S(1)} %get-tuple-element.21.query_ref, bf16[1,144,512]{2,1,0:T(8,128)(2,1)S(1)} %get-tuple-element.22.refs_0_, ...), custom_call_target="tpu_custom_call" | custom-call | tf_op jit(solution)/shard_map/attend/pallas_call | solution.py:242
  41.7 1.5 %collective-permute-start.20 = (bf16[1,128,1024]{2,1,0:T(8,128)(2,1)S(1)}, bf16[1,128,1024]{2,1,0:T(8,128)(2,1)S(1)}, u32[]{:S(2)}, u32[]{:S(2)}) collective-permute-start(bf16[1,128,1024]{2,1,0:T(8,128)(2,1)S(1)} %get-tuple-element.33.refs_0_), channel_id=1, source_target_pairs={{0,16},{8,24},{16,0},{24,8},{1,17},{9,25},{17,1},{25,9},{2,18},{10... | collective-permute-start | bytes 786440 | tf_op jit(solution)/shard_map/ppermute | solution.py:44
  43.2 0.5 collective-permute-start.10
  43.7 3.2 %collective-permute-start.9 = (bf16[1,128,1024]{2,1,0:T(8,128)(2,1)S(1)}, bf16[1,128,1024]{2,1,0:T(8,128)(2,1)S(1)}, u32[]{:S(2)}, u32[]{:S(2)}) collective-permute-start(bf16[1,128,1024]{2,1,0:T(8,128)(2,1)S(1)} %get-tuple-element.30.refs_0_), channel_id=1, source_target_pairs={{0,4},{4,6},{6,2},{2,0},{1,5},{5,7},{7,3},{3,1},{8,12},{12,14},{14... | collective-permute-start | bytes 786440 | tf_op jit(solution)/shard_map/ppermute | solution.py:28
  46.9 3.9 %collective-permute-done.19.refs_1_ = bf16[1,128,1024]{2,1,0:T(8,128)(2,1)S(1)} collective-permute-done((bf16[1,128,1024]{2,1,0:T(8,128)(2,1)S(1)}, bf16[1,128,1024]{2,1,0:T(8,128)(2,1)S(1)}, u32[]{:S(2)}, u32[]{:S(2)}) %collective-permute-start.19) | collective-permute-done | bytes 262176 | tf_op jit(solution)/shard_map/ppermute | solution.py:28
  50.8 3.3 %collective-permute-start.21 = (bf16[1,128,1024]{2,1,0:T(8,128)(2,1)S(1)}, bf16[1,128,1024]{2,1,0:T(8,128)(2,1)S(1)}, u32[]{:S(2)}, u32[]{:S(2)}) collective-permute-start(bf16[1,128,1024]{2,1,0:T(8,128)(2,1)S(1)} %collective-permute-done.19.refs_1_), channel_id=1, source_target_pairs={{0,4},{4,6},{6,2},{2,0},{1,5},{5,7},{7,3},{3,1},{8,12},{12,14},{14... | collective-permute-start | bytes 786440 | tf_op jit(solution)/shard_map/ppermute | solution.py:28
  54.1 1.5 %collective-permute-start.16 = (bf16[512,512]{1,0:T(8,128)(2,1)S(1)}, bf16[512,512]{1,0:T(8,128)(2,1)S(1)}, u32[]{:S(2)}, u32[]{:S(2)}) collective-permute-start(bf16[512,512]{1,0:T(8,128)(2,1)S(1)} %join.1.refs_6_.refs_2_), channel_id=1, source_target_pairs={{0,1},{1,0},{2,3},{3,2},{4,5},{5,4},{6,7},{7,6},{8,9},{9,8},{10,11... | collective-permute-start | bytes 1572872 | tf_op jit(solution)/shard_map/ppermute | solution.py:44
  55.6 1.5 %collective-permute-start.22 = (bf16[1,128,1024]{2,1,0:T(8,128)(2,1)S(1)}, bf16[1,128,1024]{2,1,0:T(8,128)(2,1)S(1)}, u32[]{:S(2)}, u32[]{:S(2)}) collective-permute-start(bf16[1,128,1024]{2,1,0:T(8,128)(2,1)S(1)} %collective-permute-done.19.refs_1_), channel_id=1, source_target_pairs={{0,16},{8,24},{16,0},{24,8},{1,17},{9,25},{17,1},{25,9},{2,18},{10... | collective-permute-start | bytes 786440 | tf_op jit(solution)/shard_map/ppermute | solution.py:44
  57.1 2.7 %collective-permute-start.11 = (bf16[1,128,1024]{2,1,0:T(8,128)(2,1)S(1)}, bf16[1,128,1024]{2,1,0:T(8,128)(2,1)S(1)}, u32[]{:S(2)}, u32[]{:S(2)}) collective-permute-start(bf16[1,128,1024]{2,1,0:T(8,128)(2,1)S(1)} %collective-permute-done.9.refs_1_), channel_id=1, source_target_pairs={{0,4},{4,6},{6,2},{2,0},{1,5},{5,7},{7,3},{3,1},{8,12},{12,14},{14... | collective-permute-start | bytes 786440 | tf_op jit(solution)/shard_map/ppermute | solution.py:28
  59.9 0.5 collective-permute-start.12
  60.4 1.7 %collective-permute-done.21.refs_2_ = bf16[1,128,1024]{2,1,0:T(8,128)(2,1)S(1)} collective-permute-done((bf16[1,128,1024]{2,1,0:T(8,128)(2,1)S(1)}, bf16[1,128,1024]{2,1,0:T(8,128)(2,1)S(1)}, u32[]{:S(2)}, u32[]{:S(2)}) %collective-permute-start.21) | collective-permute-done | bytes 262176 | tf_op jit(solution)/shard_map/ppermute | solution.py:28
  62.1 1.5 %collective-permute-start.17 = (bf16[512,512]{1,0:T(8,128)(2,1)S(1)}, bf16[512,512]{1,0:T(8,128)(2,1)S(1)}, u32[]{:S(2)}, u32[]{:S(2)}) collective-permute-start(bf16[512,512]{1,0:T(8,128)(2,1)S(1)} %collective-permute-done.15.refs_7_.refs_3_), channel_id=1, source_target_pairs={{0,1},{1,0},{2,3},{3,2},{4,5},{5,4},{6,7},{7,6},{8,9},{9,8},{10,11... | collective-permute-start | bytes 1572872 | tf_op jit(solution)/shard_map/ppermute | solution.py:44
  63.6 1.3 %collective-permute-done.22.refs_4_ = bf16[1,128,1024]{2,1,0:T(8,128)(2,1)S(1)} collective-permute-done((bf16[1,128,1024]{2,1,0:T(8,128)(2,1)S(1)}, bf16[1,128,1024]{2,1,0:T(8,128)(2,1)S(1)}, u32[]{:S(2)}, u32[]{:S(2)}) %collective-permute-start.22) | collective-permute-done | bytes 262176 | tf_op jit(solution)/shard_map/ppermute | solution.py:44
  64.9 1.5 %collective-permute-start.24 = (bf16[1,128,1024]{2,1,0:T(8,128)(2,1)S(1)}, bf16[1,128,1024]{2,1,0:T(8,128)(2,1)S(1)}, u32[]{:S(2)}, u32[]{:S(2)}) collective-permute-start(bf16[1,128,1024]{2,1,0:T(8,128)(2,1)S(1)} %collective-permute-done.21.refs_2_), channel_id=1, source_target_pairs={{0,16},{8,24},{16,0},{24,8},{1,17},{9,25},{17,1},{25,9},{2,18},{10... | collective-permute-start | bytes 786440 | tf_op jit(solution)/shard_map/ppermute | solution.py:44
  66.4 0.4 collective-permute-done.11.refs_2_
  66.8 3.7 %collective-permute-done.12.refs_4_ = bf16[1,128,1024]{2,1,0:T(8,128)(2,1)S(1)} collective-permute-done((bf16[1,128,1024]{2,1,0:T(8,128)(2,1)S(1)}, bf16[1,128,1024]{2,1,0:T(8,128)(2,1)S(1)}, u32[]{:S(2)}, u32[]{:S(2)}) %collective-permute-start.12) | collective-permute-done | bytes 262176 | tf_op jit(solution)/shard_map/ppermute | solution.py:44
  70.5 2.7 %collective-permute-start.13 = (bf16[1,128,1024]{2,1,0:T(8,128)(2,1)S(1)}, bf16[1,128,1024]{2,1,0:T(8,128)(2,1)S(1)}, u32[]{:S(2)}, u32[]{:S(2)}) collective-permute-start(bf16[1,128,1024]{2,1,0:T(8,128)(2,1)S(1)} %collective-permute-done.11.refs_2_), channel_id=1, source_target_pairs={{0,4},{4,6},{6,2},{2,0},{1,5},{5,7},{7,3},{3,1},{8,12},{12,14},{14... | collective-permute-start | bytes 786440 | tf_op jit(solution)/shard_map/ppermute | solution.py:28
  73.2 1.5 %collective-permute-start.18 = (bf16[1,128,1024]{2,1,0:T(8,128)(2,1)S(1)}, bf16[1,128,1024]{2,1,0:T(8,128)(2,1)S(1)}, u32[]{:S(2)}, u32[]{:S(2)}) collective-permute-start(bf16[1,128,1024]{2,1,0:T(8,128)(2,1)S(1)} %collective-permute-done.11.refs_2_), channel_id=1, source_target_pairs={{0,16},{8,24},{16,0},{24,8},{1,17},{9,25},{17,1},{25,9},{2,18},{10... | collective-permute-start | bytes 786440 | tf_op jit(solution)/shard_map/ppermute | solution.py:44
  74.7 0.3 collective-permute-start.23
  75.0 1.1 %collective-permute-done.24.refs_5_ = bf16[1,128,1024]{2,1,0:T(8,128)(2,1)S(1)} collective-permute-done((bf16[1,128,1024]{2,1,0:T(8,128)(2,1)S(1)}, bf16[1,128,1024]{2,1,0:T(8,128)(2,1)S(1)}, u32[]{:S(2)}, u32[]{:S(2)}) %collective-permute-start.24) | collective-permute-done | bytes 262176 | tf_op jit(solution)/shard_map/ppermute | solution.py:44
  76.1 2.7 %collective-permute-start.25 = (bf16[1,128,1024]{2,1,0:T(8,128)(2,1)S(1)}, bf16[1,128,1024]{2,1,0:T(8,128)(2,1)S(1)}, u32[]{:S(2)}, u32[]{:S(2)}) collective-permute-start(bf16[1,128,1024]{2,1,0:T(8,128)(2,1)S(1)} %collective-permute-done.24.refs_5_), channel_id=1, source_target_pairs={{0,4},{4,6},{6,2},{2,0},{1,5},{5,7},{7,3},{3,1},{8,12},{12,14},{14... | collective-permute-start | bytes 786440 | tf_op jit(solution)/shard_map/ppermute | solution.py:28
  78.8 1.1 %collective-permute-done.13.refs_0_ = bf16[1,128,1024]{2,1,0:T(8,128)(2,1)S(1)} collective-permute-done((bf16[1,128,1024]{2,1,0:T(8,128)(2,1)S(1)}, bf16[1,128,1024]{2,1,0:T(8,128)(2,1)S(1)}, u32[]{:S(2)}, u32[]{:S(2)}) %collective-permute-start.13) | collective-permute-done | bytes 262176 | tf_op jit(solution)/shard_map/ppermute | solution.py:28
  79.9 1.5 %collective-permute-start.14 = (bf16[1,128,1024]{2,1,0:T(8,128)(2,1)S(1)}, bf16[1,128,1024]{2,1,0:T(8,128)(2,1)S(1)}, u32[]{:S(2)}, u32[]{:S(2)}) collective-permute-start(bf16[1,128,1024]{2,1,0:T(8,128)(2,1)S(1)} %collective-permute-done.13.refs_0_), channel_id=1, source_target_pairs={{0,16},{8,24},{16,0},{24,8},{1,17},{9,25},{17,1},{25,9},{2,18},{10... | collective-permute-start | bytes 786440 | tf_op jit(solution)/shard_map/ppermute | solution.py:44
  81.5 1.8 %early.3.refs_6_ = f32[1024,1024]{1,0:T(8,128)S(1)} custom-call(bf16[1,128,1024]{2,1,0:T(8,128)(2,1)S(1)} %get-tuple-element.33.refs_0_, bf16[1,128,1024]{2,1,0:T(8,128)(2,1)S(1)} %collective-permute-done.19.refs_1_, bf16[1,128,1024]{2,1,0:T(8,128)(2,1)S(1)} %collective-permute-done.21.refs_2_, bf16[1,128,1024]{2,1,0:T(8,128)(2,1)S(1)} %collective-permute-done.20.refs_3_, ...), custom_call_target="tpu_custom_call" | custom-call | flops 1610612736 | bytes 8388608 | tf_op jit(solution)/shard_map/early/pallas_call | solution.py:272
  83.3 1.8 %early.2.refs_6_ = f32[1024,1024]{1,0:T(8,128)S(1)} custom-call(bf16[1,128,1024]{2,1,0:T(8,128)(2,1)S(1)} %get-tuple-element.30.refs_0_, bf16[1,128,1024]{2,1,0:T(8,128)(2,1)S(1)} %collective-permute-done.9.refs_1_, bf16[1,128,1024]{2,1,0:T(8,128)(2,1)S(1)} %collective-permute-done.11.refs_2_, bf16[1,128,1024]{2,1,0:T(8,128)(2,1)S(1)} %collective-permute-done.10.refs_3_, ...), custom_call_target="tpu_custom_call" | custom-call | flops 1610612736 | bytes 8388608 | tf_op jit(solution)/shard_map/early/pallas_call | solution.py:272
  85.1 1.1 %collective-permute-done.25.refs_1_ = bf16[1,128,1024]{2,1,0:T(8,128)(2,1)S(1)} collective-permute-done((bf16[1,128,1024]{2,1,0:T(8,128)(2,1)S(1)}, bf16[1,128,1024]{2,1,0:T(8,128)(2,1)S(1)}, u32[]{:S(2)}, u32[]{:S(2)}) %collective-permute-start.25) | collective-permute-done | bytes 262176 | tf_op jit(solution)/shard_map/ppermute | solution.py:28
  86.2 2.5 %finish.2.refs_7_ = bf16[1,1024,2048]{2,1,0:T(8,128)(2,1)} custom-call(bf16[1,128,1024]{2,1,0:T(8,128)(2,1)S(1)} %collective-permute-done.23.refs_0_, bf16[1,128,1024]{2,1,0:T(8,128)(2,1)S(1)} %collective-permute-done.25.refs_1_, bf16[512,512]{1,0:T(8,128)(2,1)S(1)} %join.1.refs_6_.refs_2_, bf16[512,512]{1,0:T(8,128)(2,1)S(1)} %collective-permute-done.15.refs_7_.refs_3_, ...), custom_call_target="tpu_custom_call" | custom-call | flops 536870912 | bytes 8388608 | tf_op jit(solution)/shard_map/finish/pallas_call | solution.py:297
  88.8 2.6 %finish.3 = bf16[1,1024,2048]{2,1,0:T(8,128)(2,1)} custom-call(bf16[1,128,1024]{2,1,0:T(8,128)(2,1)S(1)} %collective-permute-done.13.refs_0_, bf16[1,128,1024]{2,1,0:T(8,128)(2,1)S(1)} %collective-permute-done.14.refs_1_, bf16[512,512]{1,0:T(8,128)(2,1)S(1)} %join.1.refs_6_.refs_2_, ...), custom_call_target="tpu_custom_call", output_to_operand_aliasing={{}: (7, {})} | custom-call | flops 536870912 | bytes 8388608 | tf_op jit(solution)/shard_map/finish/pallas_call | solution.py:297
  (23 shorter events, 0.2 us)
Async XLA Ops:
  0.6 1.2 %copy-start = (bf16[1,128,4096]{2,1,0:T(8,128)(2,1)S(1)}, bf16[1,128,4096]{2,1,0:T(8,128)(2,1)}, u32[]{:S(2)}) copy-start(bf16[1,128,4096]{2,1,0:T(8,128)(2,1)} %cot_ref.1) | copy-start | bytes 3145732
  2.0 0.9 copy-start.2
  3.0 0.7 copy-start.4
  4.2 20.4 %collective-permute-start = (bf16[1,144,512]{2,1,0:T(8,128)(2,1)S(1)}, bf16[1,144,512]{2,1,0:T(8,128)(2,1)S(1)}, u32[]{:S(2)}, u32[]{:S(2)}) collective-permute-start(bf16[1,144,512]{2,1,0:T(8,128)(2,1)S(1)} %get-tuple-element.22.refs_0_), channel_id=1, source_target_pairs={{0,4},{4,6},{6,2},{2,0},{1,5},{5,7},{7,3},{3,1},{8,12},{12,14},{14... | collective-permute-start | bytes 442376 | tf_op jit(solution)/shard_map/ppermute | solution.py:28
  8.3 8.0 %collective-permute-start.1 = (bf16[512,128]{1,0:T(8,128)(2,1)S(1)}, bf16[512,128]{1,0:T(8,128)(2,1)S(1)}, u32[]{:S(2)}, u32[]{:S(2)}) collective-permute-start(bf16[512,128]{1,0:T(8,128)(2,1)S(1)} %get-tuple-element.23), channel_id=1, source_target_pairs={{0,4},{4,6},{6,2},{2,0},{1,5},{5,7},{7,3},{3,1},{8,12},{12,14},{14... | collective-permute-start | bytes 393224 | tf_op jit(solution)/shard_map/ppermute | solution.py:28
  9.8 10.1 %collective-permute-start.2 = (bf16[512,128]{1,0:T(8,128)(2,1)S(1)}, bf16[512,128]{1,0:T(8,128)(2,1)S(1)}, u32[]{:S(2)}, u32[]{:S(2)}) collective-permute-start(bf16[512,128]{1,0:T(8,128)(2,1)S(1)} %get-tuple-element.24), channel_id=1, source_target_pairs={{0,6},{4,2},{6,0},{2,4},{1,7},{5,3},{7,1},{3,5},{8,14},{12,10},{14... | collective-permute-start | bytes 393224 | tf_op jit(solution)/shard_map/ppermute | solution.py:28
  9.8 14.7 %collective-permute-start.3 = (bf16[512,128]{1,0:T(8,128)(2,1)S(1)}, bf16[512,128]{1,0:T(8,128)(2,1)S(1)}, u32[]{:S(2)}, u32[]{:S(2)}) collective-permute-start(bf16[512,128]{1,0:T(8,128)(2,1)S(1)} %get-tuple-element.25), channel_id=1, source_target_pairs={{0,2},{4,0},{6,4},{2,6},{1,3},{5,1},{7,5},{3,7},{8,10},{12,8},{14,... | collective-permute-start | bytes 393224 | tf_op jit(solution)/shard_map/ppermute | solution.py:28
  10.7 17.0 %collective-permute-start.7 = (bf16[1,128,512]{2,1,0:T(8,128)(2,1)}, bf16[1,128,512]{2,1,0:T(8,128)(2,1)S(1)}, u32[]{:S(2)}, u32[]{:S(2)}) collective-permute-start(bf16[1,128,512]{2,1,0:T(8,128)(2,1)} %value_ref.1), channel_id=1, source_target_pairs={{0,2},{4,0},{6,4},{2,6},{1,3},{5,1},{7,5},{3,7},{8,10},{12,8},{14,... | collective-permute-start | bytes 393224 | tf_op jit(solution)/shard_map/ppermute | solution.py:28
  14.2 1.0 %copy-start.1 = (bf16[1,128,2048]{2,1,0:T(8,128)(2,1)S(1)}, bf16[1,128,2048]{2,1,0:T(8,128)(2,1)}, u32[]{:S(2)}) copy-start(bf16[1,128,2048]{2,1,0:T(8,128)(2,1)} %query_ref.1) | copy-start | bytes 1572868
  15.3 0.9 copy-start.3
  16.2 20.2 %collective-permute-start.5 = (bf16[1,144,512]{2,1,0:T(8,128)(2,1)S(1)}, bf16[1,144,512]{2,1,0:T(8,128)(2,1)S(1)}, u32[]{:S(2)}, u32[]{:S(2)}) collective-permute-start(bf16[1,144,512]{2,1,0:T(8,128)(2,1)S(1)} %get-tuple-element.22.refs_0_), channel_id=1, source_target_pairs={{0,2},{4,0},{6,4},{2,6},{1,3},{5,1},{7,5},{3,7},{8,10},{12,8},{14,... | collective-permute-start | bytes 442376 | tf_op jit(solution)/shard_map/ppermute | solution.py:28
  24.6 14.6 %collective-permute-start.4 = (bf16[1,144,512]{2,1,0:T(8,128)(2,1)S(1)}, bf16[1,144,512]{2,1,0:T(8,128)(2,1)S(1)}, u32[]{:S(2)}, u32[]{:S(2)}) collective-permute-start(bf16[1,144,512]{2,1,0:T(8,128)(2,1)S(1)} %collective-permute-done.refs_1_), channel_id=1, source_target_pairs={{0,4},{4,6},{6,2},{2,0},{1,5},{5,7},{7,3},{3,1},{8,12},{12,14},{14... | collective-permute-start | bytes 442376 | tf_op jit(solution)/shard_map/ppermute | solution.py:28
  24.7 10.0 %collective-permute-start.6 = (bf16[1,128,512]{2,1,0:T(8,128)(2,1)S(1)}, bf16[1,128,512]{2,1,0:T(8,128)(2,1)S(1)}, u32[]{:S(2)}, u32[]{:S(2)}) collective-permute-start(bf16[1,128,512]{2,1,0:T(8,128)(2,1)S(1)} %copy-done.3), channel_id=1, source_target_pairs={{0,4},{4,6},{6,2},{2,0},{1,5},{5,7},{7,3},{3,1},{8,12},{12,14},{14... | collective-permute-start | bytes 393224 | tf_op jit(solution)/shard_map/ppermute | solution.py:28
  27.7 11.5 %collective-permute-start.8 = (bf16[1,128,512]{2,1,0:T(8,128)(2,1)S(1)}, bf16[1,128,512]{2,1,0:T(8,128)(2,1)S(1)}, u32[]{:S(2)}, u32[]{:S(2)}) collective-permute-start(bf16[1,128,512]{2,1,0:T(8,128)(2,1)S(1)} %collective-permute-done.7.refs_7_), channel_id=1, source_target_pairs={{0,2},{4,0},{6,4},{2,6},{1,3},{5,1},{7,5},{3,7},{8,10},{12,8},{14,... | collective-permute-start | bytes 393224 | tf_op jit(solution)/shard_map/ppermute | solution.py:28
  27.7 32.1 %collective-permute-start.15 = (bf16[512,512]{1,0:T(8,128)(2,1)S(1)}, bf16[512,512]{1,0:T(8,128)(2,1)S(1)}, u32[]{:S(2)}, u32[]{:S(2)}) collective-permute-start(bf16[512,512]{1,0:T(8,128)(2,1)S(1)} %join.1.refs_6_.refs_2_), channel_id=1, source_target_pairs={{0,16},{8,24},{16,0},{24,8},{1,17},{9,25},{17,1},{25,9},{2,18},{10... | collective-permute-start | bytes 1572872 | tf_op jit(solution)/shard_map/ppermute | solution.py:44
  41.7 9.2 %collective-permute-start.19 = (bf16[1,128,1024]{2,1,0:T(8,128)(2,1)S(1)}, bf16[1,128,1024]{2,1,0:T(8,128)(2,1)S(1)}, u32[]{:S(2)}, u32[]{:S(2)}) collective-permute-start(bf16[1,128,1024]{2,1,0:T(8,128)(2,1)S(1)} %get-tuple-element.33.refs_0_), channel_id=1, source_target_pairs={{0,4},{4,6},{6,2},{2,0},{1,5},{5,7},{7,3},{3,1},{8,12},{12,14},{14... | collective-permute-start | bytes 786440 | tf_op jit(solution)/shard_map/ppermute | solution.py:28
  41.7 9.2 %collective-permute-start.20 = (bf16[1,128,1024]{2,1,0:T(8,128)(2,1)S(1)}, bf16[1,128,1024]{2,1,0:T(8,128)(2,1)S(1)}, u32[]{:S(2)}, u32[]{:S(2)}) collective-permute-start(bf16[1,128,1024]{2,1,0:T(8,128)(2,1)S(1)} %get-tuple-element.33.refs_0_), channel_id=1, source_target_pairs={{0,16},{8,24},{16,0},{24,8},{1,17},{9,25},{17,1},{25,9},{2,18},{10... | collective-permute-start | bytes 786440 | tf_op jit(solution)/shard_map/ppermute | solution.py:44
  43.2 12.4 %collective-permute-start.10 = (bf16[1,128,1024]{2,1,0:T(8,128)(2,1)S(1)}, bf16[1,128,1024]{2,1,0:T(8,128)(2,1)S(1)}, u32[]{:S(2)}, u32[]{:S(2)}) collective-permute-start(bf16[1,128,1024]{2,1,0:T(8,128)(2,1)S(1)} %get-tuple-element.30.refs_0_), channel_id=1, source_target_pairs={{0,16},{8,24},{16,0},{24,8},{1,17},{9,25},{17,1},{25,9},{2,18},{10... | collective-permute-start | bytes 786440 | tf_op jit(solution)/shard_map/ppermute | solution.py:44
  43.7 13.4 %collective-permute-start.9 = (bf16[1,128,1024]{2,1,0:T(8,128)(2,1)S(1)}, bf16[1,128,1024]{2,1,0:T(8,128)(2,1)S(1)}, u32[]{:S(2)}, u32[]{:S(2)}) collective-permute-start(bf16[1,128,1024]{2,1,0:T(8,128)(2,1)S(1)} %get-tuple-element.30.refs_0_), channel_id=1, source_target_pairs={{0,4},{4,6},{6,2},{2,0},{1,5},{5,7},{7,3},{3,1},{8,12},{12,14},{14... | collective-permute-start | bytes 786440 | tf_op jit(solution)/shard_map/ppermute | solution.py:28
  50.8 11.2 %collective-permute-start.21 = (bf16[1,128,1024]{2,1,0:T(8,128)(2,1)S(1)}, bf16[1,128,1024]{2,1,0:T(8,128)(2,1)S(1)}, u32[]{:S(2)}, u32[]{:S(2)}) collective-permute-start(bf16[1,128,1024]{2,1,0:T(8,128)(2,1)S(1)} %collective-permute-done.19.refs_1_), channel_id=1, source_target_pairs={{0,4},{4,6},{6,2},{2,0},{1,5},{5,7},{7,3},{3,1},{8,12},{12,14},{14... | collective-permute-start | bytes 786440 | tf_op jit(solution)/shard_map/ppermute | solution.py:28
  54.1 20.6 %collective-permute-start.16 = (bf16[512,512]{1,0:T(8,128)(2,1)S(1)}, bf16[512,512]{1,0:T(8,128)(2,1)S(1)}, u32[]{:S(2)}, u32[]{:S(2)}) collective-permute-start(bf16[512,512]{1,0:T(8,128)(2,1)S(1)} %join.1.refs_6_.refs_2_), channel_id=1, source_target_pairs={{0,1},{1,0},{2,3},{3,2},{4,5},{5,4},{6,7},{7,6},{8,9},{9,8},{10,11... | collective-permute-start | bytes 1572872 | tf_op jit(solution)/shard_map/ppermute | solution.py:44
  55.6 9.2 %collective-permute-start.22 = (bf16[1,128,1024]{2,1,0:T(8,128)(2,1)S(1)}, bf16[1,128,1024]{2,1,0:T(8,128)(2,1)S(1)}, u32[]{:S(2)}, u32[]{:S(2)}) collective-permute-start(bf16[1,128,1024]{2,1,0:T(8,128)(2,1)S(1)} %collective-permute-done.19.refs_1_), channel_id=1, source_target_pairs={{0,16},{8,24},{16,0},{24,8},{1,17},{9,25},{17,1},{25,9},{2,18},{10... | collective-permute-start | bytes 786440 | tf_op jit(solution)/shard_map/ppermute | solution.py:44
  57.1 9.6 %collective-permute-start.11 = (bf16[1,128,1024]{2,1,0:T(8,128)(2,1)S(1)}, bf16[1,128,1024]{2,1,0:T(8,128)(2,1)S(1)}, u32[]{:S(2)}, u32[]{:S(2)}) collective-permute-start(bf16[1,128,1024]{2,1,0:T(8,128)(2,1)S(1)} %collective-permute-done.9.refs_1_), channel_id=1, source_target_pairs={{0,4},{4,6},{6,2},{2,0},{1,5},{5,7},{7,3},{3,1},{8,12},{12,14},{14... | collective-permute-start | bytes 786440 | tf_op jit(solution)/shard_map/ppermute | solution.py:28
  59.9 10.6 %collective-permute-start.12 = (bf16[1,128,1024]{2,1,0:T(8,128)(2,1)S(1)}, bf16[1,128,1024]{2,1,0:T(8,128)(2,1)S(1)}, u32[]{:S(2)}, u32[]{:S(2)}) collective-permute-start(bf16[1,128,1024]{2,1,0:T(8,128)(2,1)S(1)} %collective-permute-done.9.refs_1_), channel_id=1, source_target_pairs={{0,16},{8,24},{16,0},{24,8},{1,17},{9,25},{17,1},{25,9},{2,18},{10... | collective-permute-start | bytes 786440 | tf_op jit(solution)/shard_map/ppermute | solution.py:44
  62.1 19.4 %collective-permute-start.17 = (bf16[512,512]{1,0:T(8,128)(2,1)S(1)}, bf16[512,512]{1,0:T(8,128)(2,1)S(1)}, u32[]{:S(2)}, u32[]{:S(2)}) collective-permute-start(bf16[512,512]{1,0:T(8,128)(2,1)S(1)} %collective-permute-done.15.refs_7_.refs_3_), channel_id=1, source_target_pairs={{0,1},{1,0},{2,3},{3,2},{4,5},{5,4},{6,7},{7,6},{8,9},{9,8},{10,11... | collective-permute-start | bytes 1572872 | tf_op jit(solution)/shard_map/ppermute | solution.py:44
  64.9 11.2 %collective-permute-start.24 = (bf16[1,128,1024]{2,1,0:T(8,128)(2,1)S(1)}, bf16[1,128,1024]{2,1,0:T(8,128)(2,1)S(1)}, u32[]{:S(2)}, u32[]{:S(2)}) collective-permute-start(bf16[1,128,1024]{2,1,0:T(8,128)(2,1)S(1)} %collective-permute-done.21.refs_2_), channel_id=1, source_target_pairs={{0,16},{8,24},{16,0},{24,8},{1,17},{9,25},{17,1},{25,9},{2,18},{10... | collective-permute-start | bytes 786440 | tf_op jit(solution)/shard_map/ppermute | solution.py:44
  70.5 9.5 %collective-permute-start.13 = (bf16[1,128,1024]{2,1,0:T(8,128)(2,1)S(1)}, bf16[1,128,1024]{2,1,0:T(8,128)(2,1)S(1)}, u32[]{:S(2)}, u32[]{:S(2)}) collective-permute-start(bf16[1,128,1024]{2,1,0:T(8,128)(2,1)S(1)} %collective-permute-done.11.refs_2_), channel_id=1, source_target_pairs={{0,4},{4,6},{6,2},{2,0},{1,5},{5,7},{7,3},{3,1},{8,12},{12,14},{14... | collective-permute-start | bytes 786440 | tf_op jit(solution)/shard_map/ppermute | solution.py:28
  73.2 10.1 %collective-permute-start.18 = (bf16[1,128,1024]{2,1,0:T(8,128)(2,1)S(1)}, bf16[1,128,1024]{2,1,0:T(8,128)(2,1)S(1)}, u32[]{:S(2)}, u32[]{:S(2)}) collective-permute-start(bf16[1,128,1024]{2,1,0:T(8,128)(2,1)S(1)} %collective-permute-done.11.refs_2_), channel_id=1, source_target_pairs={{0,16},{8,24},{16,0},{24,8},{1,17},{9,25},{17,1},{25,9},{2,18},{10... | collective-permute-start | bytes 786440 | tf_op jit(solution)/shard_map/ppermute | solution.py:44
  74.7 10.4 %collective-permute-start.23 = (bf16[1,128,1024]{2,1,0:T(8,128)(2,1)S(1)}, bf16[1,128,1024]{2,1,0:T(8,128)(2,1)S(1)}, u32[]{:S(2)}, u32[]{:S(2)}) collective-permute-start(bf16[1,128,1024]{2,1,0:T(8,128)(2,1)S(1)} %collective-permute-done.21.refs_2_), channel_id=1, source_target_pairs={{0,4},{4,6},{6,2},{2,0},{1,5},{5,7},{7,3},{3,1},{8,12},{12,14},{14... | collective-permute-start | bytes 786440 | tf_op jit(solution)/shard_map/ppermute | solution.py:28
  76.1 10.1 %collective-permute-start.25 = (bf16[1,128,1024]{2,1,0:T(8,128)(2,1)S(1)}, bf16[1,128,1024]{2,1,0:T(8,128)(2,1)S(1)}, u32[]{:S(2)}, u32[]{:S(2)}) collective-permute-start(bf16[1,128,1024]{2,1,0:T(8,128)(2,1)S(1)} %collective-permute-done.24.refs_5_), channel_id=1, source_target_pairs={{0,4},{4,6},{6,2},{2,0},{1,5},{5,7},{7,3},{3,1},{8,12},{12,14},{14... | collective-permute-start | bytes 786440 | tf_op jit(solution)/shard_map/ppermute | solution.py:28
  79.9 8.8 %collective-permute-start.14 = (bf16[1,128,1024]{2,1,0:T(8,128)(2,1)S(1)}, bf16[1,128,1024]{2,1,0:T(8,128)(2,1)S(1)}, u32[]{:S(2)}, u32[]{:S(2)}) collective-permute-start(bf16[1,128,1024]{2,1,0:T(8,128)(2,1)S(1)} %collective-permute-done.13.refs_0_), channel_id=1, source_target_pairs={{0,16},{8,24},{16,0},{24,8},{1,17},{9,25},{17,1},{25,9},{2,18},{10... | collective-permute-start | bytes 786440 | tf_op jit(solution)/shard_map/ppermute | solution.py:44

commit v7 on v6

--- a/solution.py
+++ b/solution.py
@@ -28,15 +28,15 @@
     return lax.ppermute(x, "ctx", [(order[q], order[(q + shift) % n]) for q in range(n)])
 
 
-def gather(x, ways, gate):
+def gather(x, edges, ways, gate):
     n = lax.axis_size("ctx")
     middle = n // 2 if ways > 0 else (n - 1) // 2
     held = [x] + [None] * (n - 1)
-    for s in range(1, max(middle, n - 1 - middle) + 1):
-        if s <= middle:
-            held[s] = around(gate(held[s - 1]) if s > 1 else x, 1)
-        if s <= n - 1 - middle:
-            held[n - s] = around(gate(held[n - s + 1]) if s > 1 else x, -1)
+    held[1], held[-1] = edges
+    for s in range(2, middle + 1):
+        held[s] = around(gate(held[s - 1]), 1)
+    for s in range(2, n - middle):
+        held[n - s] = around(gate(held[n - s + 1]), -1)
     return held
 
 
@@ -228,6 +228,8 @@
         name="fetch",
     )(place, queries, values)
     turned = [turned[0]] + [around(turned[s], s) for s in range(1, n)]
+    key_edges, value_edges = ([around(x, way) for way in (1, -1)] for x in (packed, values))
+    turned[0] = after(turned[0], *key_edges, *value_edges)
     mine = pl.pallas_call(
         join_kernel,
         out_shape=jax.ShapeDtypeStruct((half, n * tokens), jnp.bfloat16),
@@ -237,8 +239,9 @@
         name="join",
     )(*turned)
     mine_far = swap(mine, "pipe", far)
-    key_ring = gather(packed, 1, lambda x: after(x, query_held, mine))
-    value_ring = gather(values, -1, lambda x: after(x, value_held, mine))
+    key_ring = gather(packed, key_edges, 1, lambda x: after(x, query_held))
+    value_ring = gather(values, value_edges, -1, lambda x: after(x, value_held))
+    query_held = after(query_held, mine)
     attention, *pieces = pl.pallas_call(
         functools.partial(attention_kernel, HQ // HK, 1.0 / math.sqrt(HD), n, spans),
         out_shape=[jax.ShapeDtypeStruct(queries.shape, jnp.bfloat16)]

time: 91.6 us -> 97.7 us (1.067)
  waiting for transfers between devices: 31.1 us -> 45.5 us
  starting transfers between devices: 42.7 us -> 34.5 us
    ppermute x10, waiting for transfers between devices: 6.11 us -> 20.1 us  [swap(): lax.ppermute(x, axis, [(i, i ^ mask) for i in range(lax.axis_size(axis))])]
    ppermute x16, starting transfers between devices: 29.6 us -> 21.2 us  [around(): lax.ppermute(x, 'ctx', [(order[q], order[(q + shift) % n]) for q in range...]
  transfers between devices with their start and end apart: 26 -> 26, of which waited for: 13 -> 13; matrix products, arithmetic and copies ran while one was open for 0% -> 0% of each run, Pallas kernels for 10% -> 9%
where the time goes in v7:
time: 97.7 us; the launch traced here: 97.5 us
  waiting for transfers between devices  45.5 us (47%)
  starting transfers between devices  34.5 us (35%)
  Pallas kernels  12.1 us (12%)
  local copies, waits for them, and re-layouts  4.72 us (5%)
    ppermute x16, waiting for transfers between devices, around(): lax.ppermute(x, 'ctx', [(order[q], order[(q + shift) % n]) for q in range...  25.3 us
    ppermute x16, starting transfers between devices, around(): lax.ppermute(x, 'ctx', [(order[q], order[(q + shift) % n]) for q in range...  21.2 us
    ppermute x10, waiting for transfers between devices, swap(): lax.ppermute(x, axis, [(i, i ^ mask) for i in range(lax.axis_size(axis))])  20.1 us
    ppermute x10, starting transfers between devices, swap(): lax.ppermute(x, axis, [(i, i ^ mask) for i in range(lax.axis_size(axis))])  13.2 us
    pallas_call x2, Pallas kernels, local(): pl.pallas_call(functools.partial(finish_kernel, slots, c * chunk), out_sh...  5.09 us
    unnamed x10, local copies, waits for them, and re-layouts  4.72 us
    pallas_call x2, Pallas kernels, local(): pl.pallas_call(functools.partial(early_kernel, first_slots), out_shape=ja...  3.6 us
    pallas_call x1, Pallas kernels, local(): pl.pallas_call(functools.partial(attention_kernel, HQ // HK, 1.0 / math.s...  2.51 us
  transfers between devices with their start and end apart: 26, of which 13 were waited for; matrix products, arithmetic and copies ran while one was open for 0% of the time, Pallas kernels for 9%

profile of v7, /device:TPU:0, one launch (start us, length us, event | category | flops | bytes accessed | tf_op | source)
XLA Modules:
  0.0 97.5 jit_solution(2504454143232762443)
XLA Ops:
  0.6 1.2 %copy-done = bf16[1,128,4096]{2,1,0:T(8,128)(2,1)S(1)} copy-done((bf16[1,128,4096]{2,1,0:T(8,128)(2,1)S(1)}, bf16[1,128,4096]{2,1,0:T(8,128)(2,1)}, u32[]{:S(2)}) %copy-start) | copy-done | bytes 1048600
  1.9 0.2 turn.1
  2.0 0.0 copy-start.2
  2.1 0.9 copy-done.2
  3.0 0.7 copy-done.4
  3.6 0.6 pack.1
  4.2 4.1 %collective-permute-start = (bf16[1,144,512]{2,1,0:T(8,128)(2,1)S(1)}, bf16[1,144,512]{2,1,0:T(8,128)(2,1)S(1)}, u32[]{:S(2)}, u32[]{:S(2)}) collective-permute-start(bf16[1,144,512]{2,1,0:T(8,128)(2,1)S(1)} %get-tuple-element.24.refs_0_), channel_id=1, source_target_pairs={{0,4},{4,6},{6,2},{2,0},{1,5},{5,7},{7,3},{3,1},{8,12},{12,14},{14... | collective-permute-start | bytes 442376 | tf_op jit(solution)/shard_map/ppermute | solution.py:28
  8.3 0.0 collective-permute-start.1
  8.3 1.9 %collective-permute-start.3 = (bf16[1,128,512]{2,1,0:T(8,128)(2,1)}, bf16[1,128,512]{2,1,0:T(8,128)(2,1)S(1)}, u32[]{:S(2)}, u32[]{:S(2)}) collective-permute-start(bf16[1,128,512]{2,1,0:T(8,128)(2,1)} %value_ref.1), channel_id=1, source_target_pairs={{0,2},{4,0},{6,4},{2,6},{1,3},{5,1},{7,5},{3,7},{8,10},{12,8},{14,... | collective-permute-start | bytes 393224 | tf_op jit(solution)/shard_map/ppermute | solution.py:28
  10.2 1.0 %collective-permute-start.2 = (bf16[1,128,512]{2,1,0:T(8,128)(2,1)}, bf16[1,128,512]{2,1,0:T(8,128)(2,1)S(1)}, u32[]{:S(2)}, u32[]{:S(2)}) collective-permute-start(bf16[1,128,512]{2,1,0:T(8,128)(2,1)} %value_ref.1), channel_id=1, source_target_pairs={{0,4},{4,6},{6,2},{2,0},{1,5},{5,7},{7,3},{3,1},{8,12},{12,14},{14... | collective-permute-start | bytes 393224 | tf_op jit(solution)/shard_map/ppermute | solution.py:28
  11.2 1.0 %copy-done.1 = bf16[1,128,2048]{2,1,0:T(8,128)(2,1)S(1)} copy-done((bf16[1,128,2048]{2,1,0:T(8,128)(2,1)S(1)}, bf16[1,128,2048]{2,1,0:T(8,128)(2,1)}, u32[]{:S(2)}) %copy-start.1) | copy-done | bytes 524312
  12.3 0.9 copy-done.3
  13.2 2.7 %collective-permute-start.7 = (bf16[1,144,512]{2,1,0:T(8,128)(2,1)S(1)}, bf16[1,144,512]{2,1,0:T(8,128)(2,1)S(1)}, u32[]{:S(2)}, u32[]{:S(2)}) collective-permute-start(bf16[1,144,512]{2,1,0:T(8,128)(2,1)S(1)} %collective-permute-done.refs_1_), channel_id=1, source_target_pairs={{0,4},{4,6},{6,2},{2,0},{1,5},{5,7},{7,3},{3,1},{8,12},{12,14},{14... | collective-permute-start | bytes 442376 | tf_op jit(solution)/shard_map/ppermute | solution.py:28
  15.9 0.9 collective-permute-start.4
  16.9 3.5 %collective-permute-done.3.refs_7_ = bf16[1,128,512]{2,1,0:T(8,128)(2,1)S(1)} collective-permute-done((bf16[1,128,512]{2,1,0:T(8,128)(2,1)}, bf16[1,128,512]{2,1,0:T(8,128)(2,1)S(1)}, u32[]{:S(2)}, u32[]{:S(2)}) %collective-permute-start.3) | collective-permute-done | bytes 131104 | tf_op jit(solution)/shard_map/ppermute | solution.py:28
  20.4 2.5 %collective-permute-start.5 = (bf16[512,128]{1,0:T(8,128)(2,1)S(1)}, bf16[512,128]{1,0:T(8,128)(2,1)S(1)}, u32[]{:S(2)}, u32[]{:S(2)}) collective-permute-start(bf16[512,128]{1,0:T(8,128)(2,1)S(1)} %get-tuple-element.27), channel_id=1, source_target_pairs={{0,6},{4,2},{6,0},{2,4},{1,7},{5,3},{7,1},{3,5},{8,14},{12,10},{14... | collective-permute-start | bytes 393224 | tf_op jit(solution)/shard_map/ppermute | solution.py:28
  22.8 0.9 collective-permute-start.6
  23.8 1.1 %collective-permute-start.8 = (bf16[1,128,512]{2,1,0:T(8,128)(2,1)S(1)}, bf16[1,128,512]{2,1,0:T(8,128)(2,1)S(1)}, u32[]{:S(2)}, u32[]{:S(2)}) collective-permute-start(bf16[1,128,512]{2,1,0:T(8,128)(2,1)S(1)} %collective-permute-done.3.refs_7_), channel_id=1, source_target_pairs={{0,2},{4,0},{6,4},{2,6},{1,3},{5,1},{7,5},{3,7},{8,10},{12,8},{14,... | collective-permute-start | bytes 393224 | tf_op jit(solution)/shard_map/ppermute | solution.py:28
  24.9 2.5 %collective-permute-done.4.refs_1_ = bf16[512,128]{1,0:T(8,128)(2,1)S(1)} collective-permute-done((bf16[512,128]{1,0:T(8,128)(2,1)S(1)}, bf16[512,128]{1,0:T(8,128)(2,1)S(1)}, u32[]{:S(2)}, u32[]{:S(2)}) %collective-permute-start.4) | collective-permute-done | bytes 131104 | tf_op jit(solution)/shard_map/ppermute | solution.py:28
  27.4 4.6 %collective-permute-done.5.refs_2_ = bf16[512,128]{1,0:T(8,128)(2,1)S(1)} collective-permute-done((bf16[512,128]{1,0:T(8,128)(2,1)S(1)}, bf16[512,128]{1,0:T(8,128)(2,1)S(1)}, u32[]{:S(2)}, u32[]{:S(2)}) %collective-permute-start.5) | collective-permute-done | bytes 131104 | tf_op jit(solution)/shard_map/ppermute | solution.py:28
  31.9 4.5 %collective-permute-done.6.refs_3_ = bf16[512,128]{1,0:T(8,128)(2,1)S(1)} collective-permute-done((bf16[512,128]{1,0:T(8,128)(2,1)S(1)}, bf16[512,128]{1,0:T(8,128)(2,1)S(1)}, u32[]{:S(2)}, u32[]{:S(2)}) %collective-permute-start.6) | collective-permute-done | bytes 131104 | tf_op jit(solution)/shard_map/ppermute | solution.py:28
  36.4 0.1 join.1.refs_6_.refs_2_
  36.5 1.6 %collective-permute-start.15 = (bf16[512,512]{1,0:T(8,128)(2,1)S(1)}, bf16[512,512]{1,0:T(8,128)(2,1)S(1)}, u32[]{:S(2)}, u32[]{:S(2)}) collective-permute-start(bf16[512,512]{1,0:T(8,128)(2,1)S(1)} %join.1.refs_6_.refs_2_), channel_id=1, source_target_pairs={{0,16},{8,24},{16,0},{24,8},{1,17},{9,25},{17,1},{25,9},{2,18},{10... | collective-permute-start | bytes 1572872 | tf_op jit(solution)/shard_map/ppermute | solution.py:44
  38.1 1.1 %collective-permute-done.8.refs_6_ = bf16[1,128,512]{2,1,0:T(8,128)(2,1)S(1)} collective-permute-done((bf16[1,128,512]{2,1,0:T(8,128)(2,1)S(1)}, bf16[1,128,512]{2,1,0:T(8,128)(2,1)S(1)}, u32[]{:S(2)}, u32[]{:S(2)}) %collective-permute-start.8) | collective-permute-done | bytes 131104 | tf_op jit(solution)/shard_map/ppermute | solution.py:28
  39.2 2.5 %attend.1 = (bf16[1,128,2048]{2,1,0:T(8,128)(2,1)}, bf16[1,128,1024]{2,1,0:T(8,128)(2,1)S(1)}, bf16[1,128,1024]{2,1,0:T(8,128)(2,1)S(1)}) custom-call(f32[128,128]{1,0:T(8,128)S(1)} %get-tuple-element.22.place_ref, bf16[1,128,2048]{2,1,0:T(8,128)(2,1)S(1)} %get-tuple-element.29.query_ref, bf16[1,144,512]{2,1,0:T(8,128)(2,1)S(1)} %get-tuple-element.24.refs_0_, ...), custom_call_target="tpu_custom_call" | custom-call | tf_op jit(solution)/shard_map/attend/pallas_call | solution.py:245
  41.7 1.5 %collective-permute-start.20 = (bf16[1,128,1024]{2,1,0:T(8,128)(2,1)S(1)}, bf16[1,128,1024]{2,1,0:T(8,128)(2,1)S(1)}, u32[]{:S(2)}, u32[]{:S(2)}) collective-permute-start(bf16[1,128,1024]{2,1,0:T(8,128)(2,1)S(1)} %get-tuple-element.37.refs_0_), channel_id=1, source_target_pairs={{0,16},{8,24},{16,0},{24,8},{1,17},{9,25},{17,1},{25,9},{2,18},{10... | collective-permute-start | bytes 786440 | tf_op jit(solution)/shard_map/ppermute | solution.py:44
  43.2 0.5 collective-permute-start.10
  43.8 3.0 %collective-permute-start.9 = (bf16[1,128,1024]{2,1,0:T(8,128)(2,1)S(1)}, bf16[1,128,1024]{2,1,0:T(8,128)(2,1)S(1)}, u32[]{:S(2)}, u32[]{:S(2)}) collective-permute-start(bf16[1,128,1024]{2,1,0:T(8,128)(2,1)S(1)} %get-tuple-element.34.refs_0_), channel_id=1, source_target_pairs={{0,4},{4,6},{6,2},{2,0},{1,5},{5,7},{7,3},{3,1},{8,12},{12,14},{14... | collective-permute-start | bytes 786440 | tf_op jit(solution)/shard_map/ppermute | solution.py:28
  46.8 4.1 %collective-permute-done.19.refs_1_ = bf16[1,128,1024]{2,1,0:T(8,128)(2,1)S(1)} collective-permute-done((bf16[1,128,1024]{2,1,0:T(8,128)(2,1)S(1)}, bf16[1,128,1024]{2,1,0:T(8,128)(2,1)S(1)}, u32[]{:S(2)}, u32[]{:S(2)}) %collective-permute-start.19) | collective-permute-done | bytes 262176 | tf_op jit(solution)/shard_map/ppermute | solution.py:28
  50.9 6.1 %collective-permute-done.20.refs_3_ = bf16[1,128,1024]{2,1,0:T(8,128)(2,1)S(1)} collective-permute-done((bf16[1,128,1024]{2,1,0:T(8,128)(2,1)S(1)}, bf16[1,128,1024]{2,1,0:T(8,128)(2,1)S(1)}, u32[]{:S(2)}, u32[]{:S(2)}) %collective-permute-start.20) | collective-permute-done | bytes 262176 | tf_op jit(solution)/shard_map/ppermute | solution.py:44
  57.0 1.5 %collective-permute-start.16 = (bf16[512,512]{1,0:T(8,128)(2,1)S(1)}, bf16[512,512]{1,0:T(8,128)(2,1)S(1)}, u32[]{:S(2)}, u32[]{:S(2)}) collective-permute-start(bf16[512,512]{1,0:T(8,128)(2,1)S(1)} %join.1.refs_6_.refs_2_), channel_id=1, source_target_pairs={{0,1},{1,0},{2,3},{3,2},{4,5},{5,4},{6,7},{7,6},{8,9},{9,8},{10,11... | collective-permute-start | bytes 1572872 | tf_op jit(solution)/shard_map/ppermute | solution.py:44
  58.5 3.2 %collective-permute-done.10.refs_3_ = bf16[1,128,1024]{2,1,0:T(8,128)(2,1)S(1)} collective-permute-done((bf16[1,128,1024]{2,1,0:T(8,128)(2,1)S(1)}, bf16[1,128,1024]{2,1,0:T(8,128)(2,1)S(1)}, u32[]{:S(2)}, u32[]{:S(2)}) %collective-permute-start.10) | collective-permute-done | bytes 262176 | tf_op jit(solution)/shard_map/ppermute | solution.py:44
  61.7 1.5 %collective-permute-start.22 = (bf16[1,128,1024]{2,1,0:T(8,128)(2,1)S(1)}, bf16[1,128,1024]{2,1,0:T(8,128)(2,1)S(1)}, u32[]{:S(2)}, u32[]{:S(2)}) collective-permute-start(bf16[1,128,1024]{2,1,0:T(8,128)(2,1)S(1)} %collective-permute-done.19.refs_1_), channel_id=1, source_target_pairs={{0,16},{8,24},{16,0},{24,8},{1,17},{9,25},{17,1},{25,9},{2,18},{10... | collective-permute-start | bytes 786440 | tf_op jit(solution)/shard_map/ppermute | solution.py:44
  63.2 0.6 collective-permute-start.12
  63.8 1.5 %collective-permute-start.17 = (bf16[512,512]{1,0:T(8,128)(2,1)S(1)}, bf16[512,512]{1,0:T(8,128)(2,1)S(1)}, u32[]{:S(2)}, u32[]{:S(2)}) collective-permute-start(bf16[512,512]{1,0:T(8,128)(2,1)S(1)} %collective-permute-done.15.refs_7_.refs_3_), channel_id=1, source_target_pairs={{0,1},{1,0},{2,3},{3,2},{4,5},{5,4},{6,7},{7,6},{8,9},{9,8},{10,11... | collective-permute-start | bytes 1572872 | tf_op jit(solution)/shard_map/ppermute | solution.py:44
  65.3 5.6 %collective-permute-done.22.refs_4_ = bf16[1,128,1024]{2,1,0:T(8,128)(2,1)S(1)} collective-permute-done((bf16[1,128,1024]{2,1,0:T(8,128)(2,1)S(1)}, bf16[1,128,1024]{2,1,0:T(8,128)(2,1)S(1)}, u32[]{:S(2)}, u32[]{:S(2)}) %collective-permute-start.22) | collective-permute-done | bytes 262176 | tf_op jit(solution)/shard_map/ppermute | solution.py:44
  70.9 1.5 %collective-permute-start.24 = (bf16[1,128,1024]{2,1,0:T(8,128)(2,1)S(1)}, bf16[1,128,1024]{2,1,0:T(8,128)(2,1)S(1)}, u32[]{:S(2)}, u32[]{:S(2)}) collective-permute-start(bf16[1,128,1024]{2,1,0:T(8,128)(2,1)S(1)} %collective-permute-done.21.refs_2_), channel_id=1, source_target_pairs={{0,16},{8,24},{16,0},{24,8},{1,17},{9,25},{17,1},{25,9},{2,18},{10... | collective-permute-start | bytes 786440 | tf_op jit(solution)/shard_map/ppermute | solution.py:44
  72.4 4.1 %collective-permute-done.12.refs_4_ = bf16[1,128,1024]{2,1,0:T(8,128)(2,1)S(1)} collective-permute-done((bf16[1,128,1024]{2,1,0:T(8,128)(2,1)S(1)}, bf16[1,128,1024]{2,1,0:T(8,128)(2,1)S(1)}, u32[]{:S(2)}, u32[]{:S(2)}) %collective-permute-start.12) | collective-permute-done | bytes 262176 | tf_op jit(solution)/shard_map/ppermute | solution.py:44
  76.5 1.5 %collective-permute-start.18 = (bf16[1,128,1024]{2,1,0:T(8,128)(2,1)S(1)}, bf16[1,128,1024]{2,1,0:T(8,128)(2,1)S(1)}, u32[]{:S(2)}, u32[]{:S(2)}) collective-permute-start(bf16[1,128,1024]{2,1,0:T(8,128)(2,1)S(1)} %collective-permute-done.11.refs_2_), channel_id=1, source_target_pairs={{0,16},{8,24},{16,0},{24,8},{1,17},{9,25},{17,1},{25,9},{2,18},{10... | collective-permute-start | bytes 786440 | tf_op jit(solution)/shard_map/ppermute | solution.py:44
  78.1 3.0 %collective-permute-start.23 = (bf16[1,128,1024]{2,1,0:T(8,128)(2,1)S(1)}, bf16[1,128,1024]{2,1,0:T(8,128)(2,1)S(1)}, u32[]{:S(2)}, u32[]{:S(2)}) collective-permute-start(bf16[1,128,1024]{2,1,0:T(8,128)(2,1)S(1)} %collective-permute-done.21.refs_2_), channel_id=1, source_target_pairs={{0,4},{4,6},{6,2},{2,0},{1,5},{5,7},{7,3},{3,1},{8,12},{12,14},{14... | collective-permute-start | bytes 786440 | tf_op jit(solution)/shard_map/ppermute | solution.py:28
  81.1 1.1 %collective-permute-done.24.refs_5_ = bf16[1,128,1024]{2,1,0:T(8,128)(2,1)S(1)} collective-permute-done((bf16[1,128,1024]{2,1,0:T(8,128)(2,1)S(1)}, bf16[1,128,1024]{2,1,0:T(8,128)(2,1)S(1)}, u32[]{:S(2)}, u32[]{:S(2)}) %collective-permute-start.24) | collective-permute-done | bytes 262176 | tf_op jit(solution)/shard_map/ppermute | solution.py:44
  82.2 3.6 %collective-permute-done.13.refs_0_ = bf16[1,128,1024]{2,1,0:T(8,128)(2,1)S(1)} collective-permute-done((bf16[1,128,1024]{2,1,0:T(8,128)(2,1)S(1)}, bf16[1,128,1024]{2,1,0:T(8,128)(2,1)S(1)}, u32[]{:S(2)}, u32[]{:S(2)}) %collective-permute-start.13) | collective-permute-done | bytes 262176 | tf_op jit(solution)/shard_map/ppermute | solution.py:28
  85.8 1.5 %collective-permute-start.14 = (bf16[1,128,1024]{2,1,0:T(8,128)(2,1)S(1)}, bf16[1,128,1024]{2,1,0:T(8,128)(2,1)S(1)}, u32[]{:S(2)}, u32[]{:S(2)}) collective-permute-start(bf16[1,128,1024]{2,1,0:T(8,128)(2,1)S(1)} %collective-permute-done.13.refs_0_), channel_id=1, source_target_pairs={{0,16},{8,24},{16,0},{24,8},{1,17},{9,25},{17,1},{25,9},{2,18},{10... | collective-permute-start | bytes 786440 | tf_op jit(solution)/shard_map/ppermute | solution.py:44
  87.3 1.8 %early.3.refs_6_ = f32[1024,1024]{1,0:T(8,128)S(1)} custom-call(bf16[1,128,1024]{2,1,0:T(8,128)(2,1)S(1)} %get-tuple-element.37.refs_0_, bf16[1,128,1024]{2,1,0:T(8,128)(2,1)S(1)} %collective-permute-done.19.refs_1_, bf16[1,128,1024]{2,1,0:T(8,128)(2,1)S(1)} %collective-permute-done.21.refs_2_, bf16[1,128,1024]{2,1,0:T(8,128)(2,1)S(1)} %collective-permute-done.20.refs_3_, ...), custom_call_target="tpu_custom_call" | custom-call | flops 1610612736 | bytes 8388608 | tf_op jit(solution)/shard_map/early/pallas_call | solution.py:275
  89.1 1.8 %early.2.refs_6_ = f32[1024,1024]{1,0:T(8,128)S(1)} custom-call(bf16[1,128,1024]{2,1,0:T(8,128)(2,1)S(1)} %get-tuple-element.34.refs_0_, bf16[1,128,1024]{2,1,0:T(8,128)(2,1)S(1)} %collective-permute-done.9.refs_1_, bf16[1,128,1024]{2,1,0:T(8,128)(2,1)S(1)} %collective-permute-done.11.refs_2_, bf16[1,128,1024]{2,1,0:T(8,128)(2,1)S(1)} %collective-permute-done.10.refs_3_, ...), custom_call_target="tpu_custom_call" | custom-call | flops 1610612736 | bytes 8388608 | tf_op jit(solution)/shard_map/early/pallas_call | solution.py:275
  90.9 1.4 %collective-permute-done.25.refs_1_ = bf16[1,128,1024]{2,1,0:T(8,128)(2,1)S(1)} collective-permute-done((bf16[1,128,1024]{2,1,0:T(8,128)(2,1)S(1)}, bf16[1,128,1024]{2,1,0:T(8,128)(2,1)S(1)}, u32[]{:S(2)}, u32[]{:S(2)}) %collective-permute-start.25) | collective-permute-done | bytes 262176 | tf_op jit(solution)/shard_map/ppermute | solution.py:28
  92.4 2.5 %finish.2.refs_7_ = bf16[1,1024,2048]{2,1,0:T(8,128)(2,1)} custom-call(bf16[1,128,1024]{2,1,0:T(8,128)(2,1)S(1)} %collective-permute-done.23.refs_0_, bf16[1,128,1024]{2,1,0:T(8,128)(2,1)S(1)} %collective-permute-done.25.refs_1_, bf16[512,512]{1,0:T(8,128)(2,1)S(1)} %join.1.refs_6_.refs_2_, bf16[512,512]{1,0:T(8,128)(2,1)S(1)} %collective-permute-done.15.refs_7_.refs_3_, ...), custom_call_target="tpu_custom_call" | custom-call | flops 536870912 | bytes 8388608 | tf_op jit(solution)/shard_map/finish/pallas_call | solution.py:300
  94.9 2.5 %finish.3 = bf16[1,1024,2048]{2,1,0:T(8,128)(2,1)} custom-call(bf16[1,128,1024]{2,1,0:T(8,128)(2,1)S(1)} %collective-permute-done.13.refs_0_, bf16[1,128,1024]{2,1,0:T(8,128)(2,1)S(1)} %collective-permute-done.14.refs_1_, bf16[512,512]{1,0:T(8,128)(2,1)S(1)} %join.1.refs_6_.refs_2_, ...), custom_call_target="tpu_custom_call", output_to_operand_aliasing={{}: (7, {})} | custom-call | flops 536870912 | bytes 8388608 | tf_op jit(solution)/shard_map/finish/pallas_call | solution.py:300
  (23 shorter events, 0.1 us)
Async XLA Ops:
  0.6 1.2 %copy-start = (bf16[1,128,4096]{2,1,0:T(8,128)(2,1)S(1)}, bf16[1,128,4096]{2,1,0:T(8,128)(2,1)}, u32[]{:S(2)}) copy-start(bf16[1,128,4096]{2,1,0:T(8,128)(2,1)} %cot_ref.1) | copy-start | bytes 3145732
  2.0 0.9 copy-start.2
  3.0 0.7 copy-start.4
  4.2 9.0 %collective-permute-start = (bf16[1,144,512]{2,1,0:T(8,128)(2,1)S(1)}, bf16[1,144,512]{2,1,0:T(8,128)(2,1)S(1)}, u32[]{:S(2)}, u32[]{:S(2)}) collective-permute-start(bf16[1,144,512]{2,1,0:T(8,128)(2,1)S(1)} %get-tuple-element.24.refs_0_), channel_id=1, source_target_pairs={{0,4},{4,6},{6,2},{2,0},{1,5},{5,7},{7,3},{3,1},{8,12},{12,14},{14... | collective-permute-start | bytes 442376 | tf_op jit(solution)/shard_map/ppermute | solution.py:28
  8.3 15.5 %collective-permute-start.1 = (bf16[1,144,512]{2,1,0:T(8,128)(2,1)S(1)}, bf16[1,144,512]{2,1,0:T(8,128)(2,1)S(1)}, u32[]{:S(2)}, u32[]{:S(2)}) collective-permute-start(bf16[1,144,512]{2,1,0:T(8,128)(2,1)S(1)} %get-tuple-element.24.refs_0_), channel_id=1, source_target_pairs={{0,2},{4,0},{6,4},{2,6},{1,3},{5,1},{7,5},{3,7},{8,10},{12,8},{14,... | collective-permute-start | bytes 442376 | tf_op jit(solution)/shard_map/ppermute | solution.py:28
  8.3 12.1 %collective-permute-start.3 = (bf16[1,128,512]{2,1,0:T(8,128)(2,1)}, bf16[1,128,512]{2,1,0:T(8,128)(2,1)S(1)}, u32[]{:S(2)}, u32[]{:S(2)}) collective-permute-start(bf16[1,128,512]{2,1,0:T(8,128)(2,1)} %value_ref.1), channel_id=1, source_target_pairs={{0,2},{4,0},{6,4},{2,6},{1,3},{5,1},{7,5},{3,7},{8,10},{12,8},{14,... | collective-permute-start | bytes 393224 | tf_op jit(solution)/shard_map/ppermute | solution.py:28
  10.2 12.7 %collective-permute-start.2 = (bf16[1,128,512]{2,1,0:T(8,128)(2,1)}, bf16[1,128,512]{2,1,0:T(8,128)(2,1)S(1)}, u32[]{:S(2)}, u32[]{:S(2)}) collective-permute-start(bf16[1,128,512]{2,1,0:T(8,128)(2,1)} %value_ref.1), channel_id=1, source_target_pairs={{0,4},{4,6},{6,2},{2,0},{1,5},{5,7},{7,3},{3,1},{8,12},{12,14},{14... | collective-permute-start | bytes 393224 | tf_op jit(solution)/shard_map/ppermute | solution.py:28
  11.2 1.0 %copy-start.1 = (bf16[1,128,2048]{2,1,0:T(8,128)(2,1)S(1)}, bf16[1,128,2048]{2,1,0:T(8,128)(2,1)}, u32[]{:S(2)}) copy-start(bf16[1,128,2048]{2,1,0:T(8,128)(2,1)} %query_ref.1) | copy-start | bytes 1572868
  12.3 0.9 copy-start.3
  13.2 26.0 %collective-permute-start.7 = (bf16[1,144,512]{2,1,0:T(8,128)(2,1)S(1)}, bf16[1,144,512]{2,1,0:T(8,128)(2,1)S(1)}, u32[]{:S(2)}, u32[]{:S(2)}) collective-permute-start(bf16[1,144,512]{2,1,0:T(8,128)(2,1)S(1)} %collective-permute-done.refs_1_), channel_id=1, source_target_pairs={{0,4},{4,6},{6,2},{2,0},{1,5},{5,7},{7,3},{3,1},{8,12},{12,14},{14... | collective-permute-start | bytes 442376 | tf_op jit(solution)/shard_map/ppermute | solution.py:28
  15.9 11.4 %collective-permute-start.4 = (bf16[512,128]{1,0:T(8,128)(2,1)S(1)}, bf16[512,128]{1,0:T(8,128)(2,1)S(1)}, u32[]{:S(2)}, u32[]{:S(2)}) collective-permute-start(bf16[512,128]{1,0:T(8,128)(2,1)S(1)} %get-tuple-element.26), channel_id=1, source_target_pairs={{0,4},{4,6},{6,2},{2,0},{1,5},{5,7},{7,3},{3,1},{8,12},{12,14},{14... | collective-permute-start | bytes 393224 | tf_op jit(solution)/shard_map/ppermute | solution.py:28
  20.4 11.6 %collective-permute-start.5 = (bf16[512,128]{1,0:T(8,128)(2,1)S(1)}, bf16[512,128]{1,0:T(8,128)(2,1)S(1)}, u32[]{:S(2)}, u32[]{:S(2)}) collective-permute-start(bf16[512,128]{1,0:T(8,128)(2,1)S(1)} %get-tuple-element.27), channel_id=1, source_target_pairs={{0,6},{4,2},{6,0},{2,4},{1,7},{5,3},{7,1},{3,5},{8,14},{12,10},{14... | collective-permute-start | bytes 393224 | tf_op jit(solution)/shard_map/ppermute | solution.py:28
  22.8 13.6 %collective-permute-start.6 = (bf16[512,128]{1,0:T(8,128)(2,1)S(1)}, bf16[512,128]{1,0:T(8,128)(2,1)S(1)}, u32[]{:S(2)}, u32[]{:S(2)}) collective-permute-start(bf16[512,128]{1,0:T(8,128)(2,1)S(1)} %get-tuple-element.28), channel_id=1, source_target_pairs={{0,2},{4,0},{6,4},{2,6},{1,3},{5,1},{7,5},{3,7},{8,10},{12,8},{14,... | collective-permute-start | bytes 393224 | tf_op jit(solution)/shard_map/ppermute | solution.py:28
  23.8 15.4 %collective-permute-start.8 = (bf16[1,128,512]{2,1,0:T(8,128)(2,1)S(1)}, bf16[1,128,512]{2,1,0:T(8,128)(2,1)S(1)}, u32[]{:S(2)}, u32[]{:S(2)}) collective-permute-start(bf16[1,128,512]{2,1,0:T(8,128)(2,1)S(1)} %collective-permute-done.3.refs_7_), channel_id=1, source_target_pairs={{0,2},{4,0},{6,4},{2,6},{1,3},{5,1},{7,5},{3,7},{8,10},{12,8},{14,... | collective-permute-start | bytes 393224 | tf_op jit(solution)/shard_map/ppermute | solution.py:28
  36.5 26.7 %collective-permute-start.15 = (bf16[512,512]{1,0:T(8,128)(2,1)S(1)}, bf16[512,512]{1,0:T(8,128)(2,1)S(1)}, u32[]{:S(2)}, u32[]{:S(2)}) collective-permute-start(bf16[512,512]{1,0:T(8,128)(2,1)S(1)} %join.1.refs_6_.refs_2_), channel_id=1, source_target_pairs={{0,16},{8,24},{16,0},{24,8},{1,17},{9,25},{17,1},{25,9},{2,18},{10... | collective-permute-start | bytes 1572872 | tf_op jit(solution)/shard_map/ppermute | solution.py:44
  41.7 9.2 %collective-permute-start.19 = (bf16[1,128,1024]{2,1,0:T(8,128)(2,1)S(1)}, bf16[1,128,1024]{2,1,0:T(8,128)(2,1)S(1)}, u32[]{:S(2)}, u32[]{:S(2)}) collective-permute-start(bf16[1,128,1024]{2,1,0:T(8,128)(2,1)S(1)} %get-tuple-element.37.refs_0_), channel_id=1, source_target_pairs={{0,4},{4,6},{6,2},{2,0},{1,5},{5,7},{7,3},{3,1},{8,12},{12,14},{14... | collective-permute-start | bytes 786440 | tf_op jit(solution)/shard_map/ppermute | solution.py:28
  41.7 15.3 %collective-permute-start.20 = (bf16[1,128,1024]{2,1,0:T(8,128)(2,1)S(1)}, bf16[1,128,1024]{2,1,0:T(8,128)(2,1)S(1)}, u32[]{:S(2)}, u32[]{:S(2)}) collective-permute-start(bf16[1,128,1024]{2,1,0:T(8,128)(2,1)S(1)} %get-tuple-element.37.refs_0_), channel_id=1, source_target_pairs={{0,16},{8,24},{16,0},{24,8},{1,17},{9,25},{17,1},{25,9},{2,18},{10... | collective-permute-start | bytes 786440 | tf_op jit(solution)/shard_map/ppermute | solution.py:44
  43.2 18.4 %collective-permute-start.10 = (bf16[1,128,1024]{2,1,0:T(8,128)(2,1)S(1)}, bf16[1,128,1024]{2,1,0:T(8,128)(2,1)S(1)}, u32[]{:S(2)}, u32[]{:S(2)}) collective-permute-start(bf16[1,128,1024]{2,1,0:T(8,128)(2,1)S(1)} %get-tuple-element.34.refs_0_), channel_id=1, source_target_pairs={{0,16},{8,24},{16,0},{24,8},{1,17},{9,25},{17,1},{25,9},{2,18},{10... | collective-permute-start | bytes 786440 | tf_op jit(solution)/shard_map/ppermute | solution.py:44
  43.8 19.5 %collective-permute-start.9 = (bf16[1,128,1024]{2,1,0:T(8,128)(2,1)S(1)}, bf16[1,128,1024]{2,1,0:T(8,128)(2,1)S(1)}, u32[]{:S(2)}, u32[]{:S(2)}) collective-permute-start(bf16[1,128,1024]{2,1,0:T(8,128)(2,1)S(1)} %get-tuple-element.34.refs_0_), channel_id=1, source_target_pairs={{0,4},{4,6},{6,2},{2,0},{1,5},{5,7},{7,3},{3,1},{8,12},{12,14},{14... | collective-permute-start | bytes 786440 | tf_op jit(solution)/shard_map/ppermute | solution.py:28
  57.0 6.8 %collective-permute-start.21 = (bf16[1,128,1024]{2,1,0:T(8,128)(2,1)S(1)}, bf16[1,128,1024]{2,1,0:T(8,128)(2,1)S(1)}, u32[]{:S(2)}, u32[]{:S(2)}) collective-permute-start(bf16[1,128,1024]{2,1,0:T(8,128)(2,1)S(1)} %collective-permute-done.19.refs_1_), channel_id=1, source_target_pairs={{0,4},{4,6},{6,2},{2,0},{1,5},{5,7},{7,3},{3,1},{8,12},{12,14},{14... | collective-permute-start | bytes 786440 | tf_op jit(solution)/shard_map/ppermute | solution.py:28
  57.0 21.1 %collective-permute-start.16 = (bf16[512,512]{1,0:T(8,128)(2,1)S(1)}, bf16[512,512]{1,0:T(8,128)(2,1)S(1)}, u32[]{:S(2)}, u32[]{:S(2)}) collective-permute-start(bf16[512,512]{1,0:T(8,128)(2,1)S(1)} %join.1.refs_6_.refs_2_), channel_id=1, source_target_pairs={{0,1},{1,0},{2,3},{3,2},{4,5},{5,4},{6,7},{7,6},{8,9},{9,8},{10,11... | collective-permute-start | bytes 1572872 | tf_op jit(solution)/shard_map/ppermute | solution.py:44
  61.7 9.2 %collective-permute-start.22 = (bf16[1,128,1024]{2,1,0:T(8,128)(2,1)S(1)}, bf16[1,128,1024]{2,1,0:T(8,128)(2,1)S(1)}, u32[]{:S(2)}, u32[]{:S(2)}) collective-permute-start(bf16[1,128,1024]{2,1,0:T(8,128)(2,1)S(1)} %collective-permute-done.19.refs_1_), channel_id=1, source_target_pairs={{0,16},{8,24},{16,0},{24,8},{1,17},{9,25},{17,1},{25,9},{2,18},{10... | collective-permute-start | bytes 786440 | tf_op jit(solution)/shard_map/ppermute | solution.py:44
  63.2 9.2 %collective-permute-start.11 = (bf16[1,128,1024]{2,1,0:T(8,128)(2,1)S(1)}, bf16[1,128,1024]{2,1,0:T(8,128)(2,1)S(1)}, u32[]{:S(2)}, u32[]{:S(2)}) collective-permute-start(bf16[1,128,1024]{2,1,0:T(8,128)(2,1)S(1)} %collective-permute-done.9.refs_1_), channel_id=1, source_target_pairs={{0,4},{4,6},{6,2},{2,0},{1,5},{5,7},{7,3},{3,1},{8,12},{12,14},{14... | collective-permute-start | bytes 786440 | tf_op jit(solution)/shard_map/ppermute | solution.py:28
  63.2 13.3 %collective-permute-start.12 = (bf16[1,128,1024]{2,1,0:T(8,128)(2,1)S(1)}, bf16[1,128,1024]{2,1,0:T(8,128)(2,1)S(1)}, u32[]{:S(2)}, u32[]{:S(2)}) collective-permute-start(bf16[1,128,1024]{2,1,0:T(8,128)(2,1)S(1)} %collective-permute-done.9.refs_1_), channel_id=1, source_target_pairs={{0,16},{8,24},{16,0},{24,8},{1,17},{9,25},{17,1},{25,9},{2,18},{10... | collective-permute-start | bytes 786440 | tf_op jit(solution)/shard_map/ppermute | solution.py:44
  63.8 23.5 %collective-permute-start.17 = (bf16[512,512]{1,0:T(8,128)(2,1)S(1)}, bf16[512,512]{1,0:T(8,128)(2,1)S(1)}, u32[]{:S(2)}, u32[]{:S(2)}) collective-permute-start(bf16[512,512]{1,0:T(8,128)(2,1)S(1)} %collective-permute-done.15.refs_7_.refs_3_), channel_id=1, source_target_pairs={{0,1},{1,0},{2,3},{3,2},{4,5},{5,4},{6,7},{7,6},{8,9},{9,8},{10,11... | collective-permute-start | bytes 1572872 | tf_op jit(solution)/shard_map/ppermute | solution.py:44
  70.9 11.2 %collective-permute-start.24 = (bf16[1,128,1024]{2,1,0:T(8,128)(2,1)S(1)}, bf16[1,128,1024]{2,1,0:T(8,128)(2,1)S(1)}, u32[]{:S(2)}, u32[]{:S(2)}) collective-permute-start(bf16[1,128,1024]{2,1,0:T(8,128)(2,1)S(1)} %collective-permute-done.21.refs_2_), channel_id=1, source_target_pairs={{0,16},{8,24},{16,0},{24,8},{1,17},{9,25},{17,1},{25,9},{2,18},{10... | collective-permute-start | bytes 786440 | tf_op jit(solution)/shard_map/ppermute | solution.py:44
  76.5 9.2 %collective-permute-start.13 = (bf16[1,128,1024]{2,1,0:T(8,128)(2,1)S(1)}, bf16[1,128,1024]{2,1,0:T(8,128)(2,1)S(1)}, u32[]{:S(2)}, u32[]{:S(2)}) collective-permute-start(bf16[1,128,1024]{2,1,0:T(8,128)(2,1)S(1)} %collective-permute-done.11.refs_2_), channel_id=1, source_target_pairs={{0,4},{4,6},{6,2},{2,0},{1,5},{5,7},{7,3},{3,1},{8,12},{12,14},{14... | collective-permute-start | bytes 786440 | tf_op jit(solution)/shard_map/ppermute | solution.py:28
  76.5 12.6 %collective-permute-start.18 = (bf16[1,128,1024]{2,1,0:T(8,128)(2,1)S(1)}, bf16[1,128,1024]{2,1,0:T(8,128)(2,1)S(1)}, u32[]{:S(2)}, u32[]{:S(2)}) collective-permute-start(bf16[1,128,1024]{2,1,0:T(8,128)(2,1)S(1)} %collective-permute-done.11.refs_2_), channel_id=1, source_target_pairs={{0,16},{8,24},{16,0},{24,8},{1,17},{9,25},{17,1},{25,9},{2,18},{10... | collective-permute-start | bytes 786440 | tf_op jit(solution)/shard_map/ppermute | solution.py:44
  78.1 12.9 %collective-permute-start.23 = (bf16[1,128,1024]{2,1,0:T(8,128)(2,1)S(1)}, bf16[1,128,1024]{2,1,0:T(8,128)(2,1)S(1)}, u32[]{:S(2)}, u32[]{:S(2)}) collective-permute-start(bf16[1,128,1024]{2,1,0:T(8,128)(2,1)S(1)} %collective-permute-done.21.refs_2_), channel_id=1, source_target_pairs={{0,4},{4,6},{6,2},{2,0},{1,5},{5,7},{7,3},{3,1},{8,12},{12,14},{14... | collective-permute-start | bytes 786440 | tf_op jit(solution)/shard_map/ppermute | solution.py:28
  82.2 10.2 %collective-permute-start.25 = (bf16[1,128,1024]{2,1,0:T(8,128)(2,1)S(1)}, bf16[1,128,1024]{2,1,0:T(8,128)(2,1)S(1)}, u32[]{:S(2)}, u32[]{:S(2)}) collective-permute-start(bf16[1,128,1024]{2,1,0:T(8,128)(2,1)S(1)} %collective-permute-done.24.refs_5_), channel_id=1, source_target_pairs={{0,4},{4,6},{6,2},{2,0},{1,5},{5,7},{7,3},{3,1},{8,12},{12,14},{14... | collective-permute-start | bytes 786440 | tf_op jit(solution)/shard_map/ppermute | solution.py:28
  85.8 9.1 %collective-permute-start.14 = (bf16[1,128,1024]{2,1,0:T(8,128)(2,1)S(1)}, bf16[1,128,1024]{2,1,0:T(8,128)(2,1)S(1)}, u32[]{:S(2)}, u32[]{:S(2)}) collective-permute-start(bf16[1,128,1024]{2,1,0:T(8,128)(2,1)S(1)} %collective-permute-done.13.refs_0_), channel_id=1, source_target_pairs={{0,16},{8,24},{16,0},{24,8},{1,17},{9,25},{17,1},{25,9},{2,18},{10... | collective-permute-start | bytes 786440 | tf_op jit(solution)/shard_map/ppermute | solution.py:44

commit v8 on v7

--- a/solution.py
+++ b/solution.py
@@ -170,9 +170,7 @@
     for at, left in left_sides(cot_refs, tokens, slots):
         for i in range(half // tall):
             here = pl.ds(pl.multiple_of(at * half + i * tall, tall), tall)
-            slot = len(copies) % 2
-            if len(copies) >= 2:
-                copies[-2].wait()
+            slot = len(copies)
             held[slot] = (
                 total_ref[here, :]
                 + jnp.dot(
@@ -185,7 +183,7 @@
                 )
             )
             copies[-1].start()
-    for copy in copies[-2:]:
+    for copy in copies:
         copy.wait()
 
 
@@ -229,7 +227,7 @@
     )(place, queries, values)
     turned = [turned[0]] + [around(turned[s], s) for s in range(1, n)]
     key_edges, value_edges = ([around(x, way) for way in (1, -1)] for x in (packed, values))
-    turned[0] = after(turned[0], *key_edges, *value_edges)
+    turned[0] = after(turned[0], *value_edges)
     mine = pl.pallas_call(
         join_kernel,
         out_shape=jax.ShapeDtypeStruct((half, n * tokens), jnp.bfloat16),
@@ -239,9 +237,8 @@
         name="join",
     )(*turned)
     mine_far = swap(mine, "pipe", far)
-    key_ring = gather(packed, key_edges, 1, lambda x: after(x, query_held))
-    value_ring = gather(values, value_edges, -1, lambda x: after(x, value_held))
-    query_held = after(query_held, mine)
+    key_ring = gather(packed, key_edges, 1, lambda x: after(x, query_held, mine))
+    value_ring = gather(values, value_edges, -1, lambda x: after(x, value_held, mine))
     attention, *pieces = pl.pallas_call(
         functools.partial(attention_kernel, HQ // HK, 1.0 / math.sqrt(HD), n, spans),
         out_shape=[jax.ShapeDtypeStruct(queries.shape, jnp.bfloat16)]
@@ -303,8 +300,8 @@
             in_specs=specs,
             out_specs=ANY,
             scratch_shapes=[
-                pltpu.VMEM((2, tall, chunk), jnp.bfloat16),
-                pltpu.SemaphoreType.DMA((2,)),
+                pltpu.VMEM((features // tall, tall, chunk), jnp.bfloat16),
+                pltpu.SemaphoreType.DMA((features // tall,)),
             ],
             input_output_aliases=aliases,
             compiler_params=params(40),

time: 97.7 us -> 90.3 us (0.924)
  waiting for transfers between devices: 45.5 us -> 41 us
  Pallas kernels: 12.1 us -> 10.3 us
  starting transfers between devices: 34.5 us -> 33.2 us
    ppermute x10, waiting for transfers between devices: 20.1 us -> 9.88 us  [swap(): lax.ppermute(x, axis, [(i, i ^ mask) for i in range(lax.axis_size(axis))])]
    ppermute x16, waiting for transfers between devices: 25.3 us -> 31.2 us  [around(): lax.ppermute(x, 'ctx', [(order[q], order[(q + shift) % n]) for q in range...]
    pallas_call x2, Pallas kernels: 5.09 us -> 3.31 us  [local(): pl.pallas_call(functools.partial(finish_kernel, slots, c * chunk), out_sh...]
    ppermute x16, starting transfers between devices: 21.2 us -> 19.8 us  [around(): lax.ppermute(x, 'ctx', [(order[q], order[(q + shift) % n]) for q in range...]
  transfers between devices with their start and end apart: 26 -> 26, of which waited for: 13 -> 14; matrix products, arithmetic and copies ran while one was open for 0% -> 0% of each run, Pallas kernels for 9% -> 10%
where the time goes in v8:
time: 90.3 us; the launch traced here: 90 us
  waiting for transfers between devices  41 us (45%)
  starting transfers between devices  33.2 us (37%)
  Pallas kernels  10.3 us (11%)
  local copies, waits for them, and re-layouts  4.72 us (5%)
    ppermute x16, waiting for transfers between devices, around(): lax.ppermute(x, 'ctx', [(order[q], order[(q + shift) % n]) for q in range...  31.2 us
    ppermute x16, starting transfers between devices, around(): lax.ppermute(x, 'ctx', [(order[q], order[(q + shift) % n]) for q in range...  19.8 us
    ppermute x10, starting transfers between devices, swap(): lax.ppermute(x, axis, [(i, i ^ mask) for i in range(lax.axis_size(axis))])  13.4 us
    ppermute x10, waiting for transfers between devices, swap(): lax.ppermute(x, axis, [(i, i ^ mask) for i in range(lax.axis_size(axis))])  9.88 us
    unnamed x10, local copies, waits for them, and re-layouts  4.72 us
    pallas_call x2, Pallas kernels, local(): pl.pallas_call(functools.partial(early_kernel, first_slots), out_shape=ja...  3.59 us
    pallas_call x2, Pallas kernels, local(): pl.pallas_call(functools.partial(finish_kernel, slots, c * chunk), out_sh...  3.31 us
    pallas_call x1, Pallas kernels, local(): pl.pallas_call(functools.partial(attention_kernel, HQ // HK, 1.0 / math.s...  2.51 us
  transfers between devices with their start and end apart: 26, of which 14 were waited for; matrix products, arithmetic and copies ran while one was open for 0% of the time, Pallas kernels for 10%

profile of v8, /device:TPU:0, one launch (start us, length us, event | category | flops | bytes accessed | tf_op | source)
XLA Modules:
  0.0 90.0 jit_solution(8697126112202056485)
XLA Ops:
  0.6 3.1 %collective-permute-start.2 = (bf16[1,128,512]{2,1,0:T(8,128)(2,1)}, bf16[1,128,512]{2,1,0:T(8,128)(2,1)S(1)}, u32[]{:S(2)}, u32[]{:S(2)}) collective-permute-start(bf16[1,128,512]{2,1,0:T(8,128)(2,1)} %value_ref.1), channel_id=1, source_target_pairs={{0,2},{4,0},{6,4},{2,6},{1,3},{5,1},{7,5},{3,7},{8,10},{12,8},{14,... | collective-permute-start | bytes 393224 | tf_op jit(solution)/shard_map/ppermute | solution.py:28
  3.7 1.2 %copy-done = bf16[1,128,4096]{2,1,0:T(8,128)(2,1)S(1)} copy-done((bf16[1,128,4096]{2,1,0:T(8,128)(2,1)S(1)}, bf16[1,128,4096]{2,1,0:T(8,128)(2,1)}, u32[]{:S(2)}) %copy-start) | copy-done | bytes 1048600
  4.9 0.2 turn.1
  5.1 0.9 copy-done.2
  6.0 0.7 copy-done.4
  6.7 0.6 pack.1
  7.3 1.1 %collective-permute-start = (bf16[1,144,512]{2,1,0:T(8,128)(2,1)S(1)}, bf16[1,144,512]{2,1,0:T(8,128)(2,1)S(1)}, u32[]{:S(2)}, u32[]{:S(2)}) collective-permute-start(bf16[1,144,512]{2,1,0:T(8,128)(2,1)S(1)} %get-tuple-element.23.refs_0_), channel_id=1, source_target_pairs={{0,4},{4,6},{6,2},{2,0},{1,5},{5,7},{7,3},{3,1},{8,12},{12,14},{14... | collective-permute-start | bytes 442376 | tf_op jit(solution)/shard_map/ppermute | solution.py:28
  8.3 2.0 %collective-permute-start.1 = (bf16[1,128,512]{2,1,0:T(8,128)(2,1)}, bf16[1,128,512]{2,1,0:T(8,128)(2,1)S(1)}, u32[]{:S(2)}, u32[]{:S(2)}) collective-permute-start(bf16[1,128,512]{2,1,0:T(8,128)(2,1)} %value_ref.1), channel_id=1, source_target_pairs={{0,4},{4,6},{6,2},{2,0},{1,5},{5,7},{7,3},{3,1},{8,12},{12,14},{14... | collective-permute-start | bytes 393224 | tf_op jit(solution)/shard_map/ppermute | solution.py:28
  10.3 2.5 %collective-permute-start.3 = (bf16[512,128]{1,0:T(8,128)(2,1)S(1)}, bf16[512,128]{1,0:T(8,128)(2,1)S(1)}, u32[]{:S(2)}, u32[]{:S(2)}) collective-permute-start(bf16[512,128]{1,0:T(8,128)(2,1)S(1)} %get-tuple-element.25), channel_id=1, source_target_pairs={{0,4},{4,6},{6,2},{2,0},{1,5},{5,7},{7,3},{3,1},{8,12},{12,14},{14... | collective-permute-start | bytes 393224 | tf_op jit(solution)/shard_map/ppermute | solution.py:28
  12.8 0.6 collective-permute-start.5
  13.5 1.0 %copy-done.1 = bf16[1,128,2048]{2,1,0:T(8,128)(2,1)S(1)} copy-done((bf16[1,128,2048]{2,1,0:T(8,128)(2,1)S(1)}, bf16[1,128,2048]{2,1,0:T(8,128)(2,1)}, u32[]{:S(2)}) %copy-start.1) | copy-done | bytes 524312
  14.5 0.9 %copy-done.3 = bf16[1,128,512]{2,1,0:T(8,128)(2,1)S(1)} copy-done((bf16[1,128,512]{2,1,0:T(8,128)(2,1)S(1)}, bf16[1,128,512]{2,1,0:T(8,128)(2,1)}, u32[]{:S(2)}) %copy-start.3) | copy-done | bytes 131096
  15.4 2.0 %collective-permute-done.1.refs_5_ = bf16[1,128,512]{2,1,0:T(8,128)(2,1)S(1)} collective-permute-done((bf16[1,128,512]{2,1,0:T(8,128)(2,1)}, bf16[1,128,512]{2,1,0:T(8,128)(2,1)S(1)}, u32[]{:S(2)}, u32[]{:S(2)}) %collective-permute-start.1) | collective-permute-done | bytes 131104 | tf_op jit(solution)/shard_map/ppermute | solution.py:28
  17.4 3.1 %collective-permute-start.7 = (bf16[1,144,512]{2,1,0:T(8,128)(2,1)S(1)}, bf16[1,144,512]{2,1,0:T(8,128)(2,1)S(1)}, u32[]{:S(2)}, u32[]{:S(2)}) collective-permute-start(bf16[1,144,512]{2,1,0:T(8,128)(2,1)S(1)} %get-tuple-element.23.refs_0_), channel_id=1, source_target_pairs={{0,2},{4,0},{6,4},{2,6},{1,3},{5,1},{7,5},{3,7},{8,10},{12,8},{14,... | collective-permute-start | bytes 442376 | tf_op jit(solution)/shard_map/ppermute | solution.py:28
  20.5 5.0 %collective-permute-done.4.refs_2_ = bf16[512,128]{1,0:T(8,128)(2,1)S(1)} collective-permute-done((bf16[512,128]{1,0:T(8,128)(2,1)S(1)}, bf16[512,128]{1,0:T(8,128)(2,1)S(1)}, u32[]{:S(2)}, u32[]{:S(2)}) %collective-permute-start.4) | collective-permute-done | bytes 131104 | tf_op jit(solution)/shard_map/ppermute | solution.py:28
  25.5 4.2 %collective-permute-done.5.refs_3_ = bf16[512,128]{1,0:T(8,128)(2,1)S(1)} collective-permute-done((bf16[512,128]{1,0:T(8,128)(2,1)S(1)}, bf16[512,128]{1,0:T(8,128)(2,1)S(1)}, u32[]{:S(2)}, u32[]{:S(2)}) %collective-permute-start.5) | collective-permute-done | bytes 131104 | tf_op jit(solution)/shard_map/ppermute | solution.py:28
  29.8 2.0 %collective-permute-start.8 = (bf16[1,128,512]{2,1,0:T(8,128)(2,1)S(1)}, bf16[1,128,512]{2,1,0:T(8,128)(2,1)S(1)}, u32[]{:S(2)}, u32[]{:S(2)}) collective-permute-start(bf16[1,128,512]{2,1,0:T(8,128)(2,1)S(1)} %collective-permute-done.2.refs_7_), channel_id=1, source_target_pairs={{0,2},{4,0},{6,4},{2,6},{1,3},{5,1},{7,5},{3,7},{8,10},{12,8},{14,... | collective-permute-start | bytes 393224 | tf_op jit(solution)/shard_map/ppermute | solution.py:28
  31.9 1.5 %collective-permute-start.15 = (bf16[512,512]{1,0:T(8,128)(2,1)S(1)}, bf16[512,512]{1,0:T(8,128)(2,1)S(1)}, u32[]{:S(2)}, u32[]{:S(2)}) collective-permute-start(bf16[512,512]{1,0:T(8,128)(2,1)S(1)} %join.1.refs_6_.refs_2_), channel_id=1, source_target_pairs={{0,16},{8,24},{16,0},{24,8},{1,17},{9,25},{17,1},{25,9},{2,18},{10... | collective-permute-start | bytes 1572872 | tf_op jit(solution)/shard_map/ppermute | solution.py:44
  33.4 2.7 %collective-permute-done.7.refs_3_ = bf16[1,144,512]{2,1,0:T(8,128)(2,1)S(1)} collective-permute-done((bf16[1,144,512]{2,1,0:T(8,128)(2,1)S(1)}, bf16[1,144,512]{2,1,0:T(8,128)(2,1)S(1)}, u32[]{:S(2)}, u32[]{:S(2)}) %collective-permute-start.7) | collective-permute-done | bytes 147488 | tf_op jit(solution)/shard_map/ppermute | solution.py:28
  36.1 2.7 %collective-permute-done.8.refs_6_ = bf16[1,128,512]{2,1,0:T(8,128)(2,1)S(1)} collective-permute-done((bf16[1,128,512]{2,1,0:T(8,128)(2,1)S(1)}, bf16[1,128,512]{2,1,0:T(8,128)(2,1)S(1)}, u32[]{:S(2)}, u32[]{:S(2)}) %collective-permute-start.8) | collective-permute-done | bytes 131104 | tf_op jit(solution)/shard_map/ppermute | solution.py:28
  38.8 1.3 %collective-permute-done.6.refs_2_ = bf16[1,144,512]{2,1,0:T(8,128)(2,1)S(1)} collective-permute-done((bf16[1,144,512]{2,1,0:T(8,128)(2,1)S(1)}, bf16[1,144,512]{2,1,0:T(8,128)(2,1)S(1)}, u32[]{:S(2)}, u32[]{:S(2)}) %collective-permute-start.6) | collective-permute-done | bytes 147488 | tf_op jit(solution)/shard_map/ppermute | solution.py:28
  40.2 2.5 %attend.1 = (bf16[1,128,2048]{2,1,0:T(8,128)(2,1)}, bf16[1,128,1024]{2,1,0:T(8,128)(2,1)S(1)}, bf16[1,128,1024]{2,1,0:T(8,128)(2,1)S(1)}) custom-call(f32[128,128]{1,0:T(8,128)S(1)} %get-tuple-element.21.place_ref, bf16[1,128,2048]{2,1,0:T(8,128)(2,1)S(1)} %get-tuple-element.22.query_ref, bf16[1,144,512]{2,1,0:T(8,128)(2,1)S(1)} %get-tuple-element.23.refs_0_, ...), custom_call_target="tpu_custom_call" | custom-call | tf_op jit(solution)/shard_map/attend/pallas_call | solution.py:242
  42.7 1.5 %collective-permute-start.20 = (bf16[1,128,1024]{2,1,0:T(8,128)(2,1)S(1)}, bf16[1,128,1024]{2,1,0:T(8,128)(2,1)S(1)}, u32[]{:S(2)}, u32[]{:S(2)}) collective-permute-start(bf16[1,128,1024]{2,1,0:T(8,128)(2,1)S(1)} %get-tuple-element.35.refs_0_), channel_id=1, source_target_pairs={{0,16},{8,24},{16,0},{24,8},{1,17},{9,25},{17,1},{25,9},{2,18},{10... | collective-permute-start | bytes 786440 | tf_op jit(solution)/shard_map/ppermute | solution.py:44
  44.2 0.5 collective-permute-start.10
  44.7 0.8 collective-permute-start.9
  45.5 6.4 %collective-permute-done.19.refs_1_ = bf16[1,128,1024]{2,1,0:T(8,128)(2,1)S(1)} collective-permute-done((bf16[1,128,1024]{2,1,0:T(8,128)(2,1)S(1)}, bf16[1,128,1024]{2,1,0:T(8,128)(2,1)S(1)}, u32[]{:S(2)}, u32[]{:S(2)}) %collective-permute-start.19) | collective-permute-done | bytes 262176 | tf_op jit(solution)/shard_map/ppermute | solution.py:28
  51.9 0.9 %collective-permute-start.21 = (bf16[1,128,1024]{2,1,0:T(8,128)(2,1)S(1)}, bf16[1,128,1024]{2,1,0:T(8,128)(2,1)S(1)}, u32[]{:S(2)}, u32[]{:S(2)}) collective-permute-start(bf16[1,128,1024]{2,1,0:T(8,128)(2,1)S(1)} %collective-permute-done.19.refs_1_), channel_id=1, source_target_pairs={{0,4},{4,6},{6,2},{2,0},{1,5},{5,7},{7,3},{3,1},{8,12},{12,14},{14... | collective-permute-start | bytes 786440 | tf_op jit(solution)/shard_map/ppermute | solution.py:28
  52.8 1.5 %collective-permute-start.16 = (bf16[512,512]{1,0:T(8,128)(2,1)S(1)}, bf16[512,512]{1,0:T(8,128)(2,1)S(1)}, u32[]{:S(2)}, u32[]{:S(2)}) collective-permute-start(bf16[512,512]{1,0:T(8,128)(2,1)S(1)} %join.1.refs_6_.refs_2_), channel_id=1, source_target_pairs={{0,1},{1,0},{2,3},{3,2},{4,5},{5,4},{6,7},{7,6},{8,9},{9,8},{10,11... | collective-permute-start | bytes 1572872 | tf_op jit(solution)/shard_map/ppermute | solution.py:44
  54.3 2.0 %collective-permute-done.10.refs_3_ = bf16[1,128,1024]{2,1,0:T(8,128)(2,1)S(1)} collective-permute-done((bf16[1,128,1024]{2,1,0:T(8,128)(2,1)S(1)}, bf16[1,128,1024]{2,1,0:T(8,128)(2,1)S(1)}, u32[]{:S(2)}, u32[]{:S(2)}) %collective-permute-start.10) | collective-permute-done | bytes 262176 | tf_op jit(solution)/shard_map/ppermute | solution.py:44
  56.3 1.5 %collective-permute-start.22 = (bf16[1,128,1024]{2,1,0:T(8,128)(2,1)S(1)}, bf16[1,128,1024]{2,1,0:T(8,128)(2,1)S(1)}, u32[]{:S(2)}, u32[]{:S(2)}) collective-permute-start(bf16[1,128,1024]{2,1,0:T(8,128)(2,1)S(1)} %collective-permute-done.19.refs_1_), channel_id=1, source_target_pairs={{0,16},{8,24},{16,0},{24,8},{1,17},{9,25},{17,1},{25,9},{2,18},{10... | collective-permute-start | bytes 786440 | tf_op jit(solution)/shard_map/ppermute | solution.py:44
  57.8 1.2 %collective-permute-start.11 = (bf16[1,128,1024]{2,1,0:T(8,128)(2,1)S(1)}, bf16[1,128,1024]{2,1,0:T(8,128)(2,1)S(1)}, u32[]{:S(2)}, u32[]{:S(2)}) collective-permute-start(bf16[1,128,1024]{2,1,0:T(8,128)(2,1)S(1)} %collective-permute-done.9.refs_1_), channel_id=1, source_target_pairs={{0,4},{4,6},{6,2},{2,0},{1,5},{5,7},{7,3},{3,1},{8,12},{12,14},{14... | collective-permute-start | bytes 786440 | tf_op jit(solution)/shard_map/ppermute | solution.py:28
  59.1 0.9 collective-permute-start.12
  59.9 3.2 %collective-permute-done.21.refs_2_ = bf16[1,128,1024]{2,1,0:T(8,128)(2,1)S(1)} collective-permute-done((bf16[1,128,1024]{2,1,0:T(8,128)(2,1)S(1)}, bf16[1,128,1024]{2,1,0:T(8,128)(2,1)S(1)}, u32[]{:S(2)}, u32[]{:S(2)}) %collective-permute-start.21) | collective-permute-done | bytes 262176 | tf_op jit(solution)/shard_map/ppermute | solution.py:28
  63.2 1.5 %collective-permute-start.17 = (bf16[512,512]{1,0:T(8,128)(2,1)S(1)}, bf16[512,512]{1,0:T(8,128)(2,1)S(1)}, u32[]{:S(2)}, u32[]{:S(2)}) collective-permute-start(bf16[512,512]{1,0:T(8,128)(2,1)S(1)} %collective-permute-done.15.refs_7_.refs_3_), channel_id=1, source_target_pairs={{0,1},{1,0},{2,3},{3,2},{4,5},{5,4},{6,7},{7,6},{8,9},{9,8},{10,11... | collective-permute-start | bytes 1572872 | tf_op jit(solution)/shard_map/ppermute | solution.py:44
  64.6 0.9 %collective-permute-done.22.refs_4_ = bf16[1,128,1024]{2,1,0:T(8,128)(2,1)S(1)} collective-permute-done((bf16[1,128,1024]{2,1,0:T(8,128)(2,1)S(1)}, bf16[1,128,1024]{2,1,0:T(8,128)(2,1)S(1)}, u32[]{:S(2)}, u32[]{:S(2)}) %collective-permute-start.22) | collective-permute-done | bytes 262176 | tf_op jit(solution)/shard_map/ppermute | solution.py:44
  65.5 1.5 %collective-permute-start.24 = (bf16[1,128,1024]{2,1,0:T(8,128)(2,1)S(1)}, bf16[1,128,1024]{2,1,0:T(8,128)(2,1)S(1)}, u32[]{:S(2)}, u32[]{:S(2)}) collective-permute-start(bf16[1,128,1024]{2,1,0:T(8,128)(2,1)S(1)} %collective-permute-done.21.refs_2_), channel_id=1, source_target_pairs={{0,16},{8,24},{16,0},{24,8},{1,17},{9,25},{17,1},{25,9},{2,18},{10... | collective-permute-start | bytes 786440 | tf_op jit(solution)/shard_map/ppermute | solution.py:44
  67.1 4.1 %collective-permute-done.12.refs_4_ = bf16[1,128,1024]{2,1,0:T(8,128)(2,1)S(1)} collective-permute-done((bf16[1,128,1024]{2,1,0:T(8,128)(2,1)S(1)}, bf16[1,128,1024]{2,1,0:T(8,128)(2,1)S(1)}, u32[]{:S(2)}, u32[]{:S(2)}) %collective-permute-start.12) | collective-permute-done | bytes 262176 | tf_op jit(solution)/shard_map/ppermute | solution.py:44
  71.1 1.2 %collective-permute-start.13 = (bf16[1,128,1024]{2,1,0:T(8,128)(2,1)S(1)}, bf16[1,128,1024]{2,1,0:T(8,128)(2,1)S(1)}, u32[]{:S(2)}, u32[]{:S(2)}) collective-permute-start(bf16[1,128,1024]{2,1,0:T(8,128)(2,1)S(1)} %collective-permute-done.11.refs_2_), channel_id=1, source_target_pairs={{0,4},{4,6},{6,2},{2,0},{1,5},{5,7},{7,3},{3,1},{8,12},{12,14},{14... | collective-permute-start | bytes 786440 | tf_op jit(solution)/shard_map/ppermute | solution.py:28
  72.4 1.5 %collective-permute-start.18 = (bf16[1,128,1024]{2,1,0:T(8,128)(2,1)S(1)}, bf16[1,128,1024]{2,1,0:T(8,128)(2,1)S(1)}, u32[]{:S(2)}, u32[]{:S(2)}) collective-permute-start(bf16[1,128,1024]{2,1,0:T(8,128)(2,1)S(1)} %collective-permute-done.11.refs_2_), channel_id=1, source_target_pairs={{0,16},{8,24},{16,0},{24,8},{1,17},{9,25},{17,1},{25,9},{2,18},{10... | collective-permute-start | bytes 786440 | tf_op jit(solution)/shard_map/ppermute | solution.py:44
  73.9 2.8 %collective-permute-done.24.refs_5_ = bf16[1,128,1024]{2,1,0:T(8,128)(2,1)S(1)} collective-permute-done((bf16[1,128,1024]{2,1,0:T(8,128)(2,1)S(1)}, bf16[1,128,1024]{2,1,0:T(8,128)(2,1)S(1)}, u32[]{:S(2)}, u32[]{:S(2)}) %collective-permute-start.24) | collective-permute-done | bytes 262176 | tf_op jit(solution)/shard_map/ppermute | solution.py:44
  76.8 1.2 %collective-permute-start.25 = (bf16[1,128,1024]{2,1,0:T(8,128)(2,1)S(1)}, bf16[1,128,1024]{2,1,0:T(8,128)(2,1)S(1)}, u32[]{:S(2)}, u32[]{:S(2)}) collective-permute-start(bf16[1,128,1024]{2,1,0:T(8,128)(2,1)S(1)} %collective-permute-done.24.refs_5_), channel_id=1, source_target_pairs={{0,4},{4,6},{6,2},{2,0},{1,5},{5,7},{7,3},{3,1},{8,12},{12,14},{14... | collective-permute-start | bytes 786440 | tf_op jit(solution)/shard_map/ppermute | solution.py:28
  78.0 2.4 %collective-permute-done.13.refs_0_ = bf16[1,128,1024]{2,1,0:T(8,128)(2,1)S(1)} collective-permute-done((bf16[1,128,1024]{2,1,0:T(8,128)(2,1)S(1)}, bf16[1,128,1024]{2,1,0:T(8,128)(2,1)S(1)}, u32[]{:S(2)}, u32[]{:S(2)}) %collective-permute-start.13) | collective-permute-done | bytes 262176 | tf_op jit(solution)/shard_map/ppermute | solution.py:28
  80.4 1.5 %collective-permute-start.14 = (bf16[1,128,1024]{2,1,0:T(8,128)(2,1)S(1)}, bf16[1,128,1024]{2,1,0:T(8,128)(2,1)S(1)}, u32[]{:S(2)}, u32[]{:S(2)}) collective-permute-start(bf16[1,128,1024]{2,1,0:T(8,128)(2,1)S(1)} %collective-permute-done.13.refs_0_), channel_id=1, source_target_pairs={{0,16},{8,24},{16,0},{24,8},{1,17},{9,25},{17,1},{25,9},{2,18},{10... | collective-permute-start | bytes 786440 | tf_op jit(solution)/shard_map/ppermute | solution.py:44
  81.9 1.8 %early.3.refs_6_ = f32[1024,1024]{1,0:T(8,128)S(1)} custom-call(bf16[1,128,1024]{2,1,0:T(8,128)(2,1)S(1)} %get-tuple-element.35.refs_0_, bf16[1,128,1024]{2,1,0:T(8,128)(2,1)S(1)} %collective-permute-done.19.refs_1_, bf16[1,128,1024]{2,1,0:T(8,128)(2,1)S(1)} %collective-permute-done.21.refs_2_, bf16[1,128,1024]{2,1,0:T(8,128)(2,1)S(1)} %collective-permute-done.20.refs_3_, ...), custom_call_target="tpu_custom_call" | custom-call | flops 1610612736 | bytes 8388608 | tf_op jit(solution)/shard_map/early/pallas_call | solution.py:272
  83.7 1.8 %early.2.refs_6_ = f32[1024,1024]{1,0:T(8,128)S(1)} custom-call(bf16[1,128,1024]{2,1,0:T(8,128)(2,1)S(1)} %get-tuple-element.32.refs_0_, bf16[1,128,1024]{2,1,0:T(8,128)(2,1)S(1)} %collective-permute-done.9.refs_1_, bf16[1,128,1024]{2,1,0:T(8,128)(2,1)S(1)} %collective-permute-done.11.refs_2_, bf16[1,128,1024]{2,1,0:T(8,128)(2,1)S(1)} %collective-permute-done.10.refs_3_, ...), custom_call_target="tpu_custom_call" | custom-call | flops 1610612736 | bytes 8388608 | tf_op jit(solution)/shard_map/early/pallas_call | solution.py:272
  85.5 1.2 %collective-permute-done.25.refs_1_ = bf16[1,128,1024]{2,1,0:T(8,128)(2,1)S(1)} collective-permute-done((bf16[1,128,1024]{2,1,0:T(8,128)(2,1)S(1)}, bf16[1,128,1024]{2,1,0:T(8,128)(2,1)S(1)}, u32[]{:S(2)}, u32[]{:S(2)}) %collective-permute-start.25) | collective-permute-done | bytes 262176 | tf_op jit(solution)/shard_map/ppermute | solution.py:28
  86.7 1.6 %finish.2.refs_7_ = bf16[1,1024,2048]{2,1,0:T(8,128)(2,1)} custom-call(bf16[1,128,1024]{2,1,0:T(8,128)(2,1)S(1)} %collective-permute-done.23.refs_0_, bf16[1,128,1024]{2,1,0:T(8,128)(2,1)S(1)} %collective-permute-done.25.refs_1_, bf16[512,512]{1,0:T(8,128)(2,1)S(1)} %join.1.refs_6_.refs_2_, bf16[512,512]{1,0:T(8,128)(2,1)S(1)} %collective-permute-done.15.refs_7_.refs_3_, ...), custom_call_target="tpu_custom_call" | custom-call | flops 536870912 | bytes 8388608 | tf_op jit(solution)/shard_map/finish/pallas_call | solution.py:297
  88.4 1.7 %finish.3 = bf16[1,1024,2048]{2,1,0:T(8,128)(2,1)} custom-call(bf16[1,128,1024]{2,1,0:T(8,128)(2,1)S(1)} %collective-permute-done.13.refs_0_, bf16[1,128,1024]{2,1,0:T(8,128)(2,1)S(1)} %collective-permute-done.14.refs_1_, bf16[512,512]{1,0:T(8,128)(2,1)S(1)} %join.1.refs_6_.refs_2_, ...), custom_call_target="tpu_custom_call", output_to_operand_aliasing={{}: (7, {})} | custom-call | flops 536870912 | bytes 8388608 | tf_op jit(solution)/shard_map/finish/pallas_call | solution.py:297
  (23 shorter events, 0.2 us)
Async XLA Ops:
  0.6 12.2 %collective-permute-start.2 = (bf16[1,128,512]{2,1,0:T(8,128)(2,1)}, bf16[1,128,512]{2,1,0:T(8,128)(2,1)S(1)}, u32[]{:S(2)}, u32[]{:S(2)}) collective-permute-start(bf16[1,128,512]{2,1,0:T(8,128)(2,1)} %value_ref.1), channel_id=1, source_target_pairs={{0,2},{4,0},{6,4},{2,6},{1,3},{5,1},{7,5},{3,7},{8,10},{12,8},{14,... | collective-permute-start | bytes 393224 | tf_op jit(solution)/shard_map/ppermute | solution.py:28
  3.7 1.2 %copy-start = (bf16[1,128,4096]{2,1,0:T(8,128)(2,1)S(1)}, bf16[1,128,4096]{2,1,0:T(8,128)(2,1)}, u32[]{:S(2)}) copy-start(bf16[1,128,4096]{2,1,0:T(8,128)(2,1)} %cot_ref.1) | copy-start | bytes 3145732
  5.1 0.9 %copy-start.2 = (bf16[1,128,512]{2,1,0:T(8,128)(2,1)S(1)}, bf16[1,128,512]{2,1,0:T(8,128)(2,1)}, u32[]{:S(2)}) copy-start(bf16[1,128,512]{2,1,0:T(8,128)(2,1)} %key_ref.1) | copy-start | bytes 393220
  6.0 0.7 copy-start.4
  7.3 22.5 %collective-permute-start = (bf16[1,144,512]{2,1,0:T(8,128)(2,1)S(1)}, bf16[1,144,512]{2,1,0:T(8,128)(2,1)S(1)}, u32[]{:S(2)}, u32[]{:S(2)}) collective-permute-start(bf16[1,144,512]{2,1,0:T(8,128)(2,1)S(1)} %get-tuple-element.23.refs_0_), channel_id=1, source_target_pairs={{0,4},{4,6},{6,2},{2,0},{1,5},{5,7},{7,3},{3,1},{8,12},{12,14},{14... | collective-permute-start | bytes 442376 | tf_op jit(solution)/shard_map/ppermute | solution.py:28
  8.3 9.1 %collective-permute-start.1 = (bf16[1,128,512]{2,1,0:T(8,128)(2,1)}, bf16[1,128,512]{2,1,0:T(8,128)(2,1)S(1)}, u32[]{:S(2)}, u32[]{:S(2)}) collective-permute-start(bf16[1,128,512]{2,1,0:T(8,128)(2,1)} %value_ref.1), channel_id=1, source_target_pairs={{0,4},{4,6},{6,2},{2,0},{1,5},{5,7},{7,3},{3,1},{8,12},{12,14},{14... | collective-permute-start | bytes 393224 | tf_op jit(solution)/shard_map/ppermute | solution.py:28
  10.3 10.1 %collective-permute-start.3 = (bf16[512,128]{1,0:T(8,128)(2,1)S(1)}, bf16[512,128]{1,0:T(8,128)(2,1)S(1)}, u32[]{:S(2)}, u32[]{:S(2)}) collective-permute-start(bf16[512,128]{1,0:T(8,128)(2,1)S(1)} %get-tuple-element.25), channel_id=1, source_target_pairs={{0,4},{4,6},{6,2},{2,0},{1,5},{5,7},{7,3},{3,1},{8,12},{12,14},{14... | collective-permute-start | bytes 393224 | tf_op jit(solution)/shard_map/ppermute | solution.py:28
  12.8 12.7 %collective-permute-start.4 = (bf16[512,128]{1,0:T(8,128)(2,1)S(1)}, bf16[512,128]{1,0:T(8,128)(2,1)S(1)}, u32[]{:S(2)}, u32[]{:S(2)}) collective-permute-start(bf16[512,128]{1,0:T(8,128)(2,1)S(1)} %get-tuple-element.26), channel_id=1, source_target_pairs={{0,6},{4,2},{6,0},{2,4},{1,7},{5,3},{7,1},{3,5},{8,14},{12,10},{14... | collective-permute-start | bytes 393224 | tf_op jit(solution)/shard_map/ppermute | solution.py:28
  12.8 16.8 %collective-permute-start.5 = (bf16[512,128]{1,0:T(8,128)(2,1)S(1)}, bf16[512,128]{1,0:T(8,128)(2,1)S(1)}, u32[]{:S(2)}, u32[]{:S(2)}) collective-permute-start(bf16[512,128]{1,0:T(8,128)(2,1)S(1)} %get-tuple-element.27), channel_id=1, source_target_pairs={{0,2},{4,0},{6,4},{2,6},{1,3},{5,1},{7,5},{3,7},{8,10},{12,8},{14,... | collective-permute-start | bytes 393224 | tf_op jit(solution)/shard_map/ppermute | solution.py:28
  13.5 1.0 %copy-start.1 = (bf16[1,128,2048]{2,1,0:T(8,128)(2,1)S(1)}, bf16[1,128,2048]{2,1,0:T(8,128)(2,1)}, u32[]{:S(2)}) copy-start(bf16[1,128,2048]{2,1,0:T(8,128)(2,1)} %query_ref.1) | copy-start | bytes 1572868
  14.5 0.9 %copy-start.3 = (bf16[1,128,512]{2,1,0:T(8,128)(2,1)S(1)}, bf16[1,128,512]{2,1,0:T(8,128)(2,1)}, u32[]{:S(2)}) copy-start(bf16[1,128,512]{2,1,0:T(8,128)(2,1)} %value_ref.1) | copy-start | bytes 393220
  17.4 18.7 %collective-permute-start.7 = (bf16[1,144,512]{2,1,0:T(8,128)(2,1)S(1)}, bf16[1,144,512]{2,1,0:T(8,128)(2,1)S(1)}, u32[]{:S(2)}, u32[]{:S(2)}) collective-permute-start(bf16[1,144,512]{2,1,0:T(8,128)(2,1)S(1)} %get-tuple-element.23.refs_0_), channel_id=1, source_target_pairs={{0,2},{4,0},{6,4},{2,6},{1,3},{5,1},{7,5},{3,7},{8,10},{12,8},{14,... | collective-permute-start | bytes 442376 | tf_op jit(solution)/shard_map/ppermute | solution.py:28
  29.8 10.4 %collective-permute-start.6 = (bf16[1,144,512]{2,1,0:T(8,128)(2,1)S(1)}, bf16[1,144,512]{2,1,0:T(8,128)(2,1)S(1)}, u32[]{:S(2)}, u32[]{:S(2)}) collective-permute-start(bf16[1,144,512]{2,1,0:T(8,128)(2,1)S(1)} %collective-permute-done.refs_1_), channel_id=1, source_target_pairs={{0,4},{4,6},{6,2},{2,0},{1,5},{5,7},{7,3},{3,1},{8,12},{12,14},{14... | collective-permute-start | bytes 442376 | tf_op jit(solution)/shard_map/ppermute | solution.py:28
  29.8 9.0 %collective-permute-start.8 = (bf16[1,128,512]{2,1,0:T(8,128)(2,1)S(1)}, bf16[1,128,512]{2,1,0:T(8,128)(2,1)S(1)}, u32[]{:S(2)}, u32[]{:S(2)}) collective-permute-start(bf16[1,128,512]{2,1,0:T(8,128)(2,1)S(1)} %collective-permute-done.2.refs_7_), channel_id=1, source_target_pairs={{0,2},{4,0},{6,4},{2,6},{1,3},{5,1},{7,5},{3,7},{8,10},{12,8},{14,... | collective-permute-start | bytes 393224 | tf_op jit(solution)/shard_map/ppermute | solution.py:28
  31.9 27.2 %collective-permute-start.15 = (bf16[512,512]{1,0:T(8,128)(2,1)S(1)}, bf16[512,512]{1,0:T(8,128)(2,1)S(1)}, u32[]{:S(2)}, u32[]{:S(2)}) collective-permute-start(bf16[512,512]{1,0:T(8,128)(2,1)S(1)} %join.1.refs_6_.refs_2_), channel_id=1, source_target_pairs={{0,16},{8,24},{16,0},{24,8},{1,17},{9,25},{17,1},{25,9},{2,18},{10... | collective-permute-start | bytes 1572872 | tf_op jit(solution)/shard_map/ppermute | solution.py:44
  42.7 9.2 %collective-permute-start.19 = (bf16[1,128,1024]{2,1,0:T(8,128)(2,1)S(1)}, bf16[1,128,1024]{2,1,0:T(8,128)(2,1)S(1)}, u32[]{:S(2)}, u32[]{:S(2)}) collective-permute-start(bf16[1,128,1024]{2,1,0:T(8,128)(2,1)S(1)} %get-tuple-element.35.refs_0_), channel_id=1, source_target_pairs={{0,4},{4,6},{6,2},{2,0},{1,5},{5,7},{7,3},{3,1},{8,12},{12,14},{14... | collective-permute-start | bytes 786440 | tf_op jit(solution)/shard_map/ppermute | solution.py:28
  42.7 9.2 %collective-permute-start.20 = (bf16[1,128,1024]{2,1,0:T(8,128)(2,1)S(1)}, bf16[1,128,1024]{2,1,0:T(8,128)(2,1)S(1)}, u32[]{:S(2)}, u32[]{:S(2)}) collective-permute-start(bf16[1,128,1024]{2,1,0:T(8,128)(2,1)S(1)} %get-tuple-element.35.refs_0_), channel_id=1, source_target_pairs={{0,16},{8,24},{16,0},{24,8},{1,17},{9,25},{17,1},{25,9},{2,18},{10... | collective-permute-start | bytes 786440 | tf_op jit(solution)/shard_map/ppermute | solution.py:44
  44.2 12.1 %collective-permute-start.10 = (bf16[1,128,1024]{2,1,0:T(8,128)(2,1)S(1)}, bf16[1,128,1024]{2,1,0:T(8,128)(2,1)S(1)}, u32[]{:S(2)}, u32[]{:S(2)}) collective-permute-start(bf16[1,128,1024]{2,1,0:T(8,128)(2,1)S(1)} %get-tuple-element.32.refs_0_), channel_id=1, source_target_pairs={{0,16},{8,24},{16,0},{24,8},{1,17},{9,25},{17,1},{25,9},{2,18},{10... | collective-permute-start | bytes 786440 | tf_op jit(solution)/shard_map/ppermute | solution.py:44
  44.7 13.1 %collective-permute-start.9 = (bf16[1,128,1024]{2,1,0:T(8,128)(2,1)S(1)}, bf16[1,128,1024]{2,1,0:T(8,128)(2,1)S(1)}, u32[]{:S(2)}, u32[]{:S(2)}) collective-permute-start(bf16[1,128,1024]{2,1,0:T(8,128)(2,1)S(1)} %get-tuple-element.32.refs_0_), channel_id=1, source_target_pairs={{0,4},{4,6},{6,2},{2,0},{1,5},{5,7},{7,3},{3,1},{8,12},{12,14},{14... | collective-permute-start | bytes 786440 | tf_op jit(solution)/shard_map/ppermute | solution.py:28
  51.9 11.2 %collective-permute-start.21 = (bf16[1,128,1024]{2,1,0:T(8,128)(2,1)S(1)}, bf16[1,128,1024]{2,1,0:T(8,128)(2,1)S(1)}, u32[]{:S(2)}, u32[]{:S(2)}) collective-permute-start(bf16[1,128,1024]{2,1,0:T(8,128)(2,1)S(1)} %collective-permute-done.19.refs_1_), channel_id=1, source_target_pairs={{0,4},{4,6},{6,2},{2,0},{1,5},{5,7},{7,3},{3,1},{8,12},{12,14},{14... | collective-permute-start | bytes 786440 | tf_op jit(solution)/shard_map/ppermute | solution.py:28
  52.8 21.1 %collective-permute-start.16 = (bf16[512,512]{1,0:T(8,128)(2,1)S(1)}, bf16[512,512]{1,0:T(8,128)(2,1)S(1)}, u32[]{:S(2)}, u32[]{:S(2)}) collective-permute-start(bf16[512,512]{1,0:T(8,128)(2,1)S(1)} %join.1.refs_6_.refs_2_), channel_id=1, source_target_pairs={{0,1},{1,0},{2,3},{3,2},{4,5},{5,4},{6,7},{7,6},{8,9},{9,8},{10,11... | collective-permute-start | bytes 1572872 | tf_op jit(solution)/shard_map/ppermute | solution.py:44
  56.3 9.2 %collective-permute-start.22 = (bf16[1,128,1024]{2,1,0:T(8,128)(2,1)S(1)}, bf16[1,128,1024]{2,1,0:T(8,128)(2,1)S(1)}, u32[]{:S(2)}, u32[]{:S(2)}) collective-permute-start(bf16[1,128,1024]{2,1,0:T(8,128)(2,1)S(1)} %collective-permute-done.19.refs_1_), channel_id=1, source_target_pairs={{0,16},{8,24},{16,0},{24,8},{1,17},{9,25},{17,1},{25,9},{2,18},{10... | collective-permute-start | bytes 786440 | tf_op jit(solution)/shard_map/ppermute | solution.py:44
  57.8 9.2 %collective-permute-start.11 = (bf16[1,128,1024]{2,1,0:T(8,128)(2,1)S(1)}, bf16[1,128,1024]{2,1,0:T(8,128)(2,1)S(1)}, u32[]{:S(2)}, u32[]{:S(2)}) collective-permute-start(bf16[1,128,1024]{2,1,0:T(8,128)(2,1)S(1)} %collective-permute-done.9.refs_1_), channel_id=1, source_target_pairs={{0,4},{4,6},{6,2},{2,0},{1,5},{5,7},{7,3},{3,1},{8,12},{12,14},{14... | collective-permute-start | bytes 786440 | tf_op jit(solution)/shard_map/ppermute | solution.py:28
  59.1 12.1 %collective-permute-start.12 = (bf16[1,128,1024]{2,1,0:T(8,128)(2,1)S(1)}, bf16[1,128,1024]{2,1,0:T(8,128)(2,1)S(1)}, u32[]{:S(2)}, u32[]{:S(2)}) collective-permute-start(bf16[1,128,1024]{2,1,0:T(8,128)(2,1)S(1)} %collective-permute-done.9.refs_1_), channel_id=1, source_target_pairs={{0,16},{8,24},{16,0},{24,8},{1,17},{9,25},{17,1},{25,9},{2,18},{10... | collective-permute-start | bytes 786440 | tf_op jit(solution)/shard_map/ppermute | solution.py:44
  63.2 18.8 %collective-permute-start.17 = (bf16[512,512]{1,0:T(8,128)(2,1)S(1)}, bf16[512,512]{1,0:T(8,128)(2,1)S(1)}, u32[]{:S(2)}, u32[]{:S(2)}) collective-permute-start(bf16[512,512]{1,0:T(8,128)(2,1)S(1)} %collective-permute-done.15.refs_7_.refs_3_), channel_id=1, source_target_pairs={{0,1},{1,0},{2,3},{3,2},{4,5},{5,4},{6,7},{7,6},{8,9},{9,8},{10,11... | collective-permute-start | bytes 1572872 | tf_op jit(solution)/shard_map/ppermute | solution.py:44
  65.5 11.2 %collective-permute-start.24 = (bf16[1,128,1024]{2,1,0:T(8,128)(2,1)S(1)}, bf16[1,128,1024]{2,1,0:T(8,128)(2,1)S(1)}, u32[]{:S(2)}, u32[]{:S(2)}) collective-permute-start(bf16[1,128,1024]{2,1,0:T(8,128)(2,1)S(1)} %collective-permute-done.21.refs_2_), channel_id=1, source_target_pairs={{0,16},{8,24},{16,0},{24,8},{1,17},{9,25},{17,1},{25,9},{2,18},{10... | collective-permute-start | bytes 786440 | tf_op jit(solution)/shard_map/ppermute | solution.py:44
  71.1 9.2 %collective-permute-start.13 = (bf16[1,128,1024]{2,1,0:T(8,128)(2,1)S(1)}, bf16[1,128,1024]{2,1,0:T(8,128)(2,1)S(1)}, u32[]{:S(2)}, u32[]{:S(2)}) collective-permute-start(bf16[1,128,1024]{2,1,0:T(8,128)(2,1)S(1)} %collective-permute-done.11.refs_2_), channel_id=1, source_target_pairs={{0,4},{4,6},{6,2},{2,0},{1,5},{5,7},{7,3},{3,1},{8,12},{12,14},{14... | collective-permute-start | bytes 786440 | tf_op jit(solution)/shard_map/ppermute | solution.py:28
  72.4 11.3 %collective-permute-start.18 = (bf16[1,128,1024]{2,1,0:T(8,128)(2,1)S(1)}, bf16[1,128,1024]{2,1,0:T(8,128)(2,1)S(1)}, u32[]{:S(2)}, u32[]{:S(2)}) collective-permute-start(bf16[1,128,1024]{2,1,0:T(8,128)(2,1)S(1)} %collective-permute-done.11.refs_2_), channel_id=1, source_target_pairs={{0,16},{8,24},{16,0},{24,8},{1,17},{9,25},{17,1},{25,9},{2,18},{10... | collective-permute-start | bytes 786440 | tf_op jit(solution)/shard_map/ppermute | solution.py:44
  73.9 11.6 %collective-permute-start.23 = (bf16[1,128,1024]{2,1,0:T(8,128)(2,1)S(1)}, bf16[1,128,1024]{2,1,0:T(8,128)(2,1)S(1)}, u32[]{:S(2)}, u32[]{:S(2)}) collective-permute-start(bf16[1,128,1024]{2,1,0:T(8,128)(2,1)S(1)} %collective-permute-done.21.refs_2_), channel_id=1, source_target_pairs={{0,4},{4,6},{6,2},{2,0},{1,5},{5,7},{7,3},{3,1},{8,12},{12,14},{14... | collective-permute-start | bytes 786440 | tf_op jit(solution)/shard_map/ppermute | solution.py:28
  76.8 9.9 %collective-permute-start.25 = (bf16[1,128,1024]{2,1,0:T(8,128)(2,1)S(1)}, bf16[1,128,1024]{2,1,0:T(8,128)(2,1)S(1)}, u32[]{:S(2)}, u32[]{:S(2)}) collective-permute-start(bf16[1,128,1024]{2,1,0:T(8,128)(2,1)S(1)} %collective-permute-done.24.refs_5_), channel_id=1, source_target_pairs={{0,4},{4,6},{6,2},{2,0},{1,5},{5,7},{7,3},{3,1},{8,12},{12,14},{14... | collective-permute-start | bytes 786440 | tf_op jit(solution)/shard_map/ppermute | solution.py:28
  80.4 8.0 %collective-permute-start.14 = (bf16[1,128,1024]{2,1,0:T(8,128)(2,1)S(1)}, bf16[1,128,1024]{2,1,0:T(8,128)(2,1)S(1)}, u32[]{:S(2)}, u32[]{:S(2)}) collective-permute-start(bf16[1,128,1024]{2,1,0:T(8,128)(2,1)S(1)} %collective-permute-done.13.refs_0_), channel_id=1, source_target_pairs={{0,16},{8,24},{16,0},{24,8},{1,17},{9,25},{17,1},{25,9},{2,18},{10... | collective-permute-start | bytes 786440 | tf_op jit(solution)/shard_map/ppermute | solution.py:44

commit v9 on v8

--- a/solution.py
+++ b/solution.py
@@ -227,7 +227,8 @@
     )(place, queries, values)
     turned = [turned[0]] + [around(turned[s], s) for s in range(1, n)]
     key_edges, value_edges = ([around(x, way) for way in (1, -1)] for x in (packed, values))
-    turned[0] = after(turned[0], *value_edges)
+    value_ring = gather(values, value_edges, -1, lambda x: after(x, value_held))
+    turned[0] = after(turned[0], key_edges[1], *value_ring[1:])
     mine = pl.pallas_call(
         join_kernel,
         out_shape=jax.ShapeDtypeStruct((half, n * tokens), jnp.bfloat16),
@@ -238,7 +239,6 @@
     )(*turned)
     mine_far = swap(mine, "pipe", far)
     key_ring = gather(packed, key_edges, 1, lambda x: after(x, query_held, mine))
-    value_ring = gather(values, value_edges, -1, lambda x: after(x, value_held, mine))
     attention, *pieces = pl.pallas_call(
         functools.partial(attention_kernel, HQ // HK, 1.0 / math.sqrt(HD), n, spans),
         out_shape=[jax.ShapeDtypeStruct(queries.shape, jnp.bfloat16)]

time: 90.3 us -> 94.7 us (1.049)
  starting transfers between devices: 33.2 us -> 53.6 us
  waiting for transfers between devices: 41 us -> 25.1 us
    ppermute x16, starting transfers between devices: 19.8 us -> 41.8 us  [around(): lax.ppermute(x, 'ctx', [(order[q], order[(q + shift) % n]) for q in range...]
    ppermute x16, waiting for transfers between devices: 31.2 us -> 17.5 us  [around(): lax.ppermute(x, 'ctx', [(order[q], order[(q + shift) % n]) for q in range...]
    ppermute x10, waiting for transfers between devices: 9.88 us -> 7.62 us  [swap(): lax.ppermute(x, axis, [(i, i ^ mask) for i in range(lax.axis_size(axis))])]
    ppermute x10, starting transfers between devices: 13.4 us -> 11.9 us  [swap(): lax.ppermute(x, axis, [(i, i ^ mask) for i in range(lax.axis_size(axis))])]
  transfers between devices with their start and end apart: 26 -> 26, of which waited for: 14 -> 9; matrix products, arithmetic and copies ran while one was open for 0% -> 0% of each run, Pallas kernels for 10% -> 8%
where the time goes in v9:
time: 94.7 us; the launch traced here: 94.5 us
  starting transfers between devices  53.6 us (57%)
  waiting for transfers between devices  25.1 us (27%)
  Pallas kernels  10.3 us (11%)
  local copies, waits for them, and re-layouts  4.72 us (5%)
    ppermute x16, starting transfers between devices, around(): lax.ppermute(x, 'ctx', [(order[q], order[(q + shift) % n]) for q in range...  41.8 us
    ppermute x16, waiting for transfers between devices, around(): lax.ppermute(x, 'ctx', [(order[q], order[(q + shift) % n]) for q in range...  17.5 us
    ppermute x10, starting transfers between devices, swap(): lax.ppermute(x, axis, [(i, i ^ mask) for i in range(lax.axis_size(axis))])  11.9 us
    ppermute x10, waiting for transfers between devices, swap(): lax.ppermute(x, axis, [(i, i ^ mask) for i in range(lax.axis_size(axis))])  7.62 us
    unnamed x10, local copies, waits for them, and re-layouts  4.72 us
    pallas_call x2, Pallas kernels, local(): pl.pallas_call(functools.partial(early_kernel, first_slots), out_shape=ja...  3.59 us
    pallas_call x2, Pallas kernels, local(): pl.pallas_call(functools.partial(finish_kernel, slots, c * chunk), out_sh...  3.31 us
    pallas_call x1, Pallas kernels, local(): pl.pallas_call(functools.partial(attention_kernel, HQ // HK, 1.0 / math.s...  2.51 us
  transfers between devices with their start and end apart: 26, of which 9 were waited for; matrix products, arithmetic and copies ran while one was open for 0% of the time, Pallas kernels for 8%

profile of v9, /device:TPU:0, one launch (start us, length us, event | category | flops | bytes accessed | tf_op | source)
XLA Modules:
  0.0 94.5 jit_solution(5496978978925938112)
XLA Ops:
  0.6 1.2 %copy-done = bf16[1,128,4096]{2,1,0:T(8,128)(2,1)S(1)} copy-done((bf16[1,128,4096]{2,1,0:T(8,128)(2,1)S(1)}, bf16[1,128,4096]{2,1,0:T(8,128)(2,1)}, u32[]{:S(2)}) %copy-start) | copy-done | bytes 1048600
  1.9 0.2 turn.1
  2.1 0.9 copy-done.2
  3.0 0.7 copy-done.4
  3.6 0.6 pack.1
  4.2 3.1 %collective-permute-start.1 = (bf16[1,144,512]{2,1,0:T(8,128)(2,1)S(1)}, bf16[1,144,512]{2,1,0:T(8,128)(2,1)S(1)}, u32[]{:S(2)}, u32[]{:S(2)}) collective-permute-start(bf16[1,144,512]{2,1,0:T(8,128)(2,1)S(1)} %get-tuple-element.23.refs_0_), channel_id=1, source_target_pairs={{0,2},{4,0},{6,4},{2,6},{1,3},{5,1},{7,5},{3,7},{8,10},{12,8},{14,... | collective-permute-start | bytes 442376 | tf_op jit(solution)/shard_map/ppermute | solution.py:28
  7.3 2.6 %collective-permute-start.3 = (bf16[1,128,512]{2,1,0:T(8,128)(2,1)}, bf16[1,128,512]{2,1,0:T(8,128)(2,1)S(1)}, u32[]{:S(2)}, u32[]{:S(2)}) collective-permute-start(bf16[1,128,512]{2,1,0:T(8,128)(2,1)} %value_ref.1), channel_id=1, source_target_pairs={{0,2},{4,0},{6,4},{2,6},{1,3},{5,1},{7,5},{3,7},{8,10},{12,8},{14,... | collective-permute-start | bytes 393224 | tf_op jit(solution)/shard_map/ppermute | solution.py:28
  9.8 0.3 collective-permute-start.2
  10.2 0.2 collective-permute-start
  10.4 2.9 %collective-permute-start.5 = (bf16[512,128]{1,0:T(8,128)(2,1)S(1)}, bf16[512,128]{1,0:T(8,128)(2,1)S(1)}, u32[]{:S(2)}, u32[]{:S(2)}) collective-permute-start(bf16[512,128]{1,0:T(8,128)(2,1)S(1)} %get-tuple-element.27), channel_id=1, source_target_pairs={{0,4},{4,6},{6,2},{2,0},{1,5},{5,7},{7,3},{3,1},{8,12},{12,14},{14... | collective-permute-start | bytes 393224 | tf_op jit(solution)/shard_map/ppermute | solution.py:28
  13.2 1.0 %copy-done.1 = bf16[1,128,2048]{2,1,0:T(8,128)(2,1)S(1)} copy-done((bf16[1,128,2048]{2,1,0:T(8,128)(2,1)S(1)}, bf16[1,128,2048]{2,1,0:T(8,128)(2,1)}, u32[]{:S(2)}) %copy-start.1) | copy-done | bytes 524312
  14.3 0.9 copy-done.3
  15.2 11.7 %collective-permute-start.4 = (bf16[1,128,512]{2,1,0:T(8,128)(2,1)S(1)}, bf16[1,128,512]{2,1,0:T(8,128)(2,1)S(1)}, u32[]{:S(2)}, u32[]{:S(2)}) collective-permute-start(bf16[1,128,512]{2,1,0:T(8,128)(2,1)S(1)} %collective-permute-done.3.refs_7_), channel_id=1, source_target_pairs={{0,2},{4,0},{6,4},{2,6},{1,3},{5,1},{7,5},{3,7},{8,10},{12,8},{14,... | collective-permute-start | bytes 393224 | tf_op jit(solution)/shard_map/ppermute | solution.py:28
  27.0 2.9 %collective-permute-start.6 = (bf16[512,128]{1,0:T(8,128)(2,1)S(1)}, bf16[512,128]{1,0:T(8,128)(2,1)S(1)}, u32[]{:S(2)}, u32[]{:S(2)}) collective-permute-start(bf16[512,128]{1,0:T(8,128)(2,1)S(1)} %get-tuple-element.28), channel_id=1, source_target_pairs={{0,6},{4,2},{6,0},{2,4},{1,7},{5,3},{7,1},{3,5},{8,14},{12,10},{14... | collective-permute-start | bytes 393224 | tf_op jit(solution)/shard_map/ppermute | solution.py:28
  29.8 0.6 collective-permute-start.7
  30.4 3.8 %collective-permute-done.6.refs_2_ = bf16[512,128]{1,0:T(8,128)(2,1)S(1)} collective-permute-done((bf16[512,128]{1,0:T(8,128)(2,1)S(1)}, bf16[512,128]{1,0:T(8,128)(2,1)S(1)}, u32[]{:S(2)}, u32[]{:S(2)}) %collective-permute-start.6) | collective-permute-done | bytes 131104 | tf_op jit(solution)/shard_map/ppermute | solution.py:28
  34.2 4.3 %collective-permute-done.7.refs_3_ = bf16[512,128]{1,0:T(8,128)(2,1)S(1)} collective-permute-done((bf16[512,128]{1,0:T(8,128)(2,1)S(1)}, bf16[512,128]{1,0:T(8,128)(2,1)S(1)}, u32[]{:S(2)}, u32[]{:S(2)}) %collective-permute-start.7) | collective-permute-done | bytes 131104 | tf_op jit(solution)/shard_map/ppermute | solution.py:28
  38.5 0.1 join.1.refs_6_.refs_2_
  38.7 0.7 collective-permute-start.8
  39.3 1.5 %collective-permute-start.15 = (bf16[512,512]{1,0:T(8,128)(2,1)S(1)}, bf16[512,512]{1,0:T(8,128)(2,1)S(1)}, u32[]{:S(2)}, u32[]{:S(2)}) collective-permute-start(bf16[512,512]{1,0:T(8,128)(2,1)S(1)} %join.1.refs_6_.refs_2_), channel_id=1, source_target_pairs={{0,16},{8,24},{16,0},{24,8},{1,17},{9,25},{17,1},{25,9},{2,18},{10... | collective-permute-start | bytes 1572872 | tf_op jit(solution)/shard_map/ppermute | solution.py:44
  40.8 4.6 %collective-permute-done.8.refs_2_ = bf16[1,144,512]{2,1,0:T(8,128)(2,1)S(1)} collective-permute-done((bf16[1,144,512]{2,1,0:T(8,128)(2,1)S(1)}, bf16[1,144,512]{2,1,0:T(8,128)(2,1)S(1)}, u32[]{:S(2)}, u32[]{:S(2)}) %collective-permute-start.8) | collective-permute-done | bytes 147488 | tf_op jit(solution)/shard_map/ppermute | solution.py:28
  45.4 2.5 %attend.1 = (bf16[1,128,2048]{2,1,0:T(8,128)(2,1)}, bf16[1,128,1024]{2,1,0:T(8,128)(2,1)S(1)}, bf16[1,128,1024]{2,1,0:T(8,128)(2,1)S(1)}) custom-call(f32[128,128]{1,0:T(8,128)S(1)} %get-tuple-element.21.place_ref, bf16[1,128,2048]{2,1,0:T(8,128)(2,1)S(1)} %get-tuple-element.22.query_ref, bf16[1,144,512]{2,1,0:T(8,128)(2,1)S(1)} %get-tuple-element.23.refs_0_, ...), custom_call_target="tpu_custom_call" | custom-call | tf_op jit(solution)/shard_map/attend/pallas_call | solution.py:242
  47.9 1.5 %collective-permute-start.10 = (bf16[1,128,1024]{2,1,0:T(8,128)(2,1)S(1)}, bf16[1,128,1024]{2,1,0:T(8,128)(2,1)S(1)}, u32[]{:S(2)}, u32[]{:S(2)}) collective-permute-start(bf16[1,128,1024]{2,1,0:T(8,128)(2,1)S(1)} %get-tuple-element.32.refs_0_), channel_id=1, source_target_pairs={{0,16},{8,24},{16,0},{24,8},{1,17},{9,25},{17,1},{25,9},{2,18},{10... | collective-permute-start | bytes 786440 | tf_op jit(solution)/shard_map/ppermute | solution.py:44
  49.5 1.0 %collective-permute-start.9 = (bf16[1,128,1024]{2,1,0:T(8,128)(2,1)S(1)}, bf16[1,128,1024]{2,1,0:T(8,128)(2,1)S(1)}, u32[]{:S(2)}, u32[]{:S(2)}) collective-permute-start(bf16[1,128,1024]{2,1,0:T(8,128)(2,1)S(1)} %get-tuple-element.32.refs_0_), channel_id=1, source_target_pairs={{0,4},{4,6},{6,2},{2,0},{1,5},{5,7},{7,3},{3,1},{8,12},{12,14},{14... | collective-permute-start | bytes 786440 | tf_op jit(solution)/shard_map/ppermute | solution.py:28
  50.5 0.4 collective-permute-start.20
  50.9 2.5 %collective-permute-start.19 = (bf16[1,128,1024]{2,1,0:T(8,128)(2,1)S(1)}, bf16[1,128,1024]{2,1,0:T(8,128)(2,1)S(1)}, u32[]{:S(2)}, u32[]{:S(2)}) collective-permute-start(bf16[1,128,1024]{2,1,0:T(8,128)(2,1)S(1)} %get-tuple-element.35.refs_0_), channel_id=1, source_target_pairs={{0,4},{4,6},{6,2},{2,0},{1,5},{5,7},{7,3},{3,1},{8,12},{12,14},{14... | collective-permute-start | bytes 786440 | tf_op jit(solution)/shard_map/ppermute | solution.py:28
  53.4 6.4 %collective-permute-done.10.refs_3_ = bf16[1,128,1024]{2,1,0:T(8,128)(2,1)S(1)} collective-permute-done((bf16[1,128,1024]{2,1,0:T(8,128)(2,1)S(1)}, bf16[1,128,1024]{2,1,0:T(8,128)(2,1)S(1)}, u32[]{:S(2)}, u32[]{:S(2)}) %collective-permute-start.10) | collective-permute-done | bytes 262176 | tf_op jit(solution)/shard_map/ppermute | solution.py:44
  59.7 1.6 %collective-permute-start.12 = (bf16[1,128,1024]{2,1,0:T(8,128)(2,1)S(1)}, bf16[1,128,1024]{2,1,0:T(8,128)(2,1)S(1)}, u32[]{:S(2)}, u32[]{:S(2)}) collective-permute-start(bf16[1,128,1024]{2,1,0:T(8,128)(2,1)S(1)} %collective-permute-done.9.refs_1_), channel_id=1, source_target_pairs={{0,16},{8,24},{16,0},{24,8},{1,17},{9,25},{17,1},{25,9},{2,18},{10... | collective-permute-start | bytes 786440 | tf_op jit(solution)/shard_map/ppermute | solution.py:44
  61.3 1.5 %collective-permute-start.16 = (bf16[512,512]{1,0:T(8,128)(2,1)S(1)}, bf16[512,512]{1,0:T(8,128)(2,1)S(1)}, u32[]{:S(2)}, u32[]{:S(2)}) collective-permute-start(bf16[512,512]{1,0:T(8,128)(2,1)S(1)} %join.1.refs_6_.refs_2_), channel_id=1, source_target_pairs={{0,1},{1,0},{2,3},{3,2},{4,5},{5,4},{6,7},{7,6},{8,9},{9,8},{10,11... | collective-permute-start | bytes 1572872 | tf_op jit(solution)/shard_map/ppermute | solution.py:44
  62.8 0.6 collective-permute-done.20.refs_3_
  63.4 2.7 %collective-permute-start.11 = (bf16[1,128,1024]{2,1,0:T(8,128)(2,1)S(1)}, bf16[1,128,1024]{2,1,0:T(8,128)(2,1)S(1)}, u32[]{:S(2)}, u32[]{:S(2)}) collective-permute-start(bf16[1,128,1024]{2,1,0:T(8,128)(2,1)S(1)} %collective-permute-done.9.refs_1_), channel_id=1, source_target_pairs={{0,4},{4,6},{6,2},{2,0},{1,5},{5,7},{7,3},{3,1},{8,12},{12,14},{14... | collective-permute-start | bytes 786440 | tf_op jit(solution)/shard_map/ppermute | solution.py:28
  66.1 1.5 %collective-permute-start.22 = (bf16[1,128,1024]{2,1,0:T(8,128)(2,1)S(1)}, bf16[1,128,1024]{2,1,0:T(8,128)(2,1)S(1)}, u32[]{:S(2)}, u32[]{:S(2)}) collective-permute-start(bf16[1,128,1024]{2,1,0:T(8,128)(2,1)S(1)} %collective-permute-done.19.refs_1_), channel_id=1, source_target_pairs={{0,16},{8,24},{16,0},{24,8},{1,17},{9,25},{17,1},{25,9},{2,18},{10... | collective-permute-start | bytes 786440 | tf_op jit(solution)/shard_map/ppermute | solution.py:44
  67.7 0.5 collective-permute-start.21
  68.1 1.5 %collective-permute-start.17 = (bf16[512,512]{1,0:T(8,128)(2,1)S(1)}, bf16[512,512]{1,0:T(8,128)(2,1)S(1)}, u32[]{:S(2)}, u32[]{:S(2)}) collective-permute-start(bf16[512,512]{1,0:T(8,128)(2,1)S(1)} %collective-permute-done.15.refs_7_.refs_3_), channel_id=1, source_target_pairs={{0,1},{1,0},{2,3},{3,2},{4,5},{5,4},{6,7},{7,6},{8,9},{9,8},{10,11... | collective-permute-start | bytes 1572872 | tf_op jit(solution)/shard_map/ppermute | solution.py:44
  69.6 2.9 %collective-permute-done.11.refs_2_ = bf16[1,128,1024]{2,1,0:T(8,128)(2,1)S(1)} collective-permute-done((bf16[1,128,1024]{2,1,0:T(8,128)(2,1)S(1)}, bf16[1,128,1024]{2,1,0:T(8,128)(2,1)S(1)}, u32[]{:S(2)}, u32[]{:S(2)}) %collective-permute-start.11) | collective-permute-done | bytes 262176 | tf_op jit(solution)/shard_map/ppermute | solution.py:28
  72.5 3.4 %collective-permute-start.13 = (bf16[1,128,1024]{2,1,0:T(8,128)(2,1)S(1)}, bf16[1,128,1024]{2,1,0:T(8,128)(2,1)S(1)}, u32[]{:S(2)}, u32[]{:S(2)}) collective-permute-start(bf16[1,128,1024]{2,1,0:T(8,128)(2,1)S(1)} %collective-permute-done.11.refs_2_), channel_id=1, source_target_pairs={{0,4},{4,6},{6,2},{2,0},{1,5},{5,7},{7,3},{3,1},{8,12},{12,14},{14... | collective-permute-start | bytes 786440 | tf_op jit(solution)/shard_map/ppermute | solution.py:28
  75.9 1.6 %collective-permute-done.21.refs_2_ = bf16[1,128,1024]{2,1,0:T(8,128)(2,1)S(1)} collective-permute-done((bf16[1,128,1024]{2,1,0:T(8,128)(2,1)S(1)}, bf16[1,128,1024]{2,1,0:T(8,128)(2,1)S(1)}, u32[]{:S(2)}, u32[]{:S(2)}) %collective-permute-start.21) | collective-permute-done | bytes 262176 | tf_op jit(solution)/shard_map/ppermute | solution.py:28
  77.5 1.6 %collective-permute-start.24 = (bf16[1,128,1024]{2,1,0:T(8,128)(2,1)S(1)}, bf16[1,128,1024]{2,1,0:T(8,128)(2,1)S(1)}, u32[]{:S(2)}, u32[]{:S(2)}) collective-permute-start(bf16[1,128,1024]{2,1,0:T(8,128)(2,1)S(1)} %collective-permute-done.21.refs_2_), channel_id=1, source_target_pairs={{0,16},{8,24},{16,0},{24,8},{1,17},{9,25},{17,1},{25,9},{2,18},{10... | collective-permute-start | bytes 786440 | tf_op jit(solution)/shard_map/ppermute | solution.py:44
  79.1 0.5 collective-permute-start.18
  79.5 3.4 %collective-permute-start.23 = (bf16[1,128,1024]{2,1,0:T(8,128)(2,1)S(1)}, bf16[1,128,1024]{2,1,0:T(8,128)(2,1)S(1)}, u32[]{:S(2)}, u32[]{:S(2)}) collective-permute-start(bf16[1,128,1024]{2,1,0:T(8,128)(2,1)S(1)} %collective-permute-done.21.refs_2_), channel_id=1, source_target_pairs={{0,4},{4,6},{6,2},{2,0},{1,5},{5,7},{7,3},{3,1},{8,12},{12,14},{14... | collective-permute-start | bytes 786440 | tf_op jit(solution)/shard_map/ppermute | solution.py:28
  82.9 0.4 collective-permute-start.14
  83.3 0.6 collective-permute-done.24.refs_5_
  83.9 3.4 %collective-permute-start.25 = (bf16[1,128,1024]{2,1,0:T(8,128)(2,1)S(1)}, bf16[1,128,1024]{2,1,0:T(8,128)(2,1)S(1)}, u32[]{:S(2)}, u32[]{:S(2)}) collective-permute-start(bf16[1,128,1024]{2,1,0:T(8,128)(2,1)S(1)} %collective-permute-done.24.refs_5_), channel_id=1, source_target_pairs={{0,4},{4,6},{6,2},{2,0},{1,5},{5,7},{7,3},{3,1},{8,12},{12,14},{14... | collective-permute-start | bytes 786440 | tf_op jit(solution)/shard_map/ppermute | solution.py:28
  87.3 1.8 %early.3.refs_6_ = f32[1024,1024]{1,0:T(8,128)S(1)} custom-call(bf16[1,128,1024]{2,1,0:T(8,128)(2,1)S(1)} %get-tuple-element.35.refs_0_, bf16[1,128,1024]{2,1,0:T(8,128)(2,1)S(1)} %collective-permute-done.19.refs_1_, bf16[1,128,1024]{2,1,0:T(8,128)(2,1)S(1)} %collective-permute-done.21.refs_2_, bf16[1,128,1024]{2,1,0:T(8,128)(2,1)S(1)} %collective-permute-done.20.refs_3_, ...), custom_call_target="tpu_custom_call" | custom-call | flops 1610612736 | bytes 8388608 | tf_op jit(solution)/shard_map/early/pallas_call | solution.py:272
  89.1 1.8 %early.2.refs_6_ = f32[1024,1024]{1,0:T(8,128)S(1)} custom-call(bf16[1,128,1024]{2,1,0:T(8,128)(2,1)S(1)} %get-tuple-element.32.refs_0_, bf16[1,128,1024]{2,1,0:T(8,128)(2,1)S(1)} %collective-permute-done.9.refs_1_, bf16[1,128,1024]{2,1,0:T(8,128)(2,1)S(1)} %collective-permute-done.11.refs_2_, bf16[1,128,1024]{2,1,0:T(8,128)(2,1)S(1)} %collective-permute-done.10.refs_3_, ...), custom_call_target="tpu_custom_call" | custom-call | flops 1610612736 | bytes 8388608 | tf_op jit(solution)/shard_map/early/pallas_call | solution.py:272
  90.9 0.3 collective-permute-done.25.refs_1_
  91.2 1.6 %finish.2.refs_7_ = bf16[1,1024,2048]{2,1,0:T(8,128)(2,1)} custom-call(bf16[1,128,1024]{2,1,0:T(8,128)(2,1)S(1)} %collective-permute-done.23.refs_0_, bf16[1,128,1024]{2,1,0:T(8,128)(2,1)S(1)} %collective-permute-done.25.refs_1_, bf16[512,512]{1,0:T(8,128)(2,1)S(1)} %join.1.refs_6_.refs_2_, bf16[512,512]{1,0:T(8,128)(2,1)S(1)} %collective-permute-done.15.refs_7_.refs_3_, ...), custom_call_target="tpu_custom_call" | custom-call | flops 536870912 | bytes 8388608 | tf_op jit(solution)/shard_map/finish/pallas_call | solution.py:297
  92.8 1.7 %finish.3 = bf16[1,1024,2048]{2,1,0:T(8,128)(2,1)} custom-call(bf16[1,128,1024]{2,1,0:T(8,128)(2,1)S(1)} %collective-permute-done.13.refs_0_, bf16[1,128,1024]{2,1,0:T(8,128)(2,1)S(1)} %collective-permute-done.14.refs_1_, bf16[512,512]{1,0:T(8,128)(2,1)S(1)} %join.1.refs_6_.refs_2_, ...), custom_call_target="tpu_custom_call", output_to_operand_aliasing={{}: (7, {})} | custom-call | flops 536870912 | bytes 8388608 | tf_op jit(solution)/shard_map/finish/pallas_call | solution.py:297
  (23 shorter events, 0.1 us)
Async XLA Ops:
  0.6 1.2 %copy-start = (bf16[1,128,4096]{2,1,0:T(8,128)(2,1)S(1)}, bf16[1,128,4096]{2,1,0:T(8,128)(2,1)}, u32[]{:S(2)}) copy-start(bf16[1,128,4096]{2,1,0:T(8,128)(2,1)} %cot_ref.1) | copy-start | bytes 3145732
  2.0 0.9 copy-start.2
  3.0 0.7 copy-start.4
  4.2 25.6 %collective-permute-start.1 = (bf16[1,144,512]{2,1,0:T(8,128)(2,1)S(1)}, bf16[1,144,512]{2,1,0:T(8,128)(2,1)S(1)}, u32[]{:S(2)}, u32[]{:S(2)}) collective-permute-start(bf16[1,144,512]{2,1,0:T(8,128)(2,1)S(1)} %get-tuple-element.23.refs_0_), channel_id=1, source_target_pairs={{0,2},{4,0},{6,4},{2,6},{1,3},{5,1},{7,5},{3,7},{8,10},{12,8},{14,... | collective-permute-start | bytes 442376 | tf_op jit(solution)/shard_map/ppermute | solution.py:28
  7.3 8.0 %collective-permute-start.3 = (bf16[1,128,512]{2,1,0:T(8,128)(2,1)}, bf16[1,128,512]{2,1,0:T(8,128)(2,1)S(1)}, u32[]{:S(2)}, u32[]{:S(2)}) collective-permute-start(bf16[1,128,512]{2,1,0:T(8,128)(2,1)} %value_ref.1), channel_id=1, source_target_pairs={{0,2},{4,0},{6,4},{2,6},{1,3},{5,1},{7,5},{3,7},{8,10},{12,8},{14,... | collective-permute-start | bytes 393224 | tf_op jit(solution)/shard_map/ppermute | solution.py:28
  9.8 17.1 %collective-permute-start.2 = (bf16[1,128,512]{2,1,0:T(8,128)(2,1)}, bf16[1,128,512]{2,1,0:T(8,128)(2,1)S(1)}, u32[]{:S(2)}, u32[]{:S(2)}) collective-permute-start(bf16[1,128,512]{2,1,0:T(8,128)(2,1)} %value_ref.1), channel_id=1, source_target_pairs={{0,4},{4,6},{6,2},{2,0},{1,5},{5,7},{7,3},{3,1},{8,12},{12,14},{14... | collective-permute-start | bytes 393224 | tf_op jit(solution)/shard_map/ppermute | solution.py:28
  10.2 28.5 %collective-permute-start = (bf16[1,144,512]{2,1,0:T(8,128)(2,1)S(1)}, bf16[1,144,512]{2,1,0:T(8,128)(2,1)S(1)}, u32[]{:S(2)}, u32[]{:S(2)}) collective-permute-start(bf16[1,144,512]{2,1,0:T(8,128)(2,1)S(1)} %get-tuple-element.23.refs_0_), channel_id=1, source_target_pairs={{0,4},{4,6},{6,2},{2,0},{1,5},{5,7},{7,3},{3,1},{8,12},{12,14},{14... | collective-permute-start | bytes 442376 | tf_op jit(solution)/shard_map/ppermute | solution.py:28
  10.4 20.1 %collective-permute-start.5 = (bf16[512,128]{1,0:T(8,128)(2,1)S(1)}, bf16[512,128]{1,0:T(8,128)(2,1)S(1)}, u32[]{:S(2)}, u32[]{:S(2)}) collective-permute-start(bf16[512,128]{1,0:T(8,128)(2,1)S(1)} %get-tuple-element.27), channel_id=1, source_target_pairs={{0,4},{4,6},{6,2},{2,0},{1,5},{5,7},{7,3},{3,1},{8,12},{12,14},{14... | collective-permute-start | bytes 393224 | tf_op jit(solution)/shard_map/ppermute | solution.py:28
  13.2 1.0 %copy-start.1 = (bf16[1,128,2048]{2,1,0:T(8,128)(2,1)S(1)}, bf16[1,128,2048]{2,1,0:T(8,128)(2,1)}, u32[]{:S(2)}) copy-start(bf16[1,128,2048]{2,1,0:T(8,128)(2,1)} %query_ref.1) | copy-start | bytes 1572868
  14.3 0.9 copy-start.3
  15.2 15.2 %collective-permute-start.4 = (bf16[1,128,512]{2,1,0:T(8,128)(2,1)S(1)}, bf16[1,128,512]{2,1,0:T(8,128)(2,1)S(1)}, u32[]{:S(2)}, u32[]{:S(2)}) collective-permute-start(bf16[1,128,512]{2,1,0:T(8,128)(2,1)S(1)} %collective-permute-done.3.refs_7_), channel_id=1, source_target_pairs={{0,2},{4,0},{6,4},{2,6},{1,3},{5,1},{7,5},{3,7},{8,10},{12,8},{14,... | collective-permute-start | bytes 393224 | tf_op jit(solution)/shard_map/ppermute | solution.py:28
  27.0 7.3 %collective-permute-start.6 = (bf16[512,128]{1,0:T(8,128)(2,1)S(1)}, bf16[512,128]{1,0:T(8,128)(2,1)S(1)}, u32[]{:S(2)}, u32[]{:S(2)}) collective-permute-start(bf16[512,128]{1,0:T(8,128)(2,1)S(1)} %get-tuple-element.28), channel_id=1, source_target_pairs={{0,6},{4,2},{6,0},{2,4},{1,7},{5,3},{7,1},{3,5},{8,14},{12,10},{14... | collective-permute-start | bytes 393224 | tf_op jit(solution)/shard_map/ppermute | solution.py:28
  29.8 8.7 %collective-permute-start.7 = (bf16[512,128]{1,0:T(8,128)(2,1)S(1)}, bf16[512,128]{1,0:T(8,128)(2,1)S(1)}, u32[]{:S(2)}, u32[]{:S(2)}) collective-permute-start(bf16[512,128]{1,0:T(8,128)(2,1)S(1)} %get-tuple-element.29), channel_id=1, source_target_pairs={{0,2},{4,0},{6,4},{2,6},{1,3},{5,1},{7,5},{3,7},{8,10},{12,8},{14,... | collective-permute-start | bytes 393224 | tf_op jit(solution)/shard_map/ppermute | solution.py:28
  38.7 6.8 %collective-permute-start.8 = (bf16[1,144,512]{2,1,0:T(8,128)(2,1)S(1)}, bf16[1,144,512]{2,1,0:T(8,128)(2,1)S(1)}, u32[]{:S(2)}, u32[]{:S(2)}) collective-permute-start(bf16[1,144,512]{2,1,0:T(8,128)(2,1)S(1)} %collective-permute-done.refs_1_), channel_id=1, source_target_pairs={{0,4},{4,6},{6,2},{2,0},{1,5},{5,7},{7,3},{3,1},{8,12},{12,14},{14... | collective-permute-start | bytes 442376 | tf_op jit(solution)/shard_map/ppermute | solution.py:28
  39.3 28.3 %collective-permute-start.15 = (bf16[512,512]{1,0:T(8,128)(2,1)S(1)}, bf16[512,512]{1,0:T(8,128)(2,1)S(1)}, u32[]{:S(2)}, u32[]{:S(2)}) collective-permute-start(bf16[512,512]{1,0:T(8,128)(2,1)S(1)} %join.1.refs_6_.refs_2_), channel_id=1, source_target_pairs={{0,16},{8,24},{16,0},{24,8},{1,17},{9,25},{17,1},{25,9},{2,18},{10... | collective-permute-start | bytes 1572872 | tf_op jit(solution)/shard_map/ppermute | solution.py:44
  47.9 11.8 %collective-permute-start.10 = (bf16[1,128,1024]{2,1,0:T(8,128)(2,1)S(1)}, bf16[1,128,1024]{2,1,0:T(8,128)(2,1)S(1)}, u32[]{:S(2)}, u32[]{:S(2)}) collective-permute-start(bf16[1,128,1024]{2,1,0:T(8,128)(2,1)S(1)} %get-tuple-element.32.refs_0_), channel_id=1, source_target_pairs={{0,16},{8,24},{16,0},{24,8},{1,17},{9,25},{17,1},{25,9},{2,18},{10... | collective-permute-start | bytes 786440 | tf_op jit(solution)/shard_map/ppermute | solution.py:44
  49.5 10.3 %collective-permute-start.9 = (bf16[1,128,1024]{2,1,0:T(8,128)(2,1)S(1)}, bf16[1,128,1024]{2,1,0:T(8,128)(2,1)S(1)}, u32[]{:S(2)}, u32[]{:S(2)}) collective-permute-start(bf16[1,128,1024]{2,1,0:T(8,128)(2,1)S(1)} %get-tuple-element.32.refs_0_), channel_id=1, source_target_pairs={{0,4},{4,6},{6,2},{2,0},{1,5},{5,7},{7,3},{3,1},{8,12},{12,14},{14... | collective-permute-start | bytes 786440 | tf_op jit(solution)/shard_map/ppermute | solution.py:28
  50.5 12.9 %collective-permute-start.20 = (bf16[1,128,1024]{2,1,0:T(8,128)(2,1)S(1)}, bf16[1,128,1024]{2,1,0:T(8,128)(2,1)S(1)}, u32[]{:S(2)}, u32[]{:S(2)}) collective-permute-start(bf16[1,128,1024]{2,1,0:T(8,128)(2,1)S(1)} %get-tuple-element.35.refs_0_), channel_id=1, source_target_pairs={{0,16},{8,24},{16,0},{24,8},{1,17},{9,25},{17,1},{25,9},{2,18},{10... | collective-permute-start | bytes 786440 | tf_op jit(solution)/shard_map/ppermute | solution.py:44
  50.9 15.3 %collective-permute-start.19 = (bf16[1,128,1024]{2,1,0:T(8,128)(2,1)S(1)}, bf16[1,128,1024]{2,1,0:T(8,128)(2,1)S(1)}, u32[]{:S(2)}, u32[]{:S(2)}) collective-permute-start(bf16[1,128,1024]{2,1,0:T(8,128)(2,1)S(1)} %get-tuple-element.35.refs_0_), channel_id=1, source_target_pairs={{0,4},{4,6},{6,2},{2,0},{1,5},{5,7},{7,3},{3,1},{8,12},{12,14},{14... | collective-permute-start | bytes 786440 | tf_op jit(solution)/shard_map/ppermute | solution.py:28
  59.7 8.4 %collective-permute-start.12 = (bf16[1,128,1024]{2,1,0:T(8,128)(2,1)S(1)}, bf16[1,128,1024]{2,1,0:T(8,128)(2,1)S(1)}, u32[]{:S(2)}, u32[]{:S(2)}) collective-permute-start(bf16[1,128,1024]{2,1,0:T(8,128)(2,1)S(1)} %collective-permute-done.9.refs_1_), channel_id=1, source_target_pairs={{0,16},{8,24},{16,0},{24,8},{1,17},{9,25},{17,1},{25,9},{2,18},{10... | collective-permute-start | bytes 786440 | tf_op jit(solution)/shard_map/ppermute | solution.py:44
  61.3 18.2 %collective-permute-start.16 = (bf16[512,512]{1,0:T(8,128)(2,1)S(1)}, bf16[512,512]{1,0:T(8,128)(2,1)S(1)}, u32[]{:S(2)}, u32[]{:S(2)}) collective-permute-start(bf16[512,512]{1,0:T(8,128)(2,1)S(1)} %join.1.refs_6_.refs_2_), channel_id=1, source_target_pairs={{0,1},{1,0},{2,3},{3,2},{4,5},{5,4},{6,7},{7,6},{8,9},{9,8},{10,11... | collective-permute-start | bytes 1572872 | tf_op jit(solution)/shard_map/ppermute | solution.py:44
  63.4 9.1 %collective-permute-start.11 = (bf16[1,128,1024]{2,1,0:T(8,128)(2,1)S(1)}, bf16[1,128,1024]{2,1,0:T(8,128)(2,1)S(1)}, u32[]{:S(2)}, u32[]{:S(2)}) collective-permute-start(bf16[1,128,1024]{2,1,0:T(8,128)(2,1)S(1)} %collective-permute-done.9.refs_1_), channel_id=1, source_target_pairs={{0,4},{4,6},{6,2},{2,0},{1,5},{5,7},{7,3},{3,1},{8,12},{12,14},{14... | collective-permute-start | bytes 786440 | tf_op jit(solution)/shard_map/ppermute | solution.py:28
  66.1 9.8 %collective-permute-start.22 = (bf16[1,128,1024]{2,1,0:T(8,128)(2,1)S(1)}, bf16[1,128,1024]{2,1,0:T(8,128)(2,1)S(1)}, u32[]{:S(2)}, u32[]{:S(2)}) collective-permute-start(bf16[1,128,1024]{2,1,0:T(8,128)(2,1)S(1)} %collective-permute-done.19.refs_1_), channel_id=1, source_target_pairs={{0,16},{8,24},{16,0},{24,8},{1,17},{9,25},{17,1},{25,9},{2,18},{10... | collective-permute-start | bytes 786440 | tf_op jit(solution)/shard_map/ppermute | solution.py:44
  67.7 9.9 %collective-permute-start.21 = (bf16[1,128,1024]{2,1,0:T(8,128)(2,1)S(1)}, bf16[1,128,1024]{2,1,0:T(8,128)(2,1)S(1)}, u32[]{:S(2)}, u32[]{:S(2)}) collective-permute-start(bf16[1,128,1024]{2,1,0:T(8,128)(2,1)S(1)} %collective-permute-done.19.refs_1_), channel_id=1, source_target_pairs={{0,4},{4,6},{6,2},{2,0},{1,5},{5,7},{7,3},{3,1},{8,12},{12,14},{14... | collective-permute-start | bytes 786440 | tf_op jit(solution)/shard_map/ppermute | solution.py:28
  68.1 19.1 %collective-permute-start.17 = (bf16[512,512]{1,0:T(8,128)(2,1)S(1)}, bf16[512,512]{1,0:T(8,128)(2,1)S(1)}, u32[]{:S(2)}, u32[]{:S(2)}) collective-permute-start(bf16[512,512]{1,0:T(8,128)(2,1)S(1)} %collective-permute-done.15.refs_7_.refs_3_), channel_id=1, source_target_pairs={{0,1},{1,0},{2,3},{3,2},{4,5},{5,4},{6,7},{7,6},{8,9},{9,8},{10,11... | collective-permute-start | bytes 1572872 | tf_op jit(solution)/shard_map/ppermute | solution.py:44
  72.5 10.4 %collective-permute-start.13 = (bf16[1,128,1024]{2,1,0:T(8,128)(2,1)S(1)}, bf16[1,128,1024]{2,1,0:T(8,128)(2,1)S(1)}, u32[]{:S(2)}, u32[]{:S(2)}) collective-permute-start(bf16[1,128,1024]{2,1,0:T(8,128)(2,1)S(1)} %collective-permute-done.11.refs_2_), channel_id=1, source_target_pairs={{0,4},{4,6},{6,2},{2,0},{1,5},{5,7},{7,3},{3,1},{8,12},{12,14},{14... | collective-permute-start | bytes 786440 | tf_op jit(solution)/shard_map/ppermute | solution.py:28
  77.5 6.4 %collective-permute-start.24 = (bf16[1,128,1024]{2,1,0:T(8,128)(2,1)S(1)}, bf16[1,128,1024]{2,1,0:T(8,128)(2,1)S(1)}, u32[]{:S(2)}, u32[]{:S(2)}) collective-permute-start(bf16[1,128,1024]{2,1,0:T(8,128)(2,1)S(1)} %collective-permute-done.21.refs_2_), channel_id=1, source_target_pairs={{0,16},{8,24},{16,0},{24,8},{1,17},{9,25},{17,1},{25,9},{2,18},{10... | collective-permute-start | bytes 786440 | tf_op jit(solution)/shard_map/ppermute | solution.py:44
  79.1 10.0 %collective-permute-start.18 = (bf16[1,128,1024]{2,1,0:T(8,128)(2,1)S(1)}, bf16[1,128,1024]{2,1,0:T(8,128)(2,1)S(1)}, u32[]{:S(2)}, u32[]{:S(2)}) collective-permute-start(bf16[1,128,1024]{2,1,0:T(8,128)(2,1)S(1)} %collective-permute-done.11.refs_2_), channel_id=1, source_target_pairs={{0,16},{8,24},{16,0},{24,8},{1,17},{9,25},{17,1},{25,9},{2,18},{10... | collective-permute-start | bytes 786440 | tf_op jit(solution)/shard_map/ppermute | solution.py:44
  79.5 11.3 %collective-permute-start.23 = (bf16[1,128,1024]{2,1,0:T(8,128)(2,1)S(1)}, bf16[1,128,1024]{2,1,0:T(8,128)(2,1)S(1)}, u32[]{:S(2)}, u32[]{:S(2)}) collective-permute-start(bf16[1,128,1024]{2,1,0:T(8,128)(2,1)S(1)} %collective-permute-done.21.refs_2_), channel_id=1, source_target_pairs={{0,4},{4,6},{6,2},{2,0},{1,5},{5,7},{7,3},{3,1},{8,12},{12,14},{14... | collective-permute-start | bytes 786440 | tf_op jit(solution)/shard_map/ppermute | solution.py:28
  82.9 9.9 %collective-permute-start.14 = (bf16[1,128,1024]{2,1,0:T(8,128)(2,1)S(1)}, bf16[1,128,1024]{2,1,0:T(8,128)(2,1)S(1)}, u32[]{:S(2)}, u32[]{:S(2)}) collective-permute-start(bf16[1,128,1024]{2,1,0:T(8,128)(2,1)S(1)} %collective-permute-done.13.refs_0_), channel_id=1, source_target_pairs={{0,16},{8,24},{16,0},{24,8},{1,17},{9,25},{17,1},{25,9},{2,18},{10... | collective-permute-start | bytes 786440 | tf_op jit(solution)/shard_map/ppermute | solution.py:44
  83.9 7.3 %collective-permute-start.25 = (bf16[1,128,1024]{2,1,0:T(8,128)(2,1)S(1)}, bf16[1,128,1024]{2,1,0:T(8,128)(2,1)S(1)}, u32[]{:S(2)}, u32[]{:S(2)}) collective-permute-start(bf16[1,128,1024]{2,1,0:T(8,128)(2,1)S(1)} %collective-permute-done.24.refs_5_), channel_id=1, source_target_pairs={{0,4},{4,6},{6,2},{2,0},{1,5},{5,7},{7,3},{3,1},{8,12},{12,14},{14... | collective-permute-start | bytes 786440 | tf_op jit(solution)/shard_map/ppermute | solution.py:28

commit v10 on v8

--- a/solution.py
+++ b/solution.py
@@ -52,9 +52,17 @@
     return lax.optimization_barrier((x, *others))[0]
 
 
-def pack_kernel(turned_ref, span_ref, key_ref, packed_ref, place_ref):
+def prepare_kernel(n, span_source, key_ref, cot_source, packed_ref, place_ref, *refs):
+    out_refs, (span_ref, cot_ref, sems) = refs[:n], refs[n:]
     tokens, width = key_ref.shape[1:]
-    packed_ref[0, :tokens, :] = key_ref[0]
+    copies = [
+        pltpu.make_async_copy(cot_source, cot_ref, sems.at[0]),
+        pltpu.make_async_copy(key_ref.at[0], packed_ref.at[0, :tokens], sems.at[1]),
+        pltpu.make_async_copy(span_source, span_ref, sems.at[2]),
+    ]
+    for copy in copies:
+        copy.start()
+    copies[2].wait()
     spans = span_ref.shape[1]
     span = tokens // spans
     lane = lax.broadcasted_iota(jnp.int32, (TAG, width), 1)
@@ -66,23 +74,23 @@
         base = jnp.where(row // span == j, span_ref[0, j] * span, base)
     packed_ref[0, tokens:, :] = ids.astype(jnp.bfloat16)
     place_ref[...] = (base + row % span).astype(jnp.float32)
-
-
-def fetch_kernel(place_ref, query_ref, value_ref, query_held, value_held):
-    query_held[...] = query_ref[...]
-    value_held[...] = value_ref[...]
-
-
-def turn_kernel(n, cot_ref, *out_refs):
     me = lax.axis_index("ctx")
     side = lax.axis_index("tp") & 1
     half = cot_ref.shape[2] // n // 2
+    copies[0].wait()
     place = jnp.where(me % 2 == 0, me // 2, n - 1 - me // 2)
     for s in range(n):
         to = (place + s) % n
         block = jnp.where(to < (n + 1) // 2, 2 * to, 2 * (n - to) - 1)
         at = pl.multiple_of((block * 2 + side) * half, 128)
         out_refs[s][...] = cot_ref[0, :, pl.ds(at, half)].T
+    copies[1].wait()
+
+
+def fetch_kernel(*refs):
+    half = len(refs) // 2
+    for ref, held_ref in zip(refs[:half], refs[half:]):
+        held_ref[...] = ref[...]
 
 
 def join_kernel(*refs):
@@ -198,33 +206,32 @@
     features = cotangent.shape[2] // n
     half = features // 2
 
-    turned = pl.pallas_call(
-        functools.partial(turn_kernel, n),
-        out_shape=[jax.ShapeDtypeStruct((half, tokens), jnp.bfloat16)] * n,
-        in_specs=[VMEM],
-        out_specs=[VMEM] * n,
-        compiler_params=params(16),
-        name="turn",
-    )(cotangent)
-    packed, place = pl.pallas_call(
-        pack_kernel,
+    packed, place, *turned = pl.pallas_call(
+        functools.partial(prepare_kernel, n),
         out_shape=[
             jax.ShapeDtypeStruct((1, tokens + TAG, width), jnp.bfloat16),
             jax.ShapeDtypeStruct((tokens, 128), jnp.float32),
+        ]
+        + [jax.ShapeDtypeStruct((half, tokens), jnp.bfloat16)] * n,
+        in_specs=[ANY] * 3,
+        out_specs=[VMEM] * (n + 2),
+        scratch_shapes=[
+            pltpu.SMEM(span_ids.shape, jnp.int32),
+            pltpu.VMEM(cotangent.shape, jnp.bfloat16),
+            pltpu.SemaphoreType.DMA((3,)),
         ],
-        in_specs=[ANY, SMEM, VMEM],
-        out_specs=[VMEM] * 2,
-        compiler_params=params(16),
-        name="pack",
-    )(turned[0], span_ids, keys)
-    query_held, value_held = pl.pallas_call(
+        compiler_params=params(56),
+        name="prepare",
+    )(span_ids, keys, cotangent)
+    fetched = (place, packed, queries, values, turned[0])
+    place, key_held, query_held, value_held, turned[0] = pl.pallas_call(
         fetch_kernel,
-        out_shape=[jax.ShapeDtypeStruct(x.shape, jnp.bfloat16) for x in (queries, values)],
-        in_specs=[ANY, VMEM, VMEM],
-        out_specs=[VMEM] * 2,
+        out_shape=[jax.ShapeDtypeStruct(x.shape, x.dtype) for x in fetched],
+        in_specs=[VMEM] * 5,
+        out_specs=[VMEM] * 5,
         compiler_params=params(16),
         name="fetch",
-    )(place, queries, values)
+    )(*fetched)
     turned = [turned[0]] + [around(turned[s], s) for s in range(1, n)]
     key_edges, value_edges = ([around(x, way) for way in (1, -1)] for x in (packed, values))
     turned[0] = after(turned[0], *value_edges)
@@ -247,7 +254,7 @@
         out_specs=[VMEM] * (1 + parts),
         compiler_params=params(40),
         name="attend",
-    )(place, query_held, *key_ring, value_held, *value_ring[1:])
+    )(place, query_held, key_held, *key_ring[1:], value_held, *value_ring[1:])
 
     near, mirrored = [], []
     for c in range(parts):

time: 90.3 us -> 89.3 us (0.989)
  waiting for transfers between devices: 41 us -> 27.1 us
  starting transfers between devices: 33.2 us -> 44.7 us
  Pallas kernels: 10.3 us -> 12.8 us
  local copies, waits for them, and re-layouts: 4.72 us -> 3.69 us
    ppermute x16, waiting for transfers between devices: 31.2 us -> 16.6 us  [around(): lax.ppermute(x, 'ctx', [(order[q], order[(q + shift) % n]) for q in range...]
    ppermute x16, starting transfers between devices: 19.8 us -> 33.9 us  [around(): lax.ppermute(x, 'ctx', [(order[q], order[(q + shift) % n]) for q in range...]
    ppermute x10, starting transfers between devices: 13.4 us -> 10.8 us  [swap(): lax.ppermute(x, axis, [(i, i ^ mask) for i in range(lax.axis_size(axis))])]
    pallas_call x3 -> x2, Pallas kernels: 0.79 us -> 3.28 us  [the longest x1 2.31 us: local(): pl.pallas_call(functools.partial(prepare_kernel, n), out_shape=[jax.Shape...]
    unnamed x10 -> x8, local copies, waits for them, and re-layouts: 4.72 us -> 3.69 us
  transfers between devices with their start and end apart: 26 -> 26, of which waited for: 14 -> 12; matrix products, arithmetic and copies ran while one was open for 0% -> 0% of each run, Pallas kernels for 10% -> 13%
where the time goes in v10:
time: 89.3 us; the launch traced here: 89 us
  starting transfers between devices  44.7 us (50%)
  waiting for transfers between devices  27.1 us (30%)
  Pallas kernels  12.8 us (14%)
  local copies, waits for them, and re-layouts  3.69 us (4%)
    ppermute x16, starting transfers between devices, around(): lax.ppermute(x, 'ctx', [(order[q], order[(q + shift) % n]) for q in range...  33.9 us
    ppermute x16, waiting for transfers between devices, around(): lax.ppermute(x, 'ctx', [(order[q], order[(q + shift) % n]) for q in range...  16.6 us
    ppermute x10, starting transfers between devices, swap(): lax.ppermute(x, axis, [(i, i ^ mask) for i in range(lax.axis_size(axis))])  10.8 us
    ppermute x10, waiting for transfers between devices, swap(): lax.ppermute(x, axis, [(i, i ^ mask) for i in range(lax.axis_size(axis))])  10.5 us
    unnamed x8, local copies, waits for them, and re-layouts  3.69 us
    pallas_call x2, Pallas kernels, local(): pl.pallas_call(functools.partial(early_kernel, first_slots), out_shape=ja...  3.59 us
    pallas_call x2, Pallas kernels, local(): pl.pallas_call(functools.partial(finish_kernel, slots, c * chunk), out_sh...  3.31 us
    pallas_call x1, Pallas kernels, local(): pl.pallas_call(functools.partial(attention_kernel, HQ // HK, 1.0 / math.s...  2.51 us
  transfers between devices with their start and end apart: 26, of which 12 were waited for; matrix products, arithmetic and copies ran while one was open for 0% of the time, Pallas kernels for 13%

profile of v10, /device:TPU:0, one launch (start us, length us, event | category | flops | bytes accessed | tf_op | source)
XLA Modules:
  0.0 89.0 jit_solution(898234787419303347)
XLA Ops:
  0.6 3.1 %collective-permute-start.2 = (bf16[1,128,512]{2,1,0:T(8,128)(2,1)}, bf16[1,128,512]{2,1,0:T(8,128)(2,1)S(1)}, u32[]{:S(2)}, u32[]{:S(2)}) collective-permute-start(bf16[1,128,512]{2,1,0:T(8,128)(2,1)} %refs_3_.1), channel_id=1, source_target_pairs={{0,2},{4,0},{6,4},{2,6},{1,3},{5,1},{7,5},{3,7},{8,10},{12,8},{14,... | collective-permute-start | bytes 393224 | tf_op jit(solution)/shard_map/ppermute | solution.py:28
  3.7 2.3 %prepare.1 = (bf16[1,144,512]{2,1,0:T(8,128)(2,1)}, f32[128,128]{1,0:T(8,128)}, bf16[512,128]{1,0:T(8,128)(2,1)}, bf16[512,128]{1,0:T(8,128)(2,1)}, bf16[512,128]{1,0:T(8,128)(2,1)}, /*index=5*/bf16[512,128]{1,0:T(8,128)(2,1)}) custom-call(s32[1,2]{1,0:T(1,128)} %span_source.1, bf16[1,128,512]{2,1,0:T(8,128)(2,1)} %key_ref.1, bf16[1,128,4096]{2,1,0:T(8,128)(2,1)} %cot_source.1), custom_call_target="tpu_custom_call" | custom-call | tf_op jit(solution)/shard_map/prepare/pallas_call | solution.py:209
  6.0 1.1 %collective-permute-start = (bf16[1,144,512]{2,1,0:T(8,128)(2,1)}, bf16[1,144,512]{2,1,0:T(8,128)(2,1)S(1)}, u32[]{:S(2)}, u32[]{:S(2)}) collective-permute-start(bf16[1,144,512]{2,1,0:T(8,128)(2,1)} %get-tuple-element.24.refs_1_), channel_id=1, source_target_pairs={{0,4},{4,6},{6,2},{2,0},{1,5},{5,7},{7,3},{3,1},{8,12},{12,14},{14... | collective-permute-start | bytes 442376 | tf_op jit(solution)/shard_map/ppermute | solution.py:28
  7.1 2.0 %collective-permute-start.1 = (bf16[1,128,512]{2,1,0:T(8,128)(2,1)}, bf16[1,128,512]{2,1,0:T(8,128)(2,1)S(1)}, u32[]{:S(2)}, u32[]{:S(2)}) collective-permute-start(bf16[1,128,512]{2,1,0:T(8,128)(2,1)} %refs_3_.1), channel_id=1, source_target_pairs={{0,4},{4,6},{6,2},{2,0},{1,5},{5,7},{7,3},{3,1},{8,12},{12,14},{14... | collective-permute-start | bytes 393224 | tf_op jit(solution)/shard_map/ppermute | solution.py:28
  9.1 2.5 %collective-permute-start.3 = (bf16[512,128]{1,0:T(8,128)(2,1)}, bf16[512,128]{1,0:T(8,128)(2,1)S(1)}, u32[]{:S(2)}, u32[]{:S(2)}) collective-permute-start(bf16[512,128]{1,0:T(8,128)(2,1)} %get-tuple-element.31), channel_id=1, source_target_pairs={{0,4},{4,6},{6,2},{2,0},{1,5},{5,7},{7,3},{3,1},{8,12},{12,14},{14... | collective-permute-start | bytes 393224 | tf_op jit(solution)/shard_map/ppermute | solution.py:28
  11.6 9.0 %collective-permute-start.5 = (bf16[512,128]{1,0:T(8,128)(2,1)}, bf16[512,128]{1,0:T(8,128)(2,1)S(1)}, u32[]{:S(2)}, u32[]{:S(2)}) collective-permute-start(bf16[512,128]{1,0:T(8,128)(2,1)} %get-tuple-element.33), channel_id=1, source_target_pairs={{0,2},{4,0},{6,4},{2,6},{1,3},{5,1},{7,5},{3,7},{8,10},{12,8},{14,... | collective-permute-start | bytes 393224 | tf_op jit(solution)/shard_map/ppermute | solution.py:28
  20.6 1.0 %copy-done = bf16[1,128,2048]{2,1,0:T(8,128)(2,1)S(1)} copy-done((bf16[1,128,2048]{2,1,0:T(8,128)(2,1)S(1)}, bf16[1,128,2048]{2,1,0:T(8,128)(2,1)}, u32[]{:S(2)}) %copy-start) | copy-done | bytes 524312
  21.6 0.9 %copy-done.1 = bf16[1,128,512]{2,1,0:T(8,128)(2,1)S(1)} copy-done((bf16[1,128,512]{2,1,0:T(8,128)(2,1)S(1)}, bf16[1,128,512]{2,1,0:T(8,128)(2,1)}, u32[]{:S(2)}) %copy-start.1) | copy-done | bytes 131096
  22.5 0.9 %copy-done.2 = bf16[512,128]{1,0:T(8,128)(2,1)S(1)} copy-done((bf16[512,128]{1,0:T(8,128)(2,1)S(1)}, bf16[512,128]{1,0:T(8,128)(2,1)}, u32[]{:S(2)}) %copy-start.2) | copy-done | bytes 131096
  23.4 0.8 copy-done.3
  24.3 1.0 %fetch.1 = (f32[128,128]{1,0:T(8,128)S(1)}, bf16[1,144,512]{2,1,0:T(8,128)(2,1)S(1)}, bf16[1,128,2048]{2,1,0:T(8,128)(2,1)S(1)}, bf16[1,128,512]{2,1,0:T(8,128)(2,1)S(1)}, bf16[512,128]{1,0:T(8,128)(2,1)S(1)}) custom-call(f32[128,128]{1,0:T(8,128)S(1)} %copy-done.3, bf16[1,144,512]{2,1,0:T(8,128)(2,1)} %get-tuple-element.24.refs_1_, ...), custom_call_target="tpu_custom_call" | custom-call | tf_op jit(solution)/shard_map/fetch/pallas_call | solution.py:227
  25.3 3.8 %collective-permute-start.7 = (bf16[1,144,512]{2,1,0:T(8,128)(2,1)}, bf16[1,144,512]{2,1,0:T(8,128)(2,1)S(1)}, u32[]{:S(2)}, u32[]{:S(2)}) collective-permute-start(bf16[1,144,512]{2,1,0:T(8,128)(2,1)} %get-tuple-element.24.refs_1_), channel_id=1, source_target_pairs={{0,2},{4,0},{6,4},{2,6},{1,3},{5,1},{7,5},{3,7},{8,10},{12,8},{14,... | collective-permute-start | bytes 442376 | tf_op jit(solution)/shard_map/ppermute | solution.py:28
  29.1 0.1 join.1.refs_6_.refs_2_
  29.2 0.1 collective-permute-start.6
  29.3 2.0 %collective-permute-start.8 = (bf16[1,128,512]{2,1,0:T(8,128)(2,1)S(1)}, bf16[1,128,512]{2,1,0:T(8,128)(2,1)S(1)}, u32[]{:S(2)}, u32[]{:S(2)}) collective-permute-start(bf16[1,128,512]{2,1,0:T(8,128)(2,1)S(1)} %collective-permute-done.2.refs_7_), channel_id=1, source_target_pairs={{0,2},{4,0},{6,4},{2,6},{1,3},{5,1},{7,5},{3,7},{8,10},{12,8},{14,... | collective-permute-start | bytes 393224 | tf_op jit(solution)/shard_map/ppermute | solution.py:28
  31.3 1.1 %collective-permute-start.15 = (bf16[512,512]{1,0:T(8,128)(2,1)S(1)}, bf16[512,512]{1,0:T(8,128)(2,1)S(1)}, u32[]{:S(2)}, u32[]{:S(2)}) collective-permute-start(bf16[512,512]{1,0:T(8,128)(2,1)S(1)} %join.1.refs_6_.refs_2_), channel_id=1, source_target_pairs={{0,16},{8,24},{16,0},{24,8},{1,17},{9,25},{17,1},{25,9},{2,18},{10... | collective-permute-start | bytes 1572872 | tf_op jit(solution)/shard_map/ppermute | solution.py:44
  32.4 3.6 %collective-permute-done.7.refs_3_ = bf16[1,144,512]{2,1,0:T(8,128)(2,1)S(1)} collective-permute-done((bf16[1,144,512]{2,1,0:T(8,128)(2,1)}, bf16[1,144,512]{2,1,0:T(8,128)(2,1)S(1)}, u32[]{:S(2)}, u32[]{:S(2)}) %collective-permute-start.7) | collective-permute-done | bytes 147488 | tf_op jit(solution)/shard_map/ppermute | solution.py:28
  36.0 1.9 %collective-permute-done.8.refs_6_ = bf16[1,128,512]{2,1,0:T(8,128)(2,1)S(1)} collective-permute-done((bf16[1,128,512]{2,1,0:T(8,128)(2,1)S(1)}, bf16[1,128,512]{2,1,0:T(8,128)(2,1)S(1)}, u32[]{:S(2)}, u32[]{:S(2)}) %collective-permute-start.8) | collective-permute-done | bytes 131104 | tf_op jit(solution)/shard_map/ppermute | solution.py:28
  37.8 1.2 %collective-permute-done.6.refs_2_ = bf16[1,144,512]{2,1,0:T(8,128)(2,1)S(1)} collective-permute-done((bf16[1,144,512]{2,1,0:T(8,128)(2,1)S(1)}, bf16[1,144,512]{2,1,0:T(8,128)(2,1)S(1)}, u32[]{:S(2)}, u32[]{:S(2)}) %collective-permute-start.6) | collective-permute-done | bytes 147488 | tf_op jit(solution)/shard_map/ppermute | solution.py:28
  39.1 2.5 %attend.1 = (bf16[1,128,2048]{2,1,0:T(8,128)(2,1)}, bf16[1,128,1024]{2,1,0:T(8,128)(2,1)S(1)}, bf16[1,128,1024]{2,1,0:T(8,128)(2,1)S(1)}) custom-call(f32[128,128]{1,0:T(8,128)S(1)} %get-tuple-element.26.place_ref, bf16[1,128,2048]{2,1,0:T(8,128)(2,1)S(1)} %get-tuple-element.27.query_ref, bf16[1,144,512]{2,1,0:T(8,128)(2,1)S(1)} %get-tuple-element.28.refs_0_, ...), custom_call_target="tpu_custom_call" | custom-call | tf_op jit(solution)/shard_map/attend/pallas_call | solution.py:249
  41.6 1.3 %collective-permute-start.10 = (bf16[1,128,1024]{2,1,0:T(8,128)(2,1)S(1)}, bf16[1,128,1024]{2,1,0:T(8,128)(2,1)S(1)}, u32[]{:S(2)}, u32[]{:S(2)}) collective-permute-start(bf16[1,128,1024]{2,1,0:T(8,128)(2,1)S(1)} %get-tuple-element.38.refs_0_), channel_id=1, source_target_pairs={{0,16},{8,24},{16,0},{24,8},{1,17},{9,25},{17,1},{25,9},{2,18},{10... | collective-permute-start | bytes 786440 | tf_op jit(solution)/shard_map/ppermute | solution.py:44
  42.8 0.8 collective-permute-start.20
  43.6 2.3 %collective-permute-start.19 = (bf16[1,128,1024]{2,1,0:T(8,128)(2,1)S(1)}, bf16[1,128,1024]{2,1,0:T(8,128)(2,1)S(1)}, u32[]{:S(2)}, u32[]{:S(2)}) collective-permute-start(bf16[1,128,1024]{2,1,0:T(8,128)(2,1)S(1)} %get-tuple-element.41.refs_0_), channel_id=1, source_target_pairs={{0,4},{4,6},{6,2},{2,0},{1,5},{5,7},{7,3},{3,1},{8,12},{12,14},{14... | collective-permute-start | bytes 786440 | tf_op jit(solution)/shard_map/ppermute | solution.py:28
  45.9 4.9 %collective-permute-done.10.refs_3_ = bf16[1,128,1024]{2,1,0:T(8,128)(2,1)S(1)} collective-permute-done((bf16[1,128,1024]{2,1,0:T(8,128)(2,1)S(1)}, bf16[1,128,1024]{2,1,0:T(8,128)(2,1)S(1)}, u32[]{:S(2)}, u32[]{:S(2)}) %collective-permute-start.10) | collective-permute-done | bytes 262176 | tf_op jit(solution)/shard_map/ppermute | solution.py:44
  50.8 1.3 %collective-permute-done.9.refs_1_ = bf16[1,128,1024]{2,1,0:T(8,128)(2,1)S(1)} collective-permute-done((bf16[1,128,1024]{2,1,0:T(8,128)(2,1)S(1)}, bf16[1,128,1024]{2,1,0:T(8,128)(2,1)S(1)}, u32[]{:S(2)}, u32[]{:S(2)}) %collective-permute-start.9) | collective-permute-done | bytes 262176 | tf_op jit(solution)/shard_map/ppermute | solution.py:28
  52.1 0.7 collective-permute-start.12
  52.8 1.2 %collective-permute-start.16 = (bf16[512,512]{1,0:T(8,128)(2,1)S(1)}, bf16[512,512]{1,0:T(8,128)(2,1)S(1)}, u32[]{:S(2)}, u32[]{:S(2)}) collective-permute-start(bf16[512,512]{1,0:T(8,128)(2,1)S(1)} %join.1.refs_6_.refs_2_), channel_id=1, source_target_pairs={{0,1},{1,0},{2,3},{3,2},{4,5},{5,4},{6,7},{7,6},{8,9},{9,8},{10,11... | collective-permute-start | bytes 1572872 | tf_op jit(solution)/shard_map/ppermute | solution.py:44
  54.1 2.3 %collective-permute-done.20.refs_3_ = bf16[1,128,1024]{2,1,0:T(8,128)(2,1)S(1)} collective-permute-done((bf16[1,128,1024]{2,1,0:T(8,128)(2,1)S(1)}, bf16[1,128,1024]{2,1,0:T(8,128)(2,1)S(1)}, u32[]{:S(2)}, u32[]{:S(2)}) %collective-permute-start.20) | collective-permute-done | bytes 262176 | tf_op jit(solution)/shard_map/ppermute | solution.py:44
  56.4 2.0 %collective-permute-start.11 = (bf16[1,128,1024]{2,1,0:T(8,128)(2,1)S(1)}, bf16[1,128,1024]{2,1,0:T(8,128)(2,1)S(1)}, u32[]{:S(2)}, u32[]{:S(2)}) collective-permute-start(bf16[1,128,1024]{2,1,0:T(8,128)(2,1)S(1)} %collective-permute-done.9.refs_1_), channel_id=1, source_target_pairs={{0,4},{4,6},{6,2},{2,0},{1,5},{5,7},{7,3},{3,1},{8,12},{12,14},{14... | collective-permute-start | bytes 786440 | tf_op jit(solution)/shard_map/ppermute | solution.py:28
  58.3 1.1 %collective-permute-start.22 = (bf16[1,128,1024]{2,1,0:T(8,128)(2,1)S(1)}, bf16[1,128,1024]{2,1,0:T(8,128)(2,1)S(1)}, u32[]{:S(2)}, u32[]{:S(2)}) collective-permute-start(bf16[1,128,1024]{2,1,0:T(8,128)(2,1)S(1)} %collective-permute-done.19.refs_1_), channel_id=1, source_target_pairs={{0,16},{8,24},{16,0},{24,8},{1,17},{9,25},{17,1},{25,9},{2,18},{10... | collective-permute-start | bytes 786440 | tf_op jit(solution)/shard_map/ppermute | solution.py:44
  59.4 0.4 collective-permute-start.21
  59.8 2.2 %collective-permute-done.12.refs_4_ = bf16[1,128,1024]{2,1,0:T(8,128)(2,1)S(1)} collective-permute-done((bf16[1,128,1024]{2,1,0:T(8,128)(2,1)S(1)}, bf16[1,128,1024]{2,1,0:T(8,128)(2,1)S(1)}, u32[]{:S(2)}, u32[]{:S(2)}) %collective-permute-start.12) | collective-permute-done | bytes 262176 | tf_op jit(solution)/shard_map/ppermute | solution.py:44
  62.0 1.3 %collective-permute-start.17 = (bf16[512,512]{1,0:T(8,128)(2,1)S(1)}, bf16[512,512]{1,0:T(8,128)(2,1)S(1)}, u32[]{:S(2)}, u32[]{:S(2)}) collective-permute-start(bf16[512,512]{1,0:T(8,128)(2,1)S(1)} %collective-permute-done.15.refs_7_.refs_3_), channel_id=1, source_target_pairs={{0,1},{1,0},{2,3},{3,2},{4,5},{5,4},{6,7},{7,6},{8,9},{9,8},{10,11... | collective-permute-start | bytes 1572872 | tf_op jit(solution)/shard_map/ppermute | solution.py:44
  63.3 2.3 %collective-permute-done.11.refs_2_ = bf16[1,128,1024]{2,1,0:T(8,128)(2,1)S(1)} collective-permute-done((bf16[1,128,1024]{2,1,0:T(8,128)(2,1)S(1)}, bf16[1,128,1024]{2,1,0:T(8,128)(2,1)S(1)}, u32[]{:S(2)}, u32[]{:S(2)}) %collective-permute-start.11) | collective-permute-done | bytes 262176 | tf_op jit(solution)/shard_map/ppermute | solution.py:28
  65.6 2.2 %collective-permute-start.13 = (bf16[1,128,1024]{2,1,0:T(8,128)(2,1)S(1)}, bf16[1,128,1024]{2,1,0:T(8,128)(2,1)S(1)}, u32[]{:S(2)}, u32[]{:S(2)}) collective-permute-start(bf16[1,128,1024]{2,1,0:T(8,128)(2,1)S(1)} %collective-permute-done.11.refs_2_), channel_id=1, source_target_pairs={{0,4},{4,6},{6,2},{2,0},{1,5},{5,7},{7,3},{3,1},{8,12},{12,14},{14... | collective-permute-start | bytes 786440 | tf_op jit(solution)/shard_map/ppermute | solution.py:28
  67.8 3.5 %collective-permute-done.21.refs_2_ = bf16[1,128,1024]{2,1,0:T(8,128)(2,1)S(1)} collective-permute-done((bf16[1,128,1024]{2,1,0:T(8,128)(2,1)S(1)}, bf16[1,128,1024]{2,1,0:T(8,128)(2,1)S(1)}, u32[]{:S(2)}, u32[]{:S(2)}) %collective-permute-start.21) | collective-permute-done | bytes 262176 | tf_op jit(solution)/shard_map/ppermute | solution.py:28
  71.2 1.3 %collective-permute-start.24 = (bf16[1,128,1024]{2,1,0:T(8,128)(2,1)S(1)}, bf16[1,128,1024]{2,1,0:T(8,128)(2,1)S(1)}, u32[]{:S(2)}, u32[]{:S(2)}) collective-permute-start(bf16[1,128,1024]{2,1,0:T(8,128)(2,1)S(1)} %collective-permute-done.21.refs_2_), channel_id=1, source_target_pairs={{0,16},{8,24},{16,0},{24,8},{1,17},{9,25},{17,1},{25,9},{2,18},{10... | collective-permute-start | bytes 786440 | tf_op jit(solution)/shard_map/ppermute | solution.py:44
  72.5 0.7 collective-permute-start.18
  73.3 2.1 %collective-permute-start.23 = (bf16[1,128,1024]{2,1,0:T(8,128)(2,1)S(1)}, bf16[1,128,1024]{2,1,0:T(8,128)(2,1)S(1)}, u32[]{:S(2)}, u32[]{:S(2)}) collective-permute-start(bf16[1,128,1024]{2,1,0:T(8,128)(2,1)S(1)} %collective-permute-done.21.refs_2_), channel_id=1, source_target_pairs={{0,4},{4,6},{6,2},{2,0},{1,5},{5,7},{7,3},{3,1},{8,12},{12,14},{14... | collective-permute-start | bytes 786440 | tf_op jit(solution)/shard_map/ppermute | solution.py:28
  75.4 1.5 %collective-permute-done.13.refs_0_ = bf16[1,128,1024]{2,1,0:T(8,128)(2,1)S(1)} collective-permute-done((bf16[1,128,1024]{2,1,0:T(8,128)(2,1)S(1)}, bf16[1,128,1024]{2,1,0:T(8,128)(2,1)S(1)}, u32[]{:S(2)}, u32[]{:S(2)}) %collective-permute-start.13) | collective-permute-done | bytes 262176 | tf_op jit(solution)/shard_map/ppermute | solution.py:28
  76.9 1.3 %collective-permute-start.14 = (bf16[1,128,1024]{2,1,0:T(8,128)(2,1)S(1)}, bf16[1,128,1024]{2,1,0:T(8,128)(2,1)S(1)}, u32[]{:S(2)}, u32[]{:S(2)}) collective-permute-start(bf16[1,128,1024]{2,1,0:T(8,128)(2,1)S(1)} %collective-permute-done.13.refs_0_), channel_id=1, source_target_pairs={{0,16},{8,24},{16,0},{24,8},{1,17},{9,25},{17,1},{25,9},{2,18},{10... | collective-permute-start | bytes 786440 | tf_op jit(solution)/shard_map/ppermute | solution.py:44
  78.2 1.2 %collective-permute-done.24.refs_5_ = bf16[1,128,1024]{2,1,0:T(8,128)(2,1)S(1)} collective-permute-done((bf16[1,128,1024]{2,1,0:T(8,128)(2,1)S(1)}, bf16[1,128,1024]{2,1,0:T(8,128)(2,1)S(1)}, u32[]{:S(2)}, u32[]{:S(2)}) %collective-permute-start.24) | collective-permute-done | bytes 262176 | tf_op jit(solution)/shard_map/ppermute | solution.py:44
  79.3 1.5 %collective-permute-start.25 = (bf16[1,128,1024]{2,1,0:T(8,128)(2,1)S(1)}, bf16[1,128,1024]{2,1,0:T(8,128)(2,1)S(1)}, u32[]{:S(2)}, u32[]{:S(2)}) collective-permute-start(bf16[1,128,1024]{2,1,0:T(8,128)(2,1)S(1)} %collective-permute-done.24.refs_5_), channel_id=1, source_target_pairs={{0,4},{4,6},{6,2},{2,0},{1,5},{5,7},{7,3},{3,1},{8,12},{12,14},{14... | collective-permute-start | bytes 786440 | tf_op jit(solution)/shard_map/ppermute | solution.py:28
  80.8 1.8 %early.3.refs_6_ = f32[1024,1024]{1,0:T(8,128)S(1)} custom-call(bf16[1,128,1024]{2,1,0:T(8,128)(2,1)S(1)} %get-tuple-element.41.refs_0_, bf16[1,128,1024]{2,1,0:T(8,128)(2,1)S(1)} %collective-permute-done.19.refs_1_, bf16[1,128,1024]{2,1,0:T(8,128)(2,1)S(1)} %collective-permute-done.21.refs_2_, bf16[1,128,1024]{2,1,0:T(8,128)(2,1)S(1)} %collective-permute-done.20.refs_3_, ...), custom_call_target="tpu_custom_call" | custom-call | flops 1610612736 | bytes 8388608 | tf_op jit(solution)/shard_map/early/pallas_call | solution.py:279
  82.6 1.8 %early.2.refs_6_ = f32[1024,1024]{1,0:T(8,128)S(1)} custom-call(bf16[1,128,1024]{2,1,0:T(8,128)(2,1)S(1)} %get-tuple-element.38.refs_0_, bf16[1,128,1024]{2,1,0:T(8,128)(2,1)S(1)} %collective-permute-done.9.refs_1_, bf16[1,128,1024]{2,1,0:T(8,128)(2,1)S(1)} %collective-permute-done.11.refs_2_, bf16[1,128,1024]{2,1,0:T(8,128)(2,1)S(1)} %collective-permute-done.10.refs_3_, ...), custom_call_target="tpu_custom_call" | custom-call | flops 1610612736 | bytes 8388608 | tf_op jit(solution)/shard_map/early/pallas_call | solution.py:279
  84.4 1.3 %collective-permute-done.25.refs_1_ = bf16[1,128,1024]{2,1,0:T(8,128)(2,1)S(1)} collective-permute-done((bf16[1,128,1024]{2,1,0:T(8,128)(2,1)S(1)}, bf16[1,128,1024]{2,1,0:T(8,128)(2,1)S(1)}, u32[]{:S(2)}, u32[]{:S(2)}) %collective-permute-start.25) | collective-permute-done | bytes 262176 | tf_op jit(solution)/shard_map/ppermute | solution.py:28
  85.7 1.6 %finish.2.refs_7_ = bf16[1,1024,2048]{2,1,0:T(8,128)(2,1)} custom-call(bf16[1,128,1024]{2,1,0:T(8,128)(2,1)S(1)} %collective-permute-done.23.refs_0_, bf16[1,128,1024]{2,1,0:T(8,128)(2,1)S(1)} %collective-permute-done.25.refs_1_, bf16[512,512]{1,0:T(8,128)(2,1)S(1)} %join.1.refs_6_.refs_2_, bf16[512,512]{1,0:T(8,128)(2,1)S(1)} %collective-permute-done.15.refs_7_.refs_3_, ...), custom_call_target="tpu_custom_call" | custom-call | flops 536870912 | bytes 8388608 | tf_op jit(solution)/shard_map/finish/pallas_call | solution.py:304
  87.4 1.7 %finish.3 = bf16[1,1024,2048]{2,1,0:T(8,128)(2,1)} custom-call(bf16[1,128,1024]{2,1,0:T(8,128)(2,1)S(1)} %collective-permute-done.13.refs_0_, bf16[1,128,1024]{2,1,0:T(8,128)(2,1)S(1)} %collective-permute-done.14.refs_1_, bf16[512,512]{1,0:T(8,128)(2,1)S(1)} %join.1.refs_6_.refs_2_, ...), custom_call_target="tpu_custom_call", output_to_operand_aliasing={{}: (7, {})} | custom-call | flops 536870912 | bytes 8388608 | tf_op jit(solution)/shard_map/finish/pallas_call | solution.py:304
  (20 shorter events, 0.0 us)
Async XLA Ops:
  0.6 11.0 %collective-permute-start.2 = (bf16[1,128,512]{2,1,0:T(8,128)(2,1)}, bf16[1,128,512]{2,1,0:T(8,128)(2,1)S(1)}, u32[]{:S(2)}, u32[]{:S(2)}) collective-permute-start(bf16[1,128,512]{2,1,0:T(8,128)(2,1)} %refs_3_.1), channel_id=1, source_target_pairs={{0,2},{4,0},{6,4},{2,6},{1,3},{5,1},{7,5},{3,7},{8,10},{12,8},{14,... | collective-permute-start | bytes 393224 | tf_op jit(solution)/shard_map/ppermute | solution.py:28
  6.0 23.2 %collective-permute-start = (bf16[1,144,512]{2,1,0:T(8,128)(2,1)}, bf16[1,144,512]{2,1,0:T(8,128)(2,1)S(1)}, u32[]{:S(2)}, u32[]{:S(2)}) collective-permute-start(bf16[1,144,512]{2,1,0:T(8,128)(2,1)} %get-tuple-element.24.refs_1_), channel_id=1, source_target_pairs={{0,4},{4,6},{6,2},{2,0},{1,5},{5,7},{7,3},{3,1},{8,12},{12,14},{14... | collective-permute-start | bytes 442376 | tf_op jit(solution)/shard_map/ppermute | solution.py:28
  7.1 18.1 %collective-permute-start.1 = (bf16[1,128,512]{2,1,0:T(8,128)(2,1)}, bf16[1,128,512]{2,1,0:T(8,128)(2,1)S(1)}, u32[]{:S(2)}, u32[]{:S(2)}) collective-permute-start(bf16[1,128,512]{2,1,0:T(8,128)(2,1)} %refs_3_.1), channel_id=1, source_target_pairs={{0,4},{4,6},{6,2},{2,0},{1,5},{5,7},{7,3},{3,1},{8,12},{12,14},{14... | collective-permute-start | bytes 393224 | tf_op jit(solution)/shard_map/ppermute | solution.py:28
  9.1 20.0 %collective-permute-start.3 = (bf16[512,128]{1,0:T(8,128)(2,1)}, bf16[512,128]{1,0:T(8,128)(2,1)S(1)}, u32[]{:S(2)}, u32[]{:S(2)}) collective-permute-start(bf16[512,128]{1,0:T(8,128)(2,1)} %get-tuple-element.31), channel_id=1, source_target_pairs={{0,4},{4,6},{6,2},{2,0},{1,5},{5,7},{7,3},{3,1},{8,12},{12,14},{14... | collective-permute-start | bytes 393224 | tf_op jit(solution)/shard_map/ppermute | solution.py:28
  11.6 17.5 %collective-permute-start.4 = (bf16[512,128]{1,0:T(8,128)(2,1)}, bf16[512,128]{1,0:T(8,128)(2,1)S(1)}, u32[]{:S(2)}, u32[]{:S(2)}) collective-permute-start(bf16[512,128]{1,0:T(8,128)(2,1)} %get-tuple-element.32), channel_id=1, source_target_pairs={{0,6},{4,2},{6,0},{2,4},{1,7},{5,3},{7,1},{3,5},{8,14},{12,10},{14... | collective-permute-start | bytes 393224 | tf_op jit(solution)/shard_map/ppermute | solution.py:28
  11.6 17.5 %collective-permute-start.5 = (bf16[512,128]{1,0:T(8,128)(2,1)}, bf16[512,128]{1,0:T(8,128)(2,1)S(1)}, u32[]{:S(2)}, u32[]{:S(2)}) collective-permute-start(bf16[512,128]{1,0:T(8,128)(2,1)} %get-tuple-element.33), channel_id=1, source_target_pairs={{0,2},{4,0},{6,4},{2,6},{1,3},{5,1},{7,5},{3,7},{8,10},{12,8},{14,... | collective-permute-start | bytes 393224 | tf_op jit(solution)/shard_map/ppermute | solution.py:28
  20.6 1.0 %copy-start = (bf16[1,128,2048]{2,1,0:T(8,128)(2,1)S(1)}, bf16[1,128,2048]{2,1,0:T(8,128)(2,1)}, u32[]{:S(2)}) copy-start(bf16[1,128,2048]{2,1,0:T(8,128)(2,1)} %refs_2_.1) | copy-start | bytes 1572868
  21.6 0.9 %copy-start.1 = (bf16[1,128,512]{2,1,0:T(8,128)(2,1)S(1)}, bf16[1,128,512]{2,1,0:T(8,128)(2,1)}, u32[]{:S(2)}) copy-start(bf16[1,128,512]{2,1,0:T(8,128)(2,1)} %refs_3_.1) | copy-start | bytes 393220
  22.5 0.9 %copy-start.2 = (bf16[512,128]{1,0:T(8,128)(2,1)S(1)}, bf16[512,128]{1,0:T(8,128)(2,1)}, u32[]{:S(2)}) copy-start(bf16[512,128]{1,0:T(8,128)(2,1)} %get-tuple-element.25.refs_4_) | copy-start | bytes 393220
  23.4 0.8 copy-start.3
  25.3 10.7 %collective-permute-start.7 = (bf16[1,144,512]{2,1,0:T(8,128)(2,1)}, bf16[1,144,512]{2,1,0:T(8,128)(2,1)S(1)}, u32[]{:S(2)}, u32[]{:S(2)}) collective-permute-start(bf16[1,144,512]{2,1,0:T(8,128)(2,1)} %get-tuple-element.24.refs_1_), channel_id=1, source_target_pairs={{0,2},{4,0},{6,4},{2,6},{1,3},{5,1},{7,5},{3,7},{8,10},{12,8},{14,... | collective-permute-start | bytes 442376 | tf_op jit(solution)/shard_map/ppermute | solution.py:28
  29.2 9.9 %collective-permute-start.6 = (bf16[1,144,512]{2,1,0:T(8,128)(2,1)S(1)}, bf16[1,144,512]{2,1,0:T(8,128)(2,1)S(1)}, u32[]{:S(2)}, u32[]{:S(2)}) collective-permute-start(bf16[1,144,512]{2,1,0:T(8,128)(2,1)S(1)} %collective-permute-done.refs_1_), channel_id=1, source_target_pairs={{0,4},{4,6},{6,2},{2,0},{1,5},{5,7},{7,3},{3,1},{8,12},{12,14},{14... | collective-permute-start | bytes 442376 | tf_op jit(solution)/shard_map/ppermute | solution.py:28
  29.3 8.6 %collective-permute-start.8 = (bf16[1,128,512]{2,1,0:T(8,128)(2,1)S(1)}, bf16[1,128,512]{2,1,0:T(8,128)(2,1)S(1)}, u32[]{:S(2)}, u32[]{:S(2)}) collective-permute-start(bf16[1,128,512]{2,1,0:T(8,128)(2,1)S(1)} %collective-permute-done.2.refs_7_), channel_id=1, source_target_pairs={{0,2},{4,0},{6,4},{2,6},{1,3},{5,1},{7,5},{3,7},{8,10},{12,8},{14,... | collective-permute-start | bytes 393224 | tf_op jit(solution)/shard_map/ppermute | solution.py:28
  31.3 28.1 %collective-permute-start.15 = (bf16[512,512]{1,0:T(8,128)(2,1)S(1)}, bf16[512,512]{1,0:T(8,128)(2,1)S(1)}, u32[]{:S(2)}, u32[]{:S(2)}) collective-permute-start(bf16[512,512]{1,0:T(8,128)(2,1)S(1)} %join.1.refs_6_.refs_2_), channel_id=1, source_target_pairs={{0,16},{8,24},{16,0},{24,8},{1,17},{9,25},{17,1},{25,9},{2,18},{10... | collective-permute-start | bytes 1572872 | tf_op jit(solution)/shard_map/ppermute | solution.py:44
  41.6 9.2 %collective-permute-start.10 = (bf16[1,128,1024]{2,1,0:T(8,128)(2,1)S(1)}, bf16[1,128,1024]{2,1,0:T(8,128)(2,1)S(1)}, u32[]{:S(2)}, u32[]{:S(2)}) collective-permute-start(bf16[1,128,1024]{2,1,0:T(8,128)(2,1)S(1)} %get-tuple-element.38.refs_0_), channel_id=1, source_target_pairs={{0,16},{8,24},{16,0},{24,8},{1,17},{9,25},{17,1},{25,9},{2,18},{10... | collective-permute-start | bytes 786440 | tf_op jit(solution)/shard_map/ppermute | solution.py:44
  42.8 9.2 %collective-permute-start.9 = (bf16[1,128,1024]{2,1,0:T(8,128)(2,1)S(1)}, bf16[1,128,1024]{2,1,0:T(8,128)(2,1)S(1)}, u32[]{:S(2)}, u32[]{:S(2)}) collective-permute-start(bf16[1,128,1024]{2,1,0:T(8,128)(2,1)S(1)} %get-tuple-element.38.refs_0_), channel_id=1, source_target_pairs={{0,4},{4,6},{6,2},{2,0},{1,5},{5,7},{7,3},{3,1},{8,12},{12,14},{14... | collective-permute-start | bytes 786440 | tf_op jit(solution)/shard_map/ppermute | solution.py:28
  42.8 13.5 %collective-permute-start.20 = (bf16[1,128,1024]{2,1,0:T(8,128)(2,1)S(1)}, bf16[1,128,1024]{2,1,0:T(8,128)(2,1)S(1)}, u32[]{:S(2)}, u32[]{:S(2)}) collective-permute-start(bf16[1,128,1024]{2,1,0:T(8,128)(2,1)S(1)} %get-tuple-element.41.refs_0_), channel_id=1, source_target_pairs={{0,16},{8,24},{16,0},{24,8},{1,17},{9,25},{17,1},{25,9},{2,18},{10... | collective-permute-start | bytes 786440 | tf_op jit(solution)/shard_map/ppermute | solution.py:44
  43.6 14.8 %collective-permute-start.19 = (bf16[1,128,1024]{2,1,0:T(8,128)(2,1)S(1)}, bf16[1,128,1024]{2,1,0:T(8,128)(2,1)S(1)}, u32[]{:S(2)}, u32[]{:S(2)}) collective-permute-start(bf16[1,128,1024]{2,1,0:T(8,128)(2,1)S(1)} %get-tuple-element.41.refs_0_), channel_id=1, source_target_pairs={{0,4},{4,6},{6,2},{2,0},{1,5},{5,7},{7,3},{3,1},{8,12},{12,14},{14... | collective-permute-start | bytes 786440 | tf_op jit(solution)/shard_map/ppermute | solution.py:28
  52.1 9.9 %collective-permute-start.12 = (bf16[1,128,1024]{2,1,0:T(8,128)(2,1)S(1)}, bf16[1,128,1024]{2,1,0:T(8,128)(2,1)S(1)}, u32[]{:S(2)}, u32[]{:S(2)}) collective-permute-start(bf16[1,128,1024]{2,1,0:T(8,128)(2,1)S(1)} %collective-permute-done.9.refs_1_), channel_id=1, source_target_pairs={{0,16},{8,24},{16,0},{24,8},{1,17},{9,25},{17,1},{25,9},{2,18},{10... | collective-permute-start | bytes 786440 | tf_op jit(solution)/shard_map/ppermute | solution.py:44
  52.8 20.4 %collective-permute-start.16 = (bf16[512,512]{1,0:T(8,128)(2,1)S(1)}, bf16[512,512]{1,0:T(8,128)(2,1)S(1)}, u32[]{:S(2)}, u32[]{:S(2)}) collective-permute-start(bf16[512,512]{1,0:T(8,128)(2,1)S(1)} %join.1.refs_6_.refs_2_), channel_id=1, source_target_pairs={{0,1},{1,0},{2,3},{3,2},{4,5},{5,4},{6,7},{7,6},{8,9},{9,8},{10,11... | collective-permute-start | bytes 1572872 | tf_op jit(solution)/shard_map/ppermute | solution.py:44
  56.4 9.2 %collective-permute-start.11 = (bf16[1,128,1024]{2,1,0:T(8,128)(2,1)S(1)}, bf16[1,128,1024]{2,1,0:T(8,128)(2,1)S(1)}, u32[]{:S(2)}, u32[]{:S(2)}) collective-permute-start(bf16[1,128,1024]{2,1,0:T(8,128)(2,1)S(1)} %collective-permute-done.9.refs_1_), channel_id=1, source_target_pairs={{0,4},{4,6},{6,2},{2,0},{1,5},{5,7},{7,3},{3,1},{8,12},{12,14},{14... | collective-permute-start | bytes 786440 | tf_op jit(solution)/shard_map/ppermute | solution.py:28
  58.3 9.4 %collective-permute-start.22 = (bf16[1,128,1024]{2,1,0:T(8,128)(2,1)S(1)}, bf16[1,128,1024]{2,1,0:T(8,128)(2,1)S(1)}, u32[]{:S(2)}, u32[]{:S(2)}) collective-permute-start(bf16[1,128,1024]{2,1,0:T(8,128)(2,1)S(1)} %collective-permute-done.19.refs_1_), channel_id=1, source_target_pairs={{0,16},{8,24},{16,0},{24,8},{1,17},{9,25},{17,1},{25,9},{2,18},{10... | collective-permute-start | bytes 786440 | tf_op jit(solution)/shard_map/ppermute | solution.py:44
  59.4 11.8 %collective-permute-start.21 = (bf16[1,128,1024]{2,1,0:T(8,128)(2,1)S(1)}, bf16[1,128,1024]{2,1,0:T(8,128)(2,1)S(1)}, u32[]{:S(2)}, u32[]{:S(2)}) collective-permute-start(bf16[1,128,1024]{2,1,0:T(8,128)(2,1)S(1)} %collective-permute-done.19.refs_1_), channel_id=1, source_target_pairs={{0,4},{4,6},{6,2},{2,0},{1,5},{5,7},{7,3},{3,1},{8,12},{12,14},{14... | collective-permute-start | bytes 786440 | tf_op jit(solution)/shard_map/ppermute | solution.py:28
  62.0 18.8 %collective-permute-start.17 = (bf16[512,512]{1,0:T(8,128)(2,1)S(1)}, bf16[512,512]{1,0:T(8,128)(2,1)S(1)}, u32[]{:S(2)}, u32[]{:S(2)}) collective-permute-start(bf16[512,512]{1,0:T(8,128)(2,1)S(1)} %collective-permute-done.15.refs_7_.refs_3_), channel_id=1, source_target_pairs={{0,1},{1,0},{2,3},{3,2},{4,5},{5,4},{6,7},{7,6},{8,9},{9,8},{10,11... | collective-permute-start | bytes 1572872 | tf_op jit(solution)/shard_map/ppermute | solution.py:44
  65.6 11.2 %collective-permute-start.13 = (bf16[1,128,1024]{2,1,0:T(8,128)(2,1)S(1)}, bf16[1,128,1024]{2,1,0:T(8,128)(2,1)S(1)}, u32[]{:S(2)}, u32[]{:S(2)}) collective-permute-start(bf16[1,128,1024]{2,1,0:T(8,128)(2,1)S(1)} %collective-permute-done.11.refs_2_), channel_id=1, source_target_pairs={{0,4},{4,6},{6,2},{2,0},{1,5},{5,7},{7,3},{3,1},{8,12},{12,14},{14... | collective-permute-start | bytes 786440 | tf_op jit(solution)/shard_map/ppermute | solution.py:28
  71.2 8.1 %collective-permute-start.24 = (bf16[1,128,1024]{2,1,0:T(8,128)(2,1)S(1)}, bf16[1,128,1024]{2,1,0:T(8,128)(2,1)S(1)}, u32[]{:S(2)}, u32[]{:S(2)}) collective-permute-start(bf16[1,128,1024]{2,1,0:T(8,128)(2,1)S(1)} %collective-permute-done.21.refs_2_), channel_id=1, source_target_pairs={{0,16},{8,24},{16,0},{24,8},{1,17},{9,25},{17,1},{25,9},{2,18},{10... | collective-permute-start | bytes 786440 | tf_op jit(solution)/shard_map/ppermute | solution.py:44
  72.5 10.1 %collective-permute-start.18 = (bf16[1,128,1024]{2,1,0:T(8,128)(2,1)S(1)}, bf16[1,128,1024]{2,1,0:T(8,128)(2,1)S(1)}, u32[]{:S(2)}, u32[]{:S(2)}) collective-permute-start(bf16[1,128,1024]{2,1,0:T(8,128)(2,1)S(1)} %collective-permute-done.11.refs_2_), channel_id=1, source_target_pairs={{0,16},{8,24},{16,0},{24,8},{1,17},{9,25},{17,1},{25,9},{2,18},{10... | collective-permute-start | bytes 786440 | tf_op jit(solution)/shard_map/ppermute | solution.py:44
  73.3 11.1 %collective-permute-start.23 = (bf16[1,128,1024]{2,1,0:T(8,128)(2,1)S(1)}, bf16[1,128,1024]{2,1,0:T(8,128)(2,1)S(1)}, u32[]{:S(2)}, u32[]{:S(2)}) collective-permute-start(bf16[1,128,1024]{2,1,0:T(8,128)(2,1)S(1)} %collective-permute-done.21.refs_2_), channel_id=1, source_target_pairs={{0,4},{4,6},{6,2},{2,0},{1,5},{5,7},{7,3},{3,1},{8,12},{12,14},{14... | collective-permute-start | bytes 786440 | tf_op jit(solution)/shard_map/ppermute | solution.py:28
  76.9 10.5 %collective-permute-start.14 = (bf16[1,128,1024]{2,1,0:T(8,128)(2,1)S(1)}, bf16[1,128,1024]{2,1,0:T(8,128)(2,1)S(1)}, u32[]{:S(2)}, u32[]{:S(2)}) collective-permute-start(bf16[1,128,1024]{2,1,0:T(8,128)(2,1)S(1)} %collective-permute-done.13.refs_0_), channel_id=1, source_target_pairs={{0,16},{8,24},{16,0},{24,8},{1,17},{9,25},{17,1},{25,9},{2,18},{10... | collective-permute-start | bytes 786440 | tf_op jit(solution)/shard_map/ppermute | solution.py:44
  79.3 6.4 %collective-permute-start.25 = (bf16[1,128,1024]{2,1,0:T(8,128)(2,1)S(1)}, bf16[1,128,1024]{2,1,0:T(8,128)(2,1)S(1)}, u32[]{:S(2)}, u32[]{:S(2)}) collective-permute-start(bf16[1,128,1024]{2,1,0:T(8,128)(2,1)S(1)} %collective-permute-done.24.refs_5_), channel_id=1, source_target_pairs={{0,4},{4,6},{6,2},{2,0},{1,5},{5,7},{7,3},{3,1},{8,12},{12,14},{14... | collective-permute-start | bytes 786440 | tf_op jit(solution)/shard_map/ppermute | solution.py:28

commit v11 on v10

--- a/solution.py
+++ b/solution.py
@@ -234,7 +234,7 @@
     )(*fetched)
     turned = [turned[0]] + [around(turned[s], s) for s in range(1, n)]
     key_edges, value_edges = ([around(x, way) for way in (1, -1)] for x in (packed, values))
-    turned[0] = after(turned[0], *value_edges)
+    turned[0] = after(turned[0], *value_edges, key_edges[1])
     mine = pl.pallas_call(
         join_kernel,
         out_shape=jax.ShapeDtypeStruct((half, n * tokens), jnp.bfloat16),

time: 89.3 us -> 90.3 us (1.011)
  waiting for transfers between devices: 27.1 us -> 35.3 us
  starting transfers between devices: 44.7 us -> 37.6 us
  local copies, waits for them, and re-layouts: 3.69 us -> 4.6 us
    ppermute x16, starting transfers between devices: 33.9 us -> 25.2 us  [around(): lax.ppermute(x, 'ctx', [(order[q], order[(q + shift) % n]) for q in range...]
    ppermute x16, waiting for transfers between devices: 16.6 us -> 23.4 us  [around(): lax.ppermute(x, 'ctx', [(order[q], order[(q + shift) % n]) for q in range...]
    ppermute x10, starting transfers between devices: 10.8 us -> 12.3 us  [swap(): lax.ppermute(x, axis, [(i, i ^ mask) for i in range(lax.axis_size(axis))])]
    ppermute x10, waiting for transfers between devices: 10.5 us -> 11.9 us  [swap(): lax.ppermute(x, axis, [(i, i ^ mask) for i in range(lax.axis_size(axis))])]
    pallas_call x1, Pallas kernels: 0.97 us -> 0.07 us  [local(): pl.pallas_call(fetch_kernel, out_shape=[jax.ShapeDtypeStruct(x.shape, x.d...]
    unnamed x8 -> x10, local copies, waits for them, and re-layouts: 3.69 us -> 4.6 us
  transfers between devices with their start and end apart: 26 -> 26, of which waited for: 12 -> 12; matrix products, arithmetic and copies ran while one was open for 0% -> 0% of each run, Pallas kernels for 13% -> 11%
where the time goes in v11:
time: 90.3 us; the launch traced here: 90 us
  starting transfers between devices  37.6 us (42%)
  waiting for transfers between devices  35.3 us (39%)
  Pallas kernels  11.9 us (13%)
  local copies, waits for them, and re-layouts  4.6 us (5%)
    ppermute x16, starting transfers between devices, around(): lax.ppermute(x, 'ctx', [(order[q], order[(q + shift) % n]) for q in range...  25.2 us
    ppermute x16, waiting for transfers between devices, around(): lax.ppermute(x, 'ctx', [(order[q], order[(q + shift) % n]) for q in range...  23.4 us
    ppermute x10, starting transfers between devices, swap(): lax.ppermute(x, axis, [(i, i ^ mask) for i in range(lax.axis_size(axis))])  12.3 us
    ppermute x10, waiting for transfers between devices, swap(): lax.ppermute(x, axis, [(i, i ^ mask) for i in range(lax.axis_size(axis))])  11.9 us
    unnamed x10, local copies, waits for them, and re-layouts  4.6 us
    pallas_call x2, Pallas kernels, local(): pl.pallas_call(functools.partial(early_kernel, first_slots), out_shape=ja...  3.59 us
    pallas_call x2, Pallas kernels, local(): pl.pallas_call(functools.partial(finish_kernel, slots, c * chunk), out_sh...  3.31 us
    pallas_call x1, Pallas kernels, local(): pl.pallas_call(functools.partial(attention_kernel, HQ // HK, 1.0 / math.s...  2.51 us
  transfers between devices with their start and end apart: 26, of which 12 were waited for; matrix products, arithmetic and copies ran while one was open for 0% of the time, Pallas kernels for 11%

profile of v11, /device:TPU:0, one launch (start us, length us, event | category | flops | bytes accessed | tf_op | source)
XLA Modules:
  0.0 90.0 jit_solution(3426289787817574638)
XLA Ops:
  0.6 3.1 %collective-permute-start.2 = (bf16[1,128,512]{2,1,0:T(8,128)(2,1)}, bf16[1,128,512]{2,1,0:T(8,128)(2,1)S(1)}, u32[]{:S(2)}, u32[]{:S(2)}) collective-permute-start(bf16[1,128,512]{2,1,0:T(8,128)(2,1)} %refs_3_.1), channel_id=1, source_target_pairs={{0,2},{4,0},{6,4},{2,6},{1,3},{5,1},{7,5},{3,7},{8,10},{12,8},{14,... | collective-permute-start | bytes 393224 | tf_op jit(solution)/shard_map/ppermute | solution.py:28
  3.7 1.1 %collective-permute-start.1 = (bf16[1,128,512]{2,1,0:T(8,128)(2,1)}, bf16[1,128,512]{2,1,0:T(8,128)(2,1)S(1)}, u32[]{:S(2)}, u32[]{:S(2)}) collective-permute-start(bf16[1,128,512]{2,1,0:T(8,128)(2,1)} %refs_3_.1), channel_id=1, source_target_pairs={{0,4},{4,6},{6,2},{2,0},{1,5},{5,7},{7,3},{3,1},{8,12},{12,14},{14... | collective-permute-start | bytes 393224 | tf_op jit(solution)/shard_map/ppermute | solution.py:28
  4.8 2.3 %prepare.1 = (bf16[1,144,512]{2,1,0:T(8,128)(2,1)}, f32[128,128]{1,0:T(8,128)}, bf16[512,128]{1,0:T(8,128)(2,1)}, bf16[512,128]{1,0:T(8,128)(2,1)}, bf16[512,128]{1,0:T(8,128)(2,1)}, /*index=5*/bf16[512,128]{1,0:T(8,128)(2,1)}) custom-call(s32[1,2]{1,0:T(1,128)} %span_source.1, bf16[1,128,512]{2,1,0:T(8,128)(2,1)} %key_ref.1, bf16[1,128,4096]{2,1,0:T(8,128)(2,1)} %cot_source.1), custom_call_target="tpu_custom_call" | custom-call | tf_op jit(solution)/shard_map/prepare/pallas_call | solution.py:209
  7.1 1.6 %collective-permute-start.3 = (bf16[1,144,512]{2,1,0:T(8,128)(2,1)}, bf16[1,144,512]{2,1,0:T(8,128)(2,1)S(1)}, u32[]{:S(2)}, u32[]{:S(2)}) collective-permute-start(bf16[1,144,512]{2,1,0:T(8,128)(2,1)} %get-tuple-element.24.refs_1_), channel_id=1, source_target_pairs={{0,2},{4,0},{6,4},{2,6},{1,3},{5,1},{7,5},{3,7},{8,10},{12,8},{14,... | collective-permute-start | bytes 442376 | tf_op jit(solution)/shard_map/ppermute | solution.py:28
  8.7 1.4 %collective-permute-start = (bf16[1,144,512]{2,1,0:T(8,128)(2,1)}, bf16[1,144,512]{2,1,0:T(8,128)(2,1)S(1)}, u32[]{:S(2)}, u32[]{:S(2)}) collective-permute-start(bf16[1,144,512]{2,1,0:T(8,128)(2,1)} %get-tuple-element.24.refs_1_), channel_id=1, source_target_pairs={{0,4},{4,6},{6,2},{2,0},{1,5},{5,7},{7,3},{3,1},{8,12},{12,14},{14... | collective-permute-start | bytes 442376 | tf_op jit(solution)/shard_map/ppermute | solution.py:28
  10.1 1.6 %collective-permute-start.4 = (bf16[512,128]{1,0:T(8,128)(2,1)}, bf16[512,128]{1,0:T(8,128)(2,1)S(1)}, u32[]{:S(2)}, u32[]{:S(2)}) collective-permute-start(bf16[512,128]{1,0:T(8,128)(2,1)} %get-tuple-element.31), channel_id=1, source_target_pairs={{0,4},{4,6},{6,2},{2,0},{1,5},{5,7},{7,3},{3,1},{8,12},{12,14},{14... | collective-permute-start | bytes 393224 | tf_op jit(solution)/shard_map/ppermute | solution.py:28
  11.6 3.8 %collective-permute-start.5 = (bf16[512,128]{1,0:T(8,128)(2,1)}, bf16[512,128]{1,0:T(8,128)(2,1)S(1)}, u32[]{:S(2)}, u32[]{:S(2)}) collective-permute-start(bf16[512,128]{1,0:T(8,128)(2,1)} %get-tuple-element.32), channel_id=1, source_target_pairs={{0,6},{4,2},{6,0},{2,4},{1,7},{5,3},{7,1},{3,5},{8,14},{12,10},{14... | collective-permute-start | bytes 393224 | tf_op jit(solution)/shard_map/ppermute | solution.py:28
  15.5 1.0 %copy-done = bf16[1,128,2048]{2,1,0:T(8,128)(2,1)S(1)} copy-done((bf16[1,128,2048]{2,1,0:T(8,128)(2,1)S(1)}, bf16[1,128,2048]{2,1,0:T(8,128)(2,1)}, u32[]{:S(2)}) %copy-start) | copy-done | bytes 524312
  16.5 0.9 %copy-done.1 = bf16[1,144,512]{2,1,0:T(8,128)(2,1)S(1)} copy-done((bf16[1,144,512]{2,1,0:T(8,128)(2,1)S(1)}, bf16[1,144,512]{2,1,0:T(8,128)(2,1)}, u32[]{:S(2)}) %copy-start.1) | copy-done | bytes 147480
  17.4 0.9 %copy-done.2 = bf16[1,128,512]{2,1,0:T(8,128)(2,1)S(1)} copy-done((bf16[1,128,512]{2,1,0:T(8,128)(2,1)S(1)}, bf16[1,128,512]{2,1,0:T(8,128)(2,1)}, u32[]{:S(2)}) %copy-start.2) | copy-done | bytes 131096
  18.4 0.9 %copy-done.3 = bf16[512,128]{1,0:T(8,128)(2,1)S(1)} copy-done((bf16[512,128]{1,0:T(8,128)(2,1)S(1)}, bf16[512,128]{1,0:T(8,128)(2,1)}, u32[]{:S(2)}) %copy-start.3) | copy-done | bytes 131096
  19.3 0.8 copy-done.4
  20.2 3.6 %collective-permute-done.3.refs_3_ = bf16[1,144,512]{2,1,0:T(8,128)(2,1)S(1)} collective-permute-done((bf16[1,144,512]{2,1,0:T(8,128)(2,1)}, bf16[1,144,512]{2,1,0:T(8,128)(2,1)S(1)}, u32[]{:S(2)}, u32[]{:S(2)}) %collective-permute-start.3) | collective-permute-done | bytes 147488 | tf_op jit(solution)/shard_map/ppermute | solution.py:28
  23.8 1.5 %collective-permute-done.5.refs_2_ = bf16[512,128]{1,0:T(8,128)(2,1)S(1)} collective-permute-done((bf16[512,128]{1,0:T(8,128)(2,1)}, bf16[512,128]{1,0:T(8,128)(2,1)S(1)}, u32[]{:S(2)}, u32[]{:S(2)}) %collective-permute-start.5) | collective-permute-done | bytes 131104 | tf_op jit(solution)/shard_map/ppermute | solution.py:28
  25.3 4.8 %collective-permute-done.6.refs_3_ = bf16[512,128]{1,0:T(8,128)(2,1)S(1)} collective-permute-done((bf16[512,128]{1,0:T(8,128)(2,1)}, bf16[512,128]{1,0:T(8,128)(2,1)S(1)}, u32[]{:S(2)}, u32[]{:S(2)}) %collective-permute-start.6) | collective-permute-done | bytes 131104 | tf_op jit(solution)/shard_map/ppermute | solution.py:28
  30.0 0.1 join.1.refs_6_.refs_2_
  30.2 2.0 %collective-permute-start.8 = (bf16[1,128,512]{2,1,0:T(8,128)(2,1)S(1)}, bf16[1,128,512]{2,1,0:T(8,128)(2,1)S(1)}, u32[]{:S(2)}, u32[]{:S(2)}) collective-permute-start(bf16[1,128,512]{2,1,0:T(8,128)(2,1)S(1)} %collective-permute-done.2.refs_7_), channel_id=1, source_target_pairs={{0,2},{4,0},{6,4},{2,6},{1,3},{5,1},{7,5},{3,7},{8,10},{12,8},{14,... | collective-permute-start | bytes 393224 | tf_op jit(solution)/shard_map/ppermute | solution.py:28
  32.2 1.5 %collective-permute-start.15 = (bf16[512,512]{1,0:T(8,128)(2,1)S(1)}, bf16[512,512]{1,0:T(8,128)(2,1)S(1)}, u32[]{:S(2)}, u32[]{:S(2)}) collective-permute-start(bf16[512,512]{1,0:T(8,128)(2,1)S(1)} %join.1.refs_6_.refs_2_), channel_id=1, source_target_pairs={{0,16},{8,24},{16,0},{24,8},{1,17},{9,25},{17,1},{25,9},{2,18},{10... | collective-permute-start | bytes 1572872 | tf_op jit(solution)/shard_map/ppermute | solution.py:44
  33.7 5.0 %collective-permute-done.8.refs_6_ = bf16[1,128,512]{2,1,0:T(8,128)(2,1)S(1)} collective-permute-done((bf16[1,128,512]{2,1,0:T(8,128)(2,1)S(1)}, bf16[1,128,512]{2,1,0:T(8,128)(2,1)S(1)}, u32[]{:S(2)}, u32[]{:S(2)}) %collective-permute-start.8) | collective-permute-done | bytes 131104 | tf_op jit(solution)/shard_map/ppermute | solution.py:28
  38.8 2.5 %attend.1 = (bf16[1,128,2048]{2,1,0:T(8,128)(2,1)}, bf16[1,128,1024]{2,1,0:T(8,128)(2,1)S(1)}, bf16[1,128,1024]{2,1,0:T(8,128)(2,1)S(1)}) custom-call(f32[128,128]{1,0:T(8,128)S(1)} %get-tuple-element.26.place_ref, bf16[1,128,2048]{2,1,0:T(8,128)(2,1)S(1)} %get-tuple-element.27.query_ref, bf16[1,144,512]{2,1,0:T(8,128)(2,1)S(1)} %get-tuple-element.28.refs_0_, ...), custom_call_target="tpu_custom_call" | custom-call | tf_op jit(solution)/shard_map/attend/pallas_call | solution.py:249
  41.3 1.5 %collective-permute-start.10 = (bf16[1,128,1024]{2,1,0:T(8,128)(2,1)S(1)}, bf16[1,128,1024]{2,1,0:T(8,128)(2,1)S(1)}, u32[]{:S(2)}, u32[]{:S(2)}) collective-permute-start(bf16[1,128,1024]{2,1,0:T(8,128)(2,1)S(1)} %get-tuple-element.38.refs_0_), channel_id=1, source_target_pairs={{0,16},{8,24},{16,0},{24,8},{1,17},{9,25},{17,1},{25,9},{2,18},{10... | collective-permute-start | bytes 786440 | tf_op jit(solution)/shard_map/ppermute | solution.py:44
  42.8 0.6 collective-permute-start.9
  43.4 0.5 collective-permute-start.20
  43.9 2.0 %collective-permute-start.19 = (bf16[1,128,1024]{2,1,0:T(8,128)(2,1)S(1)}, bf16[1,128,1024]{2,1,0:T(8,128)(2,1)S(1)}, u32[]{:S(2)}, u32[]{:S(2)}) collective-permute-start(bf16[1,128,1024]{2,1,0:T(8,128)(2,1)S(1)} %get-tuple-element.41.refs_0_), channel_id=1, source_target_pairs={{0,4},{4,6},{6,2},{2,0},{1,5},{5,7},{7,3},{3,1},{8,12},{12,14},{14... | collective-permute-start | bytes 786440 | tf_op jit(solution)/shard_map/ppermute | solution.py:28
  45.9 6.7 %collective-permute-done.10.refs_3_ = bf16[1,128,1024]{2,1,0:T(8,128)(2,1)S(1)} collective-permute-done((bf16[1,128,1024]{2,1,0:T(8,128)(2,1)S(1)}, bf16[1,128,1024]{2,1,0:T(8,128)(2,1)S(1)}, u32[]{:S(2)}, u32[]{:S(2)}) %collective-permute-start.10) | collective-permute-done | bytes 262176 | tf_op jit(solution)/shard_map/ppermute | solution.py:44
  52.6 1.3 %collective-permute-start.12 = (bf16[1,128,1024]{2,1,0:T(8,128)(2,1)S(1)}, bf16[1,128,1024]{2,1,0:T(8,128)(2,1)S(1)}, u32[]{:S(2)}, u32[]{:S(2)}) collective-permute-start(bf16[1,128,1024]{2,1,0:T(8,128)(2,1)S(1)} %collective-permute-done.9.refs_1_), channel_id=1, source_target_pairs={{0,16},{8,24},{16,0},{24,8},{1,17},{9,25},{17,1},{25,9},{2,18},{10... | collective-permute-start | bytes 786440 | tf_op jit(solution)/shard_map/ppermute | solution.py:44
  53.9 1.5 %collective-permute-start.16 = (bf16[512,512]{1,0:T(8,128)(2,1)S(1)}, bf16[512,512]{1,0:T(8,128)(2,1)S(1)}, u32[]{:S(2)}, u32[]{:S(2)}) collective-permute-start(bf16[512,512]{1,0:T(8,128)(2,1)S(1)} %join.1.refs_6_.refs_2_), channel_id=1, source_target_pairs={{0,1},{1,0},{2,3},{3,2},{4,5},{5,4},{6,7},{7,6},{8,9},{9,8},{10,11... | collective-permute-start | bytes 1572872 | tf_op jit(solution)/shard_map/ppermute | solution.py:44
  55.3 2.9 %collective-permute-done.20.refs_3_ = bf16[1,128,1024]{2,1,0:T(8,128)(2,1)S(1)} collective-permute-done((bf16[1,128,1024]{2,1,0:T(8,128)(2,1)S(1)}, bf16[1,128,1024]{2,1,0:T(8,128)(2,1)S(1)}, u32[]{:S(2)}, u32[]{:S(2)}) %collective-permute-start.20) | collective-permute-done | bytes 262176 | tf_op jit(solution)/shard_map/ppermute | solution.py:44
  58.2 1.1 %collective-permute-start.11 = (bf16[1,128,1024]{2,1,0:T(8,128)(2,1)S(1)}, bf16[1,128,1024]{2,1,0:T(8,128)(2,1)S(1)}, u32[]{:S(2)}, u32[]{:S(2)}) collective-permute-start(bf16[1,128,1024]{2,1,0:T(8,128)(2,1)S(1)} %collective-permute-done.9.refs_1_), channel_id=1, source_target_pairs={{0,4},{4,6},{6,2},{2,0},{1,5},{5,7},{7,3},{3,1},{8,12},{12,14},{14... | collective-permute-start | bytes 786440 | tf_op jit(solution)/shard_map/ppermute | solution.py:28
  59.3 1.5 %collective-permute-start.22 = (bf16[1,128,1024]{2,1,0:T(8,128)(2,1)S(1)}, bf16[1,128,1024]{2,1,0:T(8,128)(2,1)S(1)}, u32[]{:S(2)}, u32[]{:S(2)}) collective-permute-start(bf16[1,128,1024]{2,1,0:T(8,128)(2,1)S(1)} %collective-permute-done.19.refs_1_), channel_id=1, source_target_pairs={{0,16},{8,24},{16,0},{24,8},{1,17},{9,25},{17,1},{25,9},{2,18},{10... | collective-permute-start | bytes 786440 | tf_op jit(solution)/shard_map/ppermute | solution.py:44
  60.8 1.1 %collective-permute-start.21 = (bf16[1,128,1024]{2,1,0:T(8,128)(2,1)S(1)}, bf16[1,128,1024]{2,1,0:T(8,128)(2,1)S(1)}, u32[]{:S(2)}, u32[]{:S(2)}) collective-permute-start(bf16[1,128,1024]{2,1,0:T(8,128)(2,1)S(1)} %collective-permute-done.19.refs_1_), channel_id=1, source_target_pairs={{0,4},{4,6},{6,2},{2,0},{1,5},{5,7},{7,3},{3,1},{8,12},{12,14},{14... | collective-permute-start | bytes 786440 | tf_op jit(solution)/shard_map/ppermute | solution.py:28
  61.9 1.9 %collective-permute-done.12.refs_4_ = bf16[1,128,1024]{2,1,0:T(8,128)(2,1)S(1)} collective-permute-done((bf16[1,128,1024]{2,1,0:T(8,128)(2,1)S(1)}, bf16[1,128,1024]{2,1,0:T(8,128)(2,1)S(1)}, u32[]{:S(2)}, u32[]{:S(2)}) %collective-permute-start.12) | collective-permute-done | bytes 262176 | tf_op jit(solution)/shard_map/ppermute | solution.py:44
  63.8 1.2 %collective-permute-start.17 = (bf16[512,512]{1,0:T(8,128)(2,1)S(1)}, bf16[512,512]{1,0:T(8,128)(2,1)S(1)}, u32[]{:S(2)}, u32[]{:S(2)}) collective-permute-start(bf16[512,512]{1,0:T(8,128)(2,1)S(1)} %collective-permute-done.15.refs_7_.refs_3_), channel_id=1, source_target_pairs={{0,1},{1,0},{2,3},{3,2},{4,5},{5,4},{6,7},{7,6},{8,9},{9,8},{10,11... | collective-permute-start | bytes 1572872 | tf_op jit(solution)/shard_map/ppermute | solution.py:44
  65.1 2.4 %collective-permute-done.11.refs_2_ = bf16[1,128,1024]{2,1,0:T(8,128)(2,1)S(1)} collective-permute-done((bf16[1,128,1024]{2,1,0:T(8,128)(2,1)S(1)}, bf16[1,128,1024]{2,1,0:T(8,128)(2,1)S(1)}, u32[]{:S(2)}, u32[]{:S(2)}) %collective-permute-start.11) | collective-permute-done | bytes 262176 | tf_op jit(solution)/shard_map/ppermute | solution.py:28
  67.5 2.0 %collective-permute-start.13 = (bf16[1,128,1024]{2,1,0:T(8,128)(2,1)S(1)}, bf16[1,128,1024]{2,1,0:T(8,128)(2,1)S(1)}, u32[]{:S(2)}, u32[]{:S(2)}) collective-permute-start(bf16[1,128,1024]{2,1,0:T(8,128)(2,1)S(1)} %collective-permute-done.11.refs_2_), channel_id=1, source_target_pairs={{0,4},{4,6},{6,2},{2,0},{1,5},{5,7},{7,3},{3,1},{8,12},{12,14},{14... | collective-permute-start | bytes 786440 | tf_op jit(solution)/shard_map/ppermute | solution.py:28
  69.4 3.6 %collective-permute-done.21.refs_2_ = bf16[1,128,1024]{2,1,0:T(8,128)(2,1)S(1)} collective-permute-done((bf16[1,128,1024]{2,1,0:T(8,128)(2,1)S(1)}, bf16[1,128,1024]{2,1,0:T(8,128)(2,1)S(1)}, u32[]{:S(2)}, u32[]{:S(2)}) %collective-permute-start.21) | collective-permute-done | bytes 262176 | tf_op jit(solution)/shard_map/ppermute | solution.py:28
  73.1 1.3 %collective-permute-start.24 = (bf16[1,128,1024]{2,1,0:T(8,128)(2,1)S(1)}, bf16[1,128,1024]{2,1,0:T(8,128)(2,1)S(1)}, u32[]{:S(2)}, u32[]{:S(2)}) collective-permute-start(bf16[1,128,1024]{2,1,0:T(8,128)(2,1)S(1)} %collective-permute-done.21.refs_2_), channel_id=1, source_target_pairs={{0,16},{8,24},{16,0},{24,8},{1,17},{9,25},{17,1},{25,9},{2,18},{10... | collective-permute-start | bytes 786440 | tf_op jit(solution)/shard_map/ppermute | solution.py:44
  74.3 0.8 collective-permute-start.18
  75.1 2.0 %collective-permute-start.23 = (bf16[1,128,1024]{2,1,0:T(8,128)(2,1)S(1)}, bf16[1,128,1024]{2,1,0:T(8,128)(2,1)S(1)}, u32[]{:S(2)}, u32[]{:S(2)}) collective-permute-start(bf16[1,128,1024]{2,1,0:T(8,128)(2,1)S(1)} %collective-permute-done.21.refs_2_), channel_id=1, source_target_pairs={{0,4},{4,6},{6,2},{2,0},{1,5},{5,7},{7,3},{3,1},{8,12},{12,14},{14... | collective-permute-start | bytes 786440 | tf_op jit(solution)/shard_map/ppermute | solution.py:28
  77.1 1.6 %collective-permute-done.13.refs_0_ = bf16[1,128,1024]{2,1,0:T(8,128)(2,1)S(1)} collective-permute-done((bf16[1,128,1024]{2,1,0:T(8,128)(2,1)S(1)}, bf16[1,128,1024]{2,1,0:T(8,128)(2,1)S(1)}, u32[]{:S(2)}, u32[]{:S(2)}) %collective-permute-start.13) | collective-permute-done | bytes 262176 | tf_op jit(solution)/shard_map/ppermute | solution.py:28
  78.7 1.3 %collective-permute-start.14 = (bf16[1,128,1024]{2,1,0:T(8,128)(2,1)S(1)}, bf16[1,128,1024]{2,1,0:T(8,128)(2,1)S(1)}, u32[]{:S(2)}, u32[]{:S(2)}) collective-permute-start(bf16[1,128,1024]{2,1,0:T(8,128)(2,1)S(1)} %collective-permute-done.13.refs_0_), channel_id=1, source_target_pairs={{0,16},{8,24},{16,0},{24,8},{1,17},{9,25},{17,1},{25,9},{2,18},{10... | collective-permute-start | bytes 786440 | tf_op jit(solution)/shard_map/ppermute | solution.py:44
  79.9 0.4 collective-permute-done.24.refs_5_
  80.3 1.9 %collective-permute-start.25 = (bf16[1,128,1024]{2,1,0:T(8,128)(2,1)S(1)}, bf16[1,128,1024]{2,1,0:T(8,128)(2,1)S(1)}, u32[]{:S(2)}, u32[]{:S(2)}) collective-permute-start(bf16[1,128,1024]{2,1,0:T(8,128)(2,1)S(1)} %collective-permute-done.24.refs_5_), channel_id=1, source_target_pairs={{0,4},{4,6},{6,2},{2,0},{1,5},{5,7},{7,3},{3,1},{8,12},{12,14},{14... | collective-permute-start | bytes 786440 | tf_op jit(solution)/shard_map/ppermute | solution.py:28
  82.2 1.8 %early.3.refs_6_ = f32[1024,1024]{1,0:T(8,128)S(1)} custom-call(bf16[1,128,1024]{2,1,0:T(8,128)(2,1)S(1)} %get-tuple-element.41.refs_0_, bf16[1,128,1024]{2,1,0:T(8,128)(2,1)S(1)} %collective-permute-done.19.refs_1_, bf16[1,128,1024]{2,1,0:T(8,128)(2,1)S(1)} %collective-permute-done.21.refs_2_, bf16[1,128,1024]{2,1,0:T(8,128)(2,1)S(1)} %collective-permute-done.20.refs_3_, ...), custom_call_target="tpu_custom_call" | custom-call | flops 1610612736 | bytes 8388608 | tf_op jit(solution)/shard_map/early/pallas_call | solution.py:279
  84.0 1.8 %early.2.refs_6_ = f32[1024,1024]{1,0:T(8,128)S(1)} custom-call(bf16[1,128,1024]{2,1,0:T(8,128)(2,1)S(1)} %get-tuple-element.38.refs_0_, bf16[1,128,1024]{2,1,0:T(8,128)(2,1)S(1)} %collective-permute-done.9.refs_1_, bf16[1,128,1024]{2,1,0:T(8,128)(2,1)S(1)} %collective-permute-done.11.refs_2_, bf16[1,128,1024]{2,1,0:T(8,128)(2,1)S(1)} %collective-permute-done.10.refs_3_, ...), custom_call_target="tpu_custom_call" | custom-call | flops 1610612736 | bytes 8388608 | tf_op jit(solution)/shard_map/early/pallas_call | solution.py:279
  85.8 0.9 collective-permute-done.25.refs_1_
  86.7 1.6 %finish.2.refs_7_ = bf16[1,1024,2048]{2,1,0:T(8,128)(2,1)} custom-call(bf16[1,128,1024]{2,1,0:T(8,128)(2,1)S(1)} %collective-permute-done.23.refs_0_, bf16[1,128,1024]{2,1,0:T(8,128)(2,1)S(1)} %collective-permute-done.25.refs_1_, bf16[512,512]{1,0:T(8,128)(2,1)S(1)} %join.1.refs_6_.refs_2_, bf16[512,512]{1,0:T(8,128)(2,1)S(1)} %collective-permute-done.15.refs_7_.refs_3_, ...), custom_call_target="tpu_custom_call" | custom-call | flops 536870912 | bytes 8388608 | tf_op jit(solution)/shard_map/finish/pallas_call | solution.py:304
  88.4 1.7 %finish.3 = bf16[1,1024,2048]{2,1,0:T(8,128)(2,1)} custom-call(bf16[1,128,1024]{2,1,0:T(8,128)(2,1)S(1)} %collective-permute-done.13.refs_0_, bf16[1,128,1024]{2,1,0:T(8,128)(2,1)S(1)} %collective-permute-done.14.refs_1_, bf16[512,512]{1,0:T(8,128)(2,1)S(1)} %join.1.refs_6_.refs_2_, ...), custom_call_target="tpu_custom_call", output_to_operand_aliasing={{}: (7, {})} | custom-call | flops 536870912 | bytes 8388608 | tf_op jit(solution)/shard_map/finish/pallas_call | solution.py:304
  (22 shorter events, 0.2 us)
Async XLA Ops:
  0.6 11.0 %collective-permute-start.2 = (bf16[1,128,512]{2,1,0:T(8,128)(2,1)}, bf16[1,128,512]{2,1,0:T(8,128)(2,1)S(1)}, u32[]{:S(2)}, u32[]{:S(2)}) collective-permute-start(bf16[1,128,512]{2,1,0:T(8,128)(2,1)} %refs_3_.1), channel_id=1, source_target_pairs={{0,2},{4,0},{6,4},{2,6},{1,3},{5,1},{7,5},{3,7},{8,10},{12,8},{14,... | collective-permute-start | bytes 393224 | tf_op jit(solution)/shard_map/ppermute | solution.py:28
  3.7 11.8 %collective-permute-start.1 = (bf16[1,128,512]{2,1,0:T(8,128)(2,1)}, bf16[1,128,512]{2,1,0:T(8,128)(2,1)S(1)}, u32[]{:S(2)}, u32[]{:S(2)}) collective-permute-start(bf16[1,128,512]{2,1,0:T(8,128)(2,1)} %refs_3_.1), channel_id=1, source_target_pairs={{0,4},{4,6},{6,2},{2,0},{1,5},{5,7},{7,3},{3,1},{8,12},{12,14},{14... | collective-permute-start | bytes 393224 | tf_op jit(solution)/shard_map/ppermute | solution.py:28
  7.1 16.7 %collective-permute-start.3 = (bf16[1,144,512]{2,1,0:T(8,128)(2,1)}, bf16[1,144,512]{2,1,0:T(8,128)(2,1)S(1)}, u32[]{:S(2)}, u32[]{:S(2)}) collective-permute-start(bf16[1,144,512]{2,1,0:T(8,128)(2,1)} %get-tuple-element.24.refs_1_), channel_id=1, source_target_pairs={{0,2},{4,0},{6,4},{2,6},{1,3},{5,1},{7,5},{3,7},{8,10},{12,8},{14,... | collective-permute-start | bytes 442376 | tf_op jit(solution)/shard_map/ppermute | solution.py:28
  8.7 21.5 %collective-permute-start = (bf16[1,144,512]{2,1,0:T(8,128)(2,1)}, bf16[1,144,512]{2,1,0:T(8,128)(2,1)S(1)}, u32[]{:S(2)}, u32[]{:S(2)}) collective-permute-start(bf16[1,144,512]{2,1,0:T(8,128)(2,1)} %get-tuple-element.24.refs_1_), channel_id=1, source_target_pairs={{0,4},{4,6},{6,2},{2,0},{1,5},{5,7},{7,3},{3,1},{8,12},{12,14},{14... | collective-permute-start | bytes 442376 | tf_op jit(solution)/shard_map/ppermute | solution.py:28
  10.1 13.7 %collective-permute-start.4 = (bf16[512,128]{1,0:T(8,128)(2,1)}, bf16[512,128]{1,0:T(8,128)(2,1)S(1)}, u32[]{:S(2)}, u32[]{:S(2)}) collective-permute-start(bf16[512,128]{1,0:T(8,128)(2,1)} %get-tuple-element.31), channel_id=1, source_target_pairs={{0,4},{4,6},{6,2},{2,0},{1,5},{5,7},{7,3},{3,1},{8,12},{12,14},{14... | collective-permute-start | bytes 393224 | tf_op jit(solution)/shard_map/ppermute | solution.py:28
  11.6 13.6 %collective-permute-start.5 = (bf16[512,128]{1,0:T(8,128)(2,1)}, bf16[512,128]{1,0:T(8,128)(2,1)S(1)}, u32[]{:S(2)}, u32[]{:S(2)}) collective-permute-start(bf16[512,128]{1,0:T(8,128)(2,1)} %get-tuple-element.32), channel_id=1, source_target_pairs={{0,6},{4,2},{6,0},{2,4},{1,7},{5,3},{7,1},{3,5},{8,14},{12,10},{14... | collective-permute-start | bytes 393224 | tf_op jit(solution)/shard_map/ppermute | solution.py:28
  15.5 14.5 %collective-permute-start.6 = (bf16[512,128]{1,0:T(8,128)(2,1)}, bf16[512,128]{1,0:T(8,128)(2,1)S(1)}, u32[]{:S(2)}, u32[]{:S(2)}) collective-permute-start(bf16[512,128]{1,0:T(8,128)(2,1)} %get-tuple-element.33), channel_id=1, source_target_pairs={{0,2},{4,0},{6,4},{2,6},{1,3},{5,1},{7,5},{3,7},{8,10},{12,8},{14,... | collective-permute-start | bytes 393224 | tf_op jit(solution)/shard_map/ppermute | solution.py:28
  15.5 1.0 %copy-start = (bf16[1,128,2048]{2,1,0:T(8,128)(2,1)S(1)}, bf16[1,128,2048]{2,1,0:T(8,128)(2,1)}, u32[]{:S(2)}) copy-start(bf16[1,128,2048]{2,1,0:T(8,128)(2,1)} %refs_2_.1) | copy-start | bytes 1572868
  16.5 0.9 %copy-start.1 = (bf16[1,144,512]{2,1,0:T(8,128)(2,1)S(1)}, bf16[1,144,512]{2,1,0:T(8,128)(2,1)}, u32[]{:S(2)}) copy-start(bf16[1,144,512]{2,1,0:T(8,128)(2,1)} %get-tuple-element.24.refs_1_) | copy-start | bytes 442372
  17.4 0.9 %copy-start.2 = (bf16[1,128,512]{2,1,0:T(8,128)(2,1)S(1)}, bf16[1,128,512]{2,1,0:T(8,128)(2,1)}, u32[]{:S(2)}) copy-start(bf16[1,128,512]{2,1,0:T(8,128)(2,1)} %refs_3_.1) | copy-start | bytes 393220
  18.4 0.9 %copy-start.3 = (bf16[512,128]{1,0:T(8,128)(2,1)S(1)}, bf16[512,128]{1,0:T(8,128)(2,1)}, u32[]{:S(2)}) copy-start(bf16[512,128]{1,0:T(8,128)(2,1)} %get-tuple-element.25.refs_4_) | copy-start | bytes 393220
  19.3 0.8 copy-start.4
  30.1 8.6 %collective-permute-start.7 = (bf16[1,144,512]{2,1,0:T(8,128)(2,1)S(1)}, bf16[1,144,512]{2,1,0:T(8,128)(2,1)S(1)}, u32[]{:S(2)}, u32[]{:S(2)}) collective-permute-start(bf16[1,144,512]{2,1,0:T(8,128)(2,1)S(1)} %collective-permute-done.refs_1_), channel_id=1, source_target_pairs={{0,4},{4,6},{6,2},{2,0},{1,5},{5,7},{7,3},{3,1},{8,12},{12,14},{14... | collective-permute-start | bytes 442376 | tf_op jit(solution)/shard_map/ppermute | solution.py:28
  30.2 8.6 %collective-permute-start.8 = (bf16[1,128,512]{2,1,0:T(8,128)(2,1)S(1)}, bf16[1,128,512]{2,1,0:T(8,128)(2,1)S(1)}, u32[]{:S(2)}, u32[]{:S(2)}) collective-permute-start(bf16[1,128,512]{2,1,0:T(8,128)(2,1)S(1)} %collective-permute-done.2.refs_7_), channel_id=1, source_target_pairs={{0,2},{4,0},{6,4},{2,6},{1,3},{5,1},{7,5},{3,7},{8,10},{12,8},{14,... | collective-permute-start | bytes 393224 | tf_op jit(solution)/shard_map/ppermute | solution.py:28
  32.2 28.6 %collective-permute-start.15 = (bf16[512,512]{1,0:T(8,128)(2,1)S(1)}, bf16[512,512]{1,0:T(8,128)(2,1)S(1)}, u32[]{:S(2)}, u32[]{:S(2)}) collective-permute-start(bf16[512,512]{1,0:T(8,128)(2,1)S(1)} %join.1.refs_6_.refs_2_), channel_id=1, source_target_pairs={{0,16},{8,24},{16,0},{24,8},{1,17},{9,25},{17,1},{25,9},{2,18},{10... | collective-permute-start | bytes 1572872 | tf_op jit(solution)/shard_map/ppermute | solution.py:44
  41.3 11.3 %collective-permute-start.10 = (bf16[1,128,1024]{2,1,0:T(8,128)(2,1)S(1)}, bf16[1,128,1024]{2,1,0:T(8,128)(2,1)S(1)}, u32[]{:S(2)}, u32[]{:S(2)}) collective-permute-start(bf16[1,128,1024]{2,1,0:T(8,128)(2,1)S(1)} %get-tuple-element.38.refs_0_), channel_id=1, source_target_pairs={{0,16},{8,24},{16,0},{24,8},{1,17},{9,25},{17,1},{25,9},{2,18},{10... | collective-permute-start | bytes 786440 | tf_op jit(solution)/shard_map/ppermute | solution.py:44
  42.8 9.8 %collective-permute-start.9 = (bf16[1,128,1024]{2,1,0:T(8,128)(2,1)S(1)}, bf16[1,128,1024]{2,1,0:T(8,128)(2,1)S(1)}, u32[]{:S(2)}, u32[]{:S(2)}) collective-permute-start(bf16[1,128,1024]{2,1,0:T(8,128)(2,1)S(1)} %get-tuple-element.38.refs_0_), channel_id=1, source_target_pairs={{0,4},{4,6},{6,2},{2,0},{1,5},{5,7},{7,3},{3,1},{8,12},{12,14},{14... | collective-permute-start | bytes 786440 | tf_op jit(solution)/shard_map/ppermute | solution.py:28
  43.4 14.9 %collective-permute-start.20 = (bf16[1,128,1024]{2,1,0:T(8,128)(2,1)S(1)}, bf16[1,128,1024]{2,1,0:T(8,128)(2,1)S(1)}, u32[]{:S(2)}, u32[]{:S(2)}) collective-permute-start(bf16[1,128,1024]{2,1,0:T(8,128)(2,1)S(1)} %get-tuple-element.41.refs_0_), channel_id=1, source_target_pairs={{0,16},{8,24},{16,0},{24,8},{1,17},{9,25},{17,1},{25,9},{2,18},{10... | collective-permute-start | bytes 786440 | tf_op jit(solution)/shard_map/ppermute | solution.py:44
  43.9 15.4 %collective-permute-start.19 = (bf16[1,128,1024]{2,1,0:T(8,128)(2,1)S(1)}, bf16[1,128,1024]{2,1,0:T(8,128)(2,1)S(1)}, u32[]{:S(2)}, u32[]{:S(2)}) collective-permute-start(bf16[1,128,1024]{2,1,0:T(8,128)(2,1)S(1)} %get-tuple-element.41.refs_0_), channel_id=1, source_target_pairs={{0,4},{4,6},{6,2},{2,0},{1,5},{5,7},{7,3},{3,1},{8,12},{12,14},{14... | collective-permute-start | bytes 786440 | tf_op jit(solution)/shard_map/ppermute | solution.py:28
  52.6 11.2 %collective-permute-start.12 = (bf16[1,128,1024]{2,1,0:T(8,128)(2,1)S(1)}, bf16[1,128,1024]{2,1,0:T(8,128)(2,1)S(1)}, u32[]{:S(2)}, u32[]{:S(2)}) collective-permute-start(bf16[1,128,1024]{2,1,0:T(8,128)(2,1)S(1)} %collective-permute-done.9.refs_1_), channel_id=1, source_target_pairs={{0,16},{8,24},{16,0},{24,8},{1,17},{9,25},{17,1},{25,9},{2,18},{10... | collective-permute-start | bytes 786440 | tf_op jit(solution)/shard_map/ppermute | solution.py:44
  53.9 21.2 %collective-permute-start.16 = (bf16[512,512]{1,0:T(8,128)(2,1)S(1)}, bf16[512,512]{1,0:T(8,128)(2,1)S(1)}, u32[]{:S(2)}, u32[]{:S(2)}) collective-permute-start(bf16[512,512]{1,0:T(8,128)(2,1)S(1)} %join.1.refs_6_.refs_2_), channel_id=1, source_target_pairs={{0,1},{1,0},{2,3},{3,2},{4,5},{5,4},{6,7},{7,6},{8,9},{9,8},{10,11... | collective-permute-start | bytes 1572872 | tf_op jit(solution)/shard_map/ppermute | solution.py:44
  58.2 9.2 %collective-permute-start.11 = (bf16[1,128,1024]{2,1,0:T(8,128)(2,1)S(1)}, bf16[1,128,1024]{2,1,0:T(8,128)(2,1)S(1)}, u32[]{:S(2)}, u32[]{:S(2)}) collective-permute-start(bf16[1,128,1024]{2,1,0:T(8,128)(2,1)S(1)} %collective-permute-done.9.refs_1_), channel_id=1, source_target_pairs={{0,4},{4,6},{6,2},{2,0},{1,5},{5,7},{7,3},{3,1},{8,12},{12,14},{14... | collective-permute-start | bytes 786440 | tf_op jit(solution)/shard_map/ppermute | solution.py:28
  59.3 10.1 %collective-permute-start.22 = (bf16[1,128,1024]{2,1,0:T(8,128)(2,1)S(1)}, bf16[1,128,1024]{2,1,0:T(8,128)(2,1)S(1)}, u32[]{:S(2)}, u32[]{:S(2)}) collective-permute-start(bf16[1,128,1024]{2,1,0:T(8,128)(2,1)S(1)} %collective-permute-done.19.refs_1_), channel_id=1, source_target_pairs={{0,16},{8,24},{16,0},{24,8},{1,17},{9,25},{17,1},{25,9},{2,18},{10... | collective-permute-start | bytes 786440 | tf_op jit(solution)/shard_map/ppermute | solution.py:44
  60.8 12.2 %collective-permute-start.21 = (bf16[1,128,1024]{2,1,0:T(8,128)(2,1)S(1)}, bf16[1,128,1024]{2,1,0:T(8,128)(2,1)S(1)}, u32[]{:S(2)}, u32[]{:S(2)}) collective-permute-start(bf16[1,128,1024]{2,1,0:T(8,128)(2,1)S(1)} %collective-permute-done.19.refs_1_), channel_id=1, source_target_pairs={{0,4},{4,6},{6,2},{2,0},{1,5},{5,7},{7,3},{3,1},{8,12},{12,14},{14... | collective-permute-start | bytes 786440 | tf_op jit(solution)/shard_map/ppermute | solution.py:28
  63.8 18.4 %collective-permute-start.17 = (bf16[512,512]{1,0:T(8,128)(2,1)S(1)}, bf16[512,512]{1,0:T(8,128)(2,1)S(1)}, u32[]{:S(2)}, u32[]{:S(2)}) collective-permute-start(bf16[512,512]{1,0:T(8,128)(2,1)S(1)} %collective-permute-done.15.refs_7_.refs_3_), channel_id=1, source_target_pairs={{0,1},{1,0},{2,3},{3,2},{4,5},{5,4},{6,7},{7,6},{8,9},{9,8},{10,11... | collective-permute-start | bytes 1572872 | tf_op jit(solution)/shard_map/ppermute | solution.py:44
  67.5 11.2 %collective-permute-start.13 = (bf16[1,128,1024]{2,1,0:T(8,128)(2,1)S(1)}, bf16[1,128,1024]{2,1,0:T(8,128)(2,1)S(1)}, u32[]{:S(2)}, u32[]{:S(2)}) collective-permute-start(bf16[1,128,1024]{2,1,0:T(8,128)(2,1)S(1)} %collective-permute-done.11.refs_2_), channel_id=1, source_target_pairs={{0,4},{4,6},{6,2},{2,0},{1,5},{5,7},{7,3},{3,1},{8,12},{12,14},{14... | collective-permute-start | bytes 786440 | tf_op jit(solution)/shard_map/ppermute | solution.py:28
  73.1 7.3 %collective-permute-start.24 = (bf16[1,128,1024]{2,1,0:T(8,128)(2,1)S(1)}, bf16[1,128,1024]{2,1,0:T(8,128)(2,1)S(1)}, u32[]{:S(2)}, u32[]{:S(2)}) collective-permute-start(bf16[1,128,1024]{2,1,0:T(8,128)(2,1)S(1)} %collective-permute-done.21.refs_2_), channel_id=1, source_target_pairs={{0,16},{8,24},{16,0},{24,8},{1,17},{9,25},{17,1},{25,9},{2,18},{10... | collective-permute-start | bytes 786440 | tf_op jit(solution)/shard_map/ppermute | solution.py:44
  74.3 9.7 %collective-permute-start.18 = (bf16[1,128,1024]{2,1,0:T(8,128)(2,1)S(1)}, bf16[1,128,1024]{2,1,0:T(8,128)(2,1)S(1)}, u32[]{:S(2)}, u32[]{:S(2)}) collective-permute-start(bf16[1,128,1024]{2,1,0:T(8,128)(2,1)S(1)} %collective-permute-done.11.refs_2_), channel_id=1, source_target_pairs={{0,16},{8,24},{16,0},{24,8},{1,17},{9,25},{17,1},{25,9},{2,18},{10... | collective-permute-start | bytes 786440 | tf_op jit(solution)/shard_map/ppermute | solution.py:44
  75.1 10.7 %collective-permute-start.23 = (bf16[1,128,1024]{2,1,0:T(8,128)(2,1)S(1)}, bf16[1,128,1024]{2,1,0:T(8,128)(2,1)S(1)}, u32[]{:S(2)}, u32[]{:S(2)}) collective-permute-start(bf16[1,128,1024]{2,1,0:T(8,128)(2,1)S(1)} %collective-permute-done.21.refs_2_), channel_id=1, source_target_pairs={{0,4},{4,6},{6,2},{2,0},{1,5},{5,7},{7,3},{3,1},{8,12},{12,14},{14... | collective-permute-start | bytes 786440 | tf_op jit(solution)/shard_map/ppermute | solution.py:28
  78.7 9.7 %collective-permute-start.14 = (bf16[1,128,1024]{2,1,0:T(8,128)(2,1)S(1)}, bf16[1,128,1024]{2,1,0:T(8,128)(2,1)S(1)}, u32[]{:S(2)}, u32[]{:S(2)}) collective-permute-start(bf16[1,128,1024]{2,1,0:T(8,128)(2,1)S(1)} %collective-permute-done.13.refs_0_), channel_id=1, source_target_pairs={{0,16},{8,24},{16,0},{24,8},{1,17},{9,25},{17,1},{25,9},{2,18},{10... | collective-permute-start | bytes 786440 | tf_op jit(solution)/shard_map/ppermute | solution.py:44
  80.3 6.4 %collective-permute-start.25 = (bf16[1,128,1024]{2,1,0:T(8,128)(2,1)S(1)}, bf16[1,128,1024]{2,1,0:T(8,128)(2,1)S(1)}, u32[]{:S(2)}, u32[]{:S(2)}) collective-permute-start(bf16[1,128,1024]{2,1,0:T(8,128)(2,1)S(1)} %collective-permute-done.24.refs_5_), channel_id=1, source_target_pairs={{0,4},{4,6},{6,2},{2,0},{1,5},{5,7},{7,3},{3,1},{8,12},{12,14},{14... | collective-permute-start | bytes 786440 | tf_op jit(solution)/shard_map/ppermute | solution.py:28

commit v12 on v11

--- a/solution.py
+++ b/solution.py
@@ -233,8 +233,8 @@
         name="fetch",
     )(*fetched)
     turned = [turned[0]] + [around(turned[s], s) for s in range(1, n)]
-    key_edges, value_edges = ([around(x, way) for way in (1, -1)] for x in (packed, values))
-    turned[0] = after(turned[0], *value_edges, key_edges[1])
+    value_edges = [around(values, way) for way in (1, -1)]
+    key_edges = [around(after(packed, *value_edges), way) for way in (1, -1)]
     mine = pl.pallas_call(
         join_kernel,
         out_shape=jax.ShapeDtypeStruct((half, n * tokens), jnp.bfloat16),

time: 90.3 us -> 90.5 us (level)
  waiting for transfers between devices: 35.3 us -> 36.3 us
  local copies, waits for them, and re-layouts: 4.6 us -> 3.69 us
    pallas_call x1, Pallas kernels: 0.07 us -> 0.97 us  [local(): pl.pallas_call(fetch_kernel, out_shape=[jax.ShapeDtypeStruct(x.shape, x.d...]
    unnamed x10 -> x8, local copies, waits for them, and re-layouts: 4.6 us -> 3.69 us
  transfers between devices with their start and end apart: 26 -> 26, of which waited for: 12 -> 15; matrix products, arithmetic and copies ran while one was open for 0% -> 0% of each run, Pallas kernels for 11% -> 12%
where the time goes in v12:
time: 90.5 us; the launch traced here: 90.2 us
  starting transfers between devices  36.8 us (41%)
  waiting for transfers between devices  36.3 us (40%)
  Pallas kernels  12.8 us (14%)
  local copies, waits for them, and re-layouts  3.69 us (4%)
    ppermute x16, starting transfers between devices, around(): lax.ppermute(x, 'ctx', [(order[q], order[(q + shift) % n]) for q in range...  24.4 us
    ppermute x16, waiting for transfers between devices, around(): lax.ppermute(x, 'ctx', [(order[q], order[(q + shift) % n]) for q in range...  23.8 us
    ppermute x10, waiting for transfers between devices, swap(): lax.ppermute(x, axis, [(i, i ^ mask) for i in range(lax.axis_size(axis))])  12.4 us
    ppermute x10, starting transfers between devices, swap(): lax.ppermute(x, axis, [(i, i ^ mask) for i in range(lax.axis_size(axis))])  12.4 us
    unnamed x8, local copies, waits for them, and re-layouts  3.69 us
    pallas_call x2, Pallas kernels, local(): pl.pallas_call(functools.partial(early_kernel, first_slots), out_shape=ja...  3.6 us
    pallas_call x2, Pallas kernels, local(): pl.pallas_call(functools.partial(finish_kernel, slots, c * chunk), out_sh...  3.31 us
    pallas_call x1, Pallas kernels, local(): pl.pallas_call(functools.partial(attention_kernel, HQ // HK, 1.0 / math.s...  2.51 us
  transfers between devices with their start and end apart: 26, of which 15 were waited for; matrix products, arithmetic and copies ran while one was open for 0% of the time, Pallas kernels for 12%

profile of v12, /device:TPU:0, one launch (start us, length us, event | category | flops | bytes accessed | tf_op | source)
XLA Modules:
  0.0 90.2 jit_solution(4228827590248808744)
XLA Ops:
  0.6 3.1 %collective-permute-start.1 = (bf16[1,128,512]{2,1,0:T(8,128)(2,1)}, bf16[1,128,512]{2,1,0:T(8,128)(2,1)S(1)}, u32[]{:S(2)}, u32[]{:S(2)}) collective-permute-start(bf16[1,128,512]{2,1,0:T(8,128)(2,1)} %refs_3_.1), channel_id=1, source_target_pairs={{0,2},{4,0},{6,4},{2,6},{1,3},{5,1},{7,5},{3,7},{8,10},{12,8},{14,... | collective-permute-start | bytes 393224 | tf_op jit(solution)/shard_map/ppermute | solution.py:28
  3.7 1.1 %collective-permute-start = (bf16[1,128,512]{2,1,0:T(8,128)(2,1)}, bf16[1,128,512]{2,1,0:T(8,128)(2,1)S(1)}, u32[]{:S(2)}, u32[]{:S(2)}) collective-permute-start(bf16[1,128,512]{2,1,0:T(8,128)(2,1)} %refs_3_.1), channel_id=1, source_target_pairs={{0,4},{4,6},{6,2},{2,0},{1,5},{5,7},{7,3},{3,1},{8,12},{12,14},{14... | collective-permute-start | bytes 393224 | tf_op jit(solution)/shard_map/ppermute | solution.py:28
  4.8 2.3 %prepare.1 = (bf16[1,144,512]{2,1,0:T(8,128)(2,1)}, f32[128,128]{1,0:T(8,128)}, bf16[512,128]{1,0:T(8,128)(2,1)}, bf16[512,128]{1,0:T(8,128)(2,1)}, bf16[512,128]{1,0:T(8,128)(2,1)}, /*index=5*/bf16[512,128]{1,0:T(8,128)(2,1)}) custom-call(s32[1,2]{1,0:T(1,128)} %span_source.1, bf16[1,128,512]{2,1,0:T(8,128)(2,1)} %key_ref.1, bf16[1,128,4096]{2,1,0:T(8,128)(2,1)} %cot_source.1), custom_call_target="tpu_custom_call" | custom-call | tf_op jit(solution)/shard_map/prepare/pallas_call | solution.py:209
  7.1 1.4 %collective-permute-done.1.refs_7_ = bf16[1,128,512]{2,1,0:T(8,128)(2,1)S(1)} collective-permute-done((bf16[1,128,512]{2,1,0:T(8,128)(2,1)}, bf16[1,128,512]{2,1,0:T(8,128)(2,1)S(1)}, u32[]{:S(2)}, u32[]{:S(2)}) %collective-permute-start.1) | collective-permute-done | bytes 131104 | tf_op jit(solution)/shard_map/ppermute | solution.py:28
  8.5 2.7 %collective-permute-done.refs_5_ = bf16[1,128,512]{2,1,0:T(8,128)(2,1)S(1)} collective-permute-done((bf16[1,128,512]{2,1,0:T(8,128)(2,1)}, bf16[1,128,512]{2,1,0:T(8,128)(2,1)S(1)}, u32[]{:S(2)}, u32[]{:S(2)}) %collective-permute-start) | collective-permute-done | bytes 131104 | tf_op jit(solution)/shard_map/ppermute | solution.py:28
  11.2 1.7 %collective-permute-start.2 = (bf16[1,144,512]{2,1,0:T(8,128)(2,1)}, bf16[1,144,512]{2,1,0:T(8,128)(2,1)S(1)}, u32[]{:S(2)}, u32[]{:S(2)}) collective-permute-start(bf16[1,144,512]{2,1,0:T(8,128)(2,1)} %get-tuple-element.29.refs_1_), channel_id=1, source_target_pairs={{0,4},{4,6},{6,2},{2,0},{1,5},{5,7},{7,3},{3,1},{8,12},{12,14},{14... | collective-permute-start | bytes 442376 | tf_op jit(solution)/shard_map/ppermute | solution.py:28
  13.0 2.5 %collective-permute-start.3 = (bf16[512,128]{1,0:T(8,128)(2,1)}, bf16[512,128]{1,0:T(8,128)(2,1)S(1)}, u32[]{:S(2)}, u32[]{:S(2)}) collective-permute-start(bf16[512,128]{1,0:T(8,128)(2,1)} %get-tuple-element.31), channel_id=1, source_target_pairs={{0,4},{4,6},{6,2},{2,0},{1,5},{5,7},{7,3},{3,1},{8,12},{12,14},{14... | collective-permute-start | bytes 393224 | tf_op jit(solution)/shard_map/ppermute | solution.py:28
  15.6 0.8 collective-permute-start.5
  16.5 1.0 %copy-done = bf16[1,128,2048]{2,1,0:T(8,128)(2,1)S(1)} copy-done((bf16[1,128,2048]{2,1,0:T(8,128)(2,1)S(1)}, bf16[1,128,2048]{2,1,0:T(8,128)(2,1)}, u32[]{:S(2)}) %copy-start) | copy-done | bytes 524312
  17.5 0.9 copy-done.1
  18.4 0.9 copy-done.2
  19.3 0.8 copy-done.3
  20.2 1.0 %fetch.1 = (f32[128,128]{1,0:T(8,128)S(1)}, bf16[1,144,512]{2,1,0:T(8,128)(2,1)S(1)}, bf16[1,128,2048]{2,1,0:T(8,128)(2,1)S(1)}, bf16[1,128,512]{2,1,0:T(8,128)(2,1)S(1)}, bf16[512,128]{1,0:T(8,128)(2,1)S(1)}) custom-call(f32[128,128]{1,0:T(8,128)S(1)} %copy-done.3, bf16[1,144,512]{2,1,0:T(8,128)(2,1)} %get-tuple-element.29.refs_1_, ...), custom_call_target="tpu_custom_call" | custom-call | tf_op jit(solution)/shard_map/fetch/pallas_call | solution.py:227
  21.1 3.4 %collective-permute-start.7 = (bf16[1,144,512]{2,1,0:T(8,128)(2,1)}, bf16[1,144,512]{2,1,0:T(8,128)(2,1)S(1)}, u32[]{:S(2)}, u32[]{:S(2)}) collective-permute-start(bf16[1,144,512]{2,1,0:T(8,128)(2,1)} %get-tuple-element.29.refs_1_), channel_id=1, source_target_pairs={{0,2},{4,0},{6,4},{2,6},{1,3},{5,1},{7,5},{3,7},{8,10},{12,8},{14,... | collective-permute-start | bytes 442376 | tf_op jit(solution)/shard_map/ppermute | solution.py:28
  24.6 1.4 %collective-permute-done.4.refs_2_ = bf16[512,128]{1,0:T(8,128)(2,1)S(1)} collective-permute-done((bf16[512,128]{1,0:T(8,128)(2,1)}, bf16[512,128]{1,0:T(8,128)(2,1)S(1)}, u32[]{:S(2)}, u32[]{:S(2)}) %collective-permute-start.4) | collective-permute-done | bytes 131104 | tf_op jit(solution)/shard_map/ppermute | solution.py:28
  26.0 3.9 %collective-permute-done.5.refs_3_ = bf16[512,128]{1,0:T(8,128)(2,1)S(1)} collective-permute-done((bf16[512,128]{1,0:T(8,128)(2,1)}, bf16[512,128]{1,0:T(8,128)(2,1)S(1)}, u32[]{:S(2)}, u32[]{:S(2)}) %collective-permute-start.5) | collective-permute-done | bytes 131104 | tf_op jit(solution)/shard_map/ppermute | solution.py:28
  30.0 2.0 %collective-permute-start.8 = (bf16[1,128,512]{2,1,0:T(8,128)(2,1)S(1)}, bf16[1,128,512]{2,1,0:T(8,128)(2,1)S(1)}, u32[]{:S(2)}, u32[]{:S(2)}) collective-permute-start(bf16[1,128,512]{2,1,0:T(8,128)(2,1)S(1)} %collective-permute-done.1.refs_7_), channel_id=1, source_target_pairs={{0,2},{4,0},{6,4},{2,6},{1,3},{5,1},{7,5},{3,7},{8,10},{12,8},{14,... | collective-permute-start | bytes 393224 | tf_op jit(solution)/shard_map/ppermute | solution.py:28
  32.0 1.5 %collective-permute-start.15 = (bf16[512,512]{1,0:T(8,128)(2,1)S(1)}, bf16[512,512]{1,0:T(8,128)(2,1)S(1)}, u32[]{:S(2)}, u32[]{:S(2)}) collective-permute-start(bf16[512,512]{1,0:T(8,128)(2,1)S(1)} %join.1.refs_6_.refs_2_), channel_id=1, source_target_pairs={{0,16},{8,24},{16,0},{24,8},{1,17},{9,25},{17,1},{25,9},{2,18},{10... | collective-permute-start | bytes 1572872 | tf_op jit(solution)/shard_map/ppermute | solution.py:44
  33.6 5.4 %collective-permute-done.8.refs_6_ = bf16[1,128,512]{2,1,0:T(8,128)(2,1)S(1)} collective-permute-done((bf16[1,128,512]{2,1,0:T(8,128)(2,1)S(1)}, bf16[1,128,512]{2,1,0:T(8,128)(2,1)S(1)}, u32[]{:S(2)}, u32[]{:S(2)}) %collective-permute-start.8) | collective-permute-done | bytes 131104 | tf_op jit(solution)/shard_map/ppermute | solution.py:28
  39.0 0.4 collective-permute-done.6.refs_2_
  39.4 2.5 %attend.1 = (bf16[1,128,2048]{2,1,0:T(8,128)(2,1)}, bf16[1,128,1024]{2,1,0:T(8,128)(2,1)S(1)}, bf16[1,128,1024]{2,1,0:T(8,128)(2,1)S(1)}) custom-call(f32[128,128]{1,0:T(8,128)S(1)} %get-tuple-element.26.place_ref, bf16[1,128,2048]{2,1,0:T(8,128)(2,1)S(1)} %get-tuple-element.27.query_ref, bf16[1,144,512]{2,1,0:T(8,128)(2,1)S(1)} %get-tuple-element.28.refs_0_, ...), custom_call_target="tpu_custom_call" | custom-call | tf_op jit(solution)/shard_map/attend/pallas_call | solution.py:249
  41.9 1.5 %collective-permute-start.10 = (bf16[1,128,1024]{2,1,0:T(8,128)(2,1)S(1)}, bf16[1,128,1024]{2,1,0:T(8,128)(2,1)S(1)}, u32[]{:S(2)}, u32[]{:S(2)}) collective-permute-start(bf16[1,128,1024]{2,1,0:T(8,128)(2,1)S(1)} %get-tuple-element.38.refs_0_), channel_id=1, source_target_pairs={{0,16},{8,24},{16,0},{24,8},{1,17},{9,25},{17,1},{25,9},{2,18},{10... | collective-permute-start | bytes 786440 | tf_op jit(solution)/shard_map/ppermute | solution.py:44
  43.5 0.5 collective-permute-start.20
  44.0 1.7 %collective-permute-start.19 = (bf16[1,128,1024]{2,1,0:T(8,128)(2,1)S(1)}, bf16[1,128,1024]{2,1,0:T(8,128)(2,1)S(1)}, u32[]{:S(2)}, u32[]{:S(2)}) collective-permute-start(bf16[1,128,1024]{2,1,0:T(8,128)(2,1)S(1)} %get-tuple-element.41.refs_0_), channel_id=1, source_target_pairs={{0,4},{4,6},{6,2},{2,0},{1,5},{5,7},{7,3},{3,1},{8,12},{12,14},{14... | collective-permute-start | bytes 786440 | tf_op jit(solution)/shard_map/ppermute | solution.py:28
  45.7 6.3 %collective-permute-done.10.refs_3_ = bf16[1,128,1024]{2,1,0:T(8,128)(2,1)S(1)} collective-permute-done((bf16[1,128,1024]{2,1,0:T(8,128)(2,1)S(1)}, bf16[1,128,1024]{2,1,0:T(8,128)(2,1)S(1)}, u32[]{:S(2)}, u32[]{:S(2)}) %collective-permute-start.10) | collective-permute-done | bytes 262176 | tf_op jit(solution)/shard_map/ppermute | solution.py:44
  52.0 0.7 collective-permute-done.9.refs_1_
  52.7 0.8 collective-permute-start.12
  53.5 1.5 %collective-permute-start.16 = (bf16[512,512]{1,0:T(8,128)(2,1)S(1)}, bf16[512,512]{1,0:T(8,128)(2,1)S(1)}, u32[]{:S(2)}, u32[]{:S(2)}) collective-permute-start(bf16[512,512]{1,0:T(8,128)(2,1)S(1)} %join.1.refs_6_.refs_2_), channel_id=1, source_target_pairs={{0,1},{1,0},{2,3},{3,2},{4,5},{5,4},{6,7},{7,6},{8,9},{9,8},{10,11... | collective-permute-start | bytes 1572872 | tf_op jit(solution)/shard_map/ppermute | solution.py:44
  55.0 2.6 %collective-permute-done.20.refs_3_ = bf16[1,128,1024]{2,1,0:T(8,128)(2,1)S(1)} collective-permute-done((bf16[1,128,1024]{2,1,0:T(8,128)(2,1)S(1)}, bf16[1,128,1024]{2,1,0:T(8,128)(2,1)S(1)}, u32[]{:S(2)}, u32[]{:S(2)}) %collective-permute-start.20) | collective-permute-done | bytes 262176 | tf_op jit(solution)/shard_map/ppermute | solution.py:44
  57.6 1.5 %collective-permute-start.11 = (bf16[1,128,1024]{2,1,0:T(8,128)(2,1)S(1)}, bf16[1,128,1024]{2,1,0:T(8,128)(2,1)S(1)}, u32[]{:S(2)}, u32[]{:S(2)}) collective-permute-start(bf16[1,128,1024]{2,1,0:T(8,128)(2,1)S(1)} %collective-permute-done.9.refs_1_), channel_id=1, source_target_pairs={{0,4},{4,6},{6,2},{2,0},{1,5},{5,7},{7,3},{3,1},{8,12},{12,14},{14... | collective-permute-start | bytes 786440 | tf_op jit(solution)/shard_map/ppermute | solution.py:28
  59.1 1.5 %collective-permute-start.22 = (bf16[1,128,1024]{2,1,0:T(8,128)(2,1)S(1)}, bf16[1,128,1024]{2,1,0:T(8,128)(2,1)S(1)}, u32[]{:S(2)}, u32[]{:S(2)}) collective-permute-start(bf16[1,128,1024]{2,1,0:T(8,128)(2,1)S(1)} %collective-permute-done.19.refs_1_), channel_id=1, source_target_pairs={{0,16},{8,24},{16,0},{24,8},{1,17},{9,25},{17,1},{25,9},{2,18},{10... | collective-permute-start | bytes 786440 | tf_op jit(solution)/shard_map/ppermute | solution.py:44
  60.6 2.6 %collective-permute-done.12.refs_4_ = bf16[1,128,1024]{2,1,0:T(8,128)(2,1)S(1)} collective-permute-done((bf16[1,128,1024]{2,1,0:T(8,128)(2,1)S(1)}, bf16[1,128,1024]{2,1,0:T(8,128)(2,1)S(1)}, u32[]{:S(2)}, u32[]{:S(2)}) %collective-permute-start.12) | collective-permute-done | bytes 262176 | tf_op jit(solution)/shard_map/ppermute | solution.py:44
  63.2 1.5 %collective-permute-start.17 = (bf16[512,512]{1,0:T(8,128)(2,1)S(1)}, bf16[512,512]{1,0:T(8,128)(2,1)S(1)}, u32[]{:S(2)}, u32[]{:S(2)}) collective-permute-start(bf16[512,512]{1,0:T(8,128)(2,1)S(1)} %collective-permute-done.15.refs_7_.refs_3_), channel_id=1, source_target_pairs={{0,1},{1,0},{2,3},{3,2},{4,5},{5,4},{6,7},{7,6},{8,9},{9,8},{10,11... | collective-permute-start | bytes 1572872 | tf_op jit(solution)/shard_map/ppermute | solution.py:44
  64.7 2.1 %collective-permute-done.11.refs_2_ = bf16[1,128,1024]{2,1,0:T(8,128)(2,1)S(1)} collective-permute-done((bf16[1,128,1024]{2,1,0:T(8,128)(2,1)S(1)}, bf16[1,128,1024]{2,1,0:T(8,128)(2,1)S(1)}, u32[]{:S(2)}, u32[]{:S(2)}) %collective-permute-start.11) | collective-permute-done | bytes 262176 | tf_op jit(solution)/shard_map/ppermute | solution.py:28
  66.8 2.4 %collective-permute-start.13 = (bf16[1,128,1024]{2,1,0:T(8,128)(2,1)S(1)}, bf16[1,128,1024]{2,1,0:T(8,128)(2,1)S(1)}, u32[]{:S(2)}, u32[]{:S(2)}) collective-permute-start(bf16[1,128,1024]{2,1,0:T(8,128)(2,1)S(1)} %collective-permute-done.11.refs_2_), channel_id=1, source_target_pairs={{0,4},{4,6},{6,2},{2,0},{1,5},{5,7},{7,3},{3,1},{8,12},{12,14},{14... | collective-permute-start | bytes 786440 | tf_op jit(solution)/shard_map/ppermute | solution.py:28
  69.2 3.2 %collective-permute-done.21.refs_2_ = bf16[1,128,1024]{2,1,0:T(8,128)(2,1)S(1)} collective-permute-done((bf16[1,128,1024]{2,1,0:T(8,128)(2,1)S(1)}, bf16[1,128,1024]{2,1,0:T(8,128)(2,1)S(1)}, u32[]{:S(2)}, u32[]{:S(2)}) %collective-permute-start.21) | collective-permute-done | bytes 262176 | tf_op jit(solution)/shard_map/ppermute | solution.py:28
  72.4 1.5 %collective-permute-start.24 = (bf16[1,128,1024]{2,1,0:T(8,128)(2,1)S(1)}, bf16[1,128,1024]{2,1,0:T(8,128)(2,1)S(1)}, u32[]{:S(2)}, u32[]{:S(2)}) collective-permute-start(bf16[1,128,1024]{2,1,0:T(8,128)(2,1)S(1)} %collective-permute-done.21.refs_2_), channel_id=1, source_target_pairs={{0,16},{8,24},{16,0},{24,8},{1,17},{9,25},{17,1},{25,9},{2,18},{10... | collective-permute-start | bytes 786440 | tf_op jit(solution)/shard_map/ppermute | solution.py:44
  73.9 0.5 collective-permute-start.18
  74.5 2.4 %collective-permute-start.23 = (bf16[1,128,1024]{2,1,0:T(8,128)(2,1)S(1)}, bf16[1,128,1024]{2,1,0:T(8,128)(2,1)S(1)}, u32[]{:S(2)}, u32[]{:S(2)}) collective-permute-start(bf16[1,128,1024]{2,1,0:T(8,128)(2,1)S(1)} %collective-permute-done.21.refs_2_), channel_id=1, source_target_pairs={{0,4},{4,6},{6,2},{2,0},{1,5},{5,7},{7,3},{3,1},{8,12},{12,14},{14... | collective-permute-start | bytes 786440 | tf_op jit(solution)/shard_map/ppermute | solution.py:28
  76.9 1.2 %collective-permute-done.13.refs_0_ = bf16[1,128,1024]{2,1,0:T(8,128)(2,1)S(1)} collective-permute-done((bf16[1,128,1024]{2,1,0:T(8,128)(2,1)S(1)}, bf16[1,128,1024]{2,1,0:T(8,128)(2,1)S(1)}, u32[]{:S(2)}, u32[]{:S(2)}) %collective-permute-start.13) | collective-permute-done | bytes 262176 | tf_op jit(solution)/shard_map/ppermute | solution.py:28
  78.0 1.5 %collective-permute-start.14 = (bf16[1,128,1024]{2,1,0:T(8,128)(2,1)S(1)}, bf16[1,128,1024]{2,1,0:T(8,128)(2,1)S(1)}, u32[]{:S(2)}, u32[]{:S(2)}) collective-permute-start(bf16[1,128,1024]{2,1,0:T(8,128)(2,1)S(1)} %collective-permute-done.13.refs_0_), channel_id=1, source_target_pairs={{0,16},{8,24},{16,0},{24,8},{1,17},{9,25},{17,1},{25,9},{2,18},{10... | collective-permute-start | bytes 786440 | tf_op jit(solution)/shard_map/ppermute | solution.py:44
  79.6 1.0 %collective-permute-done.24.refs_5_ = bf16[1,128,1024]{2,1,0:T(8,128)(2,1)S(1)} collective-permute-done((bf16[1,128,1024]{2,1,0:T(8,128)(2,1)S(1)}, bf16[1,128,1024]{2,1,0:T(8,128)(2,1)S(1)}, u32[]{:S(2)}, u32[]{:S(2)}) %collective-permute-start.24) | collective-permute-done | bytes 262176 | tf_op jit(solution)/shard_map/ppermute | solution.py:44
  80.6 1.4 %collective-permute-start.25 = (bf16[1,128,1024]{2,1,0:T(8,128)(2,1)S(1)}, bf16[1,128,1024]{2,1,0:T(8,128)(2,1)S(1)}, u32[]{:S(2)}, u32[]{:S(2)}) collective-permute-start(bf16[1,128,1024]{2,1,0:T(8,128)(2,1)S(1)} %collective-permute-done.24.refs_5_), channel_id=1, source_target_pairs={{0,4},{4,6},{6,2},{2,0},{1,5},{5,7},{7,3},{3,1},{8,12},{12,14},{14... | collective-permute-start | bytes 786440 | tf_op jit(solution)/shard_map/ppermute | solution.py:28
  82.0 1.8 %early.3.refs_6_ = f32[1024,1024]{1,0:T(8,128)S(1)} custom-call(bf16[1,128,1024]{2,1,0:T(8,128)(2,1)S(1)} %get-tuple-element.41.refs_0_, bf16[1,128,1024]{2,1,0:T(8,128)(2,1)S(1)} %collective-permute-done.19.refs_1_, bf16[1,128,1024]{2,1,0:T(8,128)(2,1)S(1)} %collective-permute-done.21.refs_2_, bf16[1,128,1024]{2,1,0:T(8,128)(2,1)S(1)} %collective-permute-done.20.refs_3_, ...), custom_call_target="tpu_custom_call" | custom-call | flops 1610612736 | bytes 8388608 | tf_op jit(solution)/shard_map/early/pallas_call | solution.py:279
  83.8 1.8 %early.2.refs_6_ = f32[1024,1024]{1,0:T(8,128)S(1)} custom-call(bf16[1,128,1024]{2,1,0:T(8,128)(2,1)S(1)} %get-tuple-element.38.refs_0_, bf16[1,128,1024]{2,1,0:T(8,128)(2,1)S(1)} %collective-permute-done.9.refs_1_, bf16[1,128,1024]{2,1,0:T(8,128)(2,1)S(1)} %collective-permute-done.11.refs_2_, bf16[1,128,1024]{2,1,0:T(8,128)(2,1)S(1)} %collective-permute-done.10.refs_3_, ...), custom_call_target="tpu_custom_call" | custom-call | flops 1610612736 | bytes 8388608 | tf_op jit(solution)/shard_map/early/pallas_call | solution.py:279
  85.6 1.3 %collective-permute-done.25.refs_1_ = bf16[1,128,1024]{2,1,0:T(8,128)(2,1)S(1)} collective-permute-done((bf16[1,128,1024]{2,1,0:T(8,128)(2,1)S(1)}, bf16[1,128,1024]{2,1,0:T(8,128)(2,1)S(1)}, u32[]{:S(2)}, u32[]{:S(2)}) %collective-permute-start.25) | collective-permute-done | bytes 262176 | tf_op jit(solution)/shard_map/ppermute | solution.py:28
  86.9 1.6 %finish.2.refs_7_ = bf16[1,1024,2048]{2,1,0:T(8,128)(2,1)} custom-call(bf16[1,128,1024]{2,1,0:T(8,128)(2,1)S(1)} %collective-permute-done.23.refs_0_, bf16[1,128,1024]{2,1,0:T(8,128)(2,1)S(1)} %collective-permute-done.25.refs_1_, bf16[512,512]{1,0:T(8,128)(2,1)S(1)} %join.1.refs_6_.refs_2_, bf16[512,512]{1,0:T(8,128)(2,1)S(1)} %collective-permute-done.15.refs_7_.refs_3_, ...), custom_call_target="tpu_custom_call" | custom-call | flops 536870912 | bytes 8388608 | tf_op jit(solution)/shard_map/finish/pallas_call | solution.py:304
  88.6 1.7 %finish.3 = bf16[1,1024,2048]{2,1,0:T(8,128)(2,1)} custom-call(bf16[1,128,1024]{2,1,0:T(8,128)(2,1)S(1)} %collective-permute-done.13.refs_0_, bf16[1,128,1024]{2,1,0:T(8,128)(2,1)S(1)} %collective-permute-done.14.refs_1_, bf16[512,512]{1,0:T(8,128)(2,1)S(1)} %join.1.refs_6_.refs_2_, ...), custom_call_target="tpu_custom_call", output_to_operand_aliasing={{}: (7, {})} | custom-call | flops 536870912 | bytes 8388608 | tf_op jit(solution)/shard_map/finish/pallas_call | solution.py:304
  (20 shorter events, 0.4 us)
Async XLA Ops:
  0.6 7.9 %collective-permute-start.1 = (bf16[1,128,512]{2,1,0:T(8,128)(2,1)}, bf16[1,128,512]{2,1,0:T(8,128)(2,1)S(1)}, u32[]{:S(2)}, u32[]{:S(2)}) collective-permute-start(bf16[1,128,512]{2,1,0:T(8,128)(2,1)} %refs_3_.1), channel_id=1, source_target_pairs={{0,2},{4,0},{6,4},{2,6},{1,3},{5,1},{7,5},{3,7},{8,10},{12,8},{14,... | collective-permute-start | bytes 393224 | tf_op jit(solution)/shard_map/ppermute | solution.py:28
  3.7 7.5 %collective-permute-start = (bf16[1,128,512]{2,1,0:T(8,128)(2,1)}, bf16[1,128,512]{2,1,0:T(8,128)(2,1)S(1)}, u32[]{:S(2)}, u32[]{:S(2)}) collective-permute-start(bf16[1,128,512]{2,1,0:T(8,128)(2,1)} %refs_3_.1), channel_id=1, source_target_pairs={{0,4},{4,6},{6,2},{2,0},{1,5},{5,7},{7,3},{3,1},{8,12},{12,14},{14... | collective-permute-start | bytes 393224 | tf_op jit(solution)/shard_map/ppermute | solution.py:28
  11.2 18.7 %collective-permute-start.2 = (bf16[1,144,512]{2,1,0:T(8,128)(2,1)}, bf16[1,144,512]{2,1,0:T(8,128)(2,1)S(1)}, u32[]{:S(2)}, u32[]{:S(2)}) collective-permute-start(bf16[1,144,512]{2,1,0:T(8,128)(2,1)} %get-tuple-element.29.refs_1_), channel_id=1, source_target_pairs={{0,4},{4,6},{6,2},{2,0},{1,5},{5,7},{7,3},{3,1},{8,12},{12,14},{14... | collective-permute-start | bytes 442376 | tf_op jit(solution)/shard_map/ppermute | solution.py:28
  13.0 11.6 %collective-permute-start.3 = (bf16[512,128]{1,0:T(8,128)(2,1)}, bf16[512,128]{1,0:T(8,128)(2,1)S(1)}, u32[]{:S(2)}, u32[]{:S(2)}) collective-permute-start(bf16[512,128]{1,0:T(8,128)(2,1)} %get-tuple-element.31), channel_id=1, source_target_pairs={{0,4},{4,6},{6,2},{2,0},{1,5},{5,7},{7,3},{3,1},{8,12},{12,14},{14... | collective-permute-start | bytes 393224 | tf_op jit(solution)/shard_map/ppermute | solution.py:28
  15.5 10.5 %collective-permute-start.4 = (bf16[512,128]{1,0:T(8,128)(2,1)}, bf16[512,128]{1,0:T(8,128)(2,1)S(1)}, u32[]{:S(2)}, u32[]{:S(2)}) collective-permute-start(bf16[512,128]{1,0:T(8,128)(2,1)} %get-tuple-element.32), channel_id=1, source_target_pairs={{0,6},{4,2},{6,0},{2,4},{1,7},{5,3},{7,1},{3,5},{8,14},{12,10},{14... | collective-permute-start | bytes 393224 | tf_op jit(solution)/shard_map/ppermute | solution.py:28
  15.6 14.2 %collective-permute-start.5 = (bf16[512,128]{1,0:T(8,128)(2,1)}, bf16[512,128]{1,0:T(8,128)(2,1)S(1)}, u32[]{:S(2)}, u32[]{:S(2)}) collective-permute-start(bf16[512,128]{1,0:T(8,128)(2,1)} %get-tuple-element.33), channel_id=1, source_target_pairs={{0,2},{4,0},{6,4},{2,6},{1,3},{5,1},{7,5},{3,7},{8,10},{12,8},{14,... | collective-permute-start | bytes 393224 | tf_op jit(solution)/shard_map/ppermute | solution.py:28
  16.5 1.0 %copy-start = (bf16[1,128,2048]{2,1,0:T(8,128)(2,1)S(1)}, bf16[1,128,2048]{2,1,0:T(8,128)(2,1)}, u32[]{:S(2)}) copy-start(bf16[1,128,2048]{2,1,0:T(8,128)(2,1)} %refs_2_.1) | copy-start | bytes 1572868
  17.5 0.9 %copy-start.1 = (bf16[1,128,512]{2,1,0:T(8,128)(2,1)S(1)}, bf16[1,128,512]{2,1,0:T(8,128)(2,1)}, u32[]{:S(2)}) copy-start(bf16[1,128,512]{2,1,0:T(8,128)(2,1)} %refs_3_.1) | copy-start | bytes 393220
  18.4 0.9 %copy-start.2 = (bf16[512,128]{1,0:T(8,128)(2,1)S(1)}, bf16[512,128]{1,0:T(8,128)(2,1)}, u32[]{:S(2)}) copy-start(bf16[512,128]{1,0:T(8,128)(2,1)} %get-tuple-element.25.refs_4_) | copy-start | bytes 393220
  19.3 0.8 copy-start.3
  21.1 17.9 %collective-permute-start.7 = (bf16[1,144,512]{2,1,0:T(8,128)(2,1)}, bf16[1,144,512]{2,1,0:T(8,128)(2,1)S(1)}, u32[]{:S(2)}, u32[]{:S(2)}) collective-permute-start(bf16[1,144,512]{2,1,0:T(8,128)(2,1)} %get-tuple-element.29.refs_1_), channel_id=1, source_target_pairs={{0,2},{4,0},{6,4},{2,6},{1,3},{5,1},{7,5},{3,7},{8,10},{12,8},{14,... | collective-permute-start | bytes 442376 | tf_op jit(solution)/shard_map/ppermute | solution.py:28
  30.0 9.5 %collective-permute-start.6 = (bf16[1,144,512]{2,1,0:T(8,128)(2,1)S(1)}, bf16[1,144,512]{2,1,0:T(8,128)(2,1)S(1)}, u32[]{:S(2)}, u32[]{:S(2)}) collective-permute-start(bf16[1,144,512]{2,1,0:T(8,128)(2,1)S(1)} %collective-permute-done.2.refs_1_), channel_id=1, source_target_pairs={{0,4},{4,6},{6,2},{2,0},{1,5},{5,7},{7,3},{3,1},{8,12},{12,14},{14... | collective-permute-start | bytes 442376 | tf_op jit(solution)/shard_map/ppermute | solution.py:28
  30.0 9.0 %collective-permute-start.8 = (bf16[1,128,512]{2,1,0:T(8,128)(2,1)S(1)}, bf16[1,128,512]{2,1,0:T(8,128)(2,1)S(1)}, u32[]{:S(2)}, u32[]{:S(2)}) collective-permute-start(bf16[1,128,512]{2,1,0:T(8,128)(2,1)S(1)} %collective-permute-done.1.refs_7_), channel_id=1, source_target_pairs={{0,2},{4,0},{6,4},{2,6},{1,3},{5,1},{7,5},{3,7},{8,10},{12,8},{14,... | collective-permute-start | bytes 393224 | tf_op jit(solution)/shard_map/ppermute | solution.py:28
  32.0 28.6 %collective-permute-start.15 = (bf16[512,512]{1,0:T(8,128)(2,1)S(1)}, bf16[512,512]{1,0:T(8,128)(2,1)S(1)}, u32[]{:S(2)}, u32[]{:S(2)}) collective-permute-start(bf16[512,512]{1,0:T(8,128)(2,1)S(1)} %join.1.refs_6_.refs_2_), channel_id=1, source_target_pairs={{0,16},{8,24},{16,0},{24,8},{1,17},{9,25},{17,1},{25,9},{2,18},{10... | collective-permute-start | bytes 1572872 | tf_op jit(solution)/shard_map/ppermute | solution.py:44
  41.9 10.0 %collective-permute-start.10 = (bf16[1,128,1024]{2,1,0:T(8,128)(2,1)S(1)}, bf16[1,128,1024]{2,1,0:T(8,128)(2,1)S(1)}, u32[]{:S(2)}, u32[]{:S(2)}) collective-permute-start(bf16[1,128,1024]{2,1,0:T(8,128)(2,1)S(1)} %get-tuple-element.38.refs_0_), channel_id=1, source_target_pairs={{0,16},{8,24},{16,0},{24,8},{1,17},{9,25},{17,1},{25,9},{2,18},{10... | collective-permute-start | bytes 786440 | tf_op jit(solution)/shard_map/ppermute | solution.py:44
  43.4 9.2 %collective-permute-start.9 = (bf16[1,128,1024]{2,1,0:T(8,128)(2,1)S(1)}, bf16[1,128,1024]{2,1,0:T(8,128)(2,1)S(1)}, u32[]{:S(2)}, u32[]{:S(2)}) collective-permute-start(bf16[1,128,1024]{2,1,0:T(8,128)(2,1)S(1)} %get-tuple-element.38.refs_0_), channel_id=1, source_target_pairs={{0,4},{4,6},{6,2},{2,0},{1,5},{5,7},{7,3},{3,1},{8,12},{12,14},{14... | collective-permute-start | bytes 786440 | tf_op jit(solution)/shard_map/ppermute | solution.py:28
  43.5 14.1 %collective-permute-start.20 = (bf16[1,128,1024]{2,1,0:T(8,128)(2,1)S(1)}, bf16[1,128,1024]{2,1,0:T(8,128)(2,1)S(1)}, u32[]{:S(2)}, u32[]{:S(2)}) collective-permute-start(bf16[1,128,1024]{2,1,0:T(8,128)(2,1)S(1)} %get-tuple-element.41.refs_0_), channel_id=1, source_target_pairs={{0,16},{8,24},{16,0},{24,8},{1,17},{9,25},{17,1},{25,9},{2,18},{10... | collective-permute-start | bytes 786440 | tf_op jit(solution)/shard_map/ppermute | solution.py:44
  44.0 15.1 %collective-permute-start.19 = (bf16[1,128,1024]{2,1,0:T(8,128)(2,1)S(1)}, bf16[1,128,1024]{2,1,0:T(8,128)(2,1)S(1)}, u32[]{:S(2)}, u32[]{:S(2)}) collective-permute-start(bf16[1,128,1024]{2,1,0:T(8,128)(2,1)S(1)} %get-tuple-element.41.refs_0_), channel_id=1, source_target_pairs={{0,4},{4,6},{6,2},{2,0},{1,5},{5,7},{7,3},{3,1},{8,12},{12,14},{14... | collective-permute-start | bytes 786440 | tf_op jit(solution)/shard_map/ppermute | solution.py:28
  52.7 10.5 %collective-permute-start.12 = (bf16[1,128,1024]{2,1,0:T(8,128)(2,1)S(1)}, bf16[1,128,1024]{2,1,0:T(8,128)(2,1)S(1)}, u32[]{:S(2)}, u32[]{:S(2)}) collective-permute-start(bf16[1,128,1024]{2,1,0:T(8,128)(2,1)S(1)} %collective-permute-done.9.refs_1_), channel_id=1, source_target_pairs={{0,16},{8,24},{16,0},{24,8},{1,17},{9,25},{17,1},{25,9},{2,18},{10... | collective-permute-start | bytes 786440 | tf_op jit(solution)/shard_map/ppermute | solution.py:44
  53.5 21.0 %collective-permute-start.16 = (bf16[512,512]{1,0:T(8,128)(2,1)S(1)}, bf16[512,512]{1,0:T(8,128)(2,1)S(1)}, u32[]{:S(2)}, u32[]{:S(2)}) collective-permute-start(bf16[512,512]{1,0:T(8,128)(2,1)S(1)} %join.1.refs_6_.refs_2_), channel_id=1, source_target_pairs={{0,1},{1,0},{2,3},{3,2},{4,5},{5,4},{6,7},{7,6},{8,9},{9,8},{10,11... | collective-permute-start | bytes 1572872 | tf_op jit(solution)/shard_map/ppermute | solution.py:44
  57.6 9.2 %collective-permute-start.11 = (bf16[1,128,1024]{2,1,0:T(8,128)(2,1)S(1)}, bf16[1,128,1024]{2,1,0:T(8,128)(2,1)S(1)}, u32[]{:S(2)}, u32[]{:S(2)}) collective-permute-start(bf16[1,128,1024]{2,1,0:T(8,128)(2,1)S(1)} %collective-permute-done.9.refs_1_), channel_id=1, source_target_pairs={{0,4},{4,6},{6,2},{2,0},{1,5},{5,7},{7,3},{3,1},{8,12},{12,14},{14... | collective-permute-start | bytes 786440 | tf_op jit(solution)/shard_map/ppermute | solution.py:28
  59.1 10.1 %collective-permute-start.22 = (bf16[1,128,1024]{2,1,0:T(8,128)(2,1)S(1)}, bf16[1,128,1024]{2,1,0:T(8,128)(2,1)S(1)}, u32[]{:S(2)}, u32[]{:S(2)}) collective-permute-start(bf16[1,128,1024]{2,1,0:T(8,128)(2,1)S(1)} %collective-permute-done.19.refs_1_), channel_id=1, source_target_pairs={{0,16},{8,24},{16,0},{24,8},{1,17},{9,25},{17,1},{25,9},{2,18},{10... | collective-permute-start | bytes 786440 | tf_op jit(solution)/shard_map/ppermute | solution.py:44
  60.6 11.8 %collective-permute-start.21 = (bf16[1,128,1024]{2,1,0:T(8,128)(2,1)S(1)}, bf16[1,128,1024]{2,1,0:T(8,128)(2,1)S(1)}, u32[]{:S(2)}, u32[]{:S(2)}) collective-permute-start(bf16[1,128,1024]{2,1,0:T(8,128)(2,1)S(1)} %collective-permute-done.19.refs_1_), channel_id=1, source_target_pairs={{0,4},{4,6},{6,2},{2,0},{1,5},{5,7},{7,3},{3,1},{8,12},{12,14},{14... | collective-permute-start | bytes 786440 | tf_op jit(solution)/shard_map/ppermute | solution.py:28
  63.2 18.8 %collective-permute-start.17 = (bf16[512,512]{1,0:T(8,128)(2,1)S(1)}, bf16[512,512]{1,0:T(8,128)(2,1)S(1)}, u32[]{:S(2)}, u32[]{:S(2)}) collective-permute-start(bf16[512,512]{1,0:T(8,128)(2,1)S(1)} %collective-permute-done.15.refs_7_.refs_3_), channel_id=1, source_target_pairs={{0,1},{1,0},{2,3},{3,2},{4,5},{5,4},{6,7},{7,6},{8,9},{9,8},{10,11... | collective-permute-start | bytes 1572872 | tf_op jit(solution)/shard_map/ppermute | solution.py:44
  66.8 11.2 %collective-permute-start.13 = (bf16[1,128,1024]{2,1,0:T(8,128)(2,1)S(1)}, bf16[1,128,1024]{2,1,0:T(8,128)(2,1)S(1)}, u32[]{:S(2)}, u32[]{:S(2)}) collective-permute-start(bf16[1,128,1024]{2,1,0:T(8,128)(2,1)S(1)} %collective-permute-done.11.refs_2_), channel_id=1, source_target_pairs={{0,4},{4,6},{6,2},{2,0},{1,5},{5,7},{7,3},{3,1},{8,12},{12,14},{14... | collective-permute-start | bytes 786440 | tf_op jit(solution)/shard_map/ppermute | solution.py:28
  72.4 8.1 %collective-permute-start.24 = (bf16[1,128,1024]{2,1,0:T(8,128)(2,1)S(1)}, bf16[1,128,1024]{2,1,0:T(8,128)(2,1)S(1)}, u32[]{:S(2)}, u32[]{:S(2)}) collective-permute-start(bf16[1,128,1024]{2,1,0:T(8,128)(2,1)S(1)} %collective-permute-done.21.refs_2_), channel_id=1, source_target_pairs={{0,16},{8,24},{16,0},{24,8},{1,17},{9,25},{17,1},{25,9},{2,18},{10... | collective-permute-start | bytes 786440 | tf_op jit(solution)/shard_map/ppermute | solution.py:44
  73.9 9.8 %collective-permute-start.18 = (bf16[1,128,1024]{2,1,0:T(8,128)(2,1)S(1)}, bf16[1,128,1024]{2,1,0:T(8,128)(2,1)S(1)}, u32[]{:S(2)}, u32[]{:S(2)}) collective-permute-start(bf16[1,128,1024]{2,1,0:T(8,128)(2,1)S(1)} %collective-permute-done.11.refs_2_), channel_id=1, source_target_pairs={{0,16},{8,24},{16,0},{24,8},{1,17},{9,25},{17,1},{25,9},{2,18},{10... | collective-permute-start | bytes 786440 | tf_op jit(solution)/shard_map/ppermute | solution.py:44
  74.5 11.2 %collective-permute-start.23 = (bf16[1,128,1024]{2,1,0:T(8,128)(2,1)S(1)}, bf16[1,128,1024]{2,1,0:T(8,128)(2,1)S(1)}, u32[]{:S(2)}, u32[]{:S(2)}) collective-permute-start(bf16[1,128,1024]{2,1,0:T(8,128)(2,1)S(1)} %collective-permute-done.21.refs_2_), channel_id=1, source_target_pairs={{0,4},{4,6},{6,2},{2,0},{1,5},{5,7},{7,3},{3,1},{8,12},{12,14},{14... | collective-permute-start | bytes 786440 | tf_op jit(solution)/shard_map/ppermute | solution.py:28
  78.0 10.5 %collective-permute-start.14 = (bf16[1,128,1024]{2,1,0:T(8,128)(2,1)S(1)}, bf16[1,128,1024]{2,1,0:T(8,128)(2,1)S(1)}, u32[]{:S(2)}, u32[]{:S(2)}) collective-permute-start(bf16[1,128,1024]{2,1,0:T(8,128)(2,1)S(1)} %collective-permute-done.13.refs_0_), channel_id=1, source_target_pairs={{0,16},{8,24},{16,0},{24,8},{1,17},{9,25},{17,1},{25,9},{2,18},{10... | collective-permute-start | bytes 786440 | tf_op jit(solution)/shard_map/ppermute | solution.py:44
  80.6 6.4 %collective-permute-start.25 = (bf16[1,128,1024]{2,1,0:T(8,128)(2,1)S(1)}, bf16[1,128,1024]{2,1,0:T(8,128)(2,1)S(1)}, u32[]{:S(2)}, u32[]{:S(2)}) collective-permute-start(bf16[1,128,1024]{2,1,0:T(8,128)(2,1)S(1)} %collective-permute-done.24.refs_5_), channel_id=1, source_target_pairs={{0,4},{4,6},{6,2},{2,0},{1,5},{5,7},{7,3},{3,1},{8,12},{12,14},{14... | collective-permute-start | bytes 786440 | tf_op jit(solution)/shard_map/ppermute | solution.py:28

commit v13 on v10

--- a/solution.py
+++ b/solution.py
@@ -99,10 +99,10 @@
         refs[-1][:, s * tokens : (s + 1) * tokens] = ref[...]
 
 
-def attention_kernel(group, scale, n, spans, place_ref, query_ref, *refs):
-    key_refs, value_refs, (whole_ref, *part_refs) = refs[:n], refs[n : 2 * n], refs[2 * n :]
+def attention_kernel(group, scale, n, spans, first_head, place_ref, query_ref, *refs):
+    key_refs, value_refs, out_ref = refs[:n], refs[n : 2 * n], refs[2 * n]
     tokens, width = value_refs[0].shape[1:]
-    heads = width // HD
+    heads = out_ref.shape[2] // (group * HD)
     span = tokens // spans
     lane = lax.broadcasted_iota(jnp.int32, (1, tokens), 1)
     inner = (lane % span).astype(jnp.float32)
@@ -116,9 +116,8 @@
     hidden = jnp.where(key_pos <= place_ref[:, :1], 0.0, -1e30)
     hidden = jnp.concatenate([hidden] * group, axis=0)
     for j in range(heads):
-        first = j * group * HD
-        out_ref = part_refs[j * len(part_refs) // heads]
-        columns = slice(j * HD, (j + 1) * HD)
+        first = (first_head + j) * group * HD
+        columns = slice((first_head + j) * HD, (first_head + j + 1) * HD)
         key_block = jnp.concatenate([ref[0, :tokens, columns] for ref in key_refs], axis=0)
         value_block = jnp.concatenate([ref[0, :, columns] for ref in value_refs], axis=0)
         queries = jnp.concatenate(
@@ -136,10 +135,8 @@
         )
         mixed = (mixed / total).astype(jnp.bfloat16)
         for g in range(group):
-            at, piece = first + g * HD, mixed[g * tokens : (g + 1) * tokens]
-            whole_ref[0, :, at : at + HD] = piece
-            at %= out_ref.shape[2]
-            out_ref[0, :, at : at + HD] = piece
+            at = (j * group + g) * HD
+            out_ref[0, :, at : at + HD] = mixed[g * tokens : (g + 1) * tokens]
 
 
 def left_sides(refs, tokens, slots):
@@ -246,15 +243,25 @@
     mine_far = swap(mine, "pipe", far)
     key_ring = gather(packed, key_edges, 1, lambda x: after(x, query_held, mine))
     value_ring = gather(values, value_edges, -1, lambda x: after(x, value_held, mine))
-    attention, *pieces = pl.pallas_call(
-        functools.partial(attention_kernel, HQ // HK, 1.0 / math.sqrt(HD), n, spans),
-        out_shape=[jax.ShapeDtypeStruct(queries.shape, jnp.bfloat16)]
-        + [jax.ShapeDtypeStruct((1, tokens, chunk), jnp.bfloat16)] * parts,
-        in_specs=[VMEM] * (2 + 2 * n),
-        out_specs=[VMEM] * (1 + parts),
-        compiler_params=params(40),
-        name="attend",
-    )(place, query_held, key_held, *key_ring[1:], value_held, *value_ring[1:])
+    pieces = []
+    for c in range(parts):
+        pieces.append(
+            pl.pallas_call(
+                functools.partial(
+                    attention_kernel,
+                    HQ // HK,
+                    1.0 / math.sqrt(HD),
+                    n,
+                    spans,
+                    c * (width // HD // parts),
+                ),
+                out_shape=jax.ShapeDtypeStruct((1, tokens, chunk), jnp.bfloat16),
+                in_specs=[VMEM] * (2 + 2 * n),
+                out_specs=VMEM,
+                compiler_params=params(40),
+                name="attend",
+            )(place, query_held, key_held, *key_ring[1:], value_held, *value_ring[1:])
+        )
 
     near, mirrored = [], []
     for c in range(parts):
@@ -319,7 +326,7 @@
             ),
             name="finish",
         )(*operands)
-    return (attention, grad_out)
+    return (jnp.concatenate(pieces, axis=2), grad_out)
 
 
 def solution(mesh):

time: 89.3 us -> 88.4 us (0.990)
  waiting for transfers between devices: 27.1 us -> 24.9 us
  starting transfers between devices: 44.7 us -> 45.6 us
    ppermute x16, waiting for transfers between devices: 16.6 us -> 11.1 us  [around(): lax.ppermute(x, 'ctx', [(order[q], order[(q + shift) % n]) for q in range...]
    ppermute x10, starting transfers between devices: 10.8 us -> 14.5 us  [swap(): lax.ppermute(x, axis, [(i, i ^ mask) for i in range(lax.axis_size(axis))])]
    ppermute x10, waiting for transfers between devices: 10.5 us -> 13.8 us  [swap(): lax.ppermute(x, axis, [(i, i ^ mask) for i in range(lax.axis_size(axis))])]
    ppermute x16, starting transfers between devices: 33.9 us -> 31 us  [around(): lax.ppermute(x, 'ctx', [(order[q], order[(q + shift) % n]) for q in range...]
    pallas_call x1 -> x2, Pallas kernels: 2.51 us -> 2.15 us  [local(): pl.pallas_call(functools.partial(attention_kernel, HQ // HK, 1.0 / math.s...]
  transfers between devices with their start and end apart: 26 -> 26, of which waited for: 12 -> 12; matrix products, arithmetic and copies ran while one was open for 0% -> 1% of each run, Pallas kernels for 13% -> 12%
where the time goes in v13:
time: 88.4 us; the launch traced here: 88.2 us
  starting transfers between devices  45.6 us (52%)
  waiting for transfers between devices  24.9 us (28%)
  Pallas kernels  12.4 us (14%)
  local copies, waits for them, and re-layouts  3.69 us (4%)
    ppermute x16, starting transfers between devices, around(): lax.ppermute(x, 'ctx', [(order[q], order[(q + shift) % n]) for q in range...  31 us
    ppermute x10, starting transfers between devices, swap(): lax.ppermute(x, axis, [(i, i ^ mask) for i in range(lax.axis_size(axis))])  14.5 us
    ppermute x10, waiting for transfers between devices, swap(): lax.ppermute(x, axis, [(i, i ^ mask) for i in range(lax.axis_size(axis))])  13.8 us
    ppermute x16, waiting for transfers between devices, around(): lax.ppermute(x, 'ctx', [(order[q], order[(q + shift) % n]) for q in range...  11.1 us
    unnamed x8, local copies, waits for them, and re-layouts  3.69 us
    pallas_call x2, Pallas kernels, local(): pl.pallas_call(functools.partial(early_kernel, first_slots), out_shape=ja...  3.6 us
    pallas_call x2, Pallas kernels, local(): pl.pallas_call(functools.partial(finish_kernel, slots, c * chunk), out_sh...  3.31 us
    pallas_call x1, Pallas kernels, local(): pl.pallas_call(functools.partial(prepare_kernel, n), out_shape=[jax.Shape...  2.29 us
  transfers between devices with their start and end apart: 26, of which 12 were waited for; matrix products, arithmetic and copies ran while one was open for 1% of the time, Pallas kernels for 12%

profile of v13, /device:TPU:0, one launch (start us, length us, event | category | flops | bytes accessed | tf_op | source)
XLA Modules:
  0.0 88.2 jit_solution(10267802195402668277)
XLA Ops:
  0.6 3.1 %collective-permute-start.2 = (bf16[1,128,512]{2,1,0:T(8,128)(2,1)}, bf16[1,128,512]{2,1,0:T(8,128)(2,1)S(1)}, u32[]{:S(2)}, u32[]{:S(2)}) collective-permute-start(bf16[1,128,512]{2,1,0:T(8,128)(2,1)} %refs_3_.1), channel_id=1, source_target_pairs={{0,2},{4,0},{6,4},{2,6},{1,3},{5,1},{7,5},{3,7},{8,10},{12,8},{14,... | collective-permute-start | bytes 393224 | tf_op jit(solution)/shard_map/ppermute | solution.py:28
  3.7 2.3 %prepare.1 = (bf16[1,144,512]{2,1,0:T(8,128)(2,1)}, f32[128,128]{1,0:T(8,128)}, bf16[512,128]{1,0:T(8,128)(2,1)}, bf16[512,128]{1,0:T(8,128)(2,1)}, bf16[512,128]{1,0:T(8,128)(2,1)}, /*index=5*/bf16[512,128]{1,0:T(8,128)(2,1)}) custom-call(s32[1,2]{1,0:T(1,128)} %span_source.1, bf16[1,128,512]{2,1,0:T(8,128)(2,1)} %key_ref.1, bf16[1,128,4096]{2,1,0:T(8,128)(2,1)} %cot_source.1), custom_call_target="tpu_custom_call" | custom-call | tf_op jit(solution)/shard_map/prepare/pallas_call | solution.py:206
  6.0 1.1 %collective-permute-start = (bf16[1,144,512]{2,1,0:T(8,128)(2,1)}, bf16[1,144,512]{2,1,0:T(8,128)(2,1)S(1)}, u32[]{:S(2)}, u32[]{:S(2)}) collective-permute-start(bf16[1,144,512]{2,1,0:T(8,128)(2,1)} %get-tuple-element.21.refs_1_), channel_id=1, source_target_pairs={{0,4},{4,6},{6,2},{2,0},{1,5},{5,7},{7,3},{3,1},{8,12},{12,14},{14... | collective-permute-start | bytes 442376 | tf_op jit(solution)/shard_map/ppermute | solution.py:28
  7.1 2.0 %collective-permute-start.1 = (bf16[1,128,512]{2,1,0:T(8,128)(2,1)}, bf16[1,128,512]{2,1,0:T(8,128)(2,1)S(1)}, u32[]{:S(2)}, u32[]{:S(2)}) collective-permute-start(bf16[1,128,512]{2,1,0:T(8,128)(2,1)} %refs_3_.1), channel_id=1, source_target_pairs={{0,4},{4,6},{6,2},{2,0},{1,5},{5,7},{7,3},{3,1},{8,12},{12,14},{14... | collective-permute-start | bytes 393224 | tf_op jit(solution)/shard_map/ppermute | solution.py:28
  9.1 2.5 %collective-permute-start.3 = (bf16[512,128]{1,0:T(8,128)(2,1)}, bf16[512,128]{1,0:T(8,128)(2,1)S(1)}, u32[]{:S(2)}, u32[]{:S(2)}) collective-permute-start(bf16[512,128]{1,0:T(8,128)(2,1)} %get-tuple-element.28), channel_id=1, source_target_pairs={{0,4},{4,6},{6,2},{2,0},{1,5},{5,7},{7,3},{3,1},{8,12},{12,14},{14... | collective-permute-start | bytes 393224 | tf_op jit(solution)/shard_map/ppermute | solution.py:28
  11.6 9.0 %collective-permute-start.5 = (bf16[512,128]{1,0:T(8,128)(2,1)}, bf16[512,128]{1,0:T(8,128)(2,1)S(1)}, u32[]{:S(2)}, u32[]{:S(2)}) collective-permute-start(bf16[512,128]{1,0:T(8,128)(2,1)} %get-tuple-element.30), channel_id=1, source_target_pairs={{0,2},{4,0},{6,4},{2,6},{1,3},{5,1},{7,5},{3,7},{8,10},{12,8},{14,... | collective-permute-start | bytes 393224 | tf_op jit(solution)/shard_map/ppermute | solution.py:28
  20.6 1.0 %copy-done = bf16[1,128,2048]{2,1,0:T(8,128)(2,1)S(1)} copy-done((bf16[1,128,2048]{2,1,0:T(8,128)(2,1)S(1)}, bf16[1,128,2048]{2,1,0:T(8,128)(2,1)}, u32[]{:S(2)}) %copy-start) | copy-done | bytes 524312
  21.7 0.9 %copy-done.1 = bf16[1,128,512]{2,1,0:T(8,128)(2,1)S(1)} copy-done((bf16[1,128,512]{2,1,0:T(8,128)(2,1)S(1)}, bf16[1,128,512]{2,1,0:T(8,128)(2,1)}, u32[]{:S(2)}) %copy-start.1) | copy-done | bytes 131096
  22.6 0.9 %copy-done.2 = bf16[512,128]{1,0:T(8,128)(2,1)S(1)} copy-done((bf16[512,128]{1,0:T(8,128)(2,1)S(1)}, bf16[512,128]{1,0:T(8,128)(2,1)}, u32[]{:S(2)}) %copy-start.2) | copy-done | bytes 131096
  23.5 0.8 copy-done.3
  24.3 1.0 %fetch.1 = (f32[128,128]{1,0:T(8,128)S(1)}, bf16[1,144,512]{2,1,0:T(8,128)(2,1)S(1)}, bf16[1,128,2048]{2,1,0:T(8,128)(2,1)S(1)}, bf16[1,128,512]{2,1,0:T(8,128)(2,1)S(1)}, bf16[512,128]{1,0:T(8,128)(2,1)S(1)}) custom-call(f32[128,128]{1,0:T(8,128)S(1)} %copy-done.3, bf16[1,144,512]{2,1,0:T(8,128)(2,1)} %get-tuple-element.21.refs_1_, ...), custom_call_target="tpu_custom_call" | custom-call | tf_op jit(solution)/shard_map/fetch/pallas_call | solution.py:224
  25.3 3.8 %collective-permute-start.7 = (bf16[1,144,512]{2,1,0:T(8,128)(2,1)}, bf16[1,144,512]{2,1,0:T(8,128)(2,1)S(1)}, u32[]{:S(2)}, u32[]{:S(2)}) collective-permute-start(bf16[1,144,512]{2,1,0:T(8,128)(2,1)} %get-tuple-element.21.refs_1_), channel_id=1, source_target_pairs={{0,2},{4,0},{6,4},{2,6},{1,3},{5,1},{7,5},{3,7},{8,10},{12,8},{14,... | collective-permute-start | bytes 442376 | tf_op jit(solution)/shard_map/ppermute | solution.py:28
  29.1 0.1 join.1.refs_6_.refs_2_
  29.2 0.1 collective-permute-start.6
  29.3 2.0 %collective-permute-start.8 = (bf16[1,128,512]{2,1,0:T(8,128)(2,1)S(1)}, bf16[1,128,512]{2,1,0:T(8,128)(2,1)S(1)}, u32[]{:S(2)}, u32[]{:S(2)}) collective-permute-start(bf16[1,128,512]{2,1,0:T(8,128)(2,1)S(1)} %collective-permute-done.2.refs_7_), channel_id=1, source_target_pairs={{0,2},{4,0},{6,4},{2,6},{1,3},{5,1},{7,5},{3,7},{8,10},{12,8},{14,... | collective-permute-start | bytes 393224 | tf_op jit(solution)/shard_map/ppermute | solution.py:28
  31.3 1.1 %collective-permute-start.15 = (bf16[512,512]{1,0:T(8,128)(2,1)S(1)}, bf16[512,512]{1,0:T(8,128)(2,1)S(1)}, u32[]{:S(2)}, u32[]{:S(2)}) collective-permute-start(bf16[512,512]{1,0:T(8,128)(2,1)S(1)} %join.1.refs_6_.refs_2_), channel_id=1, source_target_pairs={{0,16},{8,24},{16,0},{24,8},{1,17},{9,25},{17,1},{25,9},{2,18},{10... | collective-permute-start | bytes 1572872 | tf_op jit(solution)/shard_map/ppermute | solution.py:44
  32.4 3.5 %collective-permute-done.7.refs_3_ = bf16[1,144,512]{2,1,0:T(8,128)(2,1)S(1)} collective-permute-done((bf16[1,144,512]{2,1,0:T(8,128)(2,1)}, bf16[1,144,512]{2,1,0:T(8,128)(2,1)S(1)}, u32[]{:S(2)}, u32[]{:S(2)}) %collective-permute-start.7) | collective-permute-done | bytes 147488 | tf_op jit(solution)/shard_map/ppermute | solution.py:28
  35.9 1.9 %collective-permute-done.8.refs_6_ = bf16[1,128,512]{2,1,0:T(8,128)(2,1)S(1)} collective-permute-done((bf16[1,128,512]{2,1,0:T(8,128)(2,1)S(1)}, bf16[1,128,512]{2,1,0:T(8,128)(2,1)S(1)}, u32[]{:S(2)}, u32[]{:S(2)}) %collective-permute-start.8) | collective-permute-done | bytes 131104 | tf_op jit(solution)/shard_map/ppermute | solution.py:28
  37.8 1.2 %collective-permute-done.6.refs_2_ = bf16[1,144,512]{2,1,0:T(8,128)(2,1)S(1)} collective-permute-done((bf16[1,144,512]{2,1,0:T(8,128)(2,1)S(1)}, bf16[1,144,512]{2,1,0:T(8,128)(2,1)S(1)}, u32[]{:S(2)}, u32[]{:S(2)}) %collective-permute-start.6) | collective-permute-done | bytes 147488 | tf_op jit(solution)/shard_map/ppermute | solution.py:28
  39.1 1.1 %attend.2.refs_0_ = bf16[1,128,1024]{2,1,0:T(8,128)(2,1)S(1)} custom-call(f32[128,128]{1,0:T(8,128)S(1)} %get-tuple-element.23.place_ref, bf16[1,128,2048]{2,1,0:T(8,128)(2,1)S(1)} %get-tuple-element.24.query_ref, bf16[1,144,512]{2,1,0:T(8,128)(2,1)S(1)} %get-tuple-element.25.refs_0_, bf16[1,144,512]{2,1,0:T(8,128)(2,1)S(1)} %collective-permute-done.refs_1_, ...), custom_call_target="tpu_custom_call" | custom-call | tf_op jit(solution)/shard_map/attend/pallas_call | solution.py:249
  40.2 1.3 %collective-permute-start.20 = (bf16[1,128,1024]{2,1,0:T(8,128)(2,1)S(1)}, bf16[1,128,1024]{2,1,0:T(8,128)(2,1)S(1)}, u32[]{:S(2)}, u32[]{:S(2)}) collective-permute-start(bf16[1,128,1024]{2,1,0:T(8,128)(2,1)S(1)} %attend.2.refs_0_), channel_id=1, source_target_pairs={{0,16},{8,24},{16,0},{24,8},{1,17},{9,25},{17,1},{25,9},{2,18},{10... | collective-permute-start | bytes 786440 | tf_op jit(solution)/shard_map/ppermute | solution.py:44
  41.5 1.1 %attend.3.refs_0_ = bf16[1,128,1024]{2,1,0:T(8,128)(2,1)S(1)} custom-call(f32[128,128]{1,0:T(8,128)S(1)} %get-tuple-element.23.place_ref, bf16[1,128,2048]{2,1,0:T(8,128)(2,1)S(1)} %get-tuple-element.24.query_ref, bf16[1,144,512]{2,1,0:T(8,128)(2,1)S(1)} %get-tuple-element.25.refs_0_, bf16[1,144,512]{2,1,0:T(8,128)(2,1)S(1)} %collective-permute-done.refs_1_, ...), custom_call_target="tpu_custom_call" | custom-call | tf_op jit(solution)/shard_map/attend/pallas_call | solution.py:249
  42.6 0.8 collective-permute-start.10
  43.4 2.3 %collective-permute-start.9 = (bf16[1,128,1024]{2,1,0:T(8,128)(2,1)S(1)}, bf16[1,128,1024]{2,1,0:T(8,128)(2,1)S(1)}, u32[]{:S(2)}, u32[]{:S(2)}) collective-permute-start(bf16[1,128,1024]{2,1,0:T(8,128)(2,1)S(1)} %attend.3.refs_0_), channel_id=1, source_target_pairs={{0,4},{4,6},{6,2},{2,0},{1,5},{5,7},{7,3},{3,1},{8,12},{12,14},{14... | collective-permute-start | bytes 786440 | tf_op jit(solution)/shard_map/ppermute | solution.py:28
  45.7 5.2 %collective-permute-done.20.refs_3_ = bf16[1,128,1024]{2,1,0:T(8,128)(2,1)S(1)} collective-permute-done((bf16[1,128,1024]{2,1,0:T(8,128)(2,1)S(1)}, bf16[1,128,1024]{2,1,0:T(8,128)(2,1)S(1)}, u32[]{:S(2)}, u32[]{:S(2)}) %collective-permute-start.20) | collective-permute-done | bytes 262176 | tf_op jit(solution)/shard_map/ppermute | solution.py:44
  50.9 2.0 %collective-permute-start.22 = (bf16[1,128,1024]{2,1,0:T(8,128)(2,1)S(1)}, bf16[1,128,1024]{2,1,0:T(8,128)(2,1)S(1)}, u32[]{:S(2)}, u32[]{:S(2)}) collective-permute-start(bf16[1,128,1024]{2,1,0:T(8,128)(2,1)S(1)} %collective-permute-done.19.refs_1_), channel_id=1, source_target_pairs={{0,16},{8,24},{16,0},{24,8},{1,17},{9,25},{17,1},{25,9},{2,18},{10... | collective-permute-start | bytes 786440 | tf_op jit(solution)/shard_map/ppermute | solution.py:44
  52.9 1.5 %collective-permute-start.16 = (bf16[512,512]{1,0:T(8,128)(2,1)S(1)}, bf16[512,512]{1,0:T(8,128)(2,1)S(1)}, u32[]{:S(2)}, u32[]{:S(2)}) collective-permute-start(bf16[512,512]{1,0:T(8,128)(2,1)S(1)} %join.1.refs_6_.refs_2_), channel_id=1, source_target_pairs={{0,1},{1,0},{2,3},{3,2},{4,5},{5,4},{6,7},{7,6},{8,9},{9,8},{10,11... | collective-permute-start | bytes 1572872 | tf_op jit(solution)/shard_map/ppermute | solution.py:44
  54.4 2.2 %collective-permute-done.10.refs_3_ = bf16[1,128,1024]{2,1,0:T(8,128)(2,1)S(1)} collective-permute-done((bf16[1,128,1024]{2,1,0:T(8,128)(2,1)S(1)}, bf16[1,128,1024]{2,1,0:T(8,128)(2,1)S(1)}, u32[]{:S(2)}, u32[]{:S(2)}) %collective-permute-start.10) | collective-permute-done | bytes 262176 | tf_op jit(solution)/shard_map/ppermute | solution.py:44
  56.5 1.8 %collective-permute-start.21 = (bf16[1,128,1024]{2,1,0:T(8,128)(2,1)S(1)}, bf16[1,128,1024]{2,1,0:T(8,128)(2,1)S(1)}, u32[]{:S(2)}, u32[]{:S(2)}) collective-permute-start(bf16[1,128,1024]{2,1,0:T(8,128)(2,1)S(1)} %collective-permute-done.19.refs_1_), channel_id=1, source_target_pairs={{0,4},{4,6},{6,2},{2,0},{1,5},{5,7},{7,3},{3,1},{8,12},{12,14},{14... | collective-permute-start | bytes 786440 | tf_op jit(solution)/shard_map/ppermute | solution.py:28
  58.4 1.1 %collective-permute-start.12 = (bf16[1,128,1024]{2,1,0:T(8,128)(2,1)S(1)}, bf16[1,128,1024]{2,1,0:T(8,128)(2,1)S(1)}, u32[]{:S(2)}, u32[]{:S(2)}) collective-permute-start(bf16[1,128,1024]{2,1,0:T(8,128)(2,1)S(1)} %collective-permute-done.9.refs_1_), channel_id=1, source_target_pairs={{0,16},{8,24},{16,0},{24,8},{1,17},{9,25},{17,1},{25,9},{2,18},{10... | collective-permute-start | bytes 786440 | tf_op jit(solution)/shard_map/ppermute | solution.py:44
  59.5 2.7 %collective-permute-done.22.refs_4_ = bf16[1,128,1024]{2,1,0:T(8,128)(2,1)S(1)} collective-permute-done((bf16[1,128,1024]{2,1,0:T(8,128)(2,1)S(1)}, bf16[1,128,1024]{2,1,0:T(8,128)(2,1)S(1)}, u32[]{:S(2)}, u32[]{:S(2)}) %collective-permute-start.22) | collective-permute-done | bytes 262176 | tf_op jit(solution)/shard_map/ppermute | solution.py:44
  62.2 1.9 %collective-permute-start.17 = (bf16[512,512]{1,0:T(8,128)(2,1)S(1)}, bf16[512,512]{1,0:T(8,128)(2,1)S(1)}, u32[]{:S(2)}, u32[]{:S(2)}) collective-permute-start(bf16[512,512]{1,0:T(8,128)(2,1)S(1)} %collective-permute-done.15.refs_7_.refs_3_), channel_id=1, source_target_pairs={{0,1},{1,0},{2,3},{3,2},{4,5},{5,4},{6,7},{7,6},{8,9},{9,8},{10,11... | collective-permute-start | bytes 1572872 | tf_op jit(solution)/shard_map/ppermute | solution.py:44
  64.1 1.0 %collective-permute-done.21.refs_2_ = bf16[1,128,1024]{2,1,0:T(8,128)(2,1)S(1)} collective-permute-done((bf16[1,128,1024]{2,1,0:T(8,128)(2,1)S(1)}, bf16[1,128,1024]{2,1,0:T(8,128)(2,1)S(1)}, u32[]{:S(2)}, u32[]{:S(2)}) %collective-permute-start.21) | collective-permute-done | bytes 262176 | tf_op jit(solution)/shard_map/ppermute | solution.py:28
  65.1 1.1 %collective-permute-start.24 = (bf16[1,128,1024]{2,1,0:T(8,128)(2,1)S(1)}, bf16[1,128,1024]{2,1,0:T(8,128)(2,1)S(1)}, u32[]{:S(2)}, u32[]{:S(2)}) collective-permute-start(bf16[1,128,1024]{2,1,0:T(8,128)(2,1)S(1)} %collective-permute-done.21.refs_2_), channel_id=1, source_target_pairs={{0,16},{8,24},{16,0},{24,8},{1,17},{9,25},{17,1},{25,9},{2,18},{10... | collective-permute-start | bytes 786440 | tf_op jit(solution)/shard_map/ppermute | solution.py:44
  66.2 1.6 %collective-permute-done.12.refs_4_ = bf16[1,128,1024]{2,1,0:T(8,128)(2,1)S(1)} collective-permute-done((bf16[1,128,1024]{2,1,0:T(8,128)(2,1)S(1)}, bf16[1,128,1024]{2,1,0:T(8,128)(2,1)S(1)}, u32[]{:S(2)}, u32[]{:S(2)}) %collective-permute-start.12) | collective-permute-done | bytes 262176 | tf_op jit(solution)/shard_map/ppermute | solution.py:44
  67.8 0.1 collective-permute-done.11.refs_2_
  67.9 1.7 %collective-permute-start.13 = (bf16[1,128,1024]{2,1,0:T(8,128)(2,1)S(1)}, bf16[1,128,1024]{2,1,0:T(8,128)(2,1)S(1)}, u32[]{:S(2)}, u32[]{:S(2)}) collective-permute-start(bf16[1,128,1024]{2,1,0:T(8,128)(2,1)S(1)} %collective-permute-done.11.refs_2_), channel_id=1, source_target_pairs={{0,4},{4,6},{6,2},{2,0},{1,5},{5,7},{7,3},{3,1},{8,12},{12,14},{14... | collective-permute-start | bytes 786440 | tf_op jit(solution)/shard_map/ppermute | solution.py:28
  69.6 1.8 %collective-permute-start.18 = (bf16[1,128,1024]{2,1,0:T(8,128)(2,1)S(1)}, bf16[1,128,1024]{2,1,0:T(8,128)(2,1)S(1)}, u32[]{:S(2)}, u32[]{:S(2)}) collective-permute-start(bf16[1,128,1024]{2,1,0:T(8,128)(2,1)S(1)} %collective-permute-done.11.refs_2_), channel_id=1, source_target_pairs={{0,16},{8,24},{16,0},{24,8},{1,17},{9,25},{17,1},{25,9},{2,18},{10... | collective-permute-start | bytes 786440 | tf_op jit(solution)/shard_map/ppermute | solution.py:44
  71.4 0.8 pad_maximum_fusion
  72.2 2.1 %collective-permute-done.24.refs_5_ = bf16[1,128,1024]{2,1,0:T(8,128)(2,1)S(1)} collective-permute-done((bf16[1,128,1024]{2,1,0:T(8,128)(2,1)S(1)}, bf16[1,128,1024]{2,1,0:T(8,128)(2,1)S(1)}, u32[]{:S(2)}, u32[]{:S(2)}) %collective-permute-start.24) | collective-permute-done | bytes 262176 | tf_op jit(solution)/shard_map/ppermute | solution.py:44
  74.3 1.5 %collective-permute-start.25 = (bf16[1,128,1024]{2,1,0:T(8,128)(2,1)S(1)}, bf16[1,128,1024]{2,1,0:T(8,128)(2,1)S(1)}, u32[]{:S(2)}, u32[]{:S(2)}) collective-permute-start(bf16[1,128,1024]{2,1,0:T(8,128)(2,1)S(1)} %collective-permute-done.24.refs_5_), channel_id=1, source_target_pairs={{0,4},{4,6},{6,2},{2,0},{1,5},{5,7},{7,3},{3,1},{8,12},{12,14},{14... | collective-permute-start | bytes 786440 | tf_op jit(solution)/shard_map/ppermute | solution.py:28
  75.9 1.1 %collective-permute-done.13.refs_0_ = bf16[1,128,1024]{2,1,0:T(8,128)(2,1)S(1)} collective-permute-done((bf16[1,128,1024]{2,1,0:T(8,128)(2,1)S(1)}, bf16[1,128,1024]{2,1,0:T(8,128)(2,1)S(1)}, u32[]{:S(2)}, u32[]{:S(2)}) %collective-permute-start.13) | collective-permute-done | bytes 262176 | tf_op jit(solution)/shard_map/ppermute | solution.py:28
  77.0 2.0 %collective-permute-start.14 = (bf16[1,128,1024]{2,1,0:T(8,128)(2,1)S(1)}, bf16[1,128,1024]{2,1,0:T(8,128)(2,1)S(1)}, u32[]{:S(2)}, u32[]{:S(2)}) collective-permute-start(bf16[1,128,1024]{2,1,0:T(8,128)(2,1)S(1)} %collective-permute-done.13.refs_0_), channel_id=1, source_target_pairs={{0,16},{8,24},{16,0},{24,8},{1,17},{9,25},{17,1},{25,9},{2,18},{10... | collective-permute-start | bytes 786440 | tf_op jit(solution)/shard_map/ppermute | solution.py:44
  79.0 1.8 %early.3.refs_6_ = f32[1024,1024]{1,0:T(8,128)S(1)} custom-call(bf16[1,128,1024]{2,1,0:T(8,128)(2,1)S(1)} %attend.2.refs_0_, bf16[1,128,1024]{2,1,0:T(8,128)(2,1)S(1)} %collective-permute-done.19.refs_1_, bf16[1,128,1024]{2,1,0:T(8,128)(2,1)S(1)} %collective-permute-done.21.refs_2_, bf16[1,128,1024]{2,1,0:T(8,128)(2,1)S(1)} %collective-permute-done.20.refs_3_, ...), custom_call_target="tpu_custom_call" | custom-call | flops 1610612736 | bytes 8388608 | tf_op jit(solution)/shard_map/early/pallas_call | solution.py:286
  80.8 1.8 %early.2.refs_6_ = f32[1024,1024]{1,0:T(8,128)S(1)} custom-call(bf16[1,128,1024]{2,1,0:T(8,128)(2,1)S(1)} %attend.3.refs_0_, bf16[1,128,1024]{2,1,0:T(8,128)(2,1)S(1)} %collective-permute-done.9.refs_1_, bf16[1,128,1024]{2,1,0:T(8,128)(2,1)S(1)} %collective-permute-done.11.refs_2_, bf16[1,128,1024]{2,1,0:T(8,128)(2,1)S(1)} %collective-permute-done.10.refs_3_, ...), custom_call_target="tpu_custom_call" | custom-call | flops 1610612736 | bytes 8388608 | tf_op jit(solution)/shard_map/early/pallas_call | solution.py:286
  82.6 2.2 %collective-permute-done.25.refs_1_ = bf16[1,128,1024]{2,1,0:T(8,128)(2,1)S(1)} collective-permute-done((bf16[1,128,1024]{2,1,0:T(8,128)(2,1)S(1)}, bf16[1,128,1024]{2,1,0:T(8,128)(2,1)S(1)}, u32[]{:S(2)}, u32[]{:S(2)}) %collective-permute-start.25) | collective-permute-done | bytes 262176 | tf_op jit(solution)/shard_map/ppermute | solution.py:28
  84.8 1.6 %finish.2.refs_7_ = bf16[1,1024,2048]{2,1,0:T(8,128)(2,1)} custom-call(bf16[1,128,1024]{2,1,0:T(8,128)(2,1)S(1)} %collective-permute-done.23.refs_0_, bf16[1,128,1024]{2,1,0:T(8,128)(2,1)S(1)} %collective-permute-done.25.refs_1_, bf16[512,512]{1,0:T(8,128)(2,1)S(1)} %join.1.refs_6_.refs_2_, bf16[512,512]{1,0:T(8,128)(2,1)S(1)} %collective-permute-done.15.refs_7_.refs_3_, ...), custom_call_target="tpu_custom_call" | custom-call | flops 536870912 | bytes 8388608 | tf_op jit(solution)/shard_map/finish/pallas_call | solution.py:311
  86.5 1.7 %finish.3 = bf16[1,1024,2048]{2,1,0:T(8,128)(2,1)} custom-call(bf16[1,128,1024]{2,1,0:T(8,128)(2,1)S(1)} %collective-permute-done.13.refs_0_, bf16[1,128,1024]{2,1,0:T(8,128)(2,1)S(1)} %collective-permute-done.14.refs_1_, bf16[512,512]{1,0:T(8,128)(2,1)S(1)} %join.1.refs_6_.refs_2_, ...), custom_call_target="tpu_custom_call", output_to_operand_aliasing={{}: (7, {})} | custom-call | flops 536870912 | bytes 8388608 | tf_op jit(solution)/shard_map/finish/pallas_call | solution.py:311
  (22 shorter events, 0.1 us)
Async XLA Ops:
  0.6 10.9 %collective-permute-start.2 = (bf16[1,128,512]{2,1,0:T(8,128)(2,1)}, bf16[1,128,512]{2,1,0:T(8,128)(2,1)S(1)}, u32[]{:S(2)}, u32[]{:S(2)}) collective-permute-start(bf16[1,128,512]{2,1,0:T(8,128)(2,1)} %refs_3_.1), channel_id=1, source_target_pairs={{0,2},{4,0},{6,4},{2,6},{1,3},{5,1},{7,5},{3,7},{8,10},{12,8},{14,... | collective-permute-start | bytes 393224 | tf_op jit(solution)/shard_map/ppermute | solution.py:28
  6.0 23.2 %collective-permute-start = (bf16[1,144,512]{2,1,0:T(8,128)(2,1)}, bf16[1,144,512]{2,1,0:T(8,128)(2,1)S(1)}, u32[]{:S(2)}, u32[]{:S(2)}) collective-permute-start(bf16[1,144,512]{2,1,0:T(8,128)(2,1)} %get-tuple-element.21.refs_1_), channel_id=1, source_target_pairs={{0,4},{4,6},{6,2},{2,0},{1,5},{5,7},{7,3},{3,1},{8,12},{12,14},{14... | collective-permute-start | bytes 442376 | tf_op jit(solution)/shard_map/ppermute | solution.py:28
  7.1 18.2 %collective-permute-start.1 = (bf16[1,128,512]{2,1,0:T(8,128)(2,1)}, bf16[1,128,512]{2,1,0:T(8,128)(2,1)S(1)}, u32[]{:S(2)}, u32[]{:S(2)}) collective-permute-start(bf16[1,128,512]{2,1,0:T(8,128)(2,1)} %refs_3_.1), channel_id=1, source_target_pairs={{0,4},{4,6},{6,2},{2,0},{1,5},{5,7},{7,3},{3,1},{8,12},{12,14},{14... | collective-permute-start | bytes 393224 | tf_op jit(solution)/shard_map/ppermute | solution.py:28
  9.1 20.0 %collective-permute-start.3 = (bf16[512,128]{1,0:T(8,128)(2,1)}, bf16[512,128]{1,0:T(8,128)(2,1)S(1)}, u32[]{:S(2)}, u32[]{:S(2)}) collective-permute-start(bf16[512,128]{1,0:T(8,128)(2,1)} %get-tuple-element.28), channel_id=1, source_target_pairs={{0,4},{4,6},{6,2},{2,0},{1,5},{5,7},{7,3},{3,1},{8,12},{12,14},{14... | collective-permute-start | bytes 393224 | tf_op jit(solution)/shard_map/ppermute | solution.py:28
  11.6 17.6 %collective-permute-start.4 = (bf16[512,128]{1,0:T(8,128)(2,1)}, bf16[512,128]{1,0:T(8,128)(2,1)S(1)}, u32[]{:S(2)}, u32[]{:S(2)}) collective-permute-start(bf16[512,128]{1,0:T(8,128)(2,1)} %get-tuple-element.29), channel_id=1, source_target_pairs={{0,6},{4,2},{6,0},{2,4},{1,7},{5,3},{7,1},{3,5},{8,14},{12,10},{14... | collective-permute-start | bytes 393224 | tf_op jit(solution)/shard_map/ppermute | solution.py:28
  11.6 17.6 %collective-permute-start.5 = (bf16[512,128]{1,0:T(8,128)(2,1)}, bf16[512,128]{1,0:T(8,128)(2,1)S(1)}, u32[]{:S(2)}, u32[]{:S(2)}) collective-permute-start(bf16[512,128]{1,0:T(8,128)(2,1)} %get-tuple-element.30), channel_id=1, source_target_pairs={{0,2},{4,0},{6,4},{2,6},{1,3},{5,1},{7,5},{3,7},{8,10},{12,8},{14,... | collective-permute-start | bytes 393224 | tf_op jit(solution)/shard_map/ppermute | solution.py:28
  20.6 1.0 %copy-start = (bf16[1,128,2048]{2,1,0:T(8,128)(2,1)S(1)}, bf16[1,128,2048]{2,1,0:T(8,128)(2,1)}, u32[]{:S(2)}) copy-start(bf16[1,128,2048]{2,1,0:T(8,128)(2,1)} %refs_2_.1) | copy-start | bytes 1572868
  21.7 0.9 %copy-start.1 = (bf16[1,128,512]{2,1,0:T(8,128)(2,1)S(1)}, bf16[1,128,512]{2,1,0:T(8,128)(2,1)}, u32[]{:S(2)}) copy-start(bf16[1,128,512]{2,1,0:T(8,128)(2,1)} %refs_3_.1) | copy-start | bytes 393220
  22.6 0.9 %copy-start.2 = (bf16[512,128]{1,0:T(8,128)(2,1)S(1)}, bf16[512,128]{1,0:T(8,128)(2,1)}, u32[]{:S(2)}) copy-start(bf16[512,128]{1,0:T(8,128)(2,1)} %get-tuple-element.22.refs_4_) | copy-start | bytes 393220
  23.5 0.8 copy-start.3
  25.3 10.6 %collective-permute-start.7 = (bf16[1,144,512]{2,1,0:T(8,128)(2,1)}, bf16[1,144,512]{2,1,0:T(8,128)(2,1)S(1)}, u32[]{:S(2)}, u32[]{:S(2)}) collective-permute-start(bf16[1,144,512]{2,1,0:T(8,128)(2,1)} %get-tuple-element.21.refs_1_), channel_id=1, source_target_pairs={{0,2},{4,0},{6,4},{2,6},{1,3},{5,1},{7,5},{3,7},{8,10},{12,8},{14,... | collective-permute-start | bytes 442376 | tf_op jit(solution)/shard_map/ppermute | solution.py:28
  29.2 9.8 %collective-permute-start.6 = (bf16[1,144,512]{2,1,0:T(8,128)(2,1)S(1)}, bf16[1,144,512]{2,1,0:T(8,128)(2,1)S(1)}, u32[]{:S(2)}, u32[]{:S(2)}) collective-permute-start(bf16[1,144,512]{2,1,0:T(8,128)(2,1)S(1)} %collective-permute-done.refs_1_), channel_id=1, source_target_pairs={{0,4},{4,6},{6,2},{2,0},{1,5},{5,7},{7,3},{3,1},{8,12},{12,14},{14... | collective-permute-start | bytes 442376 | tf_op jit(solution)/shard_map/ppermute | solution.py:28
  29.3 8.5 %collective-permute-start.8 = (bf16[1,128,512]{2,1,0:T(8,128)(2,1)S(1)}, bf16[1,128,512]{2,1,0:T(8,128)(2,1)S(1)}, u32[]{:S(2)}, u32[]{:S(2)}) collective-permute-start(bf16[1,128,512]{2,1,0:T(8,128)(2,1)S(1)} %collective-permute-done.2.refs_7_), channel_id=1, source_target_pairs={{0,2},{4,0},{6,4},{2,6},{1,3},{5,1},{7,5},{3,7},{8,10},{12,8},{14,... | collective-permute-start | bytes 393224 | tf_op jit(solution)/shard_map/ppermute | solution.py:28
  31.3 28.1 %collective-permute-start.15 = (bf16[512,512]{1,0:T(8,128)(2,1)S(1)}, bf16[512,512]{1,0:T(8,128)(2,1)S(1)}, u32[]{:S(2)}, u32[]{:S(2)}) collective-permute-start(bf16[512,512]{1,0:T(8,128)(2,1)S(1)} %join.1.refs_6_.refs_2_), channel_id=1, source_target_pairs={{0,16},{8,24},{16,0},{24,8},{1,17},{9,25},{17,1},{25,9},{2,18},{10... | collective-permute-start | bytes 1572872 | tf_op jit(solution)/shard_map/ppermute | solution.py:44
  40.2 10.8 %collective-permute-start.20 = (bf16[1,128,1024]{2,1,0:T(8,128)(2,1)S(1)}, bf16[1,128,1024]{2,1,0:T(8,128)(2,1)S(1)}, u32[]{:S(2)}, u32[]{:S(2)}) collective-permute-start(bf16[1,128,1024]{2,1,0:T(8,128)(2,1)S(1)} %attend.2.refs_0_), channel_id=1, source_target_pairs={{0,16},{8,24},{16,0},{24,8},{1,17},{9,25},{17,1},{25,9},{2,18},{10... | collective-permute-start | bytes 786440 | tf_op jit(solution)/shard_map/ppermute | solution.py:44
  41.5 9.4 %collective-permute-start.19 = (bf16[1,128,1024]{2,1,0:T(8,128)(2,1)S(1)}, bf16[1,128,1024]{2,1,0:T(8,128)(2,1)S(1)}, u32[]{:S(2)}, u32[]{:S(2)}) collective-permute-start(bf16[1,128,1024]{2,1,0:T(8,128)(2,1)S(1)} %attend.2.refs_0_), channel_id=1, source_target_pairs={{0,4},{4,6},{6,2},{2,0},{1,5},{5,7},{7,3},{3,1},{8,12},{12,14},{14... | collective-permute-start | bytes 786440 | tf_op jit(solution)/shard_map/ppermute | solution.py:28
  42.6 14.0 %collective-permute-start.10 = (bf16[1,128,1024]{2,1,0:T(8,128)(2,1)S(1)}, bf16[1,128,1024]{2,1,0:T(8,128)(2,1)S(1)}, u32[]{:S(2)}, u32[]{:S(2)}) collective-permute-start(bf16[1,128,1024]{2,1,0:T(8,128)(2,1)S(1)} %attend.3.refs_0_), channel_id=1, source_target_pairs={{0,16},{8,24},{16,0},{24,8},{1,17},{9,25},{17,1},{25,9},{2,18},{10... | collective-permute-start | bytes 786440 | tf_op jit(solution)/shard_map/ppermute | solution.py:44
  43.4 15.0 %collective-permute-start.9 = (bf16[1,128,1024]{2,1,0:T(8,128)(2,1)S(1)}, bf16[1,128,1024]{2,1,0:T(8,128)(2,1)S(1)}, u32[]{:S(2)}, u32[]{:S(2)}) collective-permute-start(bf16[1,128,1024]{2,1,0:T(8,128)(2,1)S(1)} %attend.3.refs_0_), channel_id=1, source_target_pairs={{0,4},{4,6},{6,2},{2,0},{1,5},{5,7},{7,3},{3,1},{8,12},{12,14},{14... | collective-permute-start | bytes 786440 | tf_op jit(solution)/shard_map/ppermute | solution.py:28
  50.9 11.2 %collective-permute-start.22 = (bf16[1,128,1024]{2,1,0:T(8,128)(2,1)S(1)}, bf16[1,128,1024]{2,1,0:T(8,128)(2,1)S(1)}, u32[]{:S(2)}, u32[]{:S(2)}) collective-permute-start(bf16[1,128,1024]{2,1,0:T(8,128)(2,1)S(1)} %collective-permute-done.19.refs_1_), channel_id=1, source_target_pairs={{0,16},{8,24},{16,0},{24,8},{1,17},{9,25},{17,1},{25,9},{2,18},{10... | collective-permute-start | bytes 786440 | tf_op jit(solution)/shard_map/ppermute | solution.py:44
  52.9 19.3 %collective-permute-start.16 = (bf16[512,512]{1,0:T(8,128)(2,1)S(1)}, bf16[512,512]{1,0:T(8,128)(2,1)S(1)}, u32[]{:S(2)}, u32[]{:S(2)}) collective-permute-start(bf16[512,512]{1,0:T(8,128)(2,1)S(1)} %join.1.refs_6_.refs_2_), channel_id=1, source_target_pairs={{0,1},{1,0},{2,3},{3,2},{4,5},{5,4},{6,7},{7,6},{8,9},{9,8},{10,11... | collective-permute-start | bytes 1572872 | tf_op jit(solution)/shard_map/ppermute | solution.py:44
  56.5 8.5 %collective-permute-start.21 = (bf16[1,128,1024]{2,1,0:T(8,128)(2,1)S(1)}, bf16[1,128,1024]{2,1,0:T(8,128)(2,1)S(1)}, u32[]{:S(2)}, u32[]{:S(2)}) collective-permute-start(bf16[1,128,1024]{2,1,0:T(8,128)(2,1)S(1)} %collective-permute-done.19.refs_1_), channel_id=1, source_target_pairs={{0,4},{4,6},{6,2},{2,0},{1,5},{5,7},{7,3},{3,1},{8,12},{12,14},{14... | collective-permute-start | bytes 786440 | tf_op jit(solution)/shard_map/ppermute | solution.py:28
  58.4 9.4 %collective-permute-start.12 = (bf16[1,128,1024]{2,1,0:T(8,128)(2,1)S(1)}, bf16[1,128,1024]{2,1,0:T(8,128)(2,1)S(1)}, u32[]{:S(2)}, u32[]{:S(2)}) collective-permute-start(bf16[1,128,1024]{2,1,0:T(8,128)(2,1)S(1)} %collective-permute-done.9.refs_1_), channel_id=1, source_target_pairs={{0,16},{8,24},{16,0},{24,8},{1,17},{9,25},{17,1},{25,9},{2,18},{10... | collective-permute-start | bytes 786440 | tf_op jit(solution)/shard_map/ppermute | solution.py:44
  59.5 8.4 %collective-permute-start.11 = (bf16[1,128,1024]{2,1,0:T(8,128)(2,1)S(1)}, bf16[1,128,1024]{2,1,0:T(8,128)(2,1)S(1)}, u32[]{:S(2)}, u32[]{:S(2)}) collective-permute-start(bf16[1,128,1024]{2,1,0:T(8,128)(2,1)S(1)} %collective-permute-done.9.refs_1_), channel_id=1, source_target_pairs={{0,4},{4,6},{6,2},{2,0},{1,5},{5,7},{7,3},{3,1},{8,12},{12,14},{14... | collective-permute-start | bytes 786440 | tf_op jit(solution)/shard_map/ppermute | solution.py:28
  62.2 16.8 %collective-permute-start.17 = (bf16[512,512]{1,0:T(8,128)(2,1)S(1)}, bf16[512,512]{1,0:T(8,128)(2,1)S(1)}, u32[]{:S(2)}, u32[]{:S(2)}) collective-permute-start(bf16[512,512]{1,0:T(8,128)(2,1)S(1)} %collective-permute-done.15.refs_7_.refs_3_), channel_id=1, source_target_pairs={{0,1},{1,0},{2,3},{3,2},{4,5},{5,4},{6,7},{7,6},{8,9},{9,8},{10,11... | collective-permute-start | bytes 1572872 | tf_op jit(solution)/shard_map/ppermute | solution.py:44
  65.1 9.2 %collective-permute-start.24 = (bf16[1,128,1024]{2,1,0:T(8,128)(2,1)S(1)}, bf16[1,128,1024]{2,1,0:T(8,128)(2,1)S(1)}, u32[]{:S(2)}, u32[]{:S(2)}) collective-permute-start(bf16[1,128,1024]{2,1,0:T(8,128)(2,1)S(1)} %collective-permute-done.21.refs_2_), channel_id=1, source_target_pairs={{0,16},{8,24},{16,0},{24,8},{1,17},{9,25},{17,1},{25,9},{2,18},{10... | collective-permute-start | bytes 786440 | tf_op jit(solution)/shard_map/ppermute | solution.py:44
  67.9 9.1 %collective-permute-start.13 = (bf16[1,128,1024]{2,1,0:T(8,128)(2,1)S(1)}, bf16[1,128,1024]{2,1,0:T(8,128)(2,1)S(1)}, u32[]{:S(2)}, u32[]{:S(2)}) collective-permute-start(bf16[1,128,1024]{2,1,0:T(8,128)(2,1)S(1)} %collective-permute-done.11.refs_2_), channel_id=1, source_target_pairs={{0,4},{4,6},{6,2},{2,0},{1,5},{5,7},{7,3},{3,1},{8,12},{12,14},{14... | collective-permute-start | bytes 786440 | tf_op jit(solution)/shard_map/ppermute | solution.py:28
  69.6 11.2 %collective-permute-start.18 = (bf16[1,128,1024]{2,1,0:T(8,128)(2,1)S(1)}, bf16[1,128,1024]{2,1,0:T(8,128)(2,1)S(1)}, u32[]{:S(2)}, u32[]{:S(2)}) collective-permute-start(bf16[1,128,1024]{2,1,0:T(8,128)(2,1)S(1)} %collective-permute-done.11.refs_2_), channel_id=1, source_target_pairs={{0,16},{8,24},{16,0},{24,8},{1,17},{9,25},{17,1},{25,9},{2,18},{10... | collective-permute-start | bytes 786440 | tf_op jit(solution)/shard_map/ppermute | solution.py:44
  72.2 10.4 %collective-permute-start.23 = (bf16[1,128,1024]{2,1,0:T(8,128)(2,1)S(1)}, bf16[1,128,1024]{2,1,0:T(8,128)(2,1)S(1)}, u32[]{:S(2)}, u32[]{:S(2)}) collective-permute-start(bf16[1,128,1024]{2,1,0:T(8,128)(2,1)S(1)} %collective-permute-done.21.refs_2_), channel_id=1, source_target_pairs={{0,4},{4,6},{6,2},{2,0},{1,5},{5,7},{7,3},{3,1},{8,12},{12,14},{14... | collective-permute-start | bytes 786440 | tf_op jit(solution)/shard_map/ppermute | solution.py:28
  74.3 10.5 %collective-permute-start.25 = (bf16[1,128,1024]{2,1,0:T(8,128)(2,1)S(1)}, bf16[1,128,1024]{2,1,0:T(8,128)(2,1)S(1)}, u32[]{:S(2)}, u32[]{:S(2)}) collective-permute-start(bf16[1,128,1024]{2,1,0:T(8,128)(2,1)S(1)} %collective-permute-done.24.refs_5_), channel_id=1, source_target_pairs={{0,4},{4,6},{6,2},{2,0},{1,5},{5,7},{7,3},{3,1},{8,12},{12,14},{14... | collective-permute-start | bytes 786440 | tf_op jit(solution)/shard_map/ppermute | solution.py:28
  77.0 9.5 %collective-permute-start.14 = (bf16[1,128,1024]{2,1,0:T(8,128)(2,1)S(1)}, bf16[1,128,1024]{2,1,0:T(8,128)(2,1)S(1)}, u32[]{:S(2)}, u32[]{:S(2)}) collective-permute-start(bf16[1,128,1024]{2,1,0:T(8,128)(2,1)S(1)} %collective-permute-done.13.refs_0_), channel_id=1, source_target_pairs={{0,16},{8,24},{16,0},{24,8},{1,17},{9,25},{17,1},{25,9},{2,18},{10... | collective-permute-start | bytes 786440 | tf_op jit(solution)/shard_map/ppermute | solution.py:44

commit v14 on v13

--- a/solution.py
+++ b/solution.py
@@ -271,7 +271,7 @@
             sent.append(around(sent[-1], 1) if by_ring else swap(held[s], "pipe", far))
             if s < n - 1:
                 arrived = around(held[s], 1)
-                held.append(after(arrived, sent[s]) if s < n - 2 else arrived)
+                held.append(after(arrived, sent[s]) if s < n - 2 - (c == 0) else arrived)
         near.append(held)
         mirrored.append(sent)
     cots = [mine, mine_far, swap(mine, "tp", 1), swap(mine_far, "tp", 1)]

time: 88.4 us -> 88.4 us (level)
  starting transfers between devices: 45.6 us -> 43 us
  waiting for transfers between devices: 24.9 us -> 27.4 us
    ppermute x10, starting transfers between devices: 14.5 us -> 12.2 us  [swap(): lax.ppermute(x, axis, [(i, i ^ mask) for i in range(lax.axis_size(axis))])]
    ppermute x16, waiting for transfers between devices: 11.1 us -> 13.2 us  [around(): lax.ppermute(x, 'ctx', [(order[q], order[(q + shift) % n]) for q in range...]
  transfers between devices with their start and end apart: 26 -> 26, of which waited for: 12 -> 10; matrix products, arithmetic and copies ran while one was open for 1% -> 1% of each run, Pallas kernels for 12% -> 12%
where the time goes in v14:
time: 88.4 us; the launch traced here: 88.1 us
  starting transfers between devices  43 us (49%)
  waiting for transfers between devices  27.4 us (31%)
  Pallas kernels  12.4 us (14%)
  local copies, waits for them, and re-layouts  3.69 us (4%)
    ppermute x16, starting transfers between devices, around(): lax.ppermute(x, 'ctx', [(order[q], order[(q + shift) % n]) for q in range...  30.8 us
    ppermute x10, waiting for transfers between devices, swap(): lax.ppermute(x, axis, [(i, i ^ mask) for i in range(lax.axis_size(axis))])  14.1 us
    ppermute x16, waiting for transfers between devices, around(): lax.ppermute(x, 'ctx', [(order[q], order[(q + shift) % n]) for q in range...  13.2 us
    ppermute x10, starting transfers between devices, swap(): lax.ppermute(x, axis, [(i, i ^ mask) for i in range(lax.axis_size(axis))])  12.2 us
    unnamed x8, local copies, waits for them, and re-layouts  3.69 us
    pallas_call x2, Pallas kernels, local(): pl.pallas_call(functools.partial(early_kernel, first_slots), out_shape=ja...  3.59 us
    pallas_call x2, Pallas kernels, local(): pl.pallas_call(functools.partial(finish_kernel, slots, c * chunk), out_sh...  3.31 us
    pallas_call x1, Pallas kernels, local(): pl.pallas_call(functools.partial(prepare_kernel, n), out_shape=[jax.Shape...  2.29 us
  transfers between devices with their start and end apart: 26, of which 10 were waited for; matrix products, arithmetic and copies ran while one was open for 1% of the time, Pallas kernels for 12%

profile of v14, /device:TPU:0, one launch (start us, length us, event | category | flops | bytes accessed | tf_op | source)
XLA Modules:
  0.0 88.1 jit_solution(4436543613965307392)
XLA Ops:
  0.6 3.1 %collective-permute-start.2 = (bf16[1,128,512]{2,1,0:T(8,128)(2,1)}, bf16[1,128,512]{2,1,0:T(8,128)(2,1)S(1)}, u32[]{:S(2)}, u32[]{:S(2)}) collective-permute-start(bf16[1,128,512]{2,1,0:T(8,128)(2,1)} %refs_3_.1), channel_id=1, source_target_pairs={{0,2},{4,0},{6,4},{2,6},{1,3},{5,1},{7,5},{3,7},{8,10},{12,8},{14,... | collective-permute-start | bytes 393224 | tf_op jit(solution)/shard_map/ppermute | solution.py:28
  3.7 2.3 %prepare.1 = (bf16[1,144,512]{2,1,0:T(8,128)(2,1)}, f32[128,128]{1,0:T(8,128)}, bf16[512,128]{1,0:T(8,128)(2,1)}, bf16[512,128]{1,0:T(8,128)(2,1)}, bf16[512,128]{1,0:T(8,128)(2,1)}, /*index=5*/bf16[512,128]{1,0:T(8,128)(2,1)}) custom-call(s32[1,2]{1,0:T(1,128)} %span_source.1, bf16[1,128,512]{2,1,0:T(8,128)(2,1)} %key_ref.1, bf16[1,128,4096]{2,1,0:T(8,128)(2,1)} %cot_source.1), custom_call_target="tpu_custom_call" | custom-call | tf_op jit(solution)/shard_map/prepare/pallas_call | solution.py:206
  6.0 1.1 %collective-permute-start = (bf16[1,144,512]{2,1,0:T(8,128)(2,1)}, bf16[1,144,512]{2,1,0:T(8,128)(2,1)S(1)}, u32[]{:S(2)}, u32[]{:S(2)}) collective-permute-start(bf16[1,144,512]{2,1,0:T(8,128)(2,1)} %get-tuple-element.20.refs_1_), channel_id=1, source_target_pairs={{0,4},{4,6},{6,2},{2,0},{1,5},{5,7},{7,3},{3,1},{8,12},{12,14},{14... | collective-permute-start | bytes 442376 | tf_op jit(solution)/shard_map/ppermute | solution.py:28
  7.1 2.0 %collective-permute-start.1 = (bf16[1,128,512]{2,1,0:T(8,128)(2,1)}, bf16[1,128,512]{2,1,0:T(8,128)(2,1)S(1)}, u32[]{:S(2)}, u32[]{:S(2)}) collective-permute-start(bf16[1,128,512]{2,1,0:T(8,128)(2,1)} %refs_3_.1), channel_id=1, source_target_pairs={{0,4},{4,6},{6,2},{2,0},{1,5},{5,7},{7,3},{3,1},{8,12},{12,14},{14... | collective-permute-start | bytes 393224 | tf_op jit(solution)/shard_map/ppermute | solution.py:28
  9.1 2.5 %collective-permute-start.3 = (bf16[512,128]{1,0:T(8,128)(2,1)}, bf16[512,128]{1,0:T(8,128)(2,1)S(1)}, u32[]{:S(2)}, u32[]{:S(2)}) collective-permute-start(bf16[512,128]{1,0:T(8,128)(2,1)} %get-tuple-element.27), channel_id=1, source_target_pairs={{0,4},{4,6},{6,2},{2,0},{1,5},{5,7},{7,3},{3,1},{8,12},{12,14},{14... | collective-permute-start | bytes 393224 | tf_op jit(solution)/shard_map/ppermute | solution.py:28
  11.6 9.0 %collective-permute-start.5 = (bf16[512,128]{1,0:T(8,128)(2,1)}, bf16[512,128]{1,0:T(8,128)(2,1)S(1)}, u32[]{:S(2)}, u32[]{:S(2)}) collective-permute-start(bf16[512,128]{1,0:T(8,128)(2,1)} %get-tuple-element.29), channel_id=1, source_target_pairs={{0,2},{4,0},{6,4},{2,6},{1,3},{5,1},{7,5},{3,7},{8,10},{12,8},{14,... | collective-permute-start | bytes 393224 | tf_op jit(solution)/shard_map/ppermute | solution.py:28
  20.6 1.0 %copy-done = bf16[1,128,2048]{2,1,0:T(8,128)(2,1)S(1)} copy-done((bf16[1,128,2048]{2,1,0:T(8,128)(2,1)S(1)}, bf16[1,128,2048]{2,1,0:T(8,128)(2,1)}, u32[]{:S(2)}) %copy-start) | copy-done | bytes 524312
  21.7 0.9 %copy-done.1 = bf16[1,128,512]{2,1,0:T(8,128)(2,1)S(1)} copy-done((bf16[1,128,512]{2,1,0:T(8,128)(2,1)S(1)}, bf16[1,128,512]{2,1,0:T(8,128)(2,1)}, u32[]{:S(2)}) %copy-start.1) | copy-done | bytes 131096
  22.6 0.9 %copy-done.2 = bf16[512,128]{1,0:T(8,128)(2,1)S(1)} copy-done((bf16[512,128]{1,0:T(8,128)(2,1)S(1)}, bf16[512,128]{1,0:T(8,128)(2,1)}, u32[]{:S(2)}) %copy-start.2) | copy-done | bytes 131096
  23.5 0.8 copy-done.3
  24.3 1.0 %fetch.1 = (f32[128,128]{1,0:T(8,128)S(1)}, bf16[1,144,512]{2,1,0:T(8,128)(2,1)S(1)}, bf16[1,128,2048]{2,1,0:T(8,128)(2,1)S(1)}, bf16[1,128,512]{2,1,0:T(8,128)(2,1)S(1)}, bf16[512,128]{1,0:T(8,128)(2,1)S(1)}) custom-call(f32[128,128]{1,0:T(8,128)S(1)} %copy-done.3, bf16[1,144,512]{2,1,0:T(8,128)(2,1)} %get-tuple-element.20.refs_1_, ...), custom_call_target="tpu_custom_call" | custom-call | tf_op jit(solution)/shard_map/fetch/pallas_call | solution.py:224
  25.3 3.8 %collective-permute-start.7 = (bf16[1,144,512]{2,1,0:T(8,128)(2,1)}, bf16[1,144,512]{2,1,0:T(8,128)(2,1)S(1)}, u32[]{:S(2)}, u32[]{:S(2)}) collective-permute-start(bf16[1,144,512]{2,1,0:T(8,128)(2,1)} %get-tuple-element.20.refs_1_), channel_id=1, source_target_pairs={{0,2},{4,0},{6,4},{2,6},{1,3},{5,1},{7,5},{3,7},{8,10},{12,8},{14,... | collective-permute-start | bytes 442376 | tf_op jit(solution)/shard_map/ppermute | solution.py:28
  29.1 0.1 join.1.refs_6_.refs_2_
  29.2 0.1 collective-permute-start.6
  29.3 2.0 %collective-permute-start.8 = (bf16[1,128,512]{2,1,0:T(8,128)(2,1)S(1)}, bf16[1,128,512]{2,1,0:T(8,128)(2,1)S(1)}, u32[]{:S(2)}, u32[]{:S(2)}) collective-permute-start(bf16[1,128,512]{2,1,0:T(8,128)(2,1)S(1)} %collective-permute-done.2.refs_7_), channel_id=1, source_target_pairs={{0,2},{4,0},{6,4},{2,6},{1,3},{5,1},{7,5},{3,7},{8,10},{12,8},{14,... | collective-permute-start | bytes 393224 | tf_op jit(solution)/shard_map/ppermute | solution.py:28
  31.3 1.1 %collective-permute-start.15 = (bf16[512,512]{1,0:T(8,128)(2,1)S(1)}, bf16[512,512]{1,0:T(8,128)(2,1)S(1)}, u32[]{:S(2)}, u32[]{:S(2)}) collective-permute-start(bf16[512,512]{1,0:T(8,128)(2,1)S(1)} %join.1.refs_6_.refs_2_), channel_id=1, source_target_pairs={{0,16},{8,24},{16,0},{24,8},{1,17},{9,25},{17,1},{25,9},{2,18},{10... | collective-permute-start | bytes 1572872 | tf_op jit(solution)/shard_map/ppermute | solution.py:44
  32.4 3.5 %collective-permute-done.7.refs_3_ = bf16[1,144,512]{2,1,0:T(8,128)(2,1)S(1)} collective-permute-done((bf16[1,144,512]{2,1,0:T(8,128)(2,1)}, bf16[1,144,512]{2,1,0:T(8,128)(2,1)S(1)}, u32[]{:S(2)}, u32[]{:S(2)}) %collective-permute-start.7) | collective-permute-done | bytes 147488 | tf_op jit(solution)/shard_map/ppermute | solution.py:28
  35.9 1.9 %collective-permute-done.8.refs_6_ = bf16[1,128,512]{2,1,0:T(8,128)(2,1)S(1)} collective-permute-done((bf16[1,128,512]{2,1,0:T(8,128)(2,1)S(1)}, bf16[1,128,512]{2,1,0:T(8,128)(2,1)S(1)}, u32[]{:S(2)}, u32[]{:S(2)}) %collective-permute-start.8) | collective-permute-done | bytes 131104 | tf_op jit(solution)/shard_map/ppermute | solution.py:28
  37.8 1.2 %collective-permute-done.6.refs_2_ = bf16[1,144,512]{2,1,0:T(8,128)(2,1)S(1)} collective-permute-done((bf16[1,144,512]{2,1,0:T(8,128)(2,1)S(1)}, bf16[1,144,512]{2,1,0:T(8,128)(2,1)S(1)}, u32[]{:S(2)}, u32[]{:S(2)}) %collective-permute-start.6) | collective-permute-done | bytes 147488 | tf_op jit(solution)/shard_map/ppermute | solution.py:28
  39.1 1.1 %attend.3.refs_0_ = bf16[1,128,1024]{2,1,0:T(8,128)(2,1)S(1)} custom-call(f32[128,128]{1,0:T(8,128)S(1)} %get-tuple-element.22.place_ref, bf16[1,128,2048]{2,1,0:T(8,128)(2,1)S(1)} %get-tuple-element.23.query_ref, bf16[1,144,512]{2,1,0:T(8,128)(2,1)S(1)} %get-tuple-element.24.refs_0_, bf16[1,144,512]{2,1,0:T(8,128)(2,1)S(1)} %collective-permute-done.refs_1_, ...), custom_call_target="tpu_custom_call" | custom-call | tf_op jit(solution)/shard_map/attend/pallas_call | solution.py:249
  40.2 1.3 %collective-permute-start.10 = (bf16[1,128,1024]{2,1,0:T(8,128)(2,1)S(1)}, bf16[1,128,1024]{2,1,0:T(8,128)(2,1)S(1)}, u32[]{:S(2)}, u32[]{:S(2)}) collective-permute-start(bf16[1,128,1024]{2,1,0:T(8,128)(2,1)S(1)} %attend.3.refs_0_), channel_id=1, source_target_pairs={{0,16},{8,24},{16,0},{24,8},{1,17},{9,25},{17,1},{25,9},{2,18},{10... | collective-permute-start | bytes 786440 | tf_op jit(solution)/shard_map/ppermute | solution.py:44
  41.5 1.1 %attend.2.refs_0_ = bf16[1,128,1024]{2,1,0:T(8,128)(2,1)S(1)} custom-call(f32[128,128]{1,0:T(8,128)S(1)} %get-tuple-element.22.place_ref, bf16[1,128,2048]{2,1,0:T(8,128)(2,1)S(1)} %get-tuple-element.23.query_ref, bf16[1,144,512]{2,1,0:T(8,128)(2,1)S(1)} %get-tuple-element.24.refs_0_, bf16[1,144,512]{2,1,0:T(8,128)(2,1)S(1)} %collective-permute-done.refs_1_, ...), custom_call_target="tpu_custom_call" | custom-call | tf_op jit(solution)/shard_map/attend/pallas_call | solution.py:249
  42.6 0.8 collective-permute-start.20
  43.4 2.3 %collective-permute-start.19 = (bf16[1,128,1024]{2,1,0:T(8,128)(2,1)S(1)}, bf16[1,128,1024]{2,1,0:T(8,128)(2,1)S(1)}, u32[]{:S(2)}, u32[]{:S(2)}) collective-permute-start(bf16[1,128,1024]{2,1,0:T(8,128)(2,1)S(1)} %attend.2.refs_0_), channel_id=1, source_target_pairs={{0,4},{4,6},{6,2},{2,0},{1,5},{5,7},{7,3},{3,1},{8,12},{12,14},{14... | collective-permute-start | bytes 786440 | tf_op jit(solution)/shard_map/ppermute | solution.py:28
  45.7 5.2 %collective-permute-done.10.refs_3_ = bf16[1,128,1024]{2,1,0:T(8,128)(2,1)S(1)} collective-permute-done((bf16[1,128,1024]{2,1,0:T(8,128)(2,1)S(1)}, bf16[1,128,1024]{2,1,0:T(8,128)(2,1)S(1)}, u32[]{:S(2)}, u32[]{:S(2)}) %collective-permute-start.10) | collective-permute-done | bytes 262176 | tf_op jit(solution)/shard_map/ppermute | solution.py:44
  50.9 1.9 %collective-permute-start.16 = (bf16[512,512]{1,0:T(8,128)(2,1)S(1)}, bf16[512,512]{1,0:T(8,128)(2,1)S(1)}, u32[]{:S(2)}, u32[]{:S(2)}) collective-permute-start(bf16[512,512]{1,0:T(8,128)(2,1)S(1)} %join.1.refs_6_.refs_2_), channel_id=1, source_target_pairs={{0,1},{1,0},{2,3},{3,2},{4,5},{5,4},{6,7},{7,6},{8,9},{9,8},{10,11... | collective-permute-start | bytes 1572872 | tf_op jit(solution)/shard_map/ppermute | solution.py:44
  52.9 1.5 %collective-permute-start.12 = (bf16[1,128,1024]{2,1,0:T(8,128)(2,1)S(1)}, bf16[1,128,1024]{2,1,0:T(8,128)(2,1)S(1)}, u32[]{:S(2)}, u32[]{:S(2)}) collective-permute-start(bf16[1,128,1024]{2,1,0:T(8,128)(2,1)S(1)} %collective-permute-done.9.refs_1_), channel_id=1, source_target_pairs={{0,16},{8,24},{16,0},{24,8},{1,17},{9,25},{17,1},{25,9},{2,18},{10... | collective-permute-start | bytes 786440 | tf_op jit(solution)/shard_map/ppermute | solution.py:44
  54.4 2.2 %collective-permute-done.20.refs_3_ = bf16[1,128,1024]{2,1,0:T(8,128)(2,1)S(1)} collective-permute-done((bf16[1,128,1024]{2,1,0:T(8,128)(2,1)S(1)}, bf16[1,128,1024]{2,1,0:T(8,128)(2,1)S(1)}, u32[]{:S(2)}, u32[]{:S(2)}) %collective-permute-start.20) | collective-permute-done | bytes 262176 | tf_op jit(solution)/shard_map/ppermute | solution.py:44
  56.5 1.8 %collective-permute-start.11 = (bf16[1,128,1024]{2,1,0:T(8,128)(2,1)S(1)}, bf16[1,128,1024]{2,1,0:T(8,128)(2,1)S(1)}, u32[]{:S(2)}, u32[]{:S(2)}) collective-permute-start(bf16[1,128,1024]{2,1,0:T(8,128)(2,1)S(1)} %collective-permute-done.9.refs_1_), channel_id=1, source_target_pairs={{0,4},{4,6},{6,2},{2,0},{1,5},{5,7},{7,3},{3,1},{8,12},{12,14},{14... | collective-permute-start | bytes 786440 | tf_op jit(solution)/shard_map/ppermute | solution.py:28
  58.4 0.0 collective-permute-start.21
  58.4 1.1 %collective-permute-start.17 = (bf16[512,512]{1,0:T(8,128)(2,1)S(1)}, bf16[512,512]{1,0:T(8,128)(2,1)S(1)}, u32[]{:S(2)}, u32[]{:S(2)}) collective-permute-start(bf16[512,512]{1,0:T(8,128)(2,1)S(1)} %collective-permute-done.15.refs_7_.refs_3_), channel_id=1, source_target_pairs={{0,1},{1,0},{2,3},{3,2},{4,5},{5,4},{6,7},{7,6},{8,9},{9,8},{10,11... | collective-permute-start | bytes 1572872 | tf_op jit(solution)/shard_map/ppermute | solution.py:44
  59.5 1.4 %collective-permute-done.12.refs_4_ = bf16[1,128,1024]{2,1,0:T(8,128)(2,1)S(1)} collective-permute-done((bf16[1,128,1024]{2,1,0:T(8,128)(2,1)S(1)}, bf16[1,128,1024]{2,1,0:T(8,128)(2,1)S(1)}, u32[]{:S(2)}, u32[]{:S(2)}) %collective-permute-start.12) | collective-permute-done | bytes 262176 | tf_op jit(solution)/shard_map/ppermute | solution.py:44
  60.9 1.5 %collective-permute-start.25 = (bf16[1,128,1024]{2,1,0:T(8,128)(2,1)S(1)}, bf16[1,128,1024]{2,1,0:T(8,128)(2,1)S(1)}, u32[]{:S(2)}, u32[]{:S(2)}) collective-permute-start(bf16[1,128,1024]{2,1,0:T(8,128)(2,1)S(1)} %collective-permute-done.19.refs_1_), channel_id=1, source_target_pairs={{0,16},{8,24},{16,0},{24,8},{1,17},{9,25},{17,1},{25,9},{2,18},{10... | collective-permute-start | bytes 786440 | tf_op jit(solution)/shard_map/ppermute | solution.py:44
  62.4 2.7 %collective-permute-done.11.refs_2_ = bf16[1,128,1024]{2,1,0:T(8,128)(2,1)S(1)} collective-permute-done((bf16[1,128,1024]{2,1,0:T(8,128)(2,1)S(1)}, bf16[1,128,1024]{2,1,0:T(8,128)(2,1)S(1)}, u32[]{:S(2)}, u32[]{:S(2)}) %collective-permute-start.11) | collective-permute-done | bytes 262176 | tf_op jit(solution)/shard_map/ppermute | solution.py:28
  65.1 3.5 %collective-permute-done.21.refs_2_ = bf16[1,128,1024]{2,1,0:T(8,128)(2,1)S(1)} collective-permute-done((bf16[1,128,1024]{2,1,0:T(8,128)(2,1)S(1)}, bf16[1,128,1024]{2,1,0:T(8,128)(2,1)S(1)}, u32[]{:S(2)}, u32[]{:S(2)}) %collective-permute-start.21) | collective-permute-done | bytes 262176 | tf_op jit(solution)/shard_map/ppermute | solution.py:28
  68.6 0.4 collective-permute-start.23
  69.0 2.5 %collective-permute-start.13 = (bf16[1,128,1024]{2,1,0:T(8,128)(2,1)S(1)}, bf16[1,128,1024]{2,1,0:T(8,128)(2,1)S(1)}, u32[]{:S(2)}, u32[]{:S(2)}) collective-permute-start(bf16[1,128,1024]{2,1,0:T(8,128)(2,1)S(1)} %collective-permute-done.11.refs_2_), channel_id=1, source_target_pairs={{0,4},{4,6},{6,2},{2,0},{1,5},{5,7},{7,3},{3,1},{8,12},{12,14},{14... | collective-permute-start | bytes 786440 | tf_op jit(solution)/shard_map/ppermute | solution.py:28
  71.6 0.0 collective-permute-start.18
  71.6 0.8 pad_maximum_fusion
  72.4 0.1 collective-permute-start.22
  72.5 5.4 %collective-permute-done.23.refs_5_ = bf16[1,128,1024]{2,1,0:T(8,128)(2,1)S(1)} collective-permute-done((bf16[1,128,1024]{2,1,0:T(8,128)(2,1)S(1)}, bf16[1,128,1024]{2,1,0:T(8,128)(2,1)S(1)}, u32[]{:S(2)}, u32[]{:S(2)}) %collective-permute-start.23) | collective-permute-done | bytes 262176 | tf_op jit(solution)/shard_map/ppermute | solution.py:44
  77.9 0.4 collective-permute-start.24
  78.3 2.5 %collective-permute-start.14 = (bf16[1,128,1024]{2,1,0:T(8,128)(2,1)S(1)}, bf16[1,128,1024]{2,1,0:T(8,128)(2,1)S(1)}, u32[]{:S(2)}, u32[]{:S(2)}) collective-permute-start(bf16[1,128,1024]{2,1,0:T(8,128)(2,1)S(1)} %collective-permute-done.13.refs_0_), channel_id=1, source_target_pairs={{0,16},{8,24},{16,0},{24,8},{1,17},{9,25},{17,1},{25,9},{2,18},{10... | collective-permute-start | bytes 786440 | tf_op jit(solution)/shard_map/ppermute | solution.py:44
  80.8 1.8 %early.3.refs_6_ = f32[1024,1024]{1,0:T(8,128)S(1)} custom-call(bf16[1,128,1024]{2,1,0:T(8,128)(2,1)S(1)} %attend.2.refs_0_, bf16[1,128,1024]{2,1,0:T(8,128)(2,1)S(1)} %collective-permute-done.19.refs_1_, bf16[1,128,1024]{2,1,0:T(8,128)(2,1)S(1)} %collective-permute-done.21.refs_2_, bf16[1,128,1024]{2,1,0:T(8,128)(2,1)S(1)} %collective-permute-done.20.refs_3_, ...), custom_call_target="tpu_custom_call" | custom-call | flops 1610612736 | bytes 8388608 | tf_op jit(solution)/shard_map/early/pallas_call | solution.py:286
  82.6 1.8 %early.2.refs_6_ = f32[1024,1024]{1,0:T(8,128)S(1)} custom-call(bf16[1,128,1024]{2,1,0:T(8,128)(2,1)S(1)} %attend.3.refs_0_, bf16[1,128,1024]{2,1,0:T(8,128)(2,1)S(1)} %collective-permute-done.9.refs_1_, bf16[1,128,1024]{2,1,0:T(8,128)(2,1)S(1)} %collective-permute-done.11.refs_2_, bf16[1,128,1024]{2,1,0:T(8,128)(2,1)S(1)} %collective-permute-done.10.refs_3_, ...), custom_call_target="tpu_custom_call" | custom-call | flops 1610612736 | bytes 8388608 | tf_op jit(solution)/shard_map/early/pallas_call | solution.py:286
  84.4 0.3 collective-permute-done.24.refs_1_
  84.8 1.6 %finish.2.refs_7_ = bf16[1,1024,2048]{2,1,0:T(8,128)(2,1)} custom-call(bf16[1,128,1024]{2,1,0:T(8,128)(2,1)S(1)} %collective-permute-done.22.refs_0_, bf16[1,128,1024]{2,1,0:T(8,128)(2,1)S(1)} %collective-permute-done.24.refs_1_, bf16[512,512]{1,0:T(8,128)(2,1)S(1)} %join.1.refs_6_.refs_2_, bf16[512,512]{1,0:T(8,128)(2,1)S(1)} %collective-permute-done.15.refs_7_.refs_3_, ...), custom_call_target="tpu_custom_call" | custom-call | flops 536870912 | bytes 8388608 | tf_op jit(solution)/shard_map/finish/pallas_call | solution.py:311
  86.4 1.7 %finish.3 = bf16[1,1024,2048]{2,1,0:T(8,128)(2,1)} custom-call(bf16[1,128,1024]{2,1,0:T(8,128)(2,1)S(1)} %collective-permute-done.13.refs_0_, bf16[1,128,1024]{2,1,0:T(8,128)(2,1)S(1)} %collective-permute-done.14.refs_1_, bf16[512,512]{1,0:T(8,128)(2,1)S(1)} %join.1.refs_6_.refs_2_, ...), custom_call_target="tpu_custom_call", output_to_operand_aliasing={{}: (7, {})} | custom-call | flops 536870912 | bytes 8388608 | tf_op jit(solution)/shard_map/finish/pallas_call | solution.py:311
  (22 shorter events, 0.1 us)
Async XLA Ops:
  0.6 10.9 %collective-permute-start.2 = (bf16[1,128,512]{2,1,0:T(8,128)(2,1)}, bf16[1,128,512]{2,1,0:T(8,128)(2,1)S(1)}, u32[]{:S(2)}, u32[]{:S(2)}) collective-permute-start(bf16[1,128,512]{2,1,0:T(8,128)(2,1)} %refs_3_.1), channel_id=1, source_target_pairs={{0,2},{4,0},{6,4},{2,6},{1,3},{5,1},{7,5},{3,7},{8,10},{12,8},{14,... | collective-permute-start | bytes 393224 | tf_op jit(solution)/shard_map/ppermute | solution.py:28
  6.0 23.2 %collective-permute-start = (bf16[1,144,512]{2,1,0:T(8,128)(2,1)}, bf16[1,144,512]{2,1,0:T(8,128)(2,1)S(1)}, u32[]{:S(2)}, u32[]{:S(2)}) collective-permute-start(bf16[1,144,512]{2,1,0:T(8,128)(2,1)} %get-tuple-element.20.refs_1_), channel_id=1, source_target_pairs={{0,4},{4,6},{6,2},{2,0},{1,5},{5,7},{7,3},{3,1},{8,12},{12,14},{14... | collective-permute-start | bytes 442376 | tf_op jit(solution)/shard_map/ppermute | solution.py:28
  7.1 18.2 %collective-permute-start.1 = (bf16[1,128,512]{2,1,0:T(8,128)(2,1)}, bf16[1,128,512]{2,1,0:T(8,128)(2,1)S(1)}, u32[]{:S(2)}, u32[]{:S(2)}) collective-permute-start(bf16[1,128,512]{2,1,0:T(8,128)(2,1)} %refs_3_.1), channel_id=1, source_target_pairs={{0,4},{4,6},{6,2},{2,0},{1,5},{5,7},{7,3},{3,1},{8,12},{12,14},{14... | collective-permute-start | bytes 393224 | tf_op jit(solution)/shard_map/ppermute | solution.py:28
  9.1 20.0 %collective-permute-start.3 = (bf16[512,128]{1,0:T(8,128)(2,1)}, bf16[512,128]{1,0:T(8,128)(2,1)S(1)}, u32[]{:S(2)}, u32[]{:S(2)}) collective-permute-start(bf16[512,128]{1,0:T(8,128)(2,1)} %get-tuple-element.27), channel_id=1, source_target_pairs={{0,4},{4,6},{6,2},{2,0},{1,5},{5,7},{7,3},{3,1},{8,12},{12,14},{14... | collective-permute-start | bytes 393224 | tf_op jit(solution)/shard_map/ppermute | solution.py:28
  11.6 17.6 %collective-permute-start.4 = (bf16[512,128]{1,0:T(8,128)(2,1)}, bf16[512,128]{1,0:T(8,128)(2,1)S(1)}, u32[]{:S(2)}, u32[]{:S(2)}) collective-permute-start(bf16[512,128]{1,0:T(8,128)(2,1)} %get-tuple-element.28), channel_id=1, source_target_pairs={{0,6},{4,2},{6,0},{2,4},{1,7},{5,3},{7,1},{3,5},{8,14},{12,10},{14... | collective-permute-start | bytes 393224 | tf_op jit(solution)/shard_map/ppermute | solution.py:28
  11.6 17.6 %collective-permute-start.5 = (bf16[512,128]{1,0:T(8,128)(2,1)}, bf16[512,128]{1,0:T(8,128)(2,1)S(1)}, u32[]{:S(2)}, u32[]{:S(2)}) collective-permute-start(bf16[512,128]{1,0:T(8,128)(2,1)} %get-tuple-element.29), channel_id=1, source_target_pairs={{0,2},{4,0},{6,4},{2,6},{1,3},{5,1},{7,5},{3,7},{8,10},{12,8},{14,... | collective-permute-start | bytes 393224 | tf_op jit(solution)/shard_map/ppermute | solution.py:28
  20.6 1.0 %copy-start = (bf16[1,128,2048]{2,1,0:T(8,128)(2,1)S(1)}, bf16[1,128,2048]{2,1,0:T(8,128)(2,1)}, u32[]{:S(2)}) copy-start(bf16[1,128,2048]{2,1,0:T(8,128)(2,1)} %refs_2_.1) | copy-start | bytes 1572868
  21.7 0.9 %copy-start.1 = (bf16[1,128,512]{2,1,0:T(8,128)(2,1)S(1)}, bf16[1,128,512]{2,1,0:T(8,128)(2,1)}, u32[]{:S(2)}) copy-start(bf16[1,128,512]{2,1,0:T(8,128)(2,1)} %refs_3_.1) | copy-start | bytes 393220
  22.6 0.9 %copy-start.2 = (bf16[512,128]{1,0:T(8,128)(2,1)S(1)}, bf16[512,128]{1,0:T(8,128)(2,1)}, u32[]{:S(2)}) copy-start(bf16[512,128]{1,0:T(8,128)(2,1)} %get-tuple-element.21.refs_4_) | copy-start | bytes 393220
  23.5 0.8 copy-start.3
  25.3 10.6 %collective-permute-start.7 = (bf16[1,144,512]{2,1,0:T(8,128)(2,1)}, bf16[1,144,512]{2,1,0:T(8,128)(2,1)S(1)}, u32[]{:S(2)}, u32[]{:S(2)}) collective-permute-start(bf16[1,144,512]{2,1,0:T(8,128)(2,1)} %get-tuple-element.20.refs_1_), channel_id=1, source_target_pairs={{0,2},{4,0},{6,4},{2,6},{1,3},{5,1},{7,5},{3,7},{8,10},{12,8},{14,... | collective-permute-start | bytes 442376 | tf_op jit(solution)/shard_map/ppermute | solution.py:28
  29.2 9.8 %collective-permute-start.6 = (bf16[1,144,512]{2,1,0:T(8,128)(2,1)S(1)}, bf16[1,144,512]{2,1,0:T(8,128)(2,1)S(1)}, u32[]{:S(2)}, u32[]{:S(2)}) collective-permute-start(bf16[1,144,512]{2,1,0:T(8,128)(2,1)S(1)} %collective-permute-done.refs_1_), channel_id=1, source_target_pairs={{0,4},{4,6},{6,2},{2,0},{1,5},{5,7},{7,3},{3,1},{8,12},{12,14},{14... | collective-permute-start | bytes 442376 | tf_op jit(solution)/shard_map/ppermute | solution.py:28
  29.3 8.5 %collective-permute-start.8 = (bf16[1,128,512]{2,1,0:T(8,128)(2,1)S(1)}, bf16[1,128,512]{2,1,0:T(8,128)(2,1)S(1)}, u32[]{:S(2)}, u32[]{:S(2)}) collective-permute-start(bf16[1,128,512]{2,1,0:T(8,128)(2,1)S(1)} %collective-permute-done.2.refs_7_), channel_id=1, source_target_pairs={{0,2},{4,0},{6,4},{2,6},{1,3},{5,1},{7,5},{3,7},{8,10},{12,8},{14,... | collective-permute-start | bytes 393224 | tf_op jit(solution)/shard_map/ppermute | solution.py:28
  31.3 27.1 %collective-permute-start.15 = (bf16[512,512]{1,0:T(8,128)(2,1)S(1)}, bf16[512,512]{1,0:T(8,128)(2,1)S(1)}, u32[]{:S(2)}, u32[]{:S(2)}) collective-permute-start(bf16[512,512]{1,0:T(8,128)(2,1)S(1)} %join.1.refs_6_.refs_2_), channel_id=1, source_target_pairs={{0,16},{8,24},{16,0},{24,8},{1,17},{9,25},{17,1},{25,9},{2,18},{10... | collective-permute-start | bytes 1572872 | tf_op jit(solution)/shard_map/ppermute | solution.py:44
  40.2 10.8 %collective-permute-start.10 = (bf16[1,128,1024]{2,1,0:T(8,128)(2,1)S(1)}, bf16[1,128,1024]{2,1,0:T(8,128)(2,1)S(1)}, u32[]{:S(2)}, u32[]{:S(2)}) collective-permute-start(bf16[1,128,1024]{2,1,0:T(8,128)(2,1)S(1)} %attend.3.refs_0_), channel_id=1, source_target_pairs={{0,16},{8,24},{16,0},{24,8},{1,17},{9,25},{17,1},{25,9},{2,18},{10... | collective-permute-start | bytes 786440 | tf_op jit(solution)/shard_map/ppermute | solution.py:44
  41.5 11.4 %collective-permute-start.9 = (bf16[1,128,1024]{2,1,0:T(8,128)(2,1)S(1)}, bf16[1,128,1024]{2,1,0:T(8,128)(2,1)S(1)}, u32[]{:S(2)}, u32[]{:S(2)}) collective-permute-start(bf16[1,128,1024]{2,1,0:T(8,128)(2,1)S(1)} %attend.3.refs_0_), channel_id=1, source_target_pairs={{0,4},{4,6},{6,2},{2,0},{1,5},{5,7},{7,3},{3,1},{8,12},{12,14},{14... | collective-permute-start | bytes 786440 | tf_op jit(solution)/shard_map/ppermute | solution.py:28
  42.6 14.0 %collective-permute-start.20 = (bf16[1,128,1024]{2,1,0:T(8,128)(2,1)S(1)}, bf16[1,128,1024]{2,1,0:T(8,128)(2,1)S(1)}, u32[]{:S(2)}, u32[]{:S(2)}) collective-permute-start(bf16[1,128,1024]{2,1,0:T(8,128)(2,1)S(1)} %attend.2.refs_0_), channel_id=1, source_target_pairs={{0,16},{8,24},{16,0},{24,8},{1,17},{9,25},{17,1},{25,9},{2,18},{10... | collective-permute-start | bytes 786440 | tf_op jit(solution)/shard_map/ppermute | solution.py:44
  43.4 15.0 %collective-permute-start.19 = (bf16[1,128,1024]{2,1,0:T(8,128)(2,1)S(1)}, bf16[1,128,1024]{2,1,0:T(8,128)(2,1)S(1)}, u32[]{:S(2)}, u32[]{:S(2)}) collective-permute-start(bf16[1,128,1024]{2,1,0:T(8,128)(2,1)S(1)} %attend.2.refs_0_), channel_id=1, source_target_pairs={{0,4},{4,6},{6,2},{2,0},{1,5},{5,7},{7,3},{3,1},{8,12},{12,14},{14... | collective-permute-start | bytes 786440 | tf_op jit(solution)/shard_map/ppermute | solution.py:28
  50.9 20.6 %collective-permute-start.16 = (bf16[512,512]{1,0:T(8,128)(2,1)S(1)}, bf16[512,512]{1,0:T(8,128)(2,1)S(1)}, u32[]{:S(2)}, u32[]{:S(2)}) collective-permute-start(bf16[512,512]{1,0:T(8,128)(2,1)S(1)} %join.1.refs_6_.refs_2_), channel_id=1, source_target_pairs={{0,1},{1,0},{2,3},{3,2},{4,5},{5,4},{6,7},{7,6},{8,9},{9,8},{10,11... | collective-permute-start | bytes 1572872 | tf_op jit(solution)/shard_map/ppermute | solution.py:44
  52.9 8.0 %collective-permute-start.12 = (bf16[1,128,1024]{2,1,0:T(8,128)(2,1)S(1)}, bf16[1,128,1024]{2,1,0:T(8,128)(2,1)S(1)}, u32[]{:S(2)}, u32[]{:S(2)}) collective-permute-start(bf16[1,128,1024]{2,1,0:T(8,128)(2,1)S(1)} %collective-permute-done.9.refs_1_), channel_id=1, source_target_pairs={{0,16},{8,24},{16,0},{24,8},{1,17},{9,25},{17,1},{25,9},{2,18},{10... | collective-permute-start | bytes 786440 | tf_op jit(solution)/shard_map/ppermute | solution.py:44
  56.5 8.5 %collective-permute-start.11 = (bf16[1,128,1024]{2,1,0:T(8,128)(2,1)S(1)}, bf16[1,128,1024]{2,1,0:T(8,128)(2,1)S(1)}, u32[]{:S(2)}, u32[]{:S(2)}) collective-permute-start(bf16[1,128,1024]{2,1,0:T(8,128)(2,1)S(1)} %collective-permute-done.9.refs_1_), channel_id=1, source_target_pairs={{0,4},{4,6},{6,2},{2,0},{1,5},{5,7},{7,3},{3,1},{8,12},{12,14},{14... | collective-permute-start | bytes 786440 | tf_op jit(solution)/shard_map/ppermute | solution.py:28
  58.4 10.2 %collective-permute-start.21 = (bf16[1,128,1024]{2,1,0:T(8,128)(2,1)S(1)}, bf16[1,128,1024]{2,1,0:T(8,128)(2,1)S(1)}, u32[]{:S(2)}, u32[]{:S(2)}) collective-permute-start(bf16[1,128,1024]{2,1,0:T(8,128)(2,1)S(1)} %collective-permute-done.19.refs_1_), channel_id=1, source_target_pairs={{0,4},{4,6},{6,2},{2,0},{1,5},{5,7},{7,3},{3,1},{8,12},{12,14},{14... | collective-permute-start | bytes 786440 | tf_op jit(solution)/shard_map/ppermute | solution.py:28
  58.4 22.4 %collective-permute-start.17 = (bf16[512,512]{1,0:T(8,128)(2,1)S(1)}, bf16[512,512]{1,0:T(8,128)(2,1)S(1)}, u32[]{:S(2)}, u32[]{:S(2)}) collective-permute-start(bf16[512,512]{1,0:T(8,128)(2,1)S(1)} %collective-permute-done.15.refs_7_.refs_3_), channel_id=1, source_target_pairs={{0,1},{1,0},{2,3},{3,2},{4,5},{5,4},{6,7},{7,6},{8,9},{9,8},{10,11... | collective-permute-start | bytes 1572872 | tf_op jit(solution)/shard_map/ppermute | solution.py:44
  60.9 11.5 %collective-permute-start.25 = (bf16[1,128,1024]{2,1,0:T(8,128)(2,1)S(1)}, bf16[1,128,1024]{2,1,0:T(8,128)(2,1)S(1)}, u32[]{:S(2)}, u32[]{:S(2)}) collective-permute-start(bf16[1,128,1024]{2,1,0:T(8,128)(2,1)S(1)} %collective-permute-done.19.refs_1_), channel_id=1, source_target_pairs={{0,16},{8,24},{16,0},{24,8},{1,17},{9,25},{17,1},{25,9},{2,18},{10... | collective-permute-start | bytes 786440 | tf_op jit(solution)/shard_map/ppermute | solution.py:44
  68.6 9.2 %collective-permute-start.23 = (bf16[1,128,1024]{2,1,0:T(8,128)(2,1)S(1)}, bf16[1,128,1024]{2,1,0:T(8,128)(2,1)S(1)}, u32[]{:S(2)}, u32[]{:S(2)}) collective-permute-start(bf16[1,128,1024]{2,1,0:T(8,128)(2,1)S(1)} %collective-permute-done.21.refs_2_), channel_id=1, source_target_pairs={{0,16},{8,24},{16,0},{24,8},{1,17},{9,25},{17,1},{25,9},{2,18},{10... | collective-permute-start | bytes 786440 | tf_op jit(solution)/shard_map/ppermute | solution.py:44
  69.0 9.3 %collective-permute-start.13 = (bf16[1,128,1024]{2,1,0:T(8,128)(2,1)S(1)}, bf16[1,128,1024]{2,1,0:T(8,128)(2,1)S(1)}, u32[]{:S(2)}, u32[]{:S(2)}) collective-permute-start(bf16[1,128,1024]{2,1,0:T(8,128)(2,1)S(1)} %collective-permute-done.11.refs_2_), channel_id=1, source_target_pairs={{0,4},{4,6},{6,2},{2,0},{1,5},{5,7},{7,3},{3,1},{8,12},{12,14},{14... | collective-permute-start | bytes 786440 | tf_op jit(solution)/shard_map/ppermute | solution.py:28
  71.6 11.1 %collective-permute-start.18 = (bf16[1,128,1024]{2,1,0:T(8,128)(2,1)S(1)}, bf16[1,128,1024]{2,1,0:T(8,128)(2,1)S(1)}, u32[]{:S(2)}, u32[]{:S(2)}) collective-permute-start(bf16[1,128,1024]{2,1,0:T(8,128)(2,1)S(1)} %collective-permute-done.11.refs_2_), channel_id=1, source_target_pairs={{0,16},{8,24},{16,0},{24,8},{1,17},{9,25},{17,1},{25,9},{2,18},{10... | collective-permute-start | bytes 786440 | tf_op jit(solution)/shard_map/ppermute | solution.py:44
  72.4 12.0 %collective-permute-start.22 = (bf16[1,128,1024]{2,1,0:T(8,128)(2,1)S(1)}, bf16[1,128,1024]{2,1,0:T(8,128)(2,1)S(1)}, u32[]{:S(2)}, u32[]{:S(2)}) collective-permute-start(bf16[1,128,1024]{2,1,0:T(8,128)(2,1)S(1)} %collective-permute-done.21.refs_2_), channel_id=1, source_target_pairs={{0,4},{4,6},{6,2},{2,0},{1,5},{5,7},{7,3},{3,1},{8,12},{12,14},{14... | collective-permute-start | bytes 786440 | tf_op jit(solution)/shard_map/ppermute | solution.py:28
  77.9 6.9 %collective-permute-start.24 = (bf16[1,128,1024]{2,1,0:T(8,128)(2,1)S(1)}, bf16[1,128,1024]{2,1,0:T(8,128)(2,1)S(1)}, u32[]{:S(2)}, u32[]{:S(2)}) collective-permute-start(bf16[1,128,1024]{2,1,0:T(8,128)(2,1)S(1)} %collective-permute-done.23.refs_5_), channel_id=1, source_target_pairs={{0,4},{4,6},{6,2},{2,0},{1,5},{5,7},{7,3},{3,1},{8,12},{12,14},{14... | collective-permute-start | bytes 786440 | tf_op jit(solution)/shard_map/ppermute | solution.py:28
  78.3 8.1 %collective-permute-start.14 = (bf16[1,128,1024]{2,1,0:T(8,128)(2,1)S(1)}, bf16[1,128,1024]{2,1,0:T(8,128)(2,1)S(1)}, u32[]{:S(2)}, u32[]{:S(2)}) collective-permute-start(bf16[1,128,1024]{2,1,0:T(8,128)(2,1)S(1)} %collective-permute-done.13.refs_0_), channel_id=1, source_target_pairs={{0,16},{8,24},{16,0},{24,8},{1,17},{9,25},{17,1},{25,9},{2,18},{10... | collective-permute-start | bytes 786440 | tf_op jit(solution)/shard_map/ppermute | solution.py:44

commit v15 on v13

--- a/solution.py
+++ b/solution.py
@@ -299,7 +299,7 @@
         for c in range(parts)
     ]
     grad_out = None
-    for c in range(parts):
+    for c in reversed(range(parts)):
         slots = [n - 1]
         operands = attended(c, slots) + cots + [totals[c]]
         specs = [VMEM] * len(operands)

time: 88.4 us -> 87 us (0.984)
  waiting for transfers between devices: 24.9 us -> 23.5 us
    ppermute x16, waiting for transfers between devices: 11.1 us -> 8.93 us  [around(): lax.ppermute(x, 'ctx', [(order[q], order[(q + shift) % n]) for q in range...]
where the time goes in v15:
time: 87 us; the launch traced here: 86.7 us
  starting transfers between devices  45.6 us (52%)
  waiting for transfers between devices  23.5 us (27%)
  Pallas kernels  12.4 us (14%)
  local copies, waits for them, and re-layouts  3.69 us (4%)
    ppermute x16, starting transfers between devices, around(): lax.ppermute(x, 'ctx', [(order[q], order[(q + shift) % n]) for q in range...  31 us
    ppermute x10, waiting for transfers between devices, swap(): lax.ppermute(x, axis, [(i, i ^ mask) for i in range(lax.axis_size(axis))])  14.5 us
    ppermute x10, starting transfers between devices, swap(): lax.ppermute(x, axis, [(i, i ^ mask) for i in range(lax.axis_size(axis))])  14.5 us
    ppermute x16, waiting for transfers between devices, around(): lax.ppermute(x, 'ctx', [(order[q], order[(q + shift) % n]) for q in range...  8.93 us
    unnamed x8, local copies, waits for them, and re-layouts  3.69 us
    pallas_call x2, Pallas kernels, local(): pl.pallas_call(functools.partial(early_kernel, first_slots), out_shape=ja...  3.6 us
    pallas_call x2, Pallas kernels, local(): pl.pallas_call(functools.partial(finish_kernel, slots, c * chunk), out_sh...  3.31 us
    pallas_call x1, Pallas kernels, local(): pl.pallas_call(functools.partial(prepare_kernel, n), out_shape=[jax.Shape...  2.29 us
  transfers between devices with their start and end apart: 26, of which 12 were waited for; matrix products, arithmetic and copies ran while one was open for 1% of the time, Pallas kernels for 12%

profile of v15, /device:TPU:0, one launch (start us, length us, event | category | flops | bytes accessed | tf_op | source)
XLA Modules:
  0.0 86.7 jit_solution(15029353561203305481)
XLA Ops:
  0.6 3.1 %collective-permute-start.2 = (bf16[1,128,512]{2,1,0:T(8,128)(2,1)}, bf16[1,128,512]{2,1,0:T(8,128)(2,1)S(1)}, u32[]{:S(2)}, u32[]{:S(2)}) collective-permute-start(bf16[1,128,512]{2,1,0:T(8,128)(2,1)} %refs_3_.1), channel_id=1, source_target_pairs={{0,2},{4,0},{6,4},{2,6},{1,3},{5,1},{7,5},{3,7},{8,10},{12,8},{14,... | collective-permute-start | bytes 393224 | tf_op jit(solution)/shard_map/ppermute | solution.py:28
  3.7 2.3 %prepare.1 = (bf16[1,144,512]{2,1,0:T(8,128)(2,1)}, f32[128,128]{1,0:T(8,128)}, bf16[512,128]{1,0:T(8,128)(2,1)}, bf16[512,128]{1,0:T(8,128)(2,1)}, bf16[512,128]{1,0:T(8,128)(2,1)}, /*index=5*/bf16[512,128]{1,0:T(8,128)(2,1)}) custom-call(s32[1,2]{1,0:T(1,128)} %span_source.1, bf16[1,128,512]{2,1,0:T(8,128)(2,1)} %key_ref.1, bf16[1,128,4096]{2,1,0:T(8,128)(2,1)} %cot_source.1), custom_call_target="tpu_custom_call" | custom-call | tf_op jit(solution)/shard_map/prepare/pallas_call | solution.py:206
  6.0 1.1 %collective-permute-start = (bf16[1,144,512]{2,1,0:T(8,128)(2,1)}, bf16[1,144,512]{2,1,0:T(8,128)(2,1)S(1)}, u32[]{:S(2)}, u32[]{:S(2)}) collective-permute-start(bf16[1,144,512]{2,1,0:T(8,128)(2,1)} %get-tuple-element.21.refs_1_), channel_id=1, source_target_pairs={{0,4},{4,6},{6,2},{2,0},{1,5},{5,7},{7,3},{3,1},{8,12},{12,14},{14... | collective-permute-start | bytes 442376 | tf_op jit(solution)/shard_map/ppermute | solution.py:28
  7.1 2.0 %collective-permute-start.1 = (bf16[1,128,512]{2,1,0:T(8,128)(2,1)}, bf16[1,128,512]{2,1,0:T(8,128)(2,1)S(1)}, u32[]{:S(2)}, u32[]{:S(2)}) collective-permute-start(bf16[1,128,512]{2,1,0:T(8,128)(2,1)} %refs_3_.1), channel_id=1, source_target_pairs={{0,4},{4,6},{6,2},{2,0},{1,5},{5,7},{7,3},{3,1},{8,12},{12,14},{14... | collective-permute-start | bytes 393224 | tf_op jit(solution)/shard_map/ppermute | solution.py:28
  9.1 2.5 %collective-permute-start.3 = (bf16[512,128]{1,0:T(8,128)(2,1)}, bf16[512,128]{1,0:T(8,128)(2,1)S(1)}, u32[]{:S(2)}, u32[]{:S(2)}) collective-permute-start(bf16[512,128]{1,0:T(8,128)(2,1)} %get-tuple-element.28), channel_id=1, source_target_pairs={{0,4},{4,6},{6,2},{2,0},{1,5},{5,7},{7,3},{3,1},{8,12},{12,14},{14... | collective-permute-start | bytes 393224 | tf_op jit(solution)/shard_map/ppermute | solution.py:28
  11.6 9.0 %collective-permute-start.5 = (bf16[512,128]{1,0:T(8,128)(2,1)}, bf16[512,128]{1,0:T(8,128)(2,1)S(1)}, u32[]{:S(2)}, u32[]{:S(2)}) collective-permute-start(bf16[512,128]{1,0:T(8,128)(2,1)} %get-tuple-element.30), channel_id=1, source_target_pairs={{0,2},{4,0},{6,4},{2,6},{1,3},{5,1},{7,5},{3,7},{8,10},{12,8},{14,... | collective-permute-start | bytes 393224 | tf_op jit(solution)/shard_map/ppermute | solution.py:28
  20.6 1.0 %copy-done = bf16[1,128,2048]{2,1,0:T(8,128)(2,1)S(1)} copy-done((bf16[1,128,2048]{2,1,0:T(8,128)(2,1)S(1)}, bf16[1,128,2048]{2,1,0:T(8,128)(2,1)}, u32[]{:S(2)}) %copy-start) | copy-done | bytes 524312
  21.7 0.9 %copy-done.1 = bf16[1,128,512]{2,1,0:T(8,128)(2,1)S(1)} copy-done((bf16[1,128,512]{2,1,0:T(8,128)(2,1)S(1)}, bf16[1,128,512]{2,1,0:T(8,128)(2,1)}, u32[]{:S(2)}) %copy-start.1) | copy-done | bytes 131096
  22.6 0.9 %copy-done.2 = bf16[512,128]{1,0:T(8,128)(2,1)S(1)} copy-done((bf16[512,128]{1,0:T(8,128)(2,1)S(1)}, bf16[512,128]{1,0:T(8,128)(2,1)}, u32[]{:S(2)}) %copy-start.2) | copy-done | bytes 131096
  23.5 0.8 copy-done.3
  24.3 1.0 %fetch.1 = (f32[128,128]{1,0:T(8,128)S(1)}, bf16[1,144,512]{2,1,0:T(8,128)(2,1)S(1)}, bf16[1,128,2048]{2,1,0:T(8,128)(2,1)S(1)}, bf16[1,128,512]{2,1,0:T(8,128)(2,1)S(1)}, bf16[512,128]{1,0:T(8,128)(2,1)S(1)}) custom-call(f32[128,128]{1,0:T(8,128)S(1)} %copy-done.3, bf16[1,144,512]{2,1,0:T(8,128)(2,1)} %get-tuple-element.21.refs_1_, ...), custom_call_target="tpu_custom_call" | custom-call | tf_op jit(solution)/shard_map/fetch/pallas_call | solution.py:224
  25.3 3.8 %collective-permute-start.7 = (bf16[1,144,512]{2,1,0:T(8,128)(2,1)}, bf16[1,144,512]{2,1,0:T(8,128)(2,1)S(1)}, u32[]{:S(2)}, u32[]{:S(2)}) collective-permute-start(bf16[1,144,512]{2,1,0:T(8,128)(2,1)} %get-tuple-element.21.refs_1_), channel_id=1, source_target_pairs={{0,2},{4,0},{6,4},{2,6},{1,3},{5,1},{7,5},{3,7},{8,10},{12,8},{14,... | collective-permute-start | bytes 442376 | tf_op jit(solution)/shard_map/ppermute | solution.py:28
  29.1 0.1 join.1.refs_6_.refs_2_
  29.2 0.1 collective-permute-start.6
  29.3 2.0 %collective-permute-start.8 = (bf16[1,128,512]{2,1,0:T(8,128)(2,1)S(1)}, bf16[1,128,512]{2,1,0:T(8,128)(2,1)S(1)}, u32[]{:S(2)}, u32[]{:S(2)}) collective-permute-start(bf16[1,128,512]{2,1,0:T(8,128)(2,1)S(1)} %collective-permute-done.2.refs_7_), channel_id=1, source_target_pairs={{0,2},{4,0},{6,4},{2,6},{1,3},{5,1},{7,5},{3,7},{8,10},{12,8},{14,... | collective-permute-start | bytes 393224 | tf_op jit(solution)/shard_map/ppermute | solution.py:28
  31.3 1.1 %collective-permute-start.16 = (bf16[512,512]{1,0:T(8,128)(2,1)S(1)}, bf16[512,512]{1,0:T(8,128)(2,1)S(1)}, u32[]{:S(2)}, u32[]{:S(2)}) collective-permute-start(bf16[512,512]{1,0:T(8,128)(2,1)S(1)} %join.1.refs_6_.refs_2_), channel_id=1, source_target_pairs={{0,16},{8,24},{16,0},{24,8},{1,17},{9,25},{17,1},{25,9},{2,18},{10... | collective-permute-start | bytes 1572872 | tf_op jit(solution)/shard_map/ppermute | solution.py:44
  32.4 3.5 %collective-permute-done.7.refs_3_ = bf16[1,144,512]{2,1,0:T(8,128)(2,1)S(1)} collective-permute-done((bf16[1,144,512]{2,1,0:T(8,128)(2,1)}, bf16[1,144,512]{2,1,0:T(8,128)(2,1)S(1)}, u32[]{:S(2)}, u32[]{:S(2)}) %collective-permute-start.7) | collective-permute-done | bytes 147488 | tf_op jit(solution)/shard_map/ppermute | solution.py:28
  35.9 1.9 %collective-permute-done.8.refs_6_ = bf16[1,128,512]{2,1,0:T(8,128)(2,1)S(1)} collective-permute-done((bf16[1,128,512]{2,1,0:T(8,128)(2,1)S(1)}, bf16[1,128,512]{2,1,0:T(8,128)(2,1)S(1)}, u32[]{:S(2)}, u32[]{:S(2)}) %collective-permute-start.8) | collective-permute-done | bytes 131104 | tf_op jit(solution)/shard_map/ppermute | solution.py:28
  37.8 1.2 %collective-permute-done.6.refs_2_ = bf16[1,144,512]{2,1,0:T(8,128)(2,1)S(1)} collective-permute-done((bf16[1,144,512]{2,1,0:T(8,128)(2,1)S(1)}, bf16[1,144,512]{2,1,0:T(8,128)(2,1)S(1)}, u32[]{:S(2)}, u32[]{:S(2)}) %collective-permute-start.6) | collective-permute-done | bytes 147488 | tf_op jit(solution)/shard_map/ppermute | solution.py:28
  39.1 1.1 %attend.2.refs_0_ = bf16[1,128,1024]{2,1,0:T(8,128)(2,1)S(1)} custom-call(f32[128,128]{1,0:T(8,128)S(1)} %get-tuple-element.23.place_ref, bf16[1,128,2048]{2,1,0:T(8,128)(2,1)S(1)} %get-tuple-element.24.query_ref, bf16[1,144,512]{2,1,0:T(8,128)(2,1)S(1)} %get-tuple-element.25.refs_0_, bf16[1,144,512]{2,1,0:T(8,128)(2,1)S(1)} %collective-permute-done.refs_1_, ...), custom_call_target="tpu_custom_call" | custom-call | tf_op jit(solution)/shard_map/attend/pallas_call | solution.py:249
  40.2 1.3 %collective-permute-start.10 = (bf16[1,128,1024]{2,1,0:T(8,128)(2,1)S(1)}, bf16[1,128,1024]{2,1,0:T(8,128)(2,1)S(1)}, u32[]{:S(2)}, u32[]{:S(2)}) collective-permute-start(bf16[1,128,1024]{2,1,0:T(8,128)(2,1)S(1)} %attend.2.refs_0_), channel_id=1, source_target_pairs={{0,16},{8,24},{16,0},{24,8},{1,17},{9,25},{17,1},{25,9},{2,18},{10... | collective-permute-start | bytes 786440 | tf_op jit(solution)/shard_map/ppermute | solution.py:44
  41.5 1.1 %attend.3.refs_0_ = bf16[1,128,1024]{2,1,0:T(8,128)(2,1)S(1)} custom-call(f32[128,128]{1,0:T(8,128)S(1)} %get-tuple-element.23.place_ref, bf16[1,128,2048]{2,1,0:T(8,128)(2,1)S(1)} %get-tuple-element.24.query_ref, bf16[1,144,512]{2,1,0:T(8,128)(2,1)S(1)} %get-tuple-element.25.refs_0_, bf16[1,144,512]{2,1,0:T(8,128)(2,1)S(1)} %collective-permute-done.refs_1_, ...), custom_call_target="tpu_custom_call" | custom-call | tf_op jit(solution)/shard_map/attend/pallas_call | solution.py:249
  42.6 0.8 collective-permute-start.20
  43.4 2.3 %collective-permute-start.19 = (bf16[1,128,1024]{2,1,0:T(8,128)(2,1)S(1)}, bf16[1,128,1024]{2,1,0:T(8,128)(2,1)S(1)}, u32[]{:S(2)}, u32[]{:S(2)}) collective-permute-start(bf16[1,128,1024]{2,1,0:T(8,128)(2,1)S(1)} %attend.3.refs_0_), channel_id=1, source_target_pairs={{0,4},{4,6},{6,2},{2,0},{1,5},{5,7},{7,3},{3,1},{8,12},{12,14},{14... | collective-permute-start | bytes 786440 | tf_op jit(solution)/shard_map/ppermute | solution.py:28
  45.7 5.2 %collective-permute-done.10.refs_3_ = bf16[1,128,1024]{2,1,0:T(8,128)(2,1)S(1)} collective-permute-done((bf16[1,128,1024]{2,1,0:T(8,128)(2,1)S(1)}, bf16[1,128,1024]{2,1,0:T(8,128)(2,1)S(1)}, u32[]{:S(2)}, u32[]{:S(2)}) %collective-permute-start.10) | collective-permute-done | bytes 262176 | tf_op jit(solution)/shard_map/ppermute | solution.py:44
  50.9 2.0 %collective-permute-start.12 = (bf16[1,128,1024]{2,1,0:T(8,128)(2,1)S(1)}, bf16[1,128,1024]{2,1,0:T(8,128)(2,1)S(1)}, u32[]{:S(2)}, u32[]{:S(2)}) collective-permute-start(bf16[1,128,1024]{2,1,0:T(8,128)(2,1)S(1)} %collective-permute-done.9.refs_1_), channel_id=1, source_target_pairs={{0,16},{8,24},{16,0},{24,8},{1,17},{9,25},{17,1},{25,9},{2,18},{10... | collective-permute-start | bytes 786440 | tf_op jit(solution)/shard_map/ppermute | solution.py:44
  52.9 1.5 %collective-permute-start.17 = (bf16[512,512]{1,0:T(8,128)(2,1)S(1)}, bf16[512,512]{1,0:T(8,128)(2,1)S(1)}, u32[]{:S(2)}, u32[]{:S(2)}) collective-permute-start(bf16[512,512]{1,0:T(8,128)(2,1)S(1)} %join.1.refs_6_.refs_2_), channel_id=1, source_target_pairs={{0,1},{1,0},{2,3},{3,2},{4,5},{5,4},{6,7},{7,6},{8,9},{9,8},{10,11... | collective-permute-start | bytes 1572872 | tf_op jit(solution)/shard_map/ppermute | solution.py:44
  54.4 2.2 %collective-permute-done.20.refs_3_ = bf16[1,128,1024]{2,1,0:T(8,128)(2,1)S(1)} collective-permute-done((bf16[1,128,1024]{2,1,0:T(8,128)(2,1)S(1)}, bf16[1,128,1024]{2,1,0:T(8,128)(2,1)S(1)}, u32[]{:S(2)}, u32[]{:S(2)}) %collective-permute-start.20) | collective-permute-done | bytes 262176 | tf_op jit(solution)/shard_map/ppermute | solution.py:44
  56.5 1.8 %collective-permute-start.11 = (bf16[1,128,1024]{2,1,0:T(8,128)(2,1)S(1)}, bf16[1,128,1024]{2,1,0:T(8,128)(2,1)S(1)}, u32[]{:S(2)}, u32[]{:S(2)}) collective-permute-start(bf16[1,128,1024]{2,1,0:T(8,128)(2,1)S(1)} %collective-permute-done.9.refs_1_), channel_id=1, source_target_pairs={{0,4},{4,6},{6,2},{2,0},{1,5},{5,7},{7,3},{3,1},{8,12},{12,14},{14... | collective-permute-start | bytes 786440 | tf_op jit(solution)/shard_map/ppermute | solution.py:28
  58.4 1.1 %collective-permute-start.22 = (bf16[1,128,1024]{2,1,0:T(8,128)(2,1)S(1)}, bf16[1,128,1024]{2,1,0:T(8,128)(2,1)S(1)}, u32[]{:S(2)}, u32[]{:S(2)}) collective-permute-start(bf16[1,128,1024]{2,1,0:T(8,128)(2,1)S(1)} %collective-permute-done.19.refs_1_), channel_id=1, source_target_pairs={{0,16},{8,24},{16,0},{24,8},{1,17},{9,25},{17,1},{25,9},{2,18},{10... | collective-permute-start | bytes 786440 | tf_op jit(solution)/shard_map/ppermute | solution.py:44
  59.5 2.7 %collective-permute-done.12.refs_4_ = bf16[1,128,1024]{2,1,0:T(8,128)(2,1)S(1)} collective-permute-done((bf16[1,128,1024]{2,1,0:T(8,128)(2,1)S(1)}, bf16[1,128,1024]{2,1,0:T(8,128)(2,1)S(1)}, u32[]{:S(2)}, u32[]{:S(2)}) %collective-permute-start.12) | collective-permute-done | bytes 262176 | tf_op jit(solution)/shard_map/ppermute | solution.py:44
  62.2 1.9 %collective-permute-start.18 = (bf16[512,512]{1,0:T(8,128)(2,1)S(1)}, bf16[512,512]{1,0:T(8,128)(2,1)S(1)}, u32[]{:S(2)}, u32[]{:S(2)}) collective-permute-start(bf16[512,512]{1,0:T(8,128)(2,1)S(1)} %collective-permute-done.16.refs_7_.refs_3_), channel_id=1, source_target_pairs={{0,1},{1,0},{2,3},{3,2},{4,5},{5,4},{6,7},{7,6},{8,9},{9,8},{10,11... | collective-permute-start | bytes 1572872 | tf_op jit(solution)/shard_map/ppermute | solution.py:44
  64.1 1.0 %collective-permute-done.11.refs_2_ = bf16[1,128,1024]{2,1,0:T(8,128)(2,1)S(1)} collective-permute-done((bf16[1,128,1024]{2,1,0:T(8,128)(2,1)S(1)}, bf16[1,128,1024]{2,1,0:T(8,128)(2,1)S(1)}, u32[]{:S(2)}, u32[]{:S(2)}) %collective-permute-start.11) | collective-permute-done | bytes 262176 | tf_op jit(solution)/shard_map/ppermute | solution.py:28
  65.1 1.1 %collective-permute-start.14 = (bf16[1,128,1024]{2,1,0:T(8,128)(2,1)S(1)}, bf16[1,128,1024]{2,1,0:T(8,128)(2,1)S(1)}, u32[]{:S(2)}, u32[]{:S(2)}) collective-permute-start(bf16[1,128,1024]{2,1,0:T(8,128)(2,1)S(1)} %collective-permute-done.11.refs_2_), channel_id=1, source_target_pairs={{0,16},{8,24},{16,0},{24,8},{1,17},{9,25},{17,1},{25,9},{2,18},{10... | collective-permute-start | bytes 786440 | tf_op jit(solution)/shard_map/ppermute | solution.py:44
  66.2 1.6 %collective-permute-done.22.refs_4_ = bf16[1,128,1024]{2,1,0:T(8,128)(2,1)S(1)} collective-permute-done((bf16[1,128,1024]{2,1,0:T(8,128)(2,1)S(1)}, bf16[1,128,1024]{2,1,0:T(8,128)(2,1)S(1)}, u32[]{:S(2)}, u32[]{:S(2)}) %collective-permute-start.22) | collective-permute-done | bytes 262176 | tf_op jit(solution)/shard_map/ppermute | solution.py:44
  67.8 0.1 collective-permute-done.21.refs_2_
  67.9 1.7 %collective-permute-start.23 = (bf16[1,128,1024]{2,1,0:T(8,128)(2,1)S(1)}, bf16[1,128,1024]{2,1,0:T(8,128)(2,1)S(1)}, u32[]{:S(2)}, u32[]{:S(2)}) collective-permute-start(bf16[1,128,1024]{2,1,0:T(8,128)(2,1)S(1)} %collective-permute-done.21.refs_2_), channel_id=1, source_target_pairs={{0,4},{4,6},{6,2},{2,0},{1,5},{5,7},{7,3},{3,1},{8,12},{12,14},{14... | collective-permute-start | bytes 786440 | tf_op jit(solution)/shard_map/ppermute | solution.py:28
  69.6 1.8 %collective-permute-start.25 = (bf16[1,128,1024]{2,1,0:T(8,128)(2,1)S(1)}, bf16[1,128,1024]{2,1,0:T(8,128)(2,1)S(1)}, u32[]{:S(2)}, u32[]{:S(2)}) collective-permute-start(bf16[1,128,1024]{2,1,0:T(8,128)(2,1)S(1)} %collective-permute-done.21.refs_2_), channel_id=1, source_target_pairs={{0,16},{8,24},{16,0},{24,8},{1,17},{9,25},{17,1},{25,9},{2,18},{10... | collective-permute-start | bytes 786440 | tf_op jit(solution)/shard_map/ppermute | solution.py:44
  71.4 0.8 pad_maximum_fusion
  72.2 2.1 %collective-permute-done.14.refs_5_ = bf16[1,128,1024]{2,1,0:T(8,128)(2,1)S(1)} collective-permute-done((bf16[1,128,1024]{2,1,0:T(8,128)(2,1)S(1)}, bf16[1,128,1024]{2,1,0:T(8,128)(2,1)S(1)}, u32[]{:S(2)}, u32[]{:S(2)}) %collective-permute-start.14) | collective-permute-done | bytes 262176 | tf_op jit(solution)/shard_map/ppermute | solution.py:44
  74.3 1.5 %collective-permute-start.15 = (bf16[1,128,1024]{2,1,0:T(8,128)(2,1)S(1)}, bf16[1,128,1024]{2,1,0:T(8,128)(2,1)S(1)}, u32[]{:S(2)}, u32[]{:S(2)}) collective-permute-start(bf16[1,128,1024]{2,1,0:T(8,128)(2,1)S(1)} %collective-permute-done.14.refs_5_), channel_id=1, source_target_pairs={{0,4},{4,6},{6,2},{2,0},{1,5},{5,7},{7,3},{3,1},{8,12},{12,14},{14... | collective-permute-start | bytes 786440 | tf_op jit(solution)/shard_map/ppermute | solution.py:28
  75.9 1.1 %collective-permute-done.23.refs_0_ = bf16[1,128,1024]{2,1,0:T(8,128)(2,1)S(1)} collective-permute-done((bf16[1,128,1024]{2,1,0:T(8,128)(2,1)S(1)}, bf16[1,128,1024]{2,1,0:T(8,128)(2,1)S(1)}, u32[]{:S(2)}, u32[]{:S(2)}) %collective-permute-start.23) | collective-permute-done | bytes 262176 | tf_op jit(solution)/shard_map/ppermute | solution.py:28
  77.0 2.0 %collective-permute-start.24 = (bf16[1,128,1024]{2,1,0:T(8,128)(2,1)S(1)}, bf16[1,128,1024]{2,1,0:T(8,128)(2,1)S(1)}, u32[]{:S(2)}, u32[]{:S(2)}) collective-permute-start(bf16[1,128,1024]{2,1,0:T(8,128)(2,1)S(1)} %collective-permute-done.23.refs_0_), channel_id=1, source_target_pairs={{0,16},{8,24},{16,0},{24,8},{1,17},{9,25},{17,1},{25,9},{2,18},{10... | collective-permute-start | bytes 786440 | tf_op jit(solution)/shard_map/ppermute | solution.py:44
  79.0 1.8 %early.2.refs_6_ = f32[1024,1024]{1,0:T(8,128)S(1)} custom-call(bf16[1,128,1024]{2,1,0:T(8,128)(2,1)S(1)} %attend.2.refs_0_, bf16[1,128,1024]{2,1,0:T(8,128)(2,1)S(1)} %collective-permute-done.9.refs_1_, bf16[1,128,1024]{2,1,0:T(8,128)(2,1)S(1)} %collective-permute-done.11.refs_2_, bf16[1,128,1024]{2,1,0:T(8,128)(2,1)S(1)} %collective-permute-done.10.refs_3_, ...), custom_call_target="tpu_custom_call" | custom-call | flops 1610612736 | bytes 8388608 | tf_op jit(solution)/shard_map/early/pallas_call | solution.py:286
  80.8 1.8 %early.3.refs_6_ = f32[1024,1024]{1,0:T(8,128)S(1)} custom-call(bf16[1,128,1024]{2,1,0:T(8,128)(2,1)S(1)} %attend.3.refs_0_, bf16[1,128,1024]{2,1,0:T(8,128)(2,1)S(1)} %collective-permute-done.19.refs_1_, bf16[1,128,1024]{2,1,0:T(8,128)(2,1)S(1)} %collective-permute-done.21.refs_2_, bf16[1,128,1024]{2,1,0:T(8,128)(2,1)S(1)} %collective-permute-done.20.refs_3_, ...), custom_call_target="tpu_custom_call" | custom-call | flops 1610612736 | bytes 8388608 | tf_op jit(solution)/shard_map/early/pallas_call | solution.py:286
  82.6 0.8 collective-permute-done.24.refs_1_
  83.4 1.6 %finish.2.refs_7_ = bf16[1,1024,2048]{2,1,0:T(8,128)(2,1)} custom-call(bf16[1,128,1024]{2,1,0:T(8,128)(2,1)S(1)} %collective-permute-done.23.refs_0_, bf16[1,128,1024]{2,1,0:T(8,128)(2,1)S(1)} %collective-permute-done.24.refs_1_, bf16[512,512]{1,0:T(8,128)(2,1)S(1)} %join.1.refs_6_.refs_2_, bf16[512,512]{1,0:T(8,128)(2,1)S(1)} %collective-permute-done.16.refs_7_.refs_3_, ...), custom_call_target="tpu_custom_call" | custom-call | flops 536870912 | bytes 8388608 | tf_op jit(solution)/shard_map/finish/pallas_call | solution.py:311
  85.1 1.7 %finish.3 = bf16[1,1024,2048]{2,1,0:T(8,128)(2,1)} custom-call(bf16[1,128,1024]{2,1,0:T(8,128)(2,1)S(1)} %collective-permute-done.13.refs_0_, bf16[1,128,1024]{2,1,0:T(8,128)(2,1)S(1)} %collective-permute-done.15.refs_1_, bf16[512,512]{1,0:T(8,128)(2,1)S(1)} %join.1.refs_6_.refs_2_, ...), custom_call_target="tpu_custom_call", output_to_operand_aliasing={{}: (7, {})} | custom-call | flops 536870912 | bytes 8388608 | tf_op jit(solution)/shard_map/finish/pallas_call | solution.py:311
  (22 shorter events, 0.1 us)
Async XLA Ops:
  0.6 10.9 %collective-permute-start.2 = (bf16[1,128,512]{2,1,0:T(8,128)(2,1)}, bf16[1,128,512]{2,1,0:T(8,128)(2,1)S(1)}, u32[]{:S(2)}, u32[]{:S(2)}) collective-permute-start(bf16[1,128,512]{2,1,0:T(8,128)(2,1)} %refs_3_.1), channel_id=1, source_target_pairs={{0,2},{4,0},{6,4},{2,6},{1,3},{5,1},{7,5},{3,7},{8,10},{12,8},{14,... | collective-permute-start | bytes 393224 | tf_op jit(solution)/shard_map/ppermute | solution.py:28
  6.0 23.2 %collective-permute-start = (bf16[1,144,512]{2,1,0:T(8,128)(2,1)}, bf16[1,144,512]{2,1,0:T(8,128)(2,1)S(1)}, u32[]{:S(2)}, u32[]{:S(2)}) collective-permute-start(bf16[1,144,512]{2,1,0:T(8,128)(2,1)} %get-tuple-element.21.refs_1_), channel_id=1, source_target_pairs={{0,4},{4,6},{6,2},{2,0},{1,5},{5,7},{7,3},{3,1},{8,12},{12,14},{14... | collective-permute-start | bytes 442376 | tf_op jit(solution)/shard_map/ppermute | solution.py:28
  7.1 18.2 %collective-permute-start.1 = (bf16[1,128,512]{2,1,0:T(8,128)(2,1)}, bf16[1,128,512]{2,1,0:T(8,128)(2,1)S(1)}, u32[]{:S(2)}, u32[]{:S(2)}) collective-permute-start(bf16[1,128,512]{2,1,0:T(8,128)(2,1)} %refs_3_.1), channel_id=1, source_target_pairs={{0,4},{4,6},{6,2},{2,0},{1,5},{5,7},{7,3},{3,1},{8,12},{12,14},{14... | collective-permute-start | bytes 393224 | tf_op jit(solution)/shard_map/ppermute | solution.py:28
  9.1 20.0 %collective-permute-start.3 = (bf16[512,128]{1,0:T(8,128)(2,1)}, bf16[512,128]{1,0:T(8,128)(2,1)S(1)}, u32[]{:S(2)}, u32[]{:S(2)}) collective-permute-start(bf16[512,128]{1,0:T(8,128)(2,1)} %get-tuple-element.28), channel_id=1, source_target_pairs={{0,4},{4,6},{6,2},{2,0},{1,5},{5,7},{7,3},{3,1},{8,12},{12,14},{14... | collective-permute-start | bytes 393224 | tf_op jit(solution)/shard_map/ppermute | solution.py:28
  11.6 17.6 %collective-permute-start.4 = (bf16[512,128]{1,0:T(8,128)(2,1)}, bf16[512,128]{1,0:T(8,128)(2,1)S(1)}, u32[]{:S(2)}, u32[]{:S(2)}) collective-permute-start(bf16[512,128]{1,0:T(8,128)(2,1)} %get-tuple-element.29), channel_id=1, source_target_pairs={{0,6},{4,2},{6,0},{2,4},{1,7},{5,3},{7,1},{3,5},{8,14},{12,10},{14... | collective-permute-start | bytes 393224 | tf_op jit(solution)/shard_map/ppermute | solution.py:28
  11.6 17.6 %collective-permute-start.5 = (bf16[512,128]{1,0:T(8,128)(2,1)}, bf16[512,128]{1,0:T(8,128)(2,1)S(1)}, u32[]{:S(2)}, u32[]{:S(2)}) collective-permute-start(bf16[512,128]{1,0:T(8,128)(2,1)} %get-tuple-element.30), channel_id=1, source_target_pairs={{0,2},{4,0},{6,4},{2,6},{1,3},{5,1},{7,5},{3,7},{8,10},{12,8},{14,... | collective-permute-start | bytes 393224 | tf_op jit(solution)/shard_map/ppermute | solution.py:28
  20.6 1.0 %copy-start = (bf16[1,128,2048]{2,1,0:T(8,128)(2,1)S(1)}, bf16[1,128,2048]{2,1,0:T(8,128)(2,1)}, u32[]{:S(2)}) copy-start(bf16[1,128,2048]{2,1,0:T(8,128)(2,1)} %refs_2_.1) | copy-start | bytes 1572868
  21.7 0.9 %copy-start.1 = (bf16[1,128,512]{2,1,0:T(8,128)(2,1)S(1)}, bf16[1,128,512]{2,1,0:T(8,128)(2,1)}, u32[]{:S(2)}) copy-start(bf16[1,128,512]{2,1,0:T(8,128)(2,1)} %refs_3_.1) | copy-start | bytes 393220
  22.6 0.9 %copy-start.2 = (bf16[512,128]{1,0:T(8,128)(2,1)S(1)}, bf16[512,128]{1,0:T(8,128)(2,1)}, u32[]{:S(2)}) copy-start(bf16[512,128]{1,0:T(8,128)(2,1)} %get-tuple-element.22.refs_4_) | copy-start | bytes 393220
  23.5 0.8 copy-start.3
  25.3 10.6 %collective-permute-start.7 = (bf16[1,144,512]{2,1,0:T(8,128)(2,1)}, bf16[1,144,512]{2,1,0:T(8,128)(2,1)S(1)}, u32[]{:S(2)}, u32[]{:S(2)}) collective-permute-start(bf16[1,144,512]{2,1,0:T(8,128)(2,1)} %get-tuple-element.21.refs_1_), channel_id=1, source_target_pairs={{0,2},{4,0},{6,4},{2,6},{1,3},{5,1},{7,5},{3,7},{8,10},{12,8},{14,... | collective-permute-start | bytes 442376 | tf_op jit(solution)/shard_map/ppermute | solution.py:28
  29.2 9.8 %collective-permute-start.6 = (bf16[1,144,512]{2,1,0:T(8,128)(2,1)S(1)}, bf16[1,144,512]{2,1,0:T(8,128)(2,1)S(1)}, u32[]{:S(2)}, u32[]{:S(2)}) collective-permute-start(bf16[1,144,512]{2,1,0:T(8,128)(2,1)S(1)} %collective-permute-done.refs_1_), channel_id=1, source_target_pairs={{0,4},{4,6},{6,2},{2,0},{1,5},{5,7},{7,3},{3,1},{8,12},{12,14},{14... | collective-permute-start | bytes 442376 | tf_op jit(solution)/shard_map/ppermute | solution.py:28
  29.3 8.5 %collective-permute-start.8 = (bf16[1,128,512]{2,1,0:T(8,128)(2,1)S(1)}, bf16[1,128,512]{2,1,0:T(8,128)(2,1)S(1)}, u32[]{:S(2)}, u32[]{:S(2)}) collective-permute-start(bf16[1,128,512]{2,1,0:T(8,128)(2,1)S(1)} %collective-permute-done.2.refs_7_), channel_id=1, source_target_pairs={{0,2},{4,0},{6,4},{2,6},{1,3},{5,1},{7,5},{3,7},{8,10},{12,8},{14,... | collective-permute-start | bytes 393224 | tf_op jit(solution)/shard_map/ppermute | solution.py:28
  31.3 28.1 %collective-permute-start.16 = (bf16[512,512]{1,0:T(8,128)(2,1)S(1)}, bf16[512,512]{1,0:T(8,128)(2,1)S(1)}, u32[]{:S(2)}, u32[]{:S(2)}) collective-permute-start(bf16[512,512]{1,0:T(8,128)(2,1)S(1)} %join.1.refs_6_.refs_2_), channel_id=1, source_target_pairs={{0,16},{8,24},{16,0},{24,8},{1,17},{9,25},{17,1},{25,9},{2,18},{10... | collective-permute-start | bytes 1572872 | tf_op jit(solution)/shard_map/ppermute | solution.py:44
  40.2 10.8 %collective-permute-start.10 = (bf16[1,128,1024]{2,1,0:T(8,128)(2,1)S(1)}, bf16[1,128,1024]{2,1,0:T(8,128)(2,1)S(1)}, u32[]{:S(2)}, u32[]{:S(2)}) collective-permute-start(bf16[1,128,1024]{2,1,0:T(8,128)(2,1)S(1)} %attend.2.refs_0_), channel_id=1, source_target_pairs={{0,16},{8,24},{16,0},{24,8},{1,17},{9,25},{17,1},{25,9},{2,18},{10... | collective-permute-start | bytes 786440 | tf_op jit(solution)/shard_map/ppermute | solution.py:44
  41.5 9.4 %collective-permute-start.9 = (bf16[1,128,1024]{2,1,0:T(8,128)(2,1)S(1)}, bf16[1,128,1024]{2,1,0:T(8,128)(2,1)S(1)}, u32[]{:S(2)}, u32[]{:S(2)}) collective-permute-start(bf16[1,128,1024]{2,1,0:T(8,128)(2,1)S(1)} %attend.2.refs_0_), channel_id=1, source_target_pairs={{0,4},{4,6},{6,2},{2,0},{1,5},{5,7},{7,3},{3,1},{8,12},{12,14},{14... | collective-permute-start | bytes 786440 | tf_op jit(solution)/shard_map/ppermute | solution.py:28
  42.6 14.0 %collective-permute-start.20 = (bf16[1,128,1024]{2,1,0:T(8,128)(2,1)S(1)}, bf16[1,128,1024]{2,1,0:T(8,128)(2,1)S(1)}, u32[]{:S(2)}, u32[]{:S(2)}) collective-permute-start(bf16[1,128,1024]{2,1,0:T(8,128)(2,1)S(1)} %attend.3.refs_0_), channel_id=1, source_target_pairs={{0,16},{8,24},{16,0},{24,8},{1,17},{9,25},{17,1},{25,9},{2,18},{10... | collective-permute-start | bytes 786440 | tf_op jit(solution)/shard_map/ppermute | solution.py:44
  43.4 15.0 %collective-permute-start.19 = (bf16[1,128,1024]{2,1,0:T(8,128)(2,1)S(1)}, bf16[1,128,1024]{2,1,0:T(8,128)(2,1)S(1)}, u32[]{:S(2)}, u32[]{:S(2)}) collective-permute-start(bf16[1,128,1024]{2,1,0:T(8,128)(2,1)S(1)} %attend.3.refs_0_), channel_id=1, source_target_pairs={{0,4},{4,6},{6,2},{2,0},{1,5},{5,7},{7,3},{3,1},{8,12},{12,14},{14... | collective-permute-start | bytes 786440 | tf_op jit(solution)/shard_map/ppermute | solution.py:28
  50.9 11.2 %collective-permute-start.12 = (bf16[1,128,1024]{2,1,0:T(8,128)(2,1)S(1)}, bf16[1,128,1024]{2,1,0:T(8,128)(2,1)S(1)}, u32[]{:S(2)}, u32[]{:S(2)}) collective-permute-start(bf16[1,128,1024]{2,1,0:T(8,128)(2,1)S(1)} %collective-permute-done.9.refs_1_), channel_id=1, source_target_pairs={{0,16},{8,24},{16,0},{24,8},{1,17},{9,25},{17,1},{25,9},{2,18},{10... | collective-permute-start | bytes 786440 | tf_op jit(solution)/shard_map/ppermute | solution.py:44
  52.9 19.3 %collective-permute-start.17 = (bf16[512,512]{1,0:T(8,128)(2,1)S(1)}, bf16[512,512]{1,0:T(8,128)(2,1)S(1)}, u32[]{:S(2)}, u32[]{:S(2)}) collective-permute-start(bf16[512,512]{1,0:T(8,128)(2,1)S(1)} %join.1.refs_6_.refs_2_), channel_id=1, source_target_pairs={{0,1},{1,0},{2,3},{3,2},{4,5},{5,4},{6,7},{7,6},{8,9},{9,8},{10,11... | collective-permute-start | bytes 1572872 | tf_op jit(solution)/shard_map/ppermute | solution.py:44
  56.5 8.5 %collective-permute-start.11 = (bf16[1,128,1024]{2,1,0:T(8,128)(2,1)S(1)}, bf16[1,128,1024]{2,1,0:T(8,128)(2,1)S(1)}, u32[]{:S(2)}, u32[]{:S(2)}) collective-permute-start(bf16[1,128,1024]{2,1,0:T(8,128)(2,1)S(1)} %collective-permute-done.9.refs_1_), channel_id=1, source_target_pairs={{0,4},{4,6},{6,2},{2,0},{1,5},{5,7},{7,3},{3,1},{8,12},{12,14},{14... | collective-permute-start | bytes 786440 | tf_op jit(solution)/shard_map/ppermute | solution.py:28
  58.4 9.4 %collective-permute-start.22 = (bf16[1,128,1024]{2,1,0:T(8,128)(2,1)S(1)}, bf16[1,128,1024]{2,1,0:T(8,128)(2,1)S(1)}, u32[]{:S(2)}, u32[]{:S(2)}) collective-permute-start(bf16[1,128,1024]{2,1,0:T(8,128)(2,1)S(1)} %collective-permute-done.19.refs_1_), channel_id=1, source_target_pairs={{0,16},{8,24},{16,0},{24,8},{1,17},{9,25},{17,1},{25,9},{2,18},{10... | collective-permute-start | bytes 786440 | tf_op jit(solution)/shard_map/ppermute | solution.py:44
  59.5 8.4 %collective-permute-start.21 = (bf16[1,128,1024]{2,1,0:T(8,128)(2,1)S(1)}, bf16[1,128,1024]{2,1,0:T(8,128)(2,1)S(1)}, u32[]{:S(2)}, u32[]{:S(2)}) collective-permute-start(bf16[1,128,1024]{2,1,0:T(8,128)(2,1)S(1)} %collective-permute-done.19.refs_1_), channel_id=1, source_target_pairs={{0,4},{4,6},{6,2},{2,0},{1,5},{5,7},{7,3},{3,1},{8,12},{12,14},{14... | collective-permute-start | bytes 786440 | tf_op jit(solution)/shard_map/ppermute | solution.py:28
  62.2 16.8 %collective-permute-start.18 = (bf16[512,512]{1,0:T(8,128)(2,1)S(1)}, bf16[512,512]{1,0:T(8,128)(2,1)S(1)}, u32[]{:S(2)}, u32[]{:S(2)}) collective-permute-start(bf16[512,512]{1,0:T(8,128)(2,1)S(1)} %collective-permute-done.16.refs_7_.refs_3_), channel_id=1, source_target_pairs={{0,1},{1,0},{2,3},{3,2},{4,5},{5,4},{6,7},{7,6},{8,9},{9,8},{10,11... | collective-permute-start | bytes 1572872 | tf_op jit(solution)/shard_map/ppermute | solution.py:44
  65.1 9.2 %collective-permute-start.14 = (bf16[1,128,1024]{2,1,0:T(8,128)(2,1)S(1)}, bf16[1,128,1024]{2,1,0:T(8,128)(2,1)S(1)}, u32[]{:S(2)}, u32[]{:S(2)}) collective-permute-start(bf16[1,128,1024]{2,1,0:T(8,128)(2,1)S(1)} %collective-permute-done.11.refs_2_), channel_id=1, source_target_pairs={{0,16},{8,24},{16,0},{24,8},{1,17},{9,25},{17,1},{25,9},{2,18},{10... | collective-permute-start | bytes 786440 | tf_op jit(solution)/shard_map/ppermute | solution.py:44
  67.9 9.1 %collective-permute-start.23 = (bf16[1,128,1024]{2,1,0:T(8,128)(2,1)S(1)}, bf16[1,128,1024]{2,1,0:T(8,128)(2,1)S(1)}, u32[]{:S(2)}, u32[]{:S(2)}) collective-permute-start(bf16[1,128,1024]{2,1,0:T(8,128)(2,1)S(1)} %collective-permute-done.21.refs_2_), channel_id=1, source_target_pairs={{0,4},{4,6},{6,2},{2,0},{1,5},{5,7},{7,3},{3,1},{8,12},{12,14},{14... | collective-permute-start | bytes 786440 | tf_op jit(solution)/shard_map/ppermute | solution.py:28
  69.6 11.2 %collective-permute-start.25 = (bf16[1,128,1024]{2,1,0:T(8,128)(2,1)S(1)}, bf16[1,128,1024]{2,1,0:T(8,128)(2,1)S(1)}, u32[]{:S(2)}, u32[]{:S(2)}) collective-permute-start(bf16[1,128,1024]{2,1,0:T(8,128)(2,1)S(1)} %collective-permute-done.21.refs_2_), channel_id=1, source_target_pairs={{0,16},{8,24},{16,0},{24,8},{1,17},{9,25},{17,1},{25,9},{2,18},{10... | collective-permute-start | bytes 786440 | tf_op jit(solution)/shard_map/ppermute | solution.py:44
  72.2 12.8 %collective-permute-start.13 = (bf16[1,128,1024]{2,1,0:T(8,128)(2,1)S(1)}, bf16[1,128,1024]{2,1,0:T(8,128)(2,1)S(1)}, u32[]{:S(2)}, u32[]{:S(2)}) collective-permute-start(bf16[1,128,1024]{2,1,0:T(8,128)(2,1)S(1)} %collective-permute-done.11.refs_2_), channel_id=1, source_target_pairs={{0,4},{4,6},{6,2},{2,0},{1,5},{5,7},{7,3},{3,1},{8,12},{12,14},{14... | collective-permute-start | bytes 786440 | tf_op jit(solution)/shard_map/ppermute | solution.py:28
  74.3 10.7 %collective-permute-start.15 = (bf16[1,128,1024]{2,1,0:T(8,128)(2,1)S(1)}, bf16[1,128,1024]{2,1,0:T(8,128)(2,1)S(1)}, u32[]{:S(2)}, u32[]{:S(2)}) collective-permute-start(bf16[1,128,1024]{2,1,0:T(8,128)(2,1)S(1)} %collective-permute-done.14.refs_5_), channel_id=1, source_target_pairs={{0,4},{4,6},{6,2},{2,0},{1,5},{5,7},{7,3},{3,1},{8,12},{12,14},{14... | collective-permute-start | bytes 786440 | tf_op jit(solution)/shard_map/ppermute | solution.py:28
  77.0 6.4 %collective-permute-start.24 = (bf16[1,128,1024]{2,1,0:T(8,128)(2,1)S(1)}, bf16[1,128,1024]{2,1,0:T(8,128)(2,1)S(1)}, u32[]{:S(2)}, u32[]{:S(2)}) collective-permute-start(bf16[1,128,1024]{2,1,0:T(8,128)(2,1)S(1)} %collective-permute-done.23.refs_0_), channel_id=1, source_target_pairs={{0,16},{8,24},{16,0},{24,8},{1,17},{9,25},{17,1},{25,9},{2,18},{10... | collective-permute-start | bytes 786440 | tf_op jit(solution)/shard_map/ppermute | solution.py:44

commit v16 on v15

--- a/solution.py
+++ b/solution.py
@@ -271,7 +271,7 @@
             sent.append(around(sent[-1], 1) if by_ring else swap(held[s], "pipe", far))
             if s < n - 1:
                 arrived = around(held[s], 1)
-                held.append(after(arrived, sent[s]) if s < n - 2 else arrived)
+                held.append(after(arrived, sent[s]) if s < n - 2 - (c == 0) else arrived)
         near.append(held)
         mirrored.append(sent)
     cots = [mine, mine_far, swap(mine, "tp", 1), swap(mine_far, "tp", 1)]

time: 87 us -> 94.3 us (1.084)
  waiting for transfers between devices: 23.5 us -> 30.2 us
    ppermute x16, waiting for transfers between devices: 8.93 us -> 13.7 us  [around(): lax.ppermute(x, 'ctx', [(order[q], order[(q + shift) % n]) for q in range...]
    ppermute x10, waiting for transfers between devices: 14.5 us -> 16.4 us  [swap(): lax.ppermute(x, axis, [(i, i ^ mask) for i in range(lax.axis_size(axis))])]
    ppermute x16, starting transfers between devices: 31 us -> 32.4 us  [around(): lax.ppermute(x, 'ctx', [(order[q], order[(q + shift) % n]) for q in range...]
  transfers between devices with their start and end apart: 26 -> 26, of which waited for: 12 -> 11; matrix products, arithmetic and copies ran while one was open for 1% -> 1% of each run, Pallas kernels for 12% -> 11%
where the time goes in v16:
time: 94.3 us; the launch traced here: 94 us
  starting transfers between devices  46.2 us (49%)
  waiting for transfers between devices  30.2 us (32%)
  Pallas kernels  12.4 us (13%)
  local copies, waits for them, and re-layouts  3.69 us (4%)
    ppermute x16, starting transfers between devices, around(): lax.ppermute(x, 'ctx', [(order[q], order[(q + shift) % n]) for q in range...  32.4 us
    ppermute x10, waiting for transfers between devices, swap(): lax.ppermute(x, axis, [(i, i ^ mask) for i in range(lax.axis_size(axis))])  16.4 us
    ppermute x10, starting transfers between devices, swap(): lax.ppermute(x, axis, [(i, i ^ mask) for i in range(lax.axis_size(axis))])  13.7 us
    ppermute x16, waiting for transfers between devices, around(): lax.ppermute(x, 'ctx', [(order[q], order[(q + shift) % n]) for q in range...  13.7 us
    unnamed x8, local copies, waits for them, and re-layouts  3.69 us
    pallas_call x2, Pallas kernels, local(): pl.pallas_call(functools.partial(early_kernel, first_slots), out_shape=ja...  3.59 us
    pallas_call x2, Pallas kernels, local(): pl.pallas_call(functools.partial(finish_kernel, slots, c * chunk), out_sh...  3.3 us
    pallas_call x1, Pallas kernels, local(): pl.pallas_call(functools.partial(prepare_kernel, n), out_shape=[jax.Shape...  2.29 us
  transfers between devices with their start and end apart: 26, of which 11 were waited for; matrix products, arithmetic and copies ran while one was open for 1% of the time, Pallas kernels for 11%

profile of v16, /device:TPU:0, one launch (start us, length us, event | category | flops | bytes accessed | tf_op | source)
XLA Modules:
  0.0 94.0 jit_solution(11920881530251980417)
XLA Ops:
  0.6 3.1 %collective-permute-start.2 = (bf16[1,128,512]{2,1,0:T(8,128)(2,1)}, bf16[1,128,512]{2,1,0:T(8,128)(2,1)S(1)}, u32[]{:S(2)}, u32[]{:S(2)}) collective-permute-start(bf16[1,128,512]{2,1,0:T(8,128)(2,1)} %refs_3_.1), channel_id=1, source_target_pairs={{0,2},{4,0},{6,4},{2,6},{1,3},{5,1},{7,5},{3,7},{8,10},{12,8},{14,... | collective-permute-start | bytes 393224 | tf_op jit(solution)/shard_map/ppermute | solution.py:28
  3.7 2.3 %prepare.1 = (bf16[1,144,512]{2,1,0:T(8,128)(2,1)}, f32[128,128]{1,0:T(8,128)}, bf16[512,128]{1,0:T(8,128)(2,1)}, bf16[512,128]{1,0:T(8,128)(2,1)}, bf16[512,128]{1,0:T(8,128)(2,1)}, /*index=5*/bf16[512,128]{1,0:T(8,128)(2,1)}) custom-call(s32[1,2]{1,0:T(1,128)} %span_source.1, bf16[1,128,512]{2,1,0:T(8,128)(2,1)} %key_ref.1, bf16[1,128,4096]{2,1,0:T(8,128)(2,1)} %cot_source.1), custom_call_target="tpu_custom_call" | custom-call | tf_op jit(solution)/shard_map/prepare/pallas_call | solution.py:206
  6.0 1.1 %collective-permute-start = (bf16[1,144,512]{2,1,0:T(8,128)(2,1)}, bf16[1,144,512]{2,1,0:T(8,128)(2,1)S(1)}, u32[]{:S(2)}, u32[]{:S(2)}) collective-permute-start(bf16[1,144,512]{2,1,0:T(8,128)(2,1)} %get-tuple-element.20.refs_1_), channel_id=1, source_target_pairs={{0,4},{4,6},{6,2},{2,0},{1,5},{5,7},{7,3},{3,1},{8,12},{12,14},{14... | collective-permute-start | bytes 442376 | tf_op jit(solution)/shard_map/ppermute | solution.py:28
  7.1 2.0 %collective-permute-start.1 = (bf16[1,128,512]{2,1,0:T(8,128)(2,1)}, bf16[1,128,512]{2,1,0:T(8,128)(2,1)S(1)}, u32[]{:S(2)}, u32[]{:S(2)}) collective-permute-start(bf16[1,128,512]{2,1,0:T(8,128)(2,1)} %refs_3_.1), channel_id=1, source_target_pairs={{0,4},{4,6},{6,2},{2,0},{1,5},{5,7},{7,3},{3,1},{8,12},{12,14},{14... | collective-permute-start | bytes 393224 | tf_op jit(solution)/shard_map/ppermute | solution.py:28
  9.1 2.5 %collective-permute-start.3 = (bf16[512,128]{1,0:T(8,128)(2,1)}, bf16[512,128]{1,0:T(8,128)(2,1)S(1)}, u32[]{:S(2)}, u32[]{:S(2)}) collective-permute-start(bf16[512,128]{1,0:T(8,128)(2,1)} %get-tuple-element.27), channel_id=1, source_target_pairs={{0,4},{4,6},{6,2},{2,0},{1,5},{5,7},{7,3},{3,1},{8,12},{12,14},{14... | collective-permute-start | bytes 393224 | tf_op jit(solution)/shard_map/ppermute | solution.py:28
  11.6 9.0 %collective-permute-start.5 = (bf16[512,128]{1,0:T(8,128)(2,1)}, bf16[512,128]{1,0:T(8,128)(2,1)S(1)}, u32[]{:S(2)}, u32[]{:S(2)}) collective-permute-start(bf16[512,128]{1,0:T(8,128)(2,1)} %get-tuple-element.29), channel_id=1, source_target_pairs={{0,2},{4,0},{6,4},{2,6},{1,3},{5,1},{7,5},{3,7},{8,10},{12,8},{14,... | collective-permute-start | bytes 393224 | tf_op jit(solution)/shard_map/ppermute | solution.py:28
  20.6 1.0 %copy-done = bf16[1,128,2048]{2,1,0:T(8,128)(2,1)S(1)} copy-done((bf16[1,128,2048]{2,1,0:T(8,128)(2,1)S(1)}, bf16[1,128,2048]{2,1,0:T(8,128)(2,1)}, u32[]{:S(2)}) %copy-start) | copy-done | bytes 524312
  21.7 0.9 copy-done.1
  22.6 0.9 copy-done.2
  23.5 0.8 copy-done.3
  24.3 1.0 %fetch.1 = (f32[128,128]{1,0:T(8,128)S(1)}, bf16[1,144,512]{2,1,0:T(8,128)(2,1)S(1)}, bf16[1,128,2048]{2,1,0:T(8,128)(2,1)S(1)}, bf16[1,128,512]{2,1,0:T(8,128)(2,1)S(1)}, bf16[512,128]{1,0:T(8,128)(2,1)S(1)}) custom-call(f32[128,128]{1,0:T(8,128)S(1)} %copy-done.3, bf16[1,144,512]{2,1,0:T(8,128)(2,1)} %get-tuple-element.20.refs_1_, ...), custom_call_target="tpu_custom_call" | custom-call | tf_op jit(solution)/shard_map/fetch/pallas_call | solution.py:224
  25.3 3.8 %collective-permute-start.7 = (bf16[1,144,512]{2,1,0:T(8,128)(2,1)}, bf16[1,144,512]{2,1,0:T(8,128)(2,1)S(1)}, u32[]{:S(2)}, u32[]{:S(2)}) collective-permute-start(bf16[1,144,512]{2,1,0:T(8,128)(2,1)} %get-tuple-element.20.refs_1_), channel_id=1, source_target_pairs={{0,2},{4,0},{6,4},{2,6},{1,3},{5,1},{7,5},{3,7},{8,10},{12,8},{14,... | collective-permute-start | bytes 442376 | tf_op jit(solution)/shard_map/ppermute | solution.py:28
  29.1 0.1 join.1.refs_6_.refs_2_
  29.2 0.1 collective-permute-start.6
  29.3 2.0 %collective-permute-start.8 = (bf16[1,128,512]{2,1,0:T(8,128)(2,1)S(1)}, bf16[1,128,512]{2,1,0:T(8,128)(2,1)S(1)}, u32[]{:S(2)}, u32[]{:S(2)}) collective-permute-start(bf16[1,128,512]{2,1,0:T(8,128)(2,1)S(1)} %collective-permute-done.2.refs_7_), channel_id=1, source_target_pairs={{0,2},{4,0},{6,4},{2,6},{1,3},{5,1},{7,5},{3,7},{8,10},{12,8},{14,... | collective-permute-start | bytes 393224 | tf_op jit(solution)/shard_map/ppermute | solution.py:28
  31.3 1.1 %collective-permute-start.15 = (bf16[512,512]{1,0:T(8,128)(2,1)S(1)}, bf16[512,512]{1,0:T(8,128)(2,1)S(1)}, u32[]{:S(2)}, u32[]{:S(2)}) collective-permute-start(bf16[512,512]{1,0:T(8,128)(2,1)S(1)} %join.1.refs_6_.refs_2_), channel_id=1, source_target_pairs={{0,16},{8,24},{16,0},{24,8},{1,17},{9,25},{17,1},{25,9},{2,18},{10... | collective-permute-start | bytes 1572872 | tf_op jit(solution)/shard_map/ppermute | solution.py:44
  32.4 3.5 %collective-permute-done.7.refs_3_ = bf16[1,144,512]{2,1,0:T(8,128)(2,1)S(1)} collective-permute-done((bf16[1,144,512]{2,1,0:T(8,128)(2,1)}, bf16[1,144,512]{2,1,0:T(8,128)(2,1)S(1)}, u32[]{:S(2)}, u32[]{:S(2)}) %collective-permute-start.7) | collective-permute-done | bytes 147488 | tf_op jit(solution)/shard_map/ppermute | solution.py:28
  35.9 1.9 %collective-permute-done.8.refs_6_ = bf16[1,128,512]{2,1,0:T(8,128)(2,1)S(1)} collective-permute-done((bf16[1,128,512]{2,1,0:T(8,128)(2,1)S(1)}, bf16[1,128,512]{2,1,0:T(8,128)(2,1)S(1)}, u32[]{:S(2)}, u32[]{:S(2)}) %collective-permute-start.8) | collective-permute-done | bytes 131104 | tf_op jit(solution)/shard_map/ppermute | solution.py:28
  37.8 1.2 %collective-permute-done.6.refs_2_ = bf16[1,144,512]{2,1,0:T(8,128)(2,1)S(1)} collective-permute-done((bf16[1,144,512]{2,1,0:T(8,128)(2,1)S(1)}, bf16[1,144,512]{2,1,0:T(8,128)(2,1)S(1)}, u32[]{:S(2)}, u32[]{:S(2)}) %collective-permute-start.6) | collective-permute-done | bytes 147488 | tf_op jit(solution)/shard_map/ppermute | solution.py:28
  39.1 1.1 %attend.3.refs_0_ = bf16[1,128,1024]{2,1,0:T(8,128)(2,1)S(1)} custom-call(f32[128,128]{1,0:T(8,128)S(1)} %get-tuple-element.22.place_ref, bf16[1,128,2048]{2,1,0:T(8,128)(2,1)S(1)} %get-tuple-element.23.query_ref, bf16[1,144,512]{2,1,0:T(8,128)(2,1)S(1)} %get-tuple-element.24.refs_0_, bf16[1,144,512]{2,1,0:T(8,128)(2,1)S(1)} %collective-permute-done.refs_1_, ...), custom_call_target="tpu_custom_call" | custom-call | tf_op jit(solution)/shard_map/attend/pallas_call | solution.py:249
  40.2 1.3 %collective-permute-start.20 = (bf16[1,128,1024]{2,1,0:T(8,128)(2,1)S(1)}, bf16[1,128,1024]{2,1,0:T(8,128)(2,1)S(1)}, u32[]{:S(2)}, u32[]{:S(2)}) collective-permute-start(bf16[1,128,1024]{2,1,0:T(8,128)(2,1)S(1)} %attend.3.refs_0_), channel_id=1, source_target_pairs={{0,16},{8,24},{16,0},{24,8},{1,17},{9,25},{17,1},{25,9},{2,18},{10... | collective-permute-start | bytes 786440 | tf_op jit(solution)/shard_map/ppermute | solution.py:44
  41.5 1.1 %attend.2.refs_0_ = bf16[1,128,1024]{2,1,0:T(8,128)(2,1)S(1)} custom-call(f32[128,128]{1,0:T(8,128)S(1)} %get-tuple-element.22.place_ref, bf16[1,128,2048]{2,1,0:T(8,128)(2,1)S(1)} %get-tuple-element.23.query_ref, bf16[1,144,512]{2,1,0:T(8,128)(2,1)S(1)} %get-tuple-element.24.refs_0_, bf16[1,144,512]{2,1,0:T(8,128)(2,1)S(1)} %collective-permute-done.refs_1_, ...), custom_call_target="tpu_custom_call" | custom-call | tf_op jit(solution)/shard_map/attend/pallas_call | solution.py:249
  42.6 0.8 collective-permute-start.10
  43.4 2.3 %collective-permute-start.9 = (bf16[1,128,1024]{2,1,0:T(8,128)(2,1)S(1)}, bf16[1,128,1024]{2,1,0:T(8,128)(2,1)S(1)}, u32[]{:S(2)}, u32[]{:S(2)}) collective-permute-start(bf16[1,128,1024]{2,1,0:T(8,128)(2,1)S(1)} %attend.2.refs_0_), channel_id=1, source_target_pairs={{0,4},{4,6},{6,2},{2,0},{1,5},{5,7},{7,3},{3,1},{8,12},{12,14},{14... | collective-permute-start | bytes 786440 | tf_op jit(solution)/shard_map/ppermute | solution.py:28
  45.7 5.2 %collective-permute-done.20.refs_3_ = bf16[1,128,1024]{2,1,0:T(8,128)(2,1)S(1)} collective-permute-done((bf16[1,128,1024]{2,1,0:T(8,128)(2,1)S(1)}, bf16[1,128,1024]{2,1,0:T(8,128)(2,1)S(1)}, u32[]{:S(2)}, u32[]{:S(2)}) %collective-permute-start.20) | collective-permute-done | bytes 262176 | tf_op jit(solution)/shard_map/ppermute | solution.py:44
  50.9 1.9 %collective-permute-start.16 = (bf16[512,512]{1,0:T(8,128)(2,1)S(1)}, bf16[512,512]{1,0:T(8,128)(2,1)S(1)}, u32[]{:S(2)}, u32[]{:S(2)}) collective-permute-start(bf16[512,512]{1,0:T(8,128)(2,1)S(1)} %join.1.refs_6_.refs_2_), channel_id=1, source_target_pairs={{0,1},{1,0},{2,3},{3,2},{4,5},{5,4},{6,7},{7,6},{8,9},{9,8},{10,11... | collective-permute-start | bytes 1572872 | tf_op jit(solution)/shard_map/ppermute | solution.py:44
  52.9 1.5 %collective-permute-start.22 = (bf16[1,128,1024]{2,1,0:T(8,128)(2,1)S(1)}, bf16[1,128,1024]{2,1,0:T(8,128)(2,1)S(1)}, u32[]{:S(2)}, u32[]{:S(2)}) collective-permute-start(bf16[1,128,1024]{2,1,0:T(8,128)(2,1)S(1)} %collective-permute-done.19.refs_1_), channel_id=1, source_target_pairs={{0,16},{8,24},{16,0},{24,8},{1,17},{9,25},{17,1},{25,9},{2,18},{10... | collective-permute-start | bytes 786440 | tf_op jit(solution)/shard_map/ppermute | solution.py:44
  54.4 2.2 %collective-permute-done.10.refs_3_ = bf16[1,128,1024]{2,1,0:T(8,128)(2,1)S(1)} collective-permute-done((bf16[1,128,1024]{2,1,0:T(8,128)(2,1)S(1)}, bf16[1,128,1024]{2,1,0:T(8,128)(2,1)S(1)}, u32[]{:S(2)}, u32[]{:S(2)}) %collective-permute-start.10) | collective-permute-done | bytes 262176 | tf_op jit(solution)/shard_map/ppermute | solution.py:44
  56.5 1.8 %collective-permute-start.21 = (bf16[1,128,1024]{2,1,0:T(8,128)(2,1)S(1)}, bf16[1,128,1024]{2,1,0:T(8,128)(2,1)S(1)}, u32[]{:S(2)}, u32[]{:S(2)}) collective-permute-start(bf16[1,128,1024]{2,1,0:T(8,128)(2,1)S(1)} %collective-permute-done.19.refs_1_), channel_id=1, source_target_pairs={{0,4},{4,6},{6,2},{2,0},{1,5},{5,7},{7,3},{3,1},{8,12},{12,14},{14... | collective-permute-start | bytes 786440 | tf_op jit(solution)/shard_map/ppermute | solution.py:28
  58.4 1.1 %collective-permute-start.17 = (bf16[512,512]{1,0:T(8,128)(2,1)S(1)}, bf16[512,512]{1,0:T(8,128)(2,1)S(1)}, u32[]{:S(2)}, u32[]{:S(2)}) collective-permute-start(bf16[512,512]{1,0:T(8,128)(2,1)S(1)} %collective-permute-done.15.refs_7_.refs_3_), channel_id=1, source_target_pairs={{0,1},{1,0},{2,3},{3,2},{4,5},{5,4},{6,7},{7,6},{8,9},{9,8},{10,11... | collective-permute-start | bytes 1572872 | tf_op jit(solution)/shard_map/ppermute | solution.py:44
  59.5 1.4 %collective-permute-done.22.refs_4_ = bf16[1,128,1024]{2,1,0:T(8,128)(2,1)S(1)} collective-permute-done((bf16[1,128,1024]{2,1,0:T(8,128)(2,1)S(1)}, bf16[1,128,1024]{2,1,0:T(8,128)(2,1)S(1)}, u32[]{:S(2)}, u32[]{:S(2)}) %collective-permute-start.22) | collective-permute-done | bytes 262176 | tf_op jit(solution)/shard_map/ppermute | solution.py:44
  60.9 4.2 %collective-permute-done.21.refs_2_ = bf16[1,128,1024]{2,1,0:T(8,128)(2,1)S(1)} collective-permute-done((bf16[1,128,1024]{2,1,0:T(8,128)(2,1)S(1)}, bf16[1,128,1024]{2,1,0:T(8,128)(2,1)S(1)}, u32[]{:S(2)}, u32[]{:S(2)}) %collective-permute-start.21) | collective-permute-done | bytes 262176 | tf_op jit(solution)/shard_map/ppermute | solution.py:28
  65.1 2.8 %collective-permute-done.11.refs_2_ = bf16[1,128,1024]{2,1,0:T(8,128)(2,1)S(1)} collective-permute-done((bf16[1,128,1024]{2,1,0:T(8,128)(2,1)S(1)}, bf16[1,128,1024]{2,1,0:T(8,128)(2,1)S(1)}, u32[]{:S(2)}, u32[]{:S(2)}) %collective-permute-start.11) | collective-permute-done | bytes 262176 | tf_op jit(solution)/shard_map/ppermute | solution.py:28
  67.9 1.1 %collective-permute-start.13 = (bf16[1,128,1024]{2,1,0:T(8,128)(2,1)S(1)}, bf16[1,128,1024]{2,1,0:T(8,128)(2,1)S(1)}, u32[]{:S(2)}, u32[]{:S(2)}) collective-permute-start(bf16[1,128,1024]{2,1,0:T(8,128)(2,1)S(1)} %collective-permute-done.11.refs_2_), channel_id=1, source_target_pairs={{0,16},{8,24},{16,0},{24,8},{1,17},{9,25},{17,1},{25,9},{2,18},{10... | collective-permute-start | bytes 786440 | tf_op jit(solution)/shard_map/ppermute | solution.py:44
  69.0 0.9 collective-permute-start.25
  69.9 1.5 %collective-permute-start.23 = (bf16[1,128,1024]{2,1,0:T(8,128)(2,1)S(1)}, bf16[1,128,1024]{2,1,0:T(8,128)(2,1)S(1)}, u32[]{:S(2)}, u32[]{:S(2)}) collective-permute-start(bf16[1,128,1024]{2,1,0:T(8,128)(2,1)S(1)} %collective-permute-done.21.refs_2_), channel_id=1, source_target_pairs={{0,4},{4,6},{6,2},{2,0},{1,5},{5,7},{7,3},{3,1},{8,12},{12,14},{14... | collective-permute-start | bytes 786440 | tf_op jit(solution)/shard_map/ppermute | solution.py:28
  71.5 2.0 %collective-permute-start.18 = (bf16[1,128,1024]{2,1,0:T(8,128)(2,1)S(1)}, bf16[1,128,1024]{2,1,0:T(8,128)(2,1)S(1)}, u32[]{:S(2)}, u32[]{:S(2)}) collective-permute-start(bf16[1,128,1024]{2,1,0:T(8,128)(2,1)S(1)} %collective-permute-done.9.refs_1_), channel_id=1, source_target_pairs={{0,16},{8,24},{16,0},{24,8},{1,17},{9,25},{17,1},{25,9},{2,18},{10... | collective-permute-start | bytes 786440 | tf_op jit(solution)/shard_map/ppermute | solution.py:44
  73.4 0.8 pad_maximum_fusion
  74.3 2.9 %collective-permute-done.13.refs_5_ = bf16[1,128,1024]{2,1,0:T(8,128)(2,1)S(1)} collective-permute-done((bf16[1,128,1024]{2,1,0:T(8,128)(2,1)S(1)}, bf16[1,128,1024]{2,1,0:T(8,128)(2,1)S(1)}, u32[]{:S(2)}, u32[]{:S(2)}) %collective-permute-start.13) | collective-permute-done | bytes 262176 | tf_op jit(solution)/shard_map/ppermute | solution.py:44
  77.1 1.5 %collective-permute-start.12 = (bf16[1,128,1024]{2,1,0:T(8,128)(2,1)S(1)}, bf16[1,128,1024]{2,1,0:T(8,128)(2,1)S(1)}, u32[]{:S(2)}, u32[]{:S(2)}) collective-permute-start(bf16[1,128,1024]{2,1,0:T(8,128)(2,1)S(1)} %collective-permute-done.11.refs_2_), channel_id=1, source_target_pairs={{0,4},{4,6},{6,2},{2,0},{1,5},{5,7},{7,3},{3,1},{8,12},{12,14},{14... | collective-permute-start | bytes 786440 | tf_op jit(solution)/shard_map/ppermute | solution.py:28
  78.7 4.1 %collective-permute-done.25.refs_5_ = bf16[1,128,1024]{2,1,0:T(8,128)(2,1)S(1)} collective-permute-done((bf16[1,128,1024]{2,1,0:T(8,128)(2,1)S(1)}, bf16[1,128,1024]{2,1,0:T(8,128)(2,1)S(1)}, u32[]{:S(2)}, u32[]{:S(2)}) %collective-permute-start.25) | collective-permute-done | bytes 262176 | tf_op jit(solution)/shard_map/ppermute | solution.py:44
  82.8 1.5 %collective-permute-start.14 = (bf16[1,128,1024]{2,1,0:T(8,128)(2,1)S(1)}, bf16[1,128,1024]{2,1,0:T(8,128)(2,1)S(1)}, u32[]{:S(2)}, u32[]{:S(2)}) collective-permute-start(bf16[1,128,1024]{2,1,0:T(8,128)(2,1)S(1)} %collective-permute-done.13.refs_5_), channel_id=1, source_target_pairs={{0,4},{4,6},{6,2},{2,0},{1,5},{5,7},{7,3},{3,1},{8,12},{12,14},{14... | collective-permute-start | bytes 786440 | tf_op jit(solution)/shard_map/ppermute | solution.py:28
  84.3 2.0 %collective-permute-start.24 = (bf16[1,128,1024]{2,1,0:T(8,128)(2,1)S(1)}, bf16[1,128,1024]{2,1,0:T(8,128)(2,1)S(1)}, u32[]{:S(2)}, u32[]{:S(2)}) collective-permute-start(bf16[1,128,1024]{2,1,0:T(8,128)(2,1)S(1)} %collective-permute-done.23.refs_0_), channel_id=1, source_target_pairs={{0,16},{8,24},{16,0},{24,8},{1,17},{9,25},{17,1},{25,9},{2,18},{10... | collective-permute-start | bytes 786440 | tf_op jit(solution)/shard_map/ppermute | solution.py:44
  86.3 1.8 %early.3.refs_6_ = f32[1024,1024]{1,0:T(8,128)S(1)} custom-call(bf16[1,128,1024]{2,1,0:T(8,128)(2,1)S(1)} %attend.3.refs_0_, bf16[1,128,1024]{2,1,0:T(8,128)(2,1)S(1)} %collective-permute-done.19.refs_1_, bf16[1,128,1024]{2,1,0:T(8,128)(2,1)S(1)} %collective-permute-done.21.refs_2_, bf16[1,128,1024]{2,1,0:T(8,128)(2,1)S(1)} %collective-permute-done.20.refs_3_, ...), custom_call_target="tpu_custom_call" | custom-call | flops 1610612736 | bytes 8388608 | tf_op jit(solution)/shard_map/early/pallas_call | solution.py:286
  88.1 1.8 %early.2.refs_6_ = f32[1024,1024]{1,0:T(8,128)S(1)} custom-call(bf16[1,128,1024]{2,1,0:T(8,128)(2,1)S(1)} %attend.2.refs_0_, bf16[1,128,1024]{2,1,0:T(8,128)(2,1)S(1)} %collective-permute-done.9.refs_1_, bf16[1,128,1024]{2,1,0:T(8,128)(2,1)S(1)} %collective-permute-done.11.refs_2_, bf16[1,128,1024]{2,1,0:T(8,128)(2,1)S(1)} %collective-permute-done.10.refs_3_, ...), custom_call_target="tpu_custom_call" | custom-call | flops 1610612736 | bytes 8388608 | tf_op jit(solution)/shard_map/early/pallas_call | solution.py:286
  89.9 0.8 collective-permute-done.24.refs_1_
  90.7 1.6 %finish.2.refs_7_ = bf16[1,1024,2048]{2,1,0:T(8,128)(2,1)} custom-call(bf16[1,128,1024]{2,1,0:T(8,128)(2,1)S(1)} %collective-permute-done.23.refs_0_, bf16[1,128,1024]{2,1,0:T(8,128)(2,1)S(1)} %collective-permute-done.24.refs_1_, bf16[512,512]{1,0:T(8,128)(2,1)S(1)} %join.1.refs_6_.refs_2_, bf16[512,512]{1,0:T(8,128)(2,1)S(1)} %collective-permute-done.15.refs_7_.refs_3_, ...), custom_call_target="tpu_custom_call" | custom-call | flops 536870912 | bytes 8388608 | tf_op jit(solution)/shard_map/finish/pallas_call | solution.py:311
  92.4 1.7 %finish.3 = bf16[1,1024,2048]{2,1,0:T(8,128)(2,1)} custom-call(bf16[1,128,1024]{2,1,0:T(8,128)(2,1)S(1)} %collective-permute-done.12.refs_0_, bf16[1,128,1024]{2,1,0:T(8,128)(2,1)S(1)} %collective-permute-done.14.refs_1_, bf16[512,512]{1,0:T(8,128)(2,1)S(1)} %join.1.refs_6_.refs_2_, ...), custom_call_target="tpu_custom_call", output_to_operand_aliasing={{}: (7, {})} | custom-call | flops 536870912 | bytes 8388608 | tf_op jit(solution)/shard_map/finish/pallas_call | solution.py:311
  (22 shorter events, 0.1 us)
Async XLA Ops:
  0.6 10.9 %collective-permute-start.2 = (bf16[1,128,512]{2,1,0:T(8,128)(2,1)}, bf16[1,128,512]{2,1,0:T(8,128)(2,1)S(1)}, u32[]{:S(2)}, u32[]{:S(2)}) collective-permute-start(bf16[1,128,512]{2,1,0:T(8,128)(2,1)} %refs_3_.1), channel_id=1, source_target_pairs={{0,2},{4,0},{6,4},{2,6},{1,3},{5,1},{7,5},{3,7},{8,10},{12,8},{14,... | collective-permute-start | bytes 393224 | tf_op jit(solution)/shard_map/ppermute | solution.py:28
  6.0 23.2 %collective-permute-start = (bf16[1,144,512]{2,1,0:T(8,128)(2,1)}, bf16[1,144,512]{2,1,0:T(8,128)(2,1)S(1)}, u32[]{:S(2)}, u32[]{:S(2)}) collective-permute-start(bf16[1,144,512]{2,1,0:T(8,128)(2,1)} %get-tuple-element.20.refs_1_), channel_id=1, source_target_pairs={{0,4},{4,6},{6,2},{2,0},{1,5},{5,7},{7,3},{3,1},{8,12},{12,14},{14... | collective-permute-start | bytes 442376 | tf_op jit(solution)/shard_map/ppermute | solution.py:28
  7.1 18.2 %collective-permute-start.1 = (bf16[1,128,512]{2,1,0:T(8,128)(2,1)}, bf16[1,128,512]{2,1,0:T(8,128)(2,1)S(1)}, u32[]{:S(2)}, u32[]{:S(2)}) collective-permute-start(bf16[1,128,512]{2,1,0:T(8,128)(2,1)} %refs_3_.1), channel_id=1, source_target_pairs={{0,4},{4,6},{6,2},{2,0},{1,5},{5,7},{7,3},{3,1},{8,12},{12,14},{14... | collective-permute-start | bytes 393224 | tf_op jit(solution)/shard_map/ppermute | solution.py:28
  9.1 20.0 %collective-permute-start.3 = (bf16[512,128]{1,0:T(8,128)(2,1)}, bf16[512,128]{1,0:T(8,128)(2,1)S(1)}, u32[]{:S(2)}, u32[]{:S(2)}) collective-permute-start(bf16[512,128]{1,0:T(8,128)(2,1)} %get-tuple-element.27), channel_id=1, source_target_pairs={{0,4},{4,6},{6,2},{2,0},{1,5},{5,7},{7,3},{3,1},{8,12},{12,14},{14... | collective-permute-start | bytes 393224 | tf_op jit(solution)/shard_map/ppermute | solution.py:28
  11.6 17.6 %collective-permute-start.4 = (bf16[512,128]{1,0:T(8,128)(2,1)}, bf16[512,128]{1,0:T(8,128)(2,1)S(1)}, u32[]{:S(2)}, u32[]{:S(2)}) collective-permute-start(bf16[512,128]{1,0:T(8,128)(2,1)} %get-tuple-element.28), channel_id=1, source_target_pairs={{0,6},{4,2},{6,0},{2,4},{1,7},{5,3},{7,1},{3,5},{8,14},{12,10},{14... | collective-permute-start | bytes 393224 | tf_op jit(solution)/shard_map/ppermute | solution.py:28
  11.6 17.6 %collective-permute-start.5 = (bf16[512,128]{1,0:T(8,128)(2,1)}, bf16[512,128]{1,0:T(8,128)(2,1)S(1)}, u32[]{:S(2)}, u32[]{:S(2)}) collective-permute-start(bf16[512,128]{1,0:T(8,128)(2,1)} %get-tuple-element.29), channel_id=1, source_target_pairs={{0,2},{4,0},{6,4},{2,6},{1,3},{5,1},{7,5},{3,7},{8,10},{12,8},{14,... | collective-permute-start | bytes 393224 | tf_op jit(solution)/shard_map/ppermute | solution.py:28
  20.6 1.0 %copy-start = (bf16[1,128,2048]{2,1,0:T(8,128)(2,1)S(1)}, bf16[1,128,2048]{2,1,0:T(8,128)(2,1)}, u32[]{:S(2)}) copy-start(bf16[1,128,2048]{2,1,0:T(8,128)(2,1)} %refs_2_.1) | copy-start | bytes 1572868
  21.7 0.9 copy-start.1
  22.6 0.9 copy-start.2
  23.5 0.8 copy-start.3
  25.3 10.6 %collective-permute-start.7 = (bf16[1,144,512]{2,1,0:T(8,128)(2,1)}, bf16[1,144,512]{2,1,0:T(8,128)(2,1)S(1)}, u32[]{:S(2)}, u32[]{:S(2)}) collective-permute-start(bf16[1,144,512]{2,1,0:T(8,128)(2,1)} %get-tuple-element.20.refs_1_), channel_id=1, source_target_pairs={{0,2},{4,0},{6,4},{2,6},{1,3},{5,1},{7,5},{3,7},{8,10},{12,8},{14,... | collective-permute-start | bytes 442376 | tf_op jit(solution)/shard_map/ppermute | solution.py:28
  29.2 9.8 %collective-permute-start.6 = (bf16[1,144,512]{2,1,0:T(8,128)(2,1)S(1)}, bf16[1,144,512]{2,1,0:T(8,128)(2,1)S(1)}, u32[]{:S(2)}, u32[]{:S(2)}) collective-permute-start(bf16[1,144,512]{2,1,0:T(8,128)(2,1)S(1)} %collective-permute-done.refs_1_), channel_id=1, source_target_pairs={{0,4},{4,6},{6,2},{2,0},{1,5},{5,7},{7,3},{3,1},{8,12},{12,14},{14... | collective-permute-start | bytes 442376 | tf_op jit(solution)/shard_map/ppermute | solution.py:28
  29.3 8.5 %collective-permute-start.8 = (bf16[1,128,512]{2,1,0:T(8,128)(2,1)S(1)}, bf16[1,128,512]{2,1,0:T(8,128)(2,1)S(1)}, u32[]{:S(2)}, u32[]{:S(2)}) collective-permute-start(bf16[1,128,512]{2,1,0:T(8,128)(2,1)S(1)} %collective-permute-done.2.refs_7_), channel_id=1, source_target_pairs={{0,2},{4,0},{6,4},{2,6},{1,3},{5,1},{7,5},{3,7},{8,10},{12,8},{14,... | collective-permute-start | bytes 393224 | tf_op jit(solution)/shard_map/ppermute | solution.py:28
  31.3 27.1 %collective-permute-start.15 = (bf16[512,512]{1,0:T(8,128)(2,1)S(1)}, bf16[512,512]{1,0:T(8,128)(2,1)S(1)}, u32[]{:S(2)}, u32[]{:S(2)}) collective-permute-start(bf16[512,512]{1,0:T(8,128)(2,1)S(1)} %join.1.refs_6_.refs_2_), channel_id=1, source_target_pairs={{0,16},{8,24},{16,0},{24,8},{1,17},{9,25},{17,1},{25,9},{2,18},{10... | collective-permute-start | bytes 1572872 | tf_op jit(solution)/shard_map/ppermute | solution.py:44
  40.2 10.8 %collective-permute-start.20 = (bf16[1,128,1024]{2,1,0:T(8,128)(2,1)S(1)}, bf16[1,128,1024]{2,1,0:T(8,128)(2,1)S(1)}, u32[]{:S(2)}, u32[]{:S(2)}) collective-permute-start(bf16[1,128,1024]{2,1,0:T(8,128)(2,1)S(1)} %attend.3.refs_0_), channel_id=1, source_target_pairs={{0,16},{8,24},{16,0},{24,8},{1,17},{9,25},{17,1},{25,9},{2,18},{10... | collective-permute-start | bytes 786440 | tf_op jit(solution)/shard_map/ppermute | solution.py:44
  41.5 11.4 %collective-permute-start.19 = (bf16[1,128,1024]{2,1,0:T(8,128)(2,1)S(1)}, bf16[1,128,1024]{2,1,0:T(8,128)(2,1)S(1)}, u32[]{:S(2)}, u32[]{:S(2)}) collective-permute-start(bf16[1,128,1024]{2,1,0:T(8,128)(2,1)S(1)} %attend.3.refs_0_), channel_id=1, source_target_pairs={{0,4},{4,6},{6,2},{2,0},{1,5},{5,7},{7,3},{3,1},{8,12},{12,14},{14... | collective-permute-start | bytes 786440 | tf_op jit(solution)/shard_map/ppermute | solution.py:28
  42.6 14.0 %collective-permute-start.10 = (bf16[1,128,1024]{2,1,0:T(8,128)(2,1)S(1)}, bf16[1,128,1024]{2,1,0:T(8,128)(2,1)S(1)}, u32[]{:S(2)}, u32[]{:S(2)}) collective-permute-start(bf16[1,128,1024]{2,1,0:T(8,128)(2,1)S(1)} %attend.2.refs_0_), channel_id=1, source_target_pairs={{0,16},{8,24},{16,0},{24,8},{1,17},{9,25},{17,1},{25,9},{2,18},{10... | collective-permute-start | bytes 786440 | tf_op jit(solution)/shard_map/ppermute | solution.py:44
  43.4 15.0 %collective-permute-start.9 = (bf16[1,128,1024]{2,1,0:T(8,128)(2,1)S(1)}, bf16[1,128,1024]{2,1,0:T(8,128)(2,1)S(1)}, u32[]{:S(2)}, u32[]{:S(2)}) collective-permute-start(bf16[1,128,1024]{2,1,0:T(8,128)(2,1)S(1)} %attend.2.refs_0_), channel_id=1, source_target_pairs={{0,4},{4,6},{6,2},{2,0},{1,5},{5,7},{7,3},{3,1},{8,12},{12,14},{14... | collective-permute-start | bytes 786440 | tf_op jit(solution)/shard_map/ppermute | solution.py:28
  50.9 20.5 %collective-permute-start.16 = (bf16[512,512]{1,0:T(8,128)(2,1)S(1)}, bf16[512,512]{1,0:T(8,128)(2,1)S(1)}, u32[]{:S(2)}, u32[]{:S(2)}) collective-permute-start(bf16[512,512]{1,0:T(8,128)(2,1)S(1)} %join.1.refs_6_.refs_2_), channel_id=1, source_target_pairs={{0,1},{1,0},{2,3},{3,2},{4,5},{5,4},{6,7},{7,6},{8,9},{9,8},{10,11... | collective-permute-start | bytes 1572872 | tf_op jit(solution)/shard_map/ppermute | solution.py:44
  52.9 8.0 %collective-permute-start.22 = (bf16[1,128,1024]{2,1,0:T(8,128)(2,1)S(1)}, bf16[1,128,1024]{2,1,0:T(8,128)(2,1)S(1)}, u32[]{:S(2)}, u32[]{:S(2)}) collective-permute-start(bf16[1,128,1024]{2,1,0:T(8,128)(2,1)S(1)} %collective-permute-done.19.refs_1_), channel_id=1, source_target_pairs={{0,16},{8,24},{16,0},{24,8},{1,17},{9,25},{17,1},{25,9},{2,18},{10... | collective-permute-start | bytes 786440 | tf_op jit(solution)/shard_map/ppermute | solution.py:44
  56.5 8.5 %collective-permute-start.21 = (bf16[1,128,1024]{2,1,0:T(8,128)(2,1)S(1)}, bf16[1,128,1024]{2,1,0:T(8,128)(2,1)S(1)}, u32[]{:S(2)}, u32[]{:S(2)}) collective-permute-start(bf16[1,128,1024]{2,1,0:T(8,128)(2,1)S(1)} %collective-permute-done.19.refs_1_), channel_id=1, source_target_pairs={{0,4},{4,6},{6,2},{2,0},{1,5},{5,7},{7,3},{3,1},{8,12},{12,14},{14... | collective-permute-start | bytes 786440 | tf_op jit(solution)/shard_map/ppermute | solution.py:28
  58.4 9.5 %collective-permute-start.11 = (bf16[1,128,1024]{2,1,0:T(8,128)(2,1)S(1)}, bf16[1,128,1024]{2,1,0:T(8,128)(2,1)S(1)}, u32[]{:S(2)}, u32[]{:S(2)}) collective-permute-start(bf16[1,128,1024]{2,1,0:T(8,128)(2,1)S(1)} %collective-permute-done.9.refs_1_), channel_id=1, source_target_pairs={{0,4},{4,6},{6,2},{2,0},{1,5},{5,7},{7,3},{3,1},{8,12},{12,14},{14... | collective-permute-start | bytes 786440 | tf_op jit(solution)/shard_map/ppermute | solution.py:28
  58.4 27.8 %collective-permute-start.17 = (bf16[512,512]{1,0:T(8,128)(2,1)S(1)}, bf16[512,512]{1,0:T(8,128)(2,1)S(1)}, u32[]{:S(2)}, u32[]{:S(2)}) collective-permute-start(bf16[512,512]{1,0:T(8,128)(2,1)S(1)} %collective-permute-done.15.refs_7_.refs_3_), channel_id=1, source_target_pairs={{0,1},{1,0},{2,3},{3,2},{4,5},{5,4},{6,7},{7,6},{8,9},{9,8},{10,11... | collective-permute-start | bytes 1572872 | tf_op jit(solution)/shard_map/ppermute | solution.py:44
  67.9 9.2 %collective-permute-start.13 = (bf16[1,128,1024]{2,1,0:T(8,128)(2,1)S(1)}, bf16[1,128,1024]{2,1,0:T(8,128)(2,1)S(1)}, u32[]{:S(2)}, u32[]{:S(2)}) collective-permute-start(bf16[1,128,1024]{2,1,0:T(8,128)(2,1)S(1)} %collective-permute-done.11.refs_2_), channel_id=1, source_target_pairs={{0,16},{8,24},{16,0},{24,8},{1,17},{9,25},{17,1},{25,9},{2,18},{10... | collective-permute-start | bytes 786440 | tf_op jit(solution)/shard_map/ppermute | solution.py:44
  69.0 13.8 %collective-permute-start.25 = (bf16[1,128,1024]{2,1,0:T(8,128)(2,1)S(1)}, bf16[1,128,1024]{2,1,0:T(8,128)(2,1)S(1)}, u32[]{:S(2)}, u32[]{:S(2)}) collective-permute-start(bf16[1,128,1024]{2,1,0:T(8,128)(2,1)S(1)} %collective-permute-done.21.refs_2_), channel_id=1, source_target_pairs={{0,16},{8,24},{16,0},{24,8},{1,17},{9,25},{17,1},{25,9},{2,18},{10... | collective-permute-start | bytes 786440 | tf_op jit(solution)/shard_map/ppermute | solution.py:44
  69.9 14.4 %collective-permute-start.23 = (bf16[1,128,1024]{2,1,0:T(8,128)(2,1)S(1)}, bf16[1,128,1024]{2,1,0:T(8,128)(2,1)S(1)}, u32[]{:S(2)}, u32[]{:S(2)}) collective-permute-start(bf16[1,128,1024]{2,1,0:T(8,128)(2,1)S(1)} %collective-permute-done.21.refs_2_), channel_id=1, source_target_pairs={{0,4},{4,6},{6,2},{2,0},{1,5},{5,7},{7,3},{3,1},{8,12},{12,14},{14... | collective-permute-start | bytes 786440 | tf_op jit(solution)/shard_map/ppermute | solution.py:28
  71.5 16.6 %collective-permute-start.18 = (bf16[1,128,1024]{2,1,0:T(8,128)(2,1)S(1)}, bf16[1,128,1024]{2,1,0:T(8,128)(2,1)S(1)}, u32[]{:S(2)}, u32[]{:S(2)}) collective-permute-start(bf16[1,128,1024]{2,1,0:T(8,128)(2,1)S(1)} %collective-permute-done.9.refs_1_), channel_id=1, source_target_pairs={{0,16},{8,24},{16,0},{24,8},{1,17},{9,25},{17,1},{25,9},{2,18},{10... | collective-permute-start | bytes 786440 | tf_op jit(solution)/shard_map/ppermute | solution.py:44
  77.1 15.2 %collective-permute-start.12 = (bf16[1,128,1024]{2,1,0:T(8,128)(2,1)S(1)}, bf16[1,128,1024]{2,1,0:T(8,128)(2,1)S(1)}, u32[]{:S(2)}, u32[]{:S(2)}) collective-permute-start(bf16[1,128,1024]{2,1,0:T(8,128)(2,1)S(1)} %collective-permute-done.11.refs_2_), channel_id=1, source_target_pairs={{0,4},{4,6},{6,2},{2,0},{1,5},{5,7},{7,3},{3,1},{8,12},{12,14},{14... | collective-permute-start | bytes 786440 | tf_op jit(solution)/shard_map/ppermute | solution.py:28
  82.8 9.6 %collective-permute-start.14 = (bf16[1,128,1024]{2,1,0:T(8,128)(2,1)S(1)}, bf16[1,128,1024]{2,1,0:T(8,128)(2,1)S(1)}, u32[]{:S(2)}, u32[]{:S(2)}) collective-permute-start(bf16[1,128,1024]{2,1,0:T(8,128)(2,1)S(1)} %collective-permute-done.13.refs_5_), channel_id=1, source_target_pairs={{0,4},{4,6},{6,2},{2,0},{1,5},{5,7},{7,3},{3,1},{8,12},{12,14},{14... | collective-permute-start | bytes 786440 | tf_op jit(solution)/shard_map/ppermute | solution.py:28
  84.3 6.4 %collective-permute-start.24 = (bf16[1,128,1024]{2,1,0:T(8,128)(2,1)S(1)}, bf16[1,128,1024]{2,1,0:T(8,128)(2,1)S(1)}, u32[]{:S(2)}, u32[]{:S(2)}) collective-permute-start(bf16[1,128,1024]{2,1,0:T(8,128)(2,1)S(1)} %collective-permute-done.23.refs_0_), channel_id=1, source_target_pairs={{0,16},{8,24},{16,0},{24,8},{1,17},{9,25},{17,1},{25,9},{2,18},{10... | collective-permute-start | bytes 786440 | tf_op jit(solution)/shard_map/ppermute | solution.py:44
